TPU v7x, 32 devices: a whole 2x2x4 slice. The times are simulated.
32 devices in a mesh: gx: 8 (over z, x), gy: 4 (over y, core).
Axes of the slice: x: 2, y: 2, z: 4, core: 2. Of those that a mesh axis runs over, the one named last changes fastest.
Arguments:
- source: float32 [5, 4, 4, 4, 16, 8, 128], P(None, None, None, None, 'gx', 'gy'), may hold values from -18 to 18
- jacobian: float32 [3, 5, 5, 16, 8, 128], P(None, None, None, 'gx', 'gy'), may hold values from -1.8 to 1.8
- damping: float32 [16, 8, 128], P('gx', 'gy'), may hold values from 0.3 to 1.2
- orient: int32 [3, 16, 8, 128], P(None, 'gx', 'gy'), may hold values 0 or 1
- smoother: bfloat16 [5, 5, 4, 4, 4, 16, 8, 128], P(None, None, None, None, None, 'gx', 'gy'), may hold values from -0.4 to 0.4, as said below
- coarse_smoother: bfloat16 [5, 5, 2, 2, 2, 16, 8, 128], P(None, None, None, None, None, 'gx', 'gy'), may hold values from -0.61 to 1.11, as said below
Outputs:
- corrected: float32 [5, 4, 4, 4, 16, 8, 128], P(None, None, None, None, 'gx', 'gy')
Inputs may be any that keep to these rules, and one draw needn't show every extreme that they name: `smoother`: each 5 x 5 block is a positive node scale times the identity plus independent entries. `coarse_smoother`: each 5 x 5 block is a positive node scale times the identity plus independent entries.
All inputs are finite; a program needn't handle non-finite values. No bound on the sum of `orient` on one device may be relied on, other than what follows from the above.
Results may differ from a plain program's by a relative error of at most 0.0003.
Values sent between devices are 32-bit elements; how exact they have to be, the bound alone decides.
No kernel may reach another device: no remote copies, remote signals or barrier semaphores. Data moves between devices by JAX's collectives and lax.ppermute only.
A program may use at most 64 MiB of HBM per device.

v0:
```python
import functools
import math

import jax
import jax.numpy as jnp
import numpy as np
from jax import lax
from jax.experimental import pallas as pl
from jax.experimental.pallas import tpu as pltpu
from jax.sharding import PartitionSpec as P


F32 = jnp.float32
OMEGA = 0.8
H4 = 3.0
ROOT = 1.0 / math.sqrt(5.0)
NEAR = (1.0 + ROOT) / 2.0
FAR = (1.0 - ROOT) / 2.0


def lobatto_slopes():
    points = np.array([-1.0, -ROOT, ROOT, 1.0])
    weights = np.ones(4)
    for i in range(4):
        for j in range(4):
            if i != j:
                weights[i] = weights[i] / (points[i] - points[j])
    slopes = np.zeros((4, 4))
    for i in range(4):
        for j in range(4):
            if i != j:
                slopes[i, j] = weights[j] / weights[i] / (points[i] - points[j])
        slopes[i, i] = -np.sum(slopes[i])
    return slopes


D4 = lobatto_slopes()


def rows():
    return lax.broadcasted_iota(jnp.int32, (8, 128), 0)


def x_low():
    return (rows() & 2) == 0


def y_low():
    return (rows() & 1) == 0


def c_low():
    return (rows() & 4) == 0


def sroll(value, shift):
    return pltpu.roll(value, shift % 8, 0)


def lroll(value, shift):
    return pltpu.roll(value, shift % 128, 1)


def twice(value):
    return jnp.concatenate([value, value], axis=0)


def axis_low(direction):
    return (x_low(), 2) if direction == 0 else (y_low(), 1)


def pack_low(first, second, direction):
    low, step = axis_low(direction)
    return jnp.where(low, first, sroll(second, step))


def pack_high(first, second, direction):
    low, step = axis_low(direction)
    return jnp.where(low, sroll(first, -step), second)


def slopes_along(u0, u1, u2, u3):
    e0, o0, e1, o1 = u0 + u3, u0 - u3, u1 + u2, u1 - u2
    diff = e1 - e0
    even_a = float((D4[0, 1] + D4[0, 2]) / 2.0) * diff
    even_b = float((D4[1, 2] - 0.0) / 2.0) * diff
    odd_a = float((D4[0, 0] - D4[0, 3]) / 2.0) * o0 + float((D4[0, 1] - D4[0, 2]) / 2.0) * o1
    odd_b = float((D4[1, 0] - D4[1, 3]) / 2.0) * o0 - float(D4[1, 2] / 2.0) * o1
    return even_a + odd_a, even_b + odd_b, odd_b - even_b, odd_a - even_a


def mix(matrix, fields):
    out = []
    for o in range(5):
        total = matrix[o][0] * fields[0]
        for i in range(1, 5):
            total = total + matrix[o][i] * fields[i]
        out.append(total)
    return out


def parity(axis):
    return lax.rem(lax.axis_index(axis), 2) == 0


def put_pair(even_ref, odd_ref, index, low_face, high_face, is_even):
    even_ref[index] = jnp.where(is_even, high_face, low_face)
    odd_ref[index] = jnp.where(is_even, low_face, high_face)


def fine_faces(u_ref, flag_ref, xe, xo, ye, yo):
    even_x, even_y = parity("gx"), parity("gy")
    fx, fy = flag_ref[0] != 0, flag_ref[1] != 0
    for v in range(5):
        for n in range(4):
            low = pack_low(u_ref[v, 0, n, 0], u_ref[v, 0, n, 1], 0)
            h = [jnp.where(fx, u_ref[v, 3, 3 - n, q], u_ref[v, 3, n, q]) for q in range(2)]
            put_pair(xe, xo, (v, n), low, pack_high(h[0], h[1], 0), even_x)
            low = pack_low(u_ref[v, n, 0, 0], u_ref[v, n, 0, 1], 1)
            h = [jnp.where(fy, u_ref[v, 3 - n, 3, q], u_ref[v, n, 3, q]) for q in range(2)]
            put_pair(ye, yo, (v, n), low, pack_high(h[0], h[1], 1), even_y)


def first_kernel(src_hbm, smooth_hbm, orient_ref, src_ref, smooth_ref, u_ref, flag_ref, xe, xo, ye, yo, sems):
    copies = []
    for slot, a in enumerate((0, 3, 1, 2)):
        pair = (
            pltpu.make_async_copy(src_hbm.at[:, a], src_ref.at[:, a], sems.at[0, slot]),
            pltpu.make_async_copy(smooth_hbm.at[:, a], smooth_ref.at[:, a], sems.at[1, slot]),
        )
        for one in pair:
            one.start()
        copies.append((a, pair))
    for d in range(3):
        flag_ref[d] = twice(orient_ref[d])
    for a, pair in copies:
        for one in pair:
            one.wait()

        def one_line(b, carry, a=a):
            src = [[src_ref[v, a, b, q] for q in range(2)] for v in range(5)]
            for o in range(5):
                total = [None, None]
                for i in range(5):
                    block = smooth_ref[5 * o + i, a, b].astype(F32)
                    for q in range(2):
                        term = block[8 * q : 8 * q + 8] * src[i][q]
                        total[q] = term if i == 0 else total[q] + term
                for q in range(2):
                    u_ref[o, a, b, q] = OMEGA * total[q]
            return carry

        lax.fori_loop(0, 4, one_line, 0)
    fine_faces(u_ref, flag_ref, xe, xo, ye, yo)


def prepare_tables(jac_ref, damp_ref, jac8_ref, damp8_ref, face_ref):
    damp = twice(damp_ref[...])
    damp8_ref[...] = damp
    for d in range(3):
        for k in range(25):
            value = twice(jac_ref[25 * d + k])
            jac8_ref[25 * d + k] = value
            if d < 2:
                low, step = axis_low(d)
                diagonal = k % 6 == 0
                upper = H4 * (value - damp if diagonal else value)
                lower = H4 * (value + damp if diagonal else value)
                face_ref[2 * d, k] = jnp.where(low, sroll(upper, -step), upper)
                face_ref[2 * d + 1, k] = jnp.where(low, lower, sroll(lower, step))


def volume(src_ref, u_ref, flag_ref, jac_ref, damp_ref, acc_ref):
    damp = H4 * damp_ref[...]

    def jacobian(d):
        return [[jac_ref[25 * d + 5 * o + i] for i in range(5)] for o in range(5)]

    def along(direction):
        low, step = axis_low(direction)
        flag = flag_ref[direction] != 0
        flag_before = sroll(flag_ref[direction], step) != 0

        def at(v, n, other, q):
            return (v, n, other, q) if direction == 0 else (v, other, n, q)

        def step_fn(j, carry):
            other, q = j // 2, j % 2
            u = [[u_ref[at(v, n, other, q)] for n in range(4)] for v in range(5)]
            waves = []
            jumps = []
            for v in range(5):
                back_low, back_high = u_ref[at(v, 0, 3 - other, q)], u_ref[at(v, 3, 3 - other, q)]
                right = sroll(jnp.where(flag_before, back_low, u[v][0]), -step)
                left = sroll(jnp.where(flag, back_high, u[v][3]), step)
                jump_right = jnp.where(low, right, 0.0) - u[v][3]
                jump_left = jnp.where(low, 0.0, left) - u[v][0]
                w = list(slopes_along(*u[v]))
                w[3] = w[3] + H4 * jump_right
                w[0] = w[0] - H4 * jump_left
                waves.append(w)
                jumps.append((damp * jump_left, None, None, damp * jump_right))
            matrix = jacobian(direction)
            for n in range(4):
                flux = mix(matrix, [waves[v][n] for v in range(5)])
                for v in range(5):
                    if direction == 0:
                        total = src_ref[at(v, n, other, q)] - 2.0 * u[v][n]
                    else:
                        total = acc_ref[at(v, n, other, q)]
                    total = total - flux[v]
                    if jumps[v][n] is not None:
                        total = total + jumps[v][n]
                    acc_ref[at(v, n, other, q)] = total
            return carry

        lax.fori_loop(0, 8, step_fn, 0)

    along(0)
    along(1)

    low = c_low()
    flag = jnp.where(low, lroll(flag_ref[2], 1), flag_ref[2]) != 0
    damp_z = damp
    coef = [
        [jnp.where(low, float(D4[2 * p, c]), float(D4[2 * p + 1, c ^ 1])).astype(F32) for c in range(4)]
        for p in range(2)
    ]

    def step_z(j, carry):
        a0, b = j // 4, j % 4
        here = (a0, 3 - a0)
        u = [[[u_ref[v, a, b, q] for q in range(2)] for v in range(5)] for a in here]
        turned = [[[sroll(u[s][v][q], 4) for q in range(2)] for v in range(5)] for s in range(2)]
        beside = []
        for s in range(2):
            line = []
            for v in range(5):
                face = jnp.where(low, turned[s][v][1], turned[s][v][0])
                line.append(jnp.where(low, lroll(face, 1), lroll(face, -1)))
            beside.append(line)
        matrix = jacobian(2)
        for s in range(2):
            waves = [[], []]
            jumps = []
            for v in range(5):
                own = jnp.where(low, u[s][v][0], u[s][v][1])
                jump = jnp.where(flag, beside[1 - s][v], beside[s][v]) - own
                jumps.append(damp_z * jump)
                lifted = H4 * jump
                for p in range(2):
                    w = coef[p][0] * u[s][v][0] + coef[p][1] * turned[s][v][0]
                    w = w + (coef[p][2] * u[s][v][1] + coef[p][3] * turned[s][v][1])
                    w = w - jnp.where(low, lifted, 0.0) if p == 0 else w + jnp.where(low, 0.0, lifted)
                    waves[p].append(w)
            for p in range(2):
                flux = mix(matrix, waves[p])
                for v in range(5):
                    part = jnp.where(low, jumps[v], 0.0) if p == 0 else jnp.where(low, 0.0, jumps[v])
                    acc_ref[v, here[s], b, p] = acc_ref[v, here[s], b, p] - flux[v] + part
        return carry

    lax.fori_loop(0, 8, step_z, 0)


def first_volume_kernel(src_ref, u_ref, flag_ref, jac_ref, damp_ref, acc_ref, jac8_ref, damp8_ref, face_ref):
    prepare_tables(jac_ref, damp_ref, jac8_ref, damp8_ref, face_ref)
    volume(src_ref, u_ref, flag_ref, jac8_ref, damp8_ref, acc_ref)


def second_volume_kernel(src_ref, u_ref, flag_ref, jac8_ref, damp8_ref, acc_ref):
    volume(src_ref, u_ref, flag_ref, jac8_ref, damp8_ref, acc_ref)


def remote_parts(even_refs, odd_refs, flag_ref, face_ref, part_ref):
    for d, axis in ((0, "gx"), (1, "gy")):
        is_even = parity(axis)
        low, step = axis_low(d)
        flag = flag_ref[d]
        flag = jnp.where(low, sroll(flag, -step), flag) != 0
        even, odd = even_refs[d], odd_refs[d]
        matrix = [[face_ref[2 * d, 5 * o + i] for i in range(5)] for o in range(5)]
        for n in range(4):
            take = lambda v, m: jnp.where(is_even, even[v, m], odd[v, m])
            right = [jnp.where(flag, take(v, 3 - n), take(v, n)) for v in range(5)]
            for v, value in enumerate(mix(matrix, right)):
                part_ref[2 * d, v, n, 0] = jnp.where(low, 0.0, -sroll(value, step))
                part_ref[2 * d, v, n, 1] = jnp.where(low, 0.0, -value)
        matrix = [[face_ref[2 * d + 1, 5 * o + i] for i in range(5)] for o in range(5)]
        for n in range(4):
            left = [jnp.where(is_even, odd[v, n], even[v, n]) for v in range(5)]
            for v, value in enumerate(mix(matrix, left)):
                part_ref[2 * d + 1, v, n, 0] = jnp.where(low, value, 0.0)
                part_ref[2 * d + 1, v, n, 1] = jnp.where(low, sroll(value, -step), 0.0)


def whole(acc_ref, part_ref, v, a, b, q):
    total = acc_ref[v, a, b, q]
    if a == 3:
        total = total + part_ref[0, v, b, q]
    if a == 0:
        total = total + part_ref[1, v, b, q]
    if b == 3:
        total = total + part_ref[2, v, a, q]
    if b == 0:
        total = total + part_ref[3, v, a, q]
    return total


def second_kernel(
    acc_ref, u_ref, smooth_ref, flag_ref, face_ref, rxe, rxo, rye, ryo, out_ref, xe, xo, ye, yo, part_ref
):
    remote_parts((rxe, rye), (rxo, ryo), flag_ref, face_ref, part_ref)
    for a in range(4):
        for b in range(4):
            left = [[whole(acc_ref, part_ref, v, a, b, q) for q in range(2)] for v in range(5)]
            for o in range(5):
                total = [None, None]
                for i in range(5):
                    block = smooth_ref[5 * o + i, a, b].astype(F32)
                    for q in range(2):
                        term = block[8 * q : 8 * q + 8] * left[i][q]
                        total[q] = term if i == 0 else total[q] + term
                for q in range(2):
                    out_ref[o, a, b, q] = u_ref[o, a, b, q] + OMEGA * total[q]
    fine_faces(out_ref, flag_ref, xe, xo, ye, yo)


def coarse_smooth(smooth_ref, fields):
    out = [[[None, None], [None, None]] for _ in range(5)]
    for i in range(2):
        for o in range(5):
            total = [None, None]
            for k in range(5):
                block = smooth_ref[5 * o + k, i].astype(F32)
                for j in range(2):
                    term = block[8 * j : 8 * j + 8] * fields[k][i][j]
                    total[j] = term if k == 0 else total[j] + term
            for j in range(2):
                out[o][i][j] = OMEGA * total[j]
    return out


def coarse_faces(field, flag_ref, xe, xo, ye, yo):
    even_x, even_y = parity("gx"), parity("gy")
    fx, fy = flag_ref[0] != 0, flag_ref[1] != 0
    for v in range(5):
        c = field[v]
        low = pack_low(c[0][0], c[0][1], 0)
        h = [jnp.where(fx, c[1][1 - j], c[1][j]) for j in range(2)]
        put_pair(xe, xo, v, low, pack_high(h[0], h[1], 0), even_x)
        low = pack_low(c[0][0], c[1][0], 1)
        h = [jnp.where(fy, c[1 - i][1], c[i][1]) for i in range(2)]
        put_pair(ye, yo, v, low, pack_high(h[0], h[1], 1), even_y)


def restrict_kernel(
    acc_ref, flag_ref, face_ref, smooth_ref, rxe, rxo, rye, ryo, rhs_ref, c_ref, xe, xo, ye, yo, part_ref
):
    remote_parts((rxe, rye), (rxo, ryo), flag_ref, face_ref, part_ref)
    low = c_low()
    rhs = [[[None, None], [None, None]] for _ in range(5)]
    for v in range(5):
        halves = [[[None, None], [None, None]] for _ in range(2)]
        for q in range(2):
            for b in range(4):
                r = [whole(acc_ref, part_ref, v, a, b, q) for a in range(4)]
                ends = (r[0] + NEAR * r[1] + FAR * r[2], r[3] + NEAR * r[2] + FAR * r[1])
                near = (1.0, NEAR, FAR, 0.0)[b], (0.0, FAR, NEAR, 1.0)[b]
                for i in range(2):
                    for j in range(2):
                        if near[j] == 0.0:
                            continue
                        term = ends[i] if near[j] == 1.0 else near[j] * ends[i]
                        halves[q][i][j] = term if halves[q][i][j] is None else halves[q][i][j] + term
        for i in range(2):
            for j in range(2):
                first, second = halves[0][i][j], halves[1][i][j]
                middle = jnp.where(low, second, first)
                value = jnp.where(low, first, second) + FAR * middle + NEAR * sroll(middle, 4)
                rhs[v][i][j] = value
                rhs_ref[v, i, j] = value
    c = coarse_smooth(smooth_ref, rhs)
    for v in range(5):
        for i in range(2):
            for j in range(2):
                c_ref[v, i, j] = c[v][i][j]
    coarse_faces(c, flag_ref, xe, xo, ye, yo)


def coarse_step(c_ref, rhs_ref, smooth_ref, flag_ref, jac_ref, damp_ref, rxe, rxo, rye, ryo):
    damp = 0.5 * damp_ref[...]
    c = [[[c_ref[v, i, j] for j in range(2)] for i in range(2)] for v in range(5)]
    acc = [[[rhs_ref[v, i, j] - 2.0 * c[v][i][j] for j in range(2)] for i in range(2)] for v in range(5)]
    for d, axis in ((0, "gx"), (1, "gy")):
        is_even = parity(axis)
        low, step = axis_low(d)
        flag = flag_ref[d] != 0
        matrix = [[jac_ref[25 * d + 5 * o + i] for i in range(5)] for o in range(5)]
        even, odd = ((rxe, rxo), (rye, ryo))[d]
        at = (lambda n, m: (n, m)) if d == 0 else (lambda n, m: (m, n))
        waves = [[[None] * 5, [None] * 5] for _ in range(2)]
        for v in range(5):
            got_right = jnp.where(is_even, even[v], odd[v])
            got_left = jnp.where(is_even, odd[v], even[v])
            lo = [c[v][at(0, m)[0]][at(0, m)[1]] for m in range(2)]
            hi = [c[v][at(1, m)[0]][at(1, m)[1]] for m in range(2)]
            right = [
                jnp.where(low, sroll(lo[0], -step), sroll(got_right, step)),
                jnp.where(low, sroll(lo[1], -step), got_right),
            ]
            right = [jnp.where(flag, right[1 - m], right[m]) for m in range(2)]
            left = [sroll(jnp.where(flag, hi[1 - m], hi[m]), step) for m in range(2)]
            left = [jnp.where(low, got_left, left[0]), jnp.where(low, sroll(got_left, -step), left[1])]
            for m in range(2):
                waves[1][m][v] = 0.5 * (right[m] - lo[m])
                waves[0][m][v] = 0.5 * (hi[m] - left[m])
                i, j = at(1, m)
                acc[v][i][j] = acc[v][i][j] + damp * (right[m] - hi[m])
                i, j = at(0, m)
                acc[v][i][j] = acc[v][i][j] + damp * (left[m] - lo[m])
        for n in range(2):
            for m in range(2):
                i, j = at(n, m)
                for v, value in enumerate(mix(matrix, waves[n][m])):
                    acc[v][i][j] = acc[v][i][j] - value
    low = c_low()
    flag = jnp.where(low, lroll(flag_ref[2], 1), flag_ref[2]) != 0
    half = jnp.where(low, 0.5, -0.5).astype(F32)
    matrix = [[jac_ref[50 + 5 * o + i] for i in range(5)] for o in range(5)]
    turned = [[[sroll(c[v][i][j], 4) for j in range(2)] for i in range(2)] for v in range(5)]
    beside = [
        [[jnp.where(low, lroll(t, 1), lroll(t, -1)) for t in turned[v][i]] for i in range(2)] for v in range(5)
    ]
    for i in range(2):
        for j in range(2):
            wave = []
            for v in range(5):
                next_to = jnp.where(flag, beside[v][1 - i][j], beside[v][i][j])
                wave.append(half * (turned[v][i][j] - next_to))
                acc[v][i][j] = acc[v][i][j] + damp * (next_to - c[v][i][j])
            for v, value in enumerate(mix(matrix, wave)):
                acc[v][i][j] = acc[v][i][j] - value
    change = coarse_smooth(smooth_ref, acc)
    return [[[c[v][i][j] + change[v][i][j] for j in range(2)] for i in range(2)] for v in range(5)]


def coarse_kernel(
    c_ref, rhs_ref, smooth_ref, flag_ref, jac_ref, damp_ref, rxe, rxo, rye, ryo, out_ref, xe, xo, ye, yo
):
    c = coarse_step(c_ref, rhs_ref, smooth_ref, flag_ref, jac_ref, damp_ref, rxe, rxo, rye, ryo)
    for v in range(5):
        for i in range(2):
            for j in range(2):
                out_ref[v, i, j] = c[v][i][j]
    coarse_faces(c, flag_ref, xe, xo, ye, yo)


def spread(first, second):
    return first, NEAR * first + FAR * second, FAR * first + NEAR * second, second


def last_kernel(
    c_ref, rhs_ref, smooth_ref, flag_ref, jac_ref, damp_ref, rxe, rxo, rye, ryo, second_ref, out_hbm, out_ref, sems
):
    c = coarse_step(c_ref, rhs_ref, smooth_ref, flag_ref, jac_ref, damp_ref, rxe, rxo, rye, ryo)
    low = c_low()
    copies = []
    for v in range(5):
        by_c = [[None, None], [None, None]]
        for i in range(2):
            for j in range(2):
                value = c[v][i][j]
                inner = FAR * value + NEAR * sroll(value, 4)
                by_c[i][j] = (jnp.where(low, value, inner), jnp.where(low, inner, value))
        for q in range(2):
            lines = [spread(by_c[i][0][q], by_c[i][1][q]) for i in range(2)]
            for b in range(4):
                for a, value in enumerate(spread(lines[0][b], lines[1][b])):
                    out_ref[v, a, b, q] = second_ref[v, a, b, q] + value
        copy = pltpu.make_async_copy(out_ref.at[v], out_hbm.at[v], sems.at[v])
        copy.start()
        copies.append(copy)
    for copy in copies:
        copy.wait()


FINE = (5, 4, 4, 2, 8, 128)
FINE_MESSAGE = (5, 4, 8, 128)
COARSE = (5, 2, 2, 8, 128)
COARSE_MESSAGE = (5, 8, 128)


def vmem(shape, dtype=F32):
    return pltpu.VMEM(shape, dtype)


def here(array):
    return pltpu.with_memory_space_constraint(array, pltpu.VMEM)


def call(kernel, args, outs, in_hbm=(), out_hbm=(), scratch=(), flops=0):
    in_specs = [
        pl.BlockSpec(memory_space=pltpu.HBM if k in in_hbm else pltpu.VMEM) for k in range(len(args))
    ]
    out_specs = [
        pl.BlockSpec(memory_space=pltpu.HBM if k in out_hbm else pltpu.VMEM) for k in range(len(outs))
    ]
    args = [pltpu.with_memory_space_constraint(a, pltpu.HBM) if k in in_hbm else here(a) for k, a in enumerate(args)]
    return pl.pallas_call(
        kernel,
        out_shape=outs,
        in_specs=in_specs,
        out_specs=out_specs,
        scratch_shapes=scratch,
        compiler_params=pltpu.CompilerParams(vmem_limit_bytes=8 * 2**20),
        cost_estimate=pl.CostEstimate(flops=flops, bytes_accessed=4 * 2**20, transcendentals=0),
    )(*args)


def partners(axis):
    size = lax.axis_size(axis)
    even = [(i, i ^ 1) for i in range(size)]
    odd = [(i, (i - 1) % size if i % 2 == 0 else (i + 1) % size) for i in range(size)]
    return even, odd


def exchange(xe, xo, ye, yo):
    even_x, odd_x = partners("gx")
    even_y, odd_y = partners("gy")
    xo = lax.ppermute(xo, "gx", odd_x)
    xe = lax.ppermute(xe, "gx", even_x)
    yo = lax.ppermute(yo, "gy", odd_y)
    ye = lax.ppermute(ye, "gy", even_y)
    return xe, xo, ye, yo


def body(source, jacobian, damping, orient, smoother, coarse_smoother):
    source = source.reshape(FINE)
    smoother = smoother.reshape(25, 4, 4, 16, 128)
    coarse_smoother = coarse_smoother.reshape(25, 2, 16, 128)
    jacobian = jacobian.reshape(75, 4, 128)
    damping = damping.reshape(4, 128)
    orient = orient.reshape(3, 4, 128)
    fine_messages = [vmem(FINE_MESSAGE)] * 4
    coarse_messages = [vmem(COARSE_MESSAGE)] * 4

    source, smoother, first, flag, *sent = call(
        first_kernel,
        (source, smoother, orient),
        [vmem(FINE), vmem(smoother.shape, smoother.dtype), vmem(FINE), vmem((3, 8, 128), jnp.int32)] + fine_messages,
        in_hbm=(0, 1),
        scratch=[pltpu.SemaphoreType.DMA((2, 4))],
        flops=2 * 25 * 64 * 512,
    )
    got = exchange(*sent)
    acc, jac8, damp8, face = call(
        first_volume_kernel,
        (source, first, flag, jacobian, damping),
        [vmem(FINE), vmem((75, 8, 128)), vmem((8, 128)), vmem((4, 25, 8, 128))],
        flops=9 * 2**20,
    )
    part = pltpu.VMEM((4, 5, 4, 2, 8, 128), F32)
    second, *sent = call(
        second_kernel,
        (acc, first, smoother, flag, face, *got),
        [vmem(FINE)] + fine_messages,
        scratch=[part],
        flops=3 * 2**20,
    )
    got = exchange(*sent)
    (acc,) = call(second_volume_kernel, (source, second, flag, jac8, damp8), [vmem(FINE)], flops=9 * 2**20)
    rhs, coarse, *sent = call(
        restrict_kernel,
        (acc, flag, face, coarse_smoother, *got),
        [vmem(COARSE), vmem(COARSE)] + coarse_messages,
        scratch=[part],
        flops=3 * 2**20,
    )
    got = exchange(*sent)
    coarse, *sent = call(
        coarse_kernel,
        (coarse, rhs, coarse_smoother, flag, jac8, damp8, *got),
        [vmem(COARSE)] + coarse_messages,
        flops=2**20,
    )
    got = exchange(*sent)
    (out,) = call(
        last_kernel,
        (coarse, rhs, coarse_smoother, flag, jac8, damp8, *got, second),
        [jax.ShapeDtypeStruct(FINE, F32)],
        out_hbm=(0,),
        scratch=[pltpu.VMEM(FINE, F32), pltpu.SemaphoreType.DMA((5,))],
        flops=2**20,
    )
    return out.reshape(5, 4, 4, 4, 2, 2, 128)


def solution(mesh):
    in_specs = (
        P(None, None, None, None, "gx", "gy", None),
        P(None, None, None, "gx", "gy", None),
        P("gx", "gy", None),
        P(None, "gx", "gy", None),
        P(None, None, None, None, None, "gx", "gy", None),
        P(None, None, None, None, None, "gx", "gy", None),
    )
    out_specs = P(None, None, None, None, "gx", "gy", None)
    return jax.shard_map(body, mesh=mesh, in_specs=in_specs, out_specs=out_specs, check_vma=False)
```

profile of v0, /device:TPU:0, one launch (start us, length us, event | category | flops | bytes accessed | tf_op | source)
XLA Modules:
  0.0 36.7 jit_solution(2313998218321303345)
XLA Ops:
  0.0 0.0 copy-start.1
  0.0 0.0 copy-start.2
  0.0 0.7 %copy-done.2 = s32[3,2,2,128]{3,2,1,0:T(2,128)S(1)} copy-done((s32[3,2,2,128]{3,2,1,0:T(2,128)S(1)}, s32[3,2,2,128]{3,2,1,0:T(2,128)}, u32[]{:S(2)}) %copy-start.2) | copy-done | bytes 6168
  0.7 0.0 copy-start.3
  0.7 1.9 %shard_map.64 = (f32[5,4,4,2,8,128]{5,4,3,2,1,0:T(8,128)S(1)}, bf16[25,4,4,16,128]{4,3,2,1,0:T(8,128)(2,1)S(1)}, f32[5,4,4,2,8,128]{5,4,3,2,1,0:T(8,128)S(1)}, s...) custom-call(f32[5,4,4,2,8,128]{5,4,3,2,1,0:T(8,128)} %bitcast.14, ...), custom_call_target="tpu_custom_call" | custom-call | flops 1638400 | bytes 4194304 | tf_op jit(solution)/shard_map/pallas_call | solution.py:510
  2.6 3.0 %collective-permute-start = (f32[5,4,8,128]{3,2,1,0:T(8,128)S(1)}, f32[5,4,8,128]{3,2,1,0:T(8,128)S(1)}, u32[]{:S(2)}, u32[]{:S(2)}) collective-permute-start(f32[5,4,8,128]{3,2,1,0:T(8,128)S(1)} %get-tuple-element.39), channel_id=1, source_target_pairs={{0,4},{4,0},{8,12},{12,8},{16,20},{20,16},{24,28},{28,24},{1,5},{5... | collective-permute-start | bytes 245768 | tf_op jit(solution)/shard_map/ppermute | solution.py:532
  5.6 3.6 %collective-permute-start.1 = (f32[5,4,8,128]{3,2,1,0:T(8,128)S(1)}, f32[5,4,8,128]{3,2,1,0:T(8,128)S(1)}, u32[]{:S(2)}, u32[]{:S(2)}) collective-permute-start(f32[5,4,8,128]{3,2,1,0:T(8,128)S(1)} %get-tuple-element.40), channel_id=1, source_target_pairs={{0,28},{4,8},{8,4},{12,16},{16,12},{20,24},{24,20},{28,0},{1,29},{... | collective-permute-start | bytes 245768 | tf_op jit(solution)/shard_map/ppermute | solution.py:531
  9.2 0.0 collective-permute-start.2
  9.2 1.6 %collective-permute-start.3 = (f32[5,4,8,128]{3,2,1,0:T(8,128)S(1)}, f32[5,4,8,128]{3,2,1,0:T(8,128)S(1)}, u32[]{:S(2)}, u32[]{:S(2)}) collective-permute-start(f32[5,4,8,128]{3,2,1,0:T(8,128)S(1)} %get-tuple-element.42), channel_id=1, source_target_pairs={{0,3},{1,2},{2,1},{3,0},{4,7},{5,6},{6,5},{7,4},{8,11},{9,10},{10,... | collective-permute-start | bytes 245768 | tf_op jit(solution)/shard_map/ppermute | solution.py:533
  10.8 0.0 copy-done.1
  10.8 0.0 copy-done.3
  10.8 2.3 %shard_map.65 = (f32[5,4,4,2,8,128]{5,4,3,2,1,0:T(8,128)S(1)}, f32[75,8,128]{2,1,0:T(8,128)S(1)}, f32[8,128]{1,0:T(8,128)S(1)}, f32[4,25,8,128]{3,2,1,0:T(8,128)S(1)}) custom-call(f32[5,4,4,2,8,128]{5,4,3,2,1,0:T(8,128)S(1)} %get-tuple-element.33.src_ref, f32[5,4,4,2,8,128]{5,4,3,2,1,0:T(8,128)S(1)} %get-tuple-element.34.u_ref, ...), custom_call_target="tpu_custom_call" | custom-call | flops 9437184 | bytes 4194304 | tf_op jit(solution)/shard_map/pallas_call | solution.py:510
  13.1 0.0 collective-permute-done.rxe
  13.1 0.0 collective-permute-done.1.rxo
  13.1 0.0 collective-permute-done.2.rye
  13.1 0.1 collective-permute-done.3.ryo
  13.3 0.6 %shard_map.66 = (f32[5,4,4,2,8,128]{5,4,3,2,1,0:T(8,128)S(1)}, f32[5,4,8,128]{3,2,1,0:T(8,128)S(1)}, f32[5,4,8,128]{3,2,1,0:T(8,128)S(1)}, f32[5,4,8,128]{3,2,1,0:T(8,128)S(1)}, f32[5,4,8,128]{3,2,1,0:T(8,128)S(1)}) custom-call(f32[5,4,4,2,8,128]{5,4,3,2,1,0:T(8,128)S(1)} %get-tuple-element.36.acc_ref, f32[5,4,4,2,8,128]{5,4,3,2,1,0:T(8,128)S(1)} %get-tuple-element.34.u_ref, ...), custom_call_target="tpu_custom_call" | custom-call | flops 3145728 | bytes 4194304 | tf_op jit(solution)/shard_map/pallas_call | solution.py:510
  13.9 0.0 copy-start
  13.9 0.1 collective-permute-start.4
  14.0 3.1 %collective-permute-start.5 = (f32[5,4,8,128]{3,2,1,0:T(8,128)S(1)}, f32[5,4,8,128]{3,2,1,0:T(8,128)S(1)}, u32[]{:S(2)}, u32[]{:S(2)}) collective-permute-start(f32[5,4,8,128]{3,2,1,0:T(8,128)S(1)} %get-tuple-element.47), channel_id=1, source_target_pairs={{0,28},{4,8},{8,4},{12,16},{16,12},{20,24},{24,20},{28,0},{1,29},{... | collective-permute-start | bytes 245768 | tf_op jit(solution)/shard_map/ppermute | solution.py:531
  17.1 0.0 collective-permute-start.6
  17.1 1.6 %collective-permute-start.7 = (f32[5,4,8,128]{3,2,1,0:T(8,128)S(1)}, f32[5,4,8,128]{3,2,1,0:T(8,128)S(1)}, u32[]{:S(2)}, u32[]{:S(2)}) collective-permute-start(f32[5,4,8,128]{3,2,1,0:T(8,128)S(1)} %get-tuple-element.49), channel_id=1, source_target_pairs={{0,3},{1,2},{2,1},{3,0},{4,7},{5,6},{6,5},{7,4},{8,11},{9,10},{10,... | collective-permute-start | bytes 245768 | tf_op jit(solution)/shard_map/ppermute | solution.py:533
  18.7 2.2 %shard_map.67.acc_ref = f32[5,4,4,2,8,128]{5,4,3,2,1,0:T(8,128)S(1)} custom-call(f32[5,4,4,2,8,128]{5,4,3,2,1,0:T(8,128)S(1)} %get-tuple-element.33.src_ref, f32[5,4,4,2,8,128]{5,4,3,2,1,0:T(8,128)S(1)} %get-tuple-element.43.u_ref.second_ref, s32[3,8,128]{2,1,0:T(8,128)S(1)} %get-tuple-element.35.flag_ref, ...), custom_call_target="tpu_custom_call" | custom-call | flops 9437184 | bytes 4194304 | tf_op jit(solution)/shard_map/pallas_call | solution.py:510
  20.9 0.0 collective-permute-done.4.rxe
  21.0 0.6 %collective-permute-done.5.rxo = f32[5,4,8,128]{3,2,1,0:T(8,128)S(1)} collective-permute-done((f32[5,4,8,128]{3,2,1,0:T(8,128)S(1)}, f32[5,4,8,128]{3,2,1,0:T(8,128)S(1)}, u32[]{:S(2)}, u32[]{:S(2)}) %collective-permute-start.5) | collective-permute-done | bytes 81952 | tf_op jit(solution)/shard_map/ppermute | solution.py:531
  21.6 0.0 collective-permute-done.6.rye
  21.6 0.0 collective-permute-done.7.ryo
  21.6 0.0 copy-done
  21.6 0.4 %shard_map.68 = (f32[5,2,2,8,128]{4,3,2,1,0:T(8,128)S(1)}, f32[5,2,2,8,128]{4,3,2,1,0:T(8,128)S(1)}, f32[5,8,128]{2,1,0:T(8,128)S(1)}, f32[5,8,128]{2,1,0:T(8,12...) custom-call(f32[5,4,4,2,8,128]{5,4,3,2,1,0:T(8,128)S(1)} %shard_map.67.acc_ref, ...), custom_call_target="tpu_custom_call" | custom-call | flops 3145728 | bytes 4194304 | tf_op jit(solution)/shard_map/pallas_call | solution.py:510
  21.9 0.1 collective-permute-start.8
  22.0 2.8 %collective-permute-start.9 = (f32[5,8,128]{2,1,0:T(8,128)S(1)}, f32[5,8,128]{2,1,0:T(8,128)S(1)}, u32[]{:S(2)}, u32[]{:S(2)}) collective-permute-start(f32[5,8,128]{2,1,0:T(8,128)S(1)} %get-tuple-element.53), channel_id=1, source_target_pairs={{0,28},{4,8},{8,4},{12,16},{16,12},{20,24},{24,20},{28,0},{1,29},{... | collective-permute-start | bytes 61448 | tf_op jit(solution)/shard_map/ppermute | solution.py:531
  24.8 0.0 collective-permute-start.10
  24.8 1.6 %collective-permute-start.11 = (f32[5,8,128]{2,1,0:T(8,128)S(1)}, f32[5,8,128]{2,1,0:T(8,128)S(1)}, u32[]{:S(2)}, u32[]{:S(2)}) collective-permute-start(f32[5,8,128]{2,1,0:T(8,128)S(1)} %get-tuple-element.55), channel_id=1, source_target_pairs={{0,3},{1,2},{2,1},{3,0},{4,7},{5,6},{6,5},{7,4},{8,11},{9,10},{10,... | collective-permute-start | bytes 61448 | tf_op jit(solution)/shard_map/ppermute | solution.py:533
  26.5 0.0 collective-permute-done.8.rxe
  26.5 2.1 %collective-permute-done.9.rxo = f32[5,8,128]{2,1,0:T(8,128)S(1)} collective-permute-done((f32[5,8,128]{2,1,0:T(8,128)S(1)}, f32[5,8,128]{2,1,0:T(8,128)S(1)}, u32[]{:S(2)}, u32[]{:S(2)}) %collective-permute-start.9) | collective-permute-done | bytes 20512 | tf_op jit(solution)/shard_map/ppermute | solution.py:531
  28.6 0.0 collective-permute-done.10.rye
  28.6 0.0 collective-permute-done.11.ryo
  28.6 0.3 shard_map.69
  28.8 0.2 collective-permute-start.12
  29.1 2.7 %collective-permute-start.13 = (f32[5,8,128]{2,1,0:T(8,128)S(1)}, f32[5,8,128]{2,1,0:T(8,128)S(1)}, u32[]{:S(2)}, u32[]{:S(2)}) collective-permute-start(f32[5,8,128]{2,1,0:T(8,128)S(1)} %get-tuple-element.58), channel_id=1, source_target_pairs={{0,28},{4,8},{8,4},{12,16},{16,12},{20,24},{24,20},{28,0},{1,29},{... | collective-permute-start | bytes 61448 | tf_op jit(solution)/shard_map/ppermute | solution.py:531
  31.7 0.0 collective-permute-start.14
  31.7 1.6 %collective-permute-start.15 = (f32[5,8,128]{2,1,0:T(8,128)S(1)}, f32[5,8,128]{2,1,0:T(8,128)S(1)}, u32[]{:S(2)}, u32[]{:S(2)}) collective-permute-start(f32[5,8,128]{2,1,0:T(8,128)S(1)} %get-tuple-element.60), channel_id=1, source_target_pairs={{0,3},{1,2},{2,1},{3,0},{4,7},{5,6},{6,5},{7,4},{8,11},{9,10},{10,... | collective-permute-start | bytes 61448 | tf_op jit(solution)/shard_map/ppermute | solution.py:533
  33.4 0.0 collective-permute-done.12.rxe
  33.4 2.2 %collective-permute-done.13.rxo = f32[5,8,128]{2,1,0:T(8,128)S(1)} collective-permute-done((f32[5,8,128]{2,1,0:T(8,128)S(1)}, f32[5,8,128]{2,1,0:T(8,128)S(1)}, u32[]{:S(2)}, u32[]{:S(2)}) %collective-permute-start.13) | collective-permute-done | bytes 20512 | tf_op jit(solution)/shard_map/ppermute | solution.py:531
  35.5 0.0 collective-permute-done.14.rye
  35.5 0.0 collective-permute-done.15.ryo
  35.5 1.2 %shard_map.70 = f32[5,4,4,2,8,128]{5,4,3,2,1,0:T(8,128)} custom-call(f32[5,2,2,8,128]{4,3,2,1,0:T(8,128)S(1)} %get-tuple-element.56.c_ref, f32[5,2,2,8,128]{4,3,2,1,0:T(8,128)S(1)} %get-tuple-element.51.rhs_ref, bf16[25,2,16,128]{3,2,1,0:T(8,128)(2,1)S(1)} %bitcast.9, s32[3,8,128]{2,1,0:T(8,128)S(1)} %get-tuple-element.35.flag_ref, ...), custom_call_target="tpu_custom_call" | custom-call | flops 1048576 | bytes 4194304 | tf_op jit(solution)/shard_map/pallas_call | solution.py:510
Async XLA Ops:
  0.0 10.8 %copy-start.1 = (f32[3,5,5,2,2,128]{5,4,3,2,1,0:T(2,128)S(1)}, f32[3,5,5,2,2,128]{5,4,3,2,1,0:T(2,128)}, u32[]{:S(2)}) copy-start(f32[3,5,5,2,2,128]{5,4,3,2,1,0:T(2,128)} %param.7) | copy-start | bytes 460804
  0.0 0.7 %copy-start.2 = (s32[3,2,2,128]{3,2,1,0:T(2,128)S(1)}, s32[3,2,2,128]{3,2,1,0:T(2,128)}, u32[]{:S(2)}) copy-start(s32[3,2,2,128]{3,2,1,0:T(2,128)} %param.9) | copy-start | bytes 18436
  0.7 10.1 %copy-start.3 = (f32[2,2,128]{2,1,0:T(2,128)S(1)}, f32[2,2,128]{2,1,0:T(2,128)}, u32[]{:S(2)}) copy-start(f32[2,2,128]{2,1,0:T(2,128)} %param.8) | copy-start | bytes 6148
  2.6 10.5 %collective-permute-start = (f32[5,4,8,128]{3,2,1,0:T(8,128)S(1)}, f32[5,4,8,128]{3,2,1,0:T(8,128)S(1)}, u32[]{:S(2)}, u32[]{:S(2)}) collective-permute-start(f32[5,4,8,128]{3,2,1,0:T(8,128)S(1)} %get-tuple-element.39), channel_id=1, source_target_pairs={{0,4},{4,0},{8,12},{12,8},{16,20},{20,16},{24,28},{28,24},{1,5},{5... | collective-permute-start | bytes 245768 | tf_op jit(solution)/shard_map/ppermute | solution.py:532
  5.6 7.5 %collective-permute-start.1 = (f32[5,4,8,128]{3,2,1,0:T(8,128)S(1)}, f32[5,4,8,128]{3,2,1,0:T(8,128)S(1)}, u32[]{:S(2)}, u32[]{:S(2)}) collective-permute-start(f32[5,4,8,128]{3,2,1,0:T(8,128)S(1)} %get-tuple-element.40), channel_id=1, source_target_pairs={{0,28},{4,8},{8,4},{12,16},{16,12},{20,24},{24,20},{28,0},{1,29},{... | collective-permute-start | bytes 245768 | tf_op jit(solution)/shard_map/ppermute | solution.py:531
  9.2 4.0 %collective-permute-start.2 = (f32[5,4,8,128]{3,2,1,0:T(8,128)S(1)}, f32[5,4,8,128]{3,2,1,0:T(8,128)S(1)}, u32[]{:S(2)}, u32[]{:S(2)}) collective-permute-start(f32[5,4,8,128]{3,2,1,0:T(8,128)S(1)} %get-tuple-element.41), channel_id=1, source_target_pairs={{0,1},{1,0},{2,3},{3,2},{4,5},{5,4},{6,7},{7,6},{8,9},{9,8},{10,11... | collective-permute-start | bytes 245768 | tf_op jit(solution)/shard_map/ppermute | solution.py:534
  9.2 4.1 %collective-permute-start.3 = (f32[5,4,8,128]{3,2,1,0:T(8,128)S(1)}, f32[5,4,8,128]{3,2,1,0:T(8,128)S(1)}, u32[]{:S(2)}, u32[]{:S(2)}) collective-permute-start(f32[5,4,8,128]{3,2,1,0:T(8,128)S(1)} %get-tuple-element.42), channel_id=1, source_target_pairs={{0,3},{1,2},{2,1},{3,0},{4,7},{5,6},{6,5},{7,4},{8,11},{9,10},{10,... | collective-permute-start | bytes 245768 | tf_op jit(solution)/shard_map/ppermute | solution.py:533
  13.9 7.7 %copy-start = (bf16[5,5,2,2,2,2,2,128]{7,6,5,4,3,2,1,0:T(2,128)(2,1)S(1)}, bf16[5,5,2,2,2,2,2,128]{7,6,5,4,3,2,1,0:T(2,128)(2,1)}, u32[]{:S(2)}) copy-start(bf16[5,5,2,2,2,2,2,128]{7,6,5,4,3,2,1,0:T(2,128)(2,1)} %param.11) | copy-start | bytes 614404
  13.9 7.1 %collective-permute-start.4 = (f32[5,4,8,128]{3,2,1,0:T(8,128)S(1)}, f32[5,4,8,128]{3,2,1,0:T(8,128)S(1)}, u32[]{:S(2)}, u32[]{:S(2)}) collective-permute-start(f32[5,4,8,128]{3,2,1,0:T(8,128)S(1)} %get-tuple-element.46), channel_id=1, source_target_pairs={{0,4},{4,0},{8,12},{12,8},{16,20},{20,16},{24,28},{28,24},{1,5},{5... | collective-permute-start | bytes 245768 | tf_op jit(solution)/shard_map/ppermute | solution.py:532
  14.0 7.6 %collective-permute-start.5 = (f32[5,4,8,128]{3,2,1,0:T(8,128)S(1)}, f32[5,4,8,128]{3,2,1,0:T(8,128)S(1)}, u32[]{:S(2)}, u32[]{:S(2)}) collective-permute-start(f32[5,4,8,128]{3,2,1,0:T(8,128)S(1)} %get-tuple-element.47), channel_id=1, source_target_pairs={{0,28},{4,8},{8,4},{12,16},{16,12},{20,24},{24,20},{28,0},{1,29},{... | collective-permute-start | bytes 245768 | tf_op jit(solution)/shard_map/ppermute | solution.py:531
  17.1 4.5 %collective-permute-start.6 = (f32[5,4,8,128]{3,2,1,0:T(8,128)S(1)}, f32[5,4,8,128]{3,2,1,0:T(8,128)S(1)}, u32[]{:S(2)}, u32[]{:S(2)}) collective-permute-start(f32[5,4,8,128]{3,2,1,0:T(8,128)S(1)} %get-tuple-element.48), channel_id=1, source_target_pairs={{0,1},{1,0},{2,3},{3,2},{4,5},{5,4},{6,7},{7,6},{8,9},{9,8},{10,11... | collective-permute-start | bytes 245768 | tf_op jit(solution)/shard_map/ppermute | solution.py:534
  17.1 4.5 %collective-permute-start.7 = (f32[5,4,8,128]{3,2,1,0:T(8,128)S(1)}, f32[5,4,8,128]{3,2,1,0:T(8,128)S(1)}, u32[]{:S(2)}, u32[]{:S(2)}) collective-permute-start(f32[5,4,8,128]{3,2,1,0:T(8,128)S(1)} %get-tuple-element.49), channel_id=1, source_target_pairs={{0,3},{1,2},{2,1},{3,0},{4,7},{5,6},{6,5},{7,4},{8,11},{9,10},{10,... | collective-permute-start | bytes 245768 | tf_op jit(solution)/shard_map/ppermute | solution.py:533
  21.9 4.5 %collective-permute-start.8 = (f32[5,8,128]{2,1,0:T(8,128)S(1)}, f32[5,8,128]{2,1,0:T(8,128)S(1)}, u32[]{:S(2)}, u32[]{:S(2)}) collective-permute-start(f32[5,8,128]{2,1,0:T(8,128)S(1)} %get-tuple-element.52), channel_id=1, source_target_pairs={{0,4},{4,0},{8,12},{12,8},{16,20},{20,16},{24,28},{28,24},{1,5},{5... | collective-permute-start | bytes 61448 | tf_op jit(solution)/shard_map/ppermute | solution.py:532
  22.0 6.5 %collective-permute-start.9 = (f32[5,8,128]{2,1,0:T(8,128)S(1)}, f32[5,8,128]{2,1,0:T(8,128)S(1)}, u32[]{:S(2)}, u32[]{:S(2)}) collective-permute-start(f32[5,8,128]{2,1,0:T(8,128)S(1)} %get-tuple-element.53), channel_id=1, source_target_pairs={{0,28},{4,8},{8,4},{12,16},{16,12},{20,24},{24,20},{28,0},{1,29},{... | collective-permute-start | bytes 61448 | tf_op jit(solution)/shard_map/ppermute | solution.py:531
  24.8 3.7 %collective-permute-start.10 = (f32[5,8,128]{2,1,0:T(8,128)S(1)}, f32[5,8,128]{2,1,0:T(8,128)S(1)}, u32[]{:S(2)}, u32[]{:S(2)}) collective-permute-start(f32[5,8,128]{2,1,0:T(8,128)S(1)} %get-tuple-element.54), channel_id=1, source_target_pairs={{0,1},{1,0},{2,3},{3,2},{4,5},{5,4},{6,7},{7,6},{8,9},{9,8},{10,11... | collective-permute-start | bytes 61448 | tf_op jit(solution)/shard_map/ppermute | solution.py:534
  24.8 3.7 %collective-permute-start.11 = (f32[5,8,128]{2,1,0:T(8,128)S(1)}, f32[5,8,128]{2,1,0:T(8,128)S(1)}, u32[]{:S(2)}, u32[]{:S(2)}) collective-permute-start(f32[5,8,128]{2,1,0:T(8,128)S(1)} %get-tuple-element.55), channel_id=1, source_target_pairs={{0,3},{1,2},{2,1},{3,0},{4,7},{5,6},{6,5},{7,4},{8,11},{9,10},{10,... | collective-permute-start | bytes 61448 | tf_op jit(solution)/shard_map/ppermute | solution.py:533
  28.8 4.5 %collective-permute-start.12 = (f32[5,8,128]{2,1,0:T(8,128)S(1)}, f32[5,8,128]{2,1,0:T(8,128)S(1)}, u32[]{:S(2)}, u32[]{:S(2)}) collective-permute-start(f32[5,8,128]{2,1,0:T(8,128)S(1)} %get-tuple-element.57), channel_id=1, source_target_pairs={{0,4},{4,0},{8,12},{12,8},{16,20},{20,16},{24,28},{28,24},{1,5},{5... | collective-permute-start | bytes 61448 | tf_op jit(solution)/shard_map/ppermute | solution.py:532
  29.1 6.5 %collective-permute-start.13 = (f32[5,8,128]{2,1,0:T(8,128)S(1)}, f32[5,8,128]{2,1,0:T(8,128)S(1)}, u32[]{:S(2)}, u32[]{:S(2)}) collective-permute-start(f32[5,8,128]{2,1,0:T(8,128)S(1)} %get-tuple-element.58), channel_id=1, source_target_pairs={{0,28},{4,8},{8,4},{12,16},{16,12},{20,24},{24,20},{28,0},{1,29},{... | collective-permute-start | bytes 61448 | tf_op jit(solution)/shard_map/ppermute | solution.py:531
  31.7 3.8 %collective-permute-start.14 = (f32[5,8,128]{2,1,0:T(8,128)S(1)}, f32[5,8,128]{2,1,0:T(8,128)S(1)}, u32[]{:S(2)}, u32[]{:S(2)}) collective-permute-start(f32[5,8,128]{2,1,0:T(8,128)S(1)} %get-tuple-element.59), channel_id=1, source_target_pairs={{0,1},{1,0},{2,3},{3,2},{4,5},{5,4},{6,7},{7,6},{8,9},{9,8},{10,11... | collective-permute-start | bytes 61448 | tf_op jit(solution)/shard_map/ppermute | solution.py:534
  31.7 3.8 %collective-permute-start.15 = (f32[5,8,128]{2,1,0:T(8,128)S(1)}, f32[5,8,128]{2,1,0:T(8,128)S(1)}, u32[]{:S(2)}, u32[]{:S(2)}) collective-permute-start(f32[5,8,128]{2,1,0:T(8,128)S(1)} %get-tuple-element.60), channel_id=1, source_target_pairs={{0,3},{1,2},{2,1},{3,0},{4,7},{5,6},{6,5},{7,4},{8,11},{9,10},{10,... | collective-permute-start | bytes 61448 | tf_op jit(solution)/shard_map/ppermute | solution.py:533
where the time goes:
time: 36.9 us; the launch traced here: 36.7 us
  starting transfers between devices  22.1 us (60%)
  Pallas kernels  8.77 us (24%)
  waiting for transfers between devices  5.04 us (14%)
  local copies, waits for them, and re-layouts  0.74 us (2%)
    ppermute x4, starting transfers between devices, exchange(): xo = lax.ppermute(xo, 'gx', odd_x)  12.2 us
    pallas_call x7, Pallas kernels, call(): pl.pallas_call(kernel, out_shape=outs, in_specs=in_specs, out_specs=out_s...  8.77 us
    ppermute x4, starting transfers between devices, exchange(): yo = lax.ppermute(yo, 'gy', odd_y)  6.53 us
    ppermute x4, waiting for transfers between devices, exchange(): xo = lax.ppermute(xo, 'gx', odd_x)  4.87 us
    ppermute x4, starting transfers between devices, exchange(): xe = lax.ppermute(xe, 'gx', even_x)  3.36 us
    unnamed x8, local copies, waits for them, and re-layouts  0.74 us
  transfers between devices with their start and end apart: 16, of which 4 were waited for; matrix products, arithmetic and copies ran while one was open for 0% of the time, Pallas kernels for 12%

commit v1 on v0

--- a/solution.py
+++ b/solution.py
@@ -108,6 +108,10 @@
     odd_ref[index] = jnp.where(is_even, low_face, high_face)
 
 
+def partner_half(both_ref):
+    return both_ref.at[jnp.where(parity("gx"), 0, 1)]
+
+
 def fine_faces(u_ref, flag_ref, xe, xo, ye, yo):
     even_x, even_y = parity("gx"), parity("gy")
     fx, fy = flag_ref[0] != 0, flag_ref[1] != 0
@@ -121,7 +125,11 @@
             put_pair(ye, yo, (v, n), low, pack_high(h[0], h[1], 1), even_y)
 
 
-def first_kernel(src_hbm, smooth_hbm, orient_ref, src_ref, smooth_ref, u_ref, flag_ref, xe, xo, ye, yo, sems):
+def first_kernel(
+    src_hbm, smooth_hbm, orient_hbm, src_ref, smooth_ref, u_ref, flag_ref, xe, xo, ye, yo, sems, orient_ref, orient_sem
+):
+    orient_copy = pltpu.make_async_copy(orient_hbm, orient_ref, orient_sem)
+    orient_copy.start()
     copies = []
     for slot, a in enumerate((0, 3, 1, 2)):
         pair = (
@@ -131,6 +139,7 @@
         for one in pair:
             one.start()
         copies.append((a, pair))
+    orient_copy.wait()
     for d in range(3):
         flag_ref[d] = twice(orient_ref[d])
     for a, pair in copies:
@@ -278,7 +287,8 @@
         low, step = axis_low(d)
         flag = flag_ref[d]
         flag = jnp.where(low, sroll(flag, -step), flag) != 0
-        even, odd = even_refs[d], odd_refs[d]
+        even = even_refs[d]
+        odd = partner_half(odd_refs[d]) if d == 0 else odd_refs[d]
         matrix = [[face_ref[2 * d, 5 * o + i] for i in range(5)] for o in range(5)]
         for n in range(4):
             take = lambda v, m: jnp.where(is_even, even[v, m], odd[v, m])
@@ -397,7 +407,7 @@
         low, step = axis_low(d)
         flag = flag_ref[d] != 0
         matrix = [[jac_ref[25 * d + 5 * o + i] for i in range(5)] for o in range(5)]
-        even, odd = ((rxe, rxo), (rye, ryo))[d]
+        even, odd = ((rxe, partner_half(rxo)), (rye, ryo))[d]
         at = (lambda n, m: (n, m)) if d == 0 else (lambda n, m: (m, n))
         waves = [[[None] * 5, [None] * 5] for _ in range(2)]
         for v in range(5):
@@ -499,14 +509,14 @@
     return pltpu.with_memory_space_constraint(array, pltpu.VMEM)
 
 
-def call(kernel, args, outs, in_hbm=(), out_hbm=(), scratch=(), flops=0):
+def call(kernel, args, outs, in_hbm=(), free=(), out_hbm=(), scratch=(), flops=0):
     in_specs = [
         pl.BlockSpec(memory_space=pltpu.HBM if k in in_hbm else pltpu.VMEM) for k in range(len(args))
     ]
     out_specs = [
         pl.BlockSpec(memory_space=pltpu.HBM if k in out_hbm else pltpu.VMEM) for k in range(len(outs))
     ]
-    args = [pltpu.with_memory_space_constraint(a, pltpu.HBM) if k in in_hbm else here(a) for k, a in enumerate(args)]
+    args = [pltpu.with_memory_space_constraint(a, pltpu.HBM) if k in in_hbm else a if k in free else here(a) for k, a in enumerate(args)]
     return pl.pallas_call(
         kernel,
         out_shape=outs,
@@ -525,10 +535,15 @@
     return even, odd
 
 
+def odd_groups(axis):
+    size = lax.axis_size(axis)
+    return [[i, (i + 1) % size] for i in range(1, size, 2)]
+
+
 def exchange(xe, xo, ye, yo):
-    even_x, odd_x = partners("gx")
+    even_x, _ = partners("gx")
     even_y, odd_y = partners("gy")
-    xo = lax.ppermute(xo, "gx", odd_x)
+    xo = lax.all_gather(xo, "gx", axis_index_groups=odd_groups("gx"))
     xe = lax.ppermute(xe, "gx", even_x)
     yo = lax.ppermute(yo, "gy", odd_y)
     ye = lax.ppermute(ye, "gy", even_y)
@@ -543,14 +558,16 @@
     damping = damping.reshape(4, 128)
     orient = orient.reshape(3, 4, 128)
     fine_messages = [vmem(FINE_MESSAGE)] * 4
+    fine_messages[1] = jax.ShapeDtypeStruct(FINE_MESSAGE, F32)
     coarse_messages = [vmem(COARSE_MESSAGE)] * 4
+    coarse_messages[1] = jax.ShapeDtypeStruct(COARSE_MESSAGE, F32)
 
     source, smoother, first, flag, *sent = call(
         first_kernel,
         (source, smoother, orient),
         [vmem(FINE), vmem(smoother.shape, smoother.dtype), vmem(FINE), vmem((3, 8, 128), jnp.int32)] + fine_messages,
-        in_hbm=(0, 1),
-        scratch=[pltpu.SemaphoreType.DMA((2, 4))],
+        in_hbm=(0, 1, 2),
+        scratch=[pltpu.SemaphoreType.DMA((2, 4)), pltpu.VMEM((3, 4, 128), jnp.int32), pltpu.SemaphoreType.DMA],
         flops=2 * 25 * 64 * 512,
     )
     got = exchange(*sent)
@@ -565,6 +582,7 @@
         second_kernel,
         (acc, first, smoother, flag, face, *got),
         [vmem(FINE)] + fine_messages,
+        free=(6,),
         scratch=[part],
         flops=3 * 2**20,
     )
@@ -574,6 +592,7 @@
         restrict_kernel,
         (acc, flag, face, coarse_smoother, *got),
         [vmem(COARSE), vmem(COARSE)] + coarse_messages,
+        free=(5,),
         scratch=[part],
         flops=3 * 2**20,
     )
@@ -582,6 +601,7 @@
         coarse_kernel,
         (coarse, rhs, coarse_smoother, flag, jac8, damp8, *got),
         [vmem(COARSE)] + coarse_messages,
+        free=(7,),
         flops=2**20,
     )
     got = exchange(*sent)
@@ -590,6 +610,7 @@
         (coarse, rhs, coarse_smoother, flag, jac8, damp8, *got, second),
         [jax.ShapeDtypeStruct(FINE, F32)],
         out_hbm=(0,),
+        free=(7,),
         scratch=[pltpu.VMEM(FINE, F32), pltpu.SemaphoreType.DMA((5,))],
         flops=2**20,
     )

time: 36.9 us -> 47.1 us (1.28)
  blocking collectives: 0 us -> 29.9 us
  starting transfers between devices: 22.1 us -> 8.02 us
  waiting for transfers between devices: 5.04 us -> 0.03 us
  local copies, waits for them, and re-layouts: 0.74 us -> 0.01 us
    all_gather x0 -> x4, blocking collectives: none -> 29.9 us  [exchange(): xo = lax.all_gather(xo, 'gx', axis_index_groups=odd_groups('gx'))]
    ppermute x4 -> x0, starting transfers between devices: 12.2 us -> none  [exchange(): xo = lax.ppermute(xo, 'gx', odd_x)]
    ppermute x4 -> x0, waiting for transfers between devices: 4.87 us -> none  [exchange(): xo = lax.ppermute(xo, 'gx', odd_x)]
    ppermute x4, starting transfers between devices: 6.53 us -> 4.5 us  [exchange(): yo = lax.ppermute(yo, 'gy', odd_y)]
    unnamed x8 -> x6, local copies, waits for them, and re-layouts: 0.74 us -> 0.01 us
  transfers between devices with their start and end apart: 16 -> 12, of which waited for: 4 -> 0; matrix products, arithmetic and copies ran while one was open for 0% -> 0% of each run, Pallas kernels for 12% -> 10%
where the time goes in v1:
time: 47.1 us; the launch traced here: 46.9 us
  blocking collectives  29.9 us (63%)
  Pallas kernels  8.83 us (19%)
  starting transfers between devices  8.02 us (17%)
    all_gather x4, blocking collectives, exchange(): xo = lax.all_gather(xo, 'gx', axis_index_groups=odd_groups('gx'))  29.9 us
    pallas_call x7, Pallas kernels, call(): pl.pallas_call(kernel, out_shape=outs, in_specs=in_specs, out_specs=out_s...  8.83 us
    ppermute x4, starting transfers between devices, exchange(): yo = lax.ppermute(yo, 'gy', odd_y)  4.5 us
    ppermute x4, starting transfers between devices, exchange(): xe = lax.ppermute(xe, 'gx', even_x)  3.43 us
  transfers between devices with their start and end apart: 12, of which 0 were waited for; matrix products, arithmetic and copies ran while one was open for 0% of the time, Pallas kernels for 10%

profile of v1, /device:TPU:0, one launch (start us, length us, event | category | flops | bytes accessed | tf_op | source)
XLA Modules:
  0.0 46.9 jit_solution(17354131580109005313)
XLA Ops:
  0.0 0.0 copy-start.2
  0.0 0.0 copy-start.1
  0.0 1.9 %shard_map.64 = (f32[5,4,4,2,8,128]{5,4,3,2,1,0:T(8,128)S(1)}, bf16[25,4,4,16,128]{4,3,2,1,0:T(8,128)(2,1)S(1)}, f32[5,4,4,2,8,128]{5,4,3,2,1,0:T(8,128)S(1)}, s...) custom-call(f32[5,4,4,2,8,128]{5,4,3,2,1,0:T(8,128)} %bitcast.21, ...), custom_call_target="tpu_custom_call" | custom-call | flops 1638400 | bytes 4194304 | tf_op jit(solution)/shard_map/pallas_call | solution.py:520
  1.9 3.0 %collective-permute-start = (f32[5,4,8,128]{3,2,1,0:T(8,128)S(1)}, f32[5,4,8,128]{3,2,1,0:T(8,128)S(1)}, u32[]{:S(2)}, u32[]{:S(2)}) collective-permute-start(f32[5,4,8,128]{3,2,1,0:T(8,128)S(1)} %get-tuple-element.39), channel_id=1, source_target_pairs={{0,4},{4,0},{8,12},{12,8},{16,20},{20,16},{24,28},{28,24},{1,5},{5... | collective-permute-start | bytes 245768 | tf_op jit(solution)/shard_map/ppermute | solution.py:547
  4.9 0.0 collective-permute-start.1
  4.9 1.6 %collective-permute-start.2 = (f32[5,4,8,128]{3,2,1,0:T(8,128)S(1)}, f32[5,4,8,128]{3,2,1,0:T(8,128)S(1)}, u32[]{:S(2)}, u32[]{:S(2)}) collective-permute-start(f32[5,4,8,128]{3,2,1,0:T(8,128)S(1)} %get-tuple-element.42), channel_id=1, source_target_pairs={{0,3},{1,2},{2,1},{3,0},{4,7},{5,6},{6,5},{7,4},{8,11},{9,10},{10,... | collective-permute-start | bytes 245768 | tf_op jit(solution)/shard_map/ppermute | solution.py:548
  6.6 0.0 copy-done.2
  6.6 0.0 copy-done.1
  6.6 2.3 %shard_map.65 = (f32[5,4,4,2,8,128]{5,4,3,2,1,0:T(8,128)S(1)}, f32[75,8,128]{2,1,0:T(8,128)S(1)}, f32[8,128]{1,0:T(8,128)S(1)}, f32[4,25,8,128]{3,2,1,0:T(8,128)S(1)}) custom-call(f32[5,4,4,2,8,128]{5,4,3,2,1,0:T(8,128)S(1)} %get-tuple-element.33.src_ref, f32[5,4,4,2,8,128]{5,4,3,2,1,0:T(8,128)S(1)} %get-tuple-element.34.u_ref, ...), custom_call_target="tpu_custom_call" | custom-call | flops 9437184 | bytes 4194304 | tf_op jit(solution)/shard_map/pallas_call | solution.py:520
  8.9 7.8 %all-gather = f32[10,4,8,128]{3,2,1,0:T(8,128)S(1)} all-gather(f32[5,4,8,128]{3,2,1,0:T(8,128)S(1)} %get-tuple-element.40), channel_id=2, replica_groups={{4,8},{12,16},{20,24},{28,0},{5,9},{13,17},{21,25},{29,1},{6,10},{14,18..., dimensions={0}, use_global_device_ids=true | all-gather | bytes 245760 | tf_op jit(solution)/shard_map/all_gather | solution.py:546
  16.7 0.0 collective-permute-done.rxe
  16.7 0.0 collective-permute-done.1.rye
  16.7 0.0 collective-permute-done.2.ryo
  16.7 0.6 %shard_map.66 = (f32[5,4,4,2,8,128]{5,4,3,2,1,0:T(8,128)S(1)}, f32[5,4,8,128]{3,2,1,0:T(8,128)S(1)}, f32[5,4,8,128]{3,2,1,0:T(8,128)S(1)}, f32[5,4,8,128]{3,2,1,0:T(8,128)S(1)}, f32[5,4,8,128]{3,2,1,0:T(8,128)S(1)}) custom-call(f32[5,4,4,2,8,128]{5,4,3,2,1,0:T(8,128)S(1)} %get-tuple-element.36.acc_ref, f32[5,4,4,2,8,128]{5,4,3,2,1,0:T(8,128)S(1)} %get-tuple-element.34.u_ref, ...), custom_call_target="tpu_custom_call" | custom-call | flops 3145728 | bytes 4194304 | tf_op jit(solution)/shard_map/pallas_call | solution.py:520
  17.3 0.0 copy-start
  17.3 0.1 collective-permute-start.3
  17.4 0.1 collective-permute-start.4
  17.5 0.6 %collective-permute-start.5 = (f32[5,4,8,128]{3,2,1,0:T(8,128)S(1)}, f32[5,4,8,128]{3,2,1,0:T(8,128)S(1)}, u32[]{:S(2)}, u32[]{:S(2)}) collective-permute-start(f32[5,4,8,128]{3,2,1,0:T(8,128)S(1)} %get-tuple-element.49), channel_id=1, source_target_pairs={{0,3},{1,2},{2,1},{3,0},{4,7},{5,6},{6,5},{7,4},{8,11},{9,10},{10,... | collective-permute-start | bytes 245768 | tf_op jit(solution)/shard_map/ppermute | solution.py:548
  18.1 2.2 %shard_map.67.acc_ref = f32[5,4,4,2,8,128]{5,4,3,2,1,0:T(8,128)S(1)} custom-call(f32[5,4,4,2,8,128]{5,4,3,2,1,0:T(8,128)S(1)} %get-tuple-element.33.src_ref, f32[5,4,4,2,8,128]{5,4,3,2,1,0:T(8,128)S(1)} %get-tuple-element.43.u_ref.second_ref, s32[3,8,128]{2,1,0:T(8,128)S(1)} %get-tuple-element.35.flag_ref, ...), custom_call_target="tpu_custom_call" | custom-call | flops 9437184 | bytes 4194304 | tf_op jit(solution)/shard_map/pallas_call | solution.py:520
  20.3 7.8 %all-gather.1 = f32[10,4,8,128]{3,2,1,0:T(8,128)S(1)} all-gather(f32[5,4,8,128]{3,2,1,0:T(8,128)S(1)} %get-tuple-element.47), channel_id=3, replica_groups={{4,8},{12,16},{20,24},{28,0},{5,9},{13,17},{21,25},{29,1},{6,10},{14,18..., dimensions={0}, use_global_device_ids=true | all-gather | bytes 245760 | tf_op jit(solution)/shard_map/all_gather | solution.py:546
  28.1 0.0 collective-permute-done.3.rxe
  28.1 0.0 collective-permute-done.4.rye
  28.1 0.0 collective-permute-done.5.ryo
  28.1 0.0 copy-done
  28.2 0.4 shard_map.68
  28.5 0.2 collective-permute-start.6
  28.7 0.0 collective-permute-start.7
  28.7 1.6 %collective-permute-start.8 = (f32[5,8,128]{2,1,0:T(8,128)S(1)}, f32[5,8,128]{2,1,0:T(8,128)S(1)}, u32[]{:S(2)}, u32[]{:S(2)}) collective-permute-start(f32[5,8,128]{2,1,0:T(8,128)S(1)} %get-tuple-element.55), channel_id=1, source_target_pairs={{0,3},{1,2},{2,1},{3,0},{4,7},{5,6},{6,5},{7,4},{8,11},{9,10},{10,... | collective-permute-start | bytes 61448 | tf_op jit(solution)/shard_map/ppermute | solution.py:548
  30.4 7.1 %all-gather.2 = f32[10,8,128]{2,1,0:T(8,128)S(1)} all-gather(f32[5,8,128]{2,1,0:T(8,128)S(1)} %get-tuple-element.53), channel_id=4, replica_groups={{4,8},{12,16},{20,24},{28,0},{5,9},{13,17},{21,25},{29,1},{6,10},{14,18..., dimensions={0}, use_global_device_ids=true | all-gather | bytes 61440 | tf_op jit(solution)/shard_map/all_gather | solution.py:546
  37.5 0.0 collective-permute-done.6.rxe
  37.5 0.0 collective-permute-done.7.rye
  37.5 0.0 collective-permute-done.8.ryo
  37.5 0.3 shard_map.69
  37.8 0.2 collective-permute-start.9
  38.0 0.0 collective-permute-start.10
  38.0 0.6 %collective-permute-start.11 = (f32[5,8,128]{2,1,0:T(8,128)S(1)}, f32[5,8,128]{2,1,0:T(8,128)S(1)}, u32[]{:S(2)}, u32[]{:S(2)}) collective-permute-start(f32[5,8,128]{2,1,0:T(8,128)S(1)} %get-tuple-element.60), channel_id=1, source_target_pairs={{0,3},{1,2},{2,1},{3,0},{4,7},{5,6},{6,5},{7,4},{8,11},{9,10},{10,... | collective-permute-start | bytes 61448 | tf_op jit(solution)/shard_map/ppermute | solution.py:548
  38.6 7.1 %all-gather.3 = f32[10,8,128]{2,1,0:T(8,128)S(1)} all-gather(f32[5,8,128]{2,1,0:T(8,128)S(1)} %get-tuple-element.58), channel_id=5, replica_groups={{4,8},{12,16},{20,24},{28,0},{5,9},{13,17},{21,25},{29,1},{6,10},{14,18..., dimensions={0}, use_global_device_ids=true | all-gather | bytes 61440 | tf_op jit(solution)/shard_map/all_gather | solution.py:546
  45.7 0.0 collective-permute-done.9.rxe
  45.7 0.0 collective-permute-done.10.rye
  45.7 0.0 collective-permute-done.11.ryo
  45.7 1.2 %shard_map.70 = f32[5,4,4,2,8,128]{5,4,3,2,1,0:T(8,128)} custom-call(f32[5,2,2,8,128]{4,3,2,1,0:T(8,128)S(1)} %get-tuple-element.56.c_ref, f32[5,2,2,8,128]{4,3,2,1,0:T(8,128)S(1)} %get-tuple-element.51.rhs_ref, bf16[25,2,16,128]{3,2,1,0:T(8,128)(2,1)S(1)} %bitcast.13, s32[3,8,128]{2,1,0:T(8,128)S(1)} %get-tuple-element.35.flag_ref, ...), custom_call_target="tpu_custom_call" | custom-call | flops 1048576 | bytes 4194304 | tf_op jit(solution)/shard_map/pallas_call | solution.py:520
Async XLA Ops:
  0.0 6.6 %copy-start.2 = (f32[2,2,128]{2,1,0:T(2,128)S(1)}, f32[2,2,128]{2,1,0:T(2,128)}, u32[]{:S(2)}) copy-start(f32[2,2,128]{2,1,0:T(2,128)} %param.8) | copy-start | bytes 6148
  0.0 6.6 %copy-start.1 = (f32[3,5,5,2,2,128]{5,4,3,2,1,0:T(2,128)S(1)}, f32[3,5,5,2,2,128]{5,4,3,2,1,0:T(2,128)}, u32[]{:S(2)}) copy-start(f32[3,5,5,2,2,128]{5,4,3,2,1,0:T(2,128)} %param.7) | copy-start | bytes 460804
  1.9 14.8 %collective-permute-start = (f32[5,4,8,128]{3,2,1,0:T(8,128)S(1)}, f32[5,4,8,128]{3,2,1,0:T(8,128)S(1)}, u32[]{:S(2)}, u32[]{:S(2)}) collective-permute-start(f32[5,4,8,128]{3,2,1,0:T(8,128)S(1)} %get-tuple-element.39), channel_id=1, source_target_pairs={{0,4},{4,0},{8,12},{12,8},{16,20},{20,16},{24,28},{28,24},{1,5},{5... | collective-permute-start | bytes 245768 | tf_op jit(solution)/shard_map/ppermute | solution.py:547
  4.9 11.8 %collective-permute-start.1 = (f32[5,4,8,128]{3,2,1,0:T(8,128)S(1)}, f32[5,4,8,128]{3,2,1,0:T(8,128)S(1)}, u32[]{:S(2)}, u32[]{:S(2)}) collective-permute-start(f32[5,4,8,128]{3,2,1,0:T(8,128)S(1)} %get-tuple-element.41), channel_id=1, source_target_pairs={{0,1},{1,0},{2,3},{3,2},{4,5},{5,4},{6,7},{7,6},{8,9},{9,8},{10,11... | collective-permute-start | bytes 245768 | tf_op jit(solution)/shard_map/ppermute | solution.py:549
  4.9 11.8 %collective-permute-start.2 = (f32[5,4,8,128]{3,2,1,0:T(8,128)S(1)}, f32[5,4,8,128]{3,2,1,0:T(8,128)S(1)}, u32[]{:S(2)}, u32[]{:S(2)}) collective-permute-start(f32[5,4,8,128]{3,2,1,0:T(8,128)S(1)} %get-tuple-element.42), channel_id=1, source_target_pairs={{0,3},{1,2},{2,1},{3,0},{4,7},{5,6},{6,5},{7,4},{8,11},{9,10},{10,... | collective-permute-start | bytes 245768 | tf_op jit(solution)/shard_map/ppermute | solution.py:548
  17.3 10.8 %copy-start = (bf16[5,5,2,2,2,2,2,128]{7,6,5,4,3,2,1,0:T(2,128)(2,1)S(1)}, bf16[5,5,2,2,2,2,2,128]{7,6,5,4,3,2,1,0:T(2,128)(2,1)}, u32[]{:S(2)}) copy-start(bf16[5,5,2,2,2,2,2,128]{7,6,5,4,3,2,1,0:T(2,128)(2,1)} %param.11) | copy-start | bytes 614404
  17.3 10.8 %collective-permute-start.3 = (f32[5,4,8,128]{3,2,1,0:T(8,128)S(1)}, f32[5,4,8,128]{3,2,1,0:T(8,128)S(1)}, u32[]{:S(2)}, u32[]{:S(2)}) collective-permute-start(f32[5,4,8,128]{3,2,1,0:T(8,128)S(1)} %get-tuple-element.46), channel_id=1, source_target_pairs={{0,4},{4,0},{8,12},{12,8},{16,20},{20,16},{24,28},{28,24},{1,5},{5... | collective-permute-start | bytes 245768 | tf_op jit(solution)/shard_map/ppermute | solution.py:547
  17.4 10.7 %collective-permute-start.4 = (f32[5,4,8,128]{3,2,1,0:T(8,128)S(1)}, f32[5,4,8,128]{3,2,1,0:T(8,128)S(1)}, u32[]{:S(2)}, u32[]{:S(2)}) collective-permute-start(f32[5,4,8,128]{3,2,1,0:T(8,128)S(1)} %get-tuple-element.48), channel_id=1, source_target_pairs={{0,1},{1,0},{2,3},{3,2},{4,5},{5,4},{6,7},{7,6},{8,9},{9,8},{10,11... | collective-permute-start | bytes 245768 | tf_op jit(solution)/shard_map/ppermute | solution.py:549
  17.5 10.7 %collective-permute-start.5 = (f32[5,4,8,128]{3,2,1,0:T(8,128)S(1)}, f32[5,4,8,128]{3,2,1,0:T(8,128)S(1)}, u32[]{:S(2)}, u32[]{:S(2)}) collective-permute-start(f32[5,4,8,128]{3,2,1,0:T(8,128)S(1)} %get-tuple-element.49), channel_id=1, source_target_pairs={{0,3},{1,2},{2,1},{3,0},{4,7},{5,6},{6,5},{7,4},{8,11},{9,10},{10,... | collective-permute-start | bytes 245768 | tf_op jit(solution)/shard_map/ppermute | solution.py:548
  28.5 9.0 %collective-permute-start.6 = (f32[5,8,128]{2,1,0:T(8,128)S(1)}, f32[5,8,128]{2,1,0:T(8,128)S(1)}, u32[]{:S(2)}, u32[]{:S(2)}) collective-permute-start(f32[5,8,128]{2,1,0:T(8,128)S(1)} %get-tuple-element.52), channel_id=1, source_target_pairs={{0,4},{4,0},{8,12},{12,8},{16,20},{20,16},{24,28},{28,24},{1,5},{5... | collective-permute-start | bytes 61448 | tf_op jit(solution)/shard_map/ppermute | solution.py:547
  28.7 8.8 %collective-permute-start.7 = (f32[5,8,128]{2,1,0:T(8,128)S(1)}, f32[5,8,128]{2,1,0:T(8,128)S(1)}, u32[]{:S(2)}, u32[]{:S(2)}) collective-permute-start(f32[5,8,128]{2,1,0:T(8,128)S(1)} %get-tuple-element.54), channel_id=1, source_target_pairs={{0,1},{1,0},{2,3},{3,2},{4,5},{5,4},{6,7},{7,6},{8,9},{9,8},{10,11... | collective-permute-start | bytes 61448 | tf_op jit(solution)/shard_map/ppermute | solution.py:549
  28.7 8.8 %collective-permute-start.8 = (f32[5,8,128]{2,1,0:T(8,128)S(1)}, f32[5,8,128]{2,1,0:T(8,128)S(1)}, u32[]{:S(2)}, u32[]{:S(2)}) collective-permute-start(f32[5,8,128]{2,1,0:T(8,128)S(1)} %get-tuple-element.55), channel_id=1, source_target_pairs={{0,3},{1,2},{2,1},{3,0},{4,7},{5,6},{6,5},{7,4},{8,11},{9,10},{10,... | collective-permute-start | bytes 61448 | tf_op jit(solution)/shard_map/ppermute | solution.py:548
  37.8 7.9 %collective-permute-start.9 = (f32[5,8,128]{2,1,0:T(8,128)S(1)}, f32[5,8,128]{2,1,0:T(8,128)S(1)}, u32[]{:S(2)}, u32[]{:S(2)}) collective-permute-start(f32[5,8,128]{2,1,0:T(8,128)S(1)} %get-tuple-element.57), channel_id=1, source_target_pairs={{0,4},{4,0},{8,12},{12,8},{16,20},{20,16},{24,28},{28,24},{1,5},{5... | collective-permute-start | bytes 61448 | tf_op jit(solution)/shard_map/ppermute | solution.py:547
  38.0 7.8 %collective-permute-start.10 = (f32[5,8,128]{2,1,0:T(8,128)S(1)}, f32[5,8,128]{2,1,0:T(8,128)S(1)}, u32[]{:S(2)}, u32[]{:S(2)}) collective-permute-start(f32[5,8,128]{2,1,0:T(8,128)S(1)} %get-tuple-element.59), channel_id=1, source_target_pairs={{0,1},{1,0},{2,3},{3,2},{4,5},{5,4},{6,7},{7,6},{8,9},{9,8},{10,11... | collective-permute-start | bytes 61448 | tf_op jit(solution)/shard_map/ppermute | solution.py:549
  38.0 7.8 %collective-permute-start.11 = (f32[5,8,128]{2,1,0:T(8,128)S(1)}, f32[5,8,128]{2,1,0:T(8,128)S(1)}, u32[]{:S(2)}, u32[]{:S(2)}) collective-permute-start(f32[5,8,128]{2,1,0:T(8,128)S(1)} %get-tuple-element.60), channel_id=1, source_target_pairs={{0,3},{1,2},{2,1},{3,0},{4,7},{5,6},{6,5},{7,4},{8,11},{9,10},{10,... | collective-permute-start | bytes 61448 | tf_op jit(solution)/shard_map/ppermute | solution.py:548

commit v2 on v0

--- a/solution.py
+++ b/solution.py
@@ -35,6 +35,14 @@
 
 
 D4 = lobatto_slopes()
+PD = np.array([[1.0, NEAR, FAR, 0.0], [0.0, FAR, NEAR, 1.0]]) @ D4
+
+
+def sum_of(terms):
+    total = None
+    for weight, value in terms:
+        total = weight * value if total is None else total + weight * value
+    return total
 
 
 def rows():
@@ -108,7 +116,7 @@
     odd_ref[index] = jnp.where(is_even, low_face, high_face)
 
 
-def fine_faces(u_ref, flag_ref, xe, xo, ye, yo):
+def fine_faces(u_ref, flag_ref, xo, xe, yo, ye):
     even_x, even_y = parity("gx"), parity("gy")
     fx, fy = flag_ref[0] != 0, flag_ref[1] != 0
     for v in range(5):
@@ -121,7 +129,42 @@
             put_pair(ye, yo, (v, n), low, pack_high(h[0], h[1], 1), even_y)
 
 
-def first_kernel(src_hbm, smooth_hbm, orient_ref, src_ref, smooth_ref, u_ref, flag_ref, xe, xo, ye, yo, sems):
+def restrict_c(first, second):
+    low = c_low()
+    middle = jnp.where(low, second, first)
+    return jnp.where(low, first, second) + FAR * middle + NEAR * sroll(middle, 4)
+
+
+def restrict_four(values):
+    return values[0] + NEAR * values[1] + FAR * values[2], values[3] + NEAR * values[2] + FAR * values[1]
+
+
+def put_coarse_faces(v, lows, highs, flag_ref, pairs):
+    for d, axis in ((0, "gx"), (1, "gy")):
+        flag = flag_ref[d] != 0
+        low, high = lows[d], highs[d]
+        turned = [jnp.where(flag, high[1 - m], high[m]) for m in range(2)]
+        even_ref, odd_ref = pairs[d]
+        put_pair(even_ref, odd_ref, v, pack_low(*low, d), pack_high(*turned, d), parity(axis))
+
+
+def restricted_faces(u_ref, flag_ref, xo, xe, yo, ye):
+    for v in range(5):
+        line = {}
+        for a in range(4):
+            for b in range(4):
+                if a in (0, 3) or b in (0, 3):
+                    line[a, b] = restrict_c(u_ref[v, a, b, 0], u_ref[v, a, b, 1])
+        lows = [restrict_four([line[0, n] for n in range(4)]), restrict_four([line[n, 0] for n in range(4)])]
+        highs = [restrict_four([line[3, n] for n in range(4)]), restrict_four([line[n, 3] for n in range(4)])]
+        put_coarse_faces(v, lows, highs, flag_ref, ((xe, xo), (ye, yo)))
+
+
+def first_kernel(
+    src_hbm, smooth_hbm, orient_hbm, src_ref, smooth_ref, u_ref, flag_ref, xo, xe, yo, ye, sems, orient_ref, orient_sem
+):
+    orient_copy = pltpu.make_async_copy(orient_hbm, orient_ref, orient_sem)
+    orient_copy.start()
     copies = []
     for slot, a in enumerate((0, 3, 1, 2)):
         pair = (
@@ -131,6 +174,7 @@
         for one in pair:
             one.start()
         copies.append((a, pair))
+    orient_copy.wait()
     for d in range(3):
         flag_ref[d] = twice(orient_ref[d])
     for a, pair in copies:
@@ -151,7 +195,7 @@
             return carry
 
         lax.fori_loop(0, 4, one_line, 0)
-    fine_faces(u_ref, flag_ref, xe, xo, ye, yo)
+    fine_faces(u_ref, flag_ref, xo, xe, yo, ye)
 
 
 def prepare_tables(jac_ref, damp_ref, jac8_ref, damp8_ref, face_ref):
@@ -268,10 +312,6 @@
     volume(src_ref, u_ref, flag_ref, jac8_ref, damp8_ref, acc_ref)
 
 
-def second_volume_kernel(src_ref, u_ref, flag_ref, jac8_ref, damp8_ref, acc_ref):
-    volume(src_ref, u_ref, flag_ref, jac8_ref, damp8_ref, acc_ref)
-
-
 def remote_parts(even_refs, odd_refs, flag_ref, face_ref, part_ref):
     for d, axis in ((0, "gx"), (1, "gy")):
         is_even = parity(axis)
@@ -308,7 +348,7 @@
 
 
 def second_kernel(
-    acc_ref, u_ref, smooth_ref, flag_ref, face_ref, rxe, rxo, rye, ryo, out_ref, xe, xo, ye, yo, part_ref
+    acc_ref, u_ref, smooth_ref, flag_ref, face_ref, rxo, rxe, ryo, rye, out_ref, xo, xe, yo, ye, part_ref
 ):
     remote_parts((rxe, rye), (rxo, ryo), flag_ref, face_ref, part_ref)
     for a in range(4):
@@ -323,7 +363,7 @@
                         total[q] = term if i == 0 else total[q] + term
                 for q in range(2):
                     out_ref[o, a, b, q] = u_ref[o, a, b, q] + OMEGA * total[q]
-    fine_faces(out_ref, flag_ref, xe, xo, ye, yo)
+    restricted_faces(out_ref, flag_ref, xo, xe, yo, ye)
 
 
 def coarse_smooth(smooth_ref, fields):
@@ -341,54 +381,130 @@
     return out
 
 
-def coarse_faces(field, flag_ref, xe, xo, ye, yo):
-    even_x, even_y = parity("gx"), parity("gy")
-    fx, fy = flag_ref[0] != 0, flag_ref[1] != 0
+def coarse_faces(field, flag_ref, xo, xe, yo, ye):
     for v in range(5):
         c = field[v]
-        low = pack_low(c[0][0], c[0][1], 0)
-        h = [jnp.where(fx, c[1][1 - j], c[1][j]) for j in range(2)]
-        put_pair(xe, xo, v, low, pack_high(h[0], h[1], 0), even_x)
-        low = pack_low(c[0][0], c[1][0], 1)
-        h = [jnp.where(fy, c[1 - i][1], c[i][1]) for i in range(2)]
-        put_pair(ye, yo, v, low, pack_high(h[0], h[1], 1), even_y)
-
-
-def restrict_kernel(
-    acc_ref, flag_ref, face_ref, smooth_ref, rxe, rxo, rye, ryo, rhs_ref, c_ref, xe, xo, ye, yo, part_ref
-):
-    remote_parts((rxe, rye), (rxo, ryo), flag_ref, face_ref, part_ref)
-    low = c_low()
-    rhs = [[[None, None], [None, None]] for _ in range(5)]
+        lows = [[c[0][0], c[0][1]], [c[0][0], c[1][0]]]
+        highs = [[c[1][0], c[1][1]], [c[0][1], c[1][1]]]
+        put_coarse_faces(v, lows, highs, flag_ref, ((xe, xo), (ye, yo)))
+
+
+def restricted_volume_kernel(src_ref, u_ref, flag_ref, jac_ref, damp_ref, acc_ref):
+    damp = H4 * damp_ref[...]
+    low_c = c_low()
+    slope = [
+        jnp.where(low_c, float(PD[0, c]), float(PD[1, c ^ 1])).astype(F32) for c in range(4)
+    ]
+    flags = [flag_ref[0] != 0, flag_ref[1] != 0, jnp.where(low_c, lroll(flag_ref[2], 1), flag_ref[2]) != 0]
+    sign = jnp.where(low_c, -H4, H4).astype(F32)
+    waves = [[[[None] * 5 for _ in range(2)] for _ in range(2)] for _ in range(3)]
+
+    def slopes_four(values):
+        return [sum_of([(float(PD[i, n]), values[n]) for n in range(4)]) for i in range(2)]
+
     for v in range(5):
-        halves = [[[None, None], [None, None]] for _ in range(2)]
-        for q in range(2):
+        line, slope_c, ends = {}, {}, {}
+        for a in range(4):
             for b in range(4):
-                r = [whole(acc_ref, part_ref, v, a, b, q) for a in range(4)]
-                ends = (r[0] + NEAR * r[1] + FAR * r[2], r[3] + NEAR * r[2] + FAR * r[1])
-                near = (1.0, NEAR, FAR, 0.0)[b], (0.0, FAR, NEAR, 1.0)[b]
-                for i in range(2):
-                    for j in range(2):
-                        if near[j] == 0.0:
-                            continue
-                        term = ends[i] if near[j] == 1.0 else near[j] * ends[i]
-                        halves[q][i][j] = term if halves[q][i][j] is None else halves[q][i][j] + term
+                first, second = u_ref[v, a, b, 0], u_ref[v, a, b, 1]
+                line[a, b] = restrict_c(first, second)
+                slope_c[a, b] = (slope[0] * first + slope[1] * sroll(first, 4)) + (
+                    slope[2] * second + slope[3] * sroll(second, 4)
+                )
+                ends[a, b] = jnp.where(low_c, first, second)
+
+        def along_b(table):
+            return [restrict_four([table[a, b] for b in range(4)]) for a in range(4)]
+
+        def both(table):
+            by_b = along_b(table)
+            return [restrict_four([by_b[a][j] for a in range(4)]) for j in range(2)]
+
+        by_b = along_b(line)
+        by_a = [restrict_four([line[a, b] for a in range(4)]) for b in range(4)]
+        flux_z = both(slope_c)
+        trace_z = both(ends)
+        sources = both({(a, b): restrict_c(src_ref[v, a, b, 0], src_ref[v, a, b, 1]) for a in range(4) for b in range(4)})
+        acc = [[None, None], [None, None]]
+        for j in range(2):
+            value = restrict_four([by_b[a][j] for a in range(4)])
+            flux = slopes_four([by_b[a][j] for a in range(4)])
+            for i in range(2):
+                acc[i][j] = sources[j][i] - 2.0 * value[i]
+                waves[0][i][j][v] = flux[i]
+        for i in range(2):
+            flux = slopes_four([by_a[b][i] for b in range(4)])
+            for j in range(2):
+                waves[1][i][j][v] = flux[j]
+        for d, lo, hi in ((0, by_b[0], by_b[3]), (1, by_a[0], by_a[3])):
+            low, step = axis_low(d)
+            flag = flags[d]
+            flag_before = sroll(flag_ref[d], step) != 0
+            for m in range(2):
+                right = sroll(jnp.where(flag_before, lo[1 - m], lo[m]), -step)
+                left = sroll(jnp.where(flag, hi[1 - m], hi[m]), step)
+                jump_right = jnp.where(low, right, 0.0) - hi[m]
+                jump_left = jnp.where(low, 0.0, left) - lo[m]
+                i, j = (1, m) if d == 0 else (m, 1)
+                waves[d][i][j][v] = waves[d][i][j][v] + H4 * jump_right
+                acc[i][j] = acc[i][j] + damp * jump_right
+                i, j = (0, m) if d == 0 else (m, 0)
+                waves[d][i][j][v] = waves[d][i][j][v] - H4 * jump_left
+                acc[i][j] = acc[i][j] + damp * jump_left
+        beside = []
+        for j in range(2):
+            turned = [sroll(trace_z[j][i], 4) for i in range(2)]
+            beside.append([jnp.where(low_c, lroll(t, 1), lroll(t, -1)) for t in turned])
         for i in range(2):
             for j in range(2):
-                first, second = halves[0][i][j], halves[1][i][j]
-                middle = jnp.where(low, second, first)
-                value = jnp.where(low, first, second) + FAR * middle + NEAR * sroll(middle, 4)
-                rhs[v][i][j] = value
-                rhs_ref[v, i, j] = value
+                jump = jnp.where(flags[2], beside[j][1 - i], beside[j][i]) - trace_z[j][i]
+                waves[2][i][j][v] = flux_z[j][i] + sign * jump
+                acc_ref[v, i, j] = acc[i][j] + damp * jump
+    for d in range(3):
+        matrix = [[jac_ref[25 * d + 5 * o + i] for i in range(5)] for o in range(5)]
+        for i in range(2):
+            for j in range(2):
+                for v, value in enumerate(mix(matrix, waves[d][i][j])):
+                    acc_ref[v, i, j] = acc_ref[v, i, j] - value
+
+
+def restrict_kernel(
+    acc_ref, flag_ref, face_ref, smooth_ref, rxo, rxe, ryo, rye, rhs_ref, c_ref, xo, xe, yo, ye
+):
+    rhs = [[[acc_ref[v, i, j] for j in range(2)] for i in range(2)] for v in range(5)]
+    for d, axis in ((0, "gx"), (1, "gy")):
+        is_even = parity(axis)
+        low, step = axis_low(d)
+        flag = flag_ref[d]
+        flag = jnp.where(low, sroll(flag, -step), flag) != 0
+        even, odd = ((rxe, rxo), (rye, ryo))[d]
+        at = (lambda n, m: (n, m)) if d == 0 else (lambda n, m: (m, n))
+        right, left = [], []
+        for v in range(5):
+            value = jnp.where(is_even, even[v], odd[v])
+            swapped = jnp.where(low, sroll(value, -step), sroll(value, step))
+            right.append(jnp.where(flag, swapped, value))
+            left.append(jnp.where(is_even, odd[v], even[v]))
+        upper = [[face_ref[2 * d, 5 * o + i] for i in range(5)] for o in range(5)]
+        lower = [[face_ref[2 * d + 1, 5 * o + i] for i in range(5)] for o in range(5)]
+        for v, value in enumerate(mix(upper, right)):
+            for m, part in enumerate((sroll(value, step), value)):
+                i, j = at(1, m)
+                rhs[v][i][j] = rhs[v][i][j] - jnp.where(low, 0.0, part)
+        for v, value in enumerate(mix(lower, left)):
+            for m, part in enumerate((value, sroll(value, -step))):
+                i, j = at(0, m)
+                rhs[v][i][j] = rhs[v][i][j] + jnp.where(low, part, 0.0)
     c = coarse_smooth(smooth_ref, rhs)
     for v in range(5):
         for i in range(2):
             for j in range(2):
+                rhs_ref[v, i, j] = rhs[v][i][j]
                 c_ref[v, i, j] = c[v][i][j]
-    coarse_faces(c, flag_ref, xe, xo, ye, yo)
-
-
-def coarse_step(c_ref, rhs_ref, smooth_ref, flag_ref, jac_ref, damp_ref, rxe, rxo, rye, ryo):
+    coarse_faces(c, flag_ref, xo, xe, yo, ye)
+
+
+def coarse_step(c_ref, rhs_ref, smooth_ref, flag_ref, jac_ref, damp_ref, rxo, rxe, ryo, rye):
     damp = 0.5 * damp_ref[...]
     c = [[[c_ref[v, i, j] for j in range(2)] for i in range(2)] for v in range(5)]
     acc = [[[rhs_ref[v, i, j] - 2.0 * c[v][i][j] for j in range(2)] for i in range(2)] for v in range(5)]
@@ -446,14 +562,14 @@
 
 
 def coarse_kernel(
-    c_ref, rhs_ref, smooth_ref, flag_ref, jac_ref, damp_ref, rxe, rxo, rye, ryo, out_ref, xe, xo, ye, yo
+    c_ref, rhs_ref, smooth_ref, flag_ref, jac_ref, damp_ref, rxo, rxe, ryo, rye, out_ref, xo, xe, yo, ye
 ):
-    c = coarse_step(c_ref, rhs_ref, smooth_ref, flag_ref, jac_ref, damp_ref, rxe, rxo, rye, ryo)
+    c = coarse_step(c_ref, rhs_ref, smooth_ref, flag_ref, jac_ref, damp_ref, rxo, rxe, ryo, rye)
     for v in range(5):
         for i in range(2):
             for j in range(2):
                 out_ref[v, i, j] = c[v][i][j]
-    coarse_faces(c, flag_ref, xe, xo, ye, yo)
+    coarse_faces(c, flag_ref, xo, xe, yo, ye)
 
 
 def spread(first, second):
@@ -461,9 +577,9 @@
 
 
 def last_kernel(
-    c_ref, rhs_ref, smooth_ref, flag_ref, jac_ref, damp_ref, rxe, rxo, rye, ryo, second_ref, out_hbm, out_ref, sems
+    c_ref, rhs_ref, smooth_ref, flag_ref, jac_ref, damp_ref, rxo, rxe, ryo, rye, second_ref, out_hbm, out_ref, sems
 ):
-    c = coarse_step(c_ref, rhs_ref, smooth_ref, flag_ref, jac_ref, damp_ref, rxe, rxo, rye, ryo)
+    c = coarse_step(c_ref, rhs_ref, smooth_ref, flag_ref, jac_ref, damp_ref, rxo, rxe, ryo, rye)
     low = c_low()
     copies = []
     for v in range(5):
@@ -525,14 +641,14 @@
     return even, odd
 
 
-def exchange(xe, xo, ye, yo):
+def exchange(xo, xe, yo, ye):
     even_x, odd_x = partners("gx")
     even_y, odd_y = partners("gy")
     xo = lax.ppermute(xo, "gx", odd_x)
     xe = lax.ppermute(xe, "gx", even_x)
     yo = lax.ppermute(yo, "gy", odd_y)
     ye = lax.ppermute(ye, "gy", even_y)
-    return xe, xo, ye, yo
+    return xo, xe, yo, ye
 
 
 def body(source, jacobian, damping, orient, smoother, coarse_smoother):
@@ -549,8 +665,8 @@
         first_kernel,
         (source, smoother, orient),
         [vmem(FINE), vmem(smoother.shape, smoother.dtype), vmem(FINE), vmem((3, 8, 128), jnp.int32)] + fine_messages,
-        in_hbm=(0, 1),
-        scratch=[pltpu.SemaphoreType.DMA((2, 4))],
+        in_hbm=(0, 1, 2),
+        scratch=[pltpu.SemaphoreType.DMA((2, 4)), pltpu.VMEM((3, 4, 128), jnp.int32), pltpu.SemaphoreType.DMA],
         flops=2 * 25 * 64 * 512,
     )
     got = exchange(*sent)
@@ -560,22 +676,20 @@
         [vmem(FINE), vmem((75, 8, 128)), vmem((8, 128)), vmem((4, 25, 8, 128))],
         flops=9 * 2**20,
     )
-    part = pltpu.VMEM((4, 5, 4, 2, 8, 128), F32)
     second, *sent = call(
         second_kernel,
         (acc, first, smoother, flag, face, *got),
-        [vmem(FINE)] + fine_messages,
-        scratch=[part],
+        [vmem(FINE)] + coarse_messages,
+        scratch=[pltpu.VMEM((4, 5, 4, 2, 8, 128), F32)],
         flops=3 * 2**20,
     )
     got = exchange(*sent)
-    (acc,) = call(second_volume_kernel, (source, second, flag, jac8, damp8), [vmem(FINE)], flops=9 * 2**20)
+    (acc,) = call(restricted_volume_kernel, (source, second, flag, jac8, damp8), [vmem(COARSE)], flops=4 * 2**20)
     rhs, coarse, *sent = call(
         restrict_kernel,
         (acc, flag, face, coarse_smoother, *got),
         [vmem(COARSE), vmem(COARSE)] + coarse_messages,
-        scratch=[part],
-        flops=3 * 2**20,
+        flops=2**20,
     )
     got = exchange(*sent)
     coarse, *sent = call(

time: 36.9 us -> 34.7 us (0.940)
  waiting for transfers between devices: 5.04 us -> 7.21 us
  starting transfers between devices: 22.1 us -> 20.2 us
  Pallas kernels: 8.77 us -> 7.04 us
  local copies, waits for them, and re-layouts: 0.74 us -> 0.01 us
    ppermute x4, starting transfers between devices: 0.01 us -> 5.85 us  [exchange(): ye = lax.ppermute(ye, 'gy', even_y)]
    ppermute x4, starting transfers between devices: 6.53 us -> 0.69 us  [exchange(): yo = lax.ppermute(yo, 'gy', odd_y)]
    ppermute x4, starting transfers between devices: 3.36 us -> 0.01 us  [exchange(): xe = lax.ppermute(xe, 'gx', even_x)]
    pallas_call x7, Pallas kernels: 8.77 us -> 7.04 us  [call(): pl.pallas_call(kernel, out_shape=outs, in_specs=in_specs, out_specs=out_s...]
    ppermute x4, waiting for transfers between devices: 4.87 us -> 6.46 us  [exchange(): xo = lax.ppermute(xo, 'gx', odd_x)]
    ppermute x4, starting transfers between devices: 12.2 us -> 13.7 us  [exchange(): xo = lax.ppermute(xo, 'gx', odd_x)]
    unnamed x8 -> x6, local copies, waits for them, and re-layouts: 0.74 us -> 0.01 us
    ppermute x4, waiting for transfers between devices: 0.01 us -> 0.51 us  [exchange(): xe = lax.ppermute(xe, 'gx', even_x)]
  transfers between devices with their start and end apart: 16 -> 16, of which waited for: 4 -> 5; matrix products, arithmetic and copies ran while one was open for 0% -> 0% of each run, Pallas kernels for 12% -> 8%
where the time goes in v2:
time: 34.7 us; the launch traced here: 34.6 us
  starting transfers between devices  20.2 us (58%)
  waiting for transfers between devices  7.21 us (21%)
  Pallas kernels  7.04 us (20%)
    ppermute x4, starting transfers between devices, exchange(): xo = lax.ppermute(xo, 'gx', odd_x)  13.7 us
    pallas_call x7, Pallas kernels, call(): pl.pallas_call(kernel, out_shape=outs, in_specs=in_specs, out_specs=out_s...  7.04 us
    ppermute x4, waiting for transfers between devices, exchange(): xo = lax.ppermute(xo, 'gx', odd_x)  6.46 us
    ppermute x4, starting transfers between devices, exchange(): ye = lax.ppermute(ye, 'gy', even_y)  5.85 us
  transfers between devices with their start and end apart: 16, of which 5 were waited for; matrix products, arithmetic and copies ran while one was open for 0% of the time, Pallas kernels for 8%

profile of v2, /device:TPU:0, one launch (start us, length us, event | category | flops | bytes accessed | tf_op | source)
XLA Modules:
  0.0 34.6 jit_solution(17869944682276175877)
XLA Ops:
  0.0 0.0 copy-start.2
  0.0 0.0 copy-start.1
  0.0 1.9 %shard_map.64 = (f32[5,4,4,2,8,128]{5,4,3,2,1,0:T(8,128)S(1)}, bf16[25,4,4,16,128]{4,3,2,1,0:T(8,128)(2,1)S(1)}, f32[5,4,4,2,8,128]{5,4,3,2,1,0:T(8,128)S(1)}, s...) custom-call(f32[5,4,4,2,8,128]{5,4,3,2,1,0:T(8,128)} %bitcast.13, ...), custom_call_target="tpu_custom_call" | custom-call | flops 1638400 | bytes 4194304 | tf_op jit(solution)/shard_map/pallas_call | solution.py:626
  1.9 6.0 %collective-permute-start = (f32[5,4,8,128]{3,2,1,0:T(8,128)S(1)}, f32[5,4,8,128]{3,2,1,0:T(8,128)S(1)}, u32[]{:S(2)}, u32[]{:S(2)}) collective-permute-start(f32[5,4,8,128]{3,2,1,0:T(8,128)S(1)} %get-tuple-element.39), channel_id=1, source_target_pairs={{0,28},{4,8},{8,4},{12,16},{16,12},{20,24},{24,20},{28,0},{1,29},{... | collective-permute-start | bytes 245768 | tf_op jit(solution)/shard_map/ppermute | solution.py:647
  8.0 0.0 collective-permute-start.1
  8.0 0.7 %collective-permute-start.2 = (f32[5,4,8,128]{3,2,1,0:T(8,128)S(1)}, f32[5,4,8,128]{3,2,1,0:T(8,128)S(1)}, u32[]{:S(2)}, u32[]{:S(2)}) collective-permute-start(f32[5,4,8,128]{3,2,1,0:T(8,128)S(1)} %get-tuple-element.41), channel_id=1, source_target_pairs={{0,3},{1,2},{2,1},{3,0},{4,7},{5,6},{6,5},{7,4},{8,11},{9,10},{10,... | collective-permute-start | bytes 245768 | tf_op jit(solution)/shard_map/ppermute | solution.py:649
  8.7 1.0 %collective-permute-start.3 = (f32[5,4,8,128]{3,2,1,0:T(8,128)S(1)}, f32[5,4,8,128]{3,2,1,0:T(8,128)S(1)}, u32[]{:S(2)}, u32[]{:S(2)}) collective-permute-start(f32[5,4,8,128]{3,2,1,0:T(8,128)S(1)} %get-tuple-element.42), channel_id=1, source_target_pairs={{0,1},{1,0},{2,3},{3,2},{4,5},{5,4},{6,7},{7,6},{8,9},{9,8},{10,11... | collective-permute-start | bytes 245768 | tf_op jit(solution)/shard_map/ppermute | solution.py:650
  9.6 0.0 copy-done.2
  9.6 0.0 copy-done.1
  9.6 2.3 %shard_map.65 = (f32[5,4,4,2,8,128]{5,4,3,2,1,0:T(8,128)S(1)}, f32[75,8,128]{2,1,0:T(8,128)S(1)}, f32[8,128]{1,0:T(8,128)S(1)}, f32[4,25,8,128]{3,2,1,0:T(8,128)S(1)}) custom-call(f32[5,4,4,2,8,128]{5,4,3,2,1,0:T(8,128)S(1)} %get-tuple-element.33.src_ref, f32[5,4,4,2,8,128]{5,4,3,2,1,0:T(8,128)S(1)} %get-tuple-element.34.u_ref, ...), custom_call_target="tpu_custom_call" | custom-call | flops 9437184 | bytes 4194304 | tf_op jit(solution)/shard_map/pallas_call | solution.py:626
  11.9 0.0 collective-permute-done.rxo
  11.9 0.5 %collective-permute-done.1.rxe = f32[5,4,8,128]{3,2,1,0:T(8,128)S(1)} collective-permute-done((f32[5,4,8,128]{3,2,1,0:T(8,128)S(1)}, f32[5,4,8,128]{3,2,1,0:T(8,128)S(1)}, u32[]{:S(2)}, u32[]{:S(2)}) %collective-permute-start.1) | collective-permute-done | bytes 81952 | tf_op jit(solution)/shard_map/ppermute | solution.py:648
  12.4 0.2 collective-permute-done.2.ryo
  12.7 0.0 collective-permute-done.3.rye
  12.7 0.6 %shard_map.66 = (f32[5,4,4,2,8,128]{5,4,3,2,1,0:T(8,128)S(1)}, f32[5,8,128]{2,1,0:T(8,128)S(1)}, f32[5,8,128]{2,1,0:T(8,128)S(1)}, f32[5,8,128]{2,1,0:T(8,128)S(1)}, f32[5,8,128]{2,1,0:T(8,128)S(1)}) custom-call(f32[5,4,4,2,8,128]{5,4,3,2,1,0:T(8,128)S(1)} %get-tuple-element.36.acc_ref, f32[5,4,4,2,8,128]{5,4,3,2,1,0:T(8,128)S(1)} %get-tuple-element.34.u_ref, ...), custom_call_target="tpu_custom_call" | custom-call | flops 3145728 | bytes 4194304 | tf_op jit(solution)/shard_map/pallas_call | solution.py:626
  13.3 0.0 copy-start
  13.3 2.5 %collective-permute-start.4 = (f32[5,8,128]{2,1,0:T(8,128)S(1)}, f32[5,8,128]{2,1,0:T(8,128)S(1)}, u32[]{:S(2)}, u32[]{:S(2)}) collective-permute-start(f32[5,8,128]{2,1,0:T(8,128)S(1)} %get-tuple-element.46), channel_id=1, source_target_pairs={{0,28},{4,8},{8,4},{12,16},{16,12},{20,24},{24,20},{28,0},{1,29},{... | collective-permute-start | bytes 61448 | tf_op jit(solution)/shard_map/ppermute | solution.py:647
  15.9 0.0 collective-permute-start.5
  15.9 0.0 collective-permute-start.6
  15.9 1.6 %collective-permute-start.7 = (f32[5,8,128]{2,1,0:T(8,128)S(1)}, f32[5,8,128]{2,1,0:T(8,128)S(1)}, u32[]{:S(2)}, u32[]{:S(2)}) collective-permute-start(f32[5,8,128]{2,1,0:T(8,128)S(1)} %get-tuple-element.49), channel_id=1, source_target_pairs={{0,1},{1,0},{2,3},{3,2},{4,5},{5,4},{6,7},{7,6},{8,9},{9,8},{10,11... | collective-permute-start | bytes 61448 | tf_op jit(solution)/shard_map/ppermute | solution.py:650
  17.5 0.6 %shard_map.67.acc_ref = f32[5,2,2,8,128]{4,3,2,1,0:T(8,128)S(1)} custom-call(f32[5,4,4,2,8,128]{5,4,3,2,1,0:T(8,128)S(1)} %get-tuple-element.33.src_ref, f32[5,4,4,2,8,128]{5,4,3,2,1,0:T(8,128)S(1)} %get-tuple-element.43.u_ref.second_ref, s32[3,8,128]{2,1,0:T(8,128)S(1)} %get-tuple-element.35.flag_ref, f32[75,8,128]{2,1,0:T(8,128)S(1)} %get-tuple-element.44.jac_ref, ...), custom_call_target="tpu_custom_call" | custom-call | flops 4194304 | bytes 4194304 | tf_op jit(solution)/shard_map/pallas_call | solution.py:626
  18.1 1.7 %collective-permute-done.4.rxo = f32[5,8,128]{2,1,0:T(8,128)S(1)} collective-permute-done((f32[5,8,128]{2,1,0:T(8,128)S(1)}, f32[5,8,128]{2,1,0:T(8,128)S(1)}, u32[]{:S(2)}, u32[]{:S(2)}) %collective-permute-start.4) | collective-permute-done | bytes 20512 | tf_op jit(solution)/shard_map/ppermute | solution.py:647
  19.9 0.0 collective-permute-done.5.rxe
  19.9 0.0 collective-permute-done.6.ryo
  19.9 0.0 collective-permute-done.7.rye
  19.9 0.0 copy-done
  19.9 0.1 shard_map.68
  20.0 2.5 %collective-permute-start.8 = (f32[5,8,128]{2,1,0:T(8,128)S(1)}, f32[5,8,128]{2,1,0:T(8,128)S(1)}, u32[]{:S(2)}, u32[]{:S(2)}) collective-permute-start(f32[5,8,128]{2,1,0:T(8,128)S(1)} %get-tuple-element.52), channel_id=1, source_target_pairs={{0,28},{4,8},{8,4},{12,16},{16,12},{20,24},{24,20},{28,0},{1,29},{... | collective-permute-start | bytes 61448 | tf_op jit(solution)/shard_map/ppermute | solution.py:647
  22.6 0.0 collective-permute-start.9
  22.6 0.0 collective-permute-start.10
  22.6 1.6 %collective-permute-start.11 = (f32[5,8,128]{2,1,0:T(8,128)S(1)}, f32[5,8,128]{2,1,0:T(8,128)S(1)}, u32[]{:S(2)}, u32[]{:S(2)}) collective-permute-start(f32[5,8,128]{2,1,0:T(8,128)S(1)} %get-tuple-element.55), channel_id=1, source_target_pairs={{0,1},{1,0},{2,3},{3,2},{4,5},{5,4},{6,7},{7,6},{8,9},{9,8},{10,11... | collective-permute-start | bytes 61448 | tf_op jit(solution)/shard_map/ppermute | solution.py:650
  24.2 2.4 %collective-permute-done.8.rxo = f32[5,8,128]{2,1,0:T(8,128)S(1)} collective-permute-done((f32[5,8,128]{2,1,0:T(8,128)S(1)}, f32[5,8,128]{2,1,0:T(8,128)S(1)}, u32[]{:S(2)}, u32[]{:S(2)}) %collective-permute-start.8) | collective-permute-done | bytes 20512 | tf_op jit(solution)/shard_map/ppermute | solution.py:647
  26.6 0.0 collective-permute-done.9.rxe
  26.6 0.0 collective-permute-done.10.ryo
  26.6 0.0 collective-permute-done.11.rye
  26.6 0.3 shard_map.69
  26.8 2.5 %collective-permute-start.12 = (f32[5,8,128]{2,1,0:T(8,128)S(1)}, f32[5,8,128]{2,1,0:T(8,128)S(1)}, u32[]{:S(2)}, u32[]{:S(2)}) collective-permute-start(f32[5,8,128]{2,1,0:T(8,128)S(1)} %get-tuple-element.57), channel_id=1, source_target_pairs={{0,28},{4,8},{8,4},{12,16},{16,12},{20,24},{24,20},{28,0},{1,29},{... | collective-permute-start | bytes 61448 | tf_op jit(solution)/shard_map/ppermute | solution.py:647
  29.4 0.0 collective-permute-start.13
  29.4 0.0 collective-permute-start.14
  29.4 1.6 %collective-permute-start.15 = (f32[5,8,128]{2,1,0:T(8,128)S(1)}, f32[5,8,128]{2,1,0:T(8,128)S(1)}, u32[]{:S(2)}, u32[]{:S(2)}) collective-permute-start(f32[5,8,128]{2,1,0:T(8,128)S(1)} %get-tuple-element.60), channel_id=1, source_target_pairs={{0,1},{1,0},{2,3},{3,2},{4,5},{5,4},{6,7},{7,6},{8,9},{9,8},{10,11... | collective-permute-start | bytes 61448 | tf_op jit(solution)/shard_map/ppermute | solution.py:650
  31.0 2.4 %collective-permute-done.12.rxo = f32[5,8,128]{2,1,0:T(8,128)S(1)} collective-permute-done((f32[5,8,128]{2,1,0:T(8,128)S(1)}, f32[5,8,128]{2,1,0:T(8,128)S(1)}, u32[]{:S(2)}, u32[]{:S(2)}) %collective-permute-start.12) | collective-permute-done | bytes 20512 | tf_op jit(solution)/shard_map/ppermute | solution.py:647
  33.4 0.0 collective-permute-done.13.rxe
  33.4 0.0 collective-permute-done.14.ryo
  33.4 0.0 collective-permute-done.15.rye
  33.4 1.2 %shard_map.70 = f32[5,4,4,2,8,128]{5,4,3,2,1,0:T(8,128)} custom-call(f32[5,2,2,8,128]{4,3,2,1,0:T(8,128)S(1)} %get-tuple-element.56.c_ref, f32[5,2,2,8,128]{4,3,2,1,0:T(8,128)S(1)} %get-tuple-element.51.rhs_ref, bf16[25,2,16,128]{3,2,1,0:T(8,128)(2,1)S(1)} %bitcast.9, s32[3,8,128]{2,1,0:T(8,128)S(1)} %get-tuple-element.35.flag_ref, ...), custom_call_target="tpu_custom_call" | custom-call | flops 1048576 | bytes 4194304 | tf_op jit(solution)/shard_map/pallas_call | solution.py:626
Async XLA Ops:
  0.0 9.6 %copy-start.2 = (f32[2,2,128]{2,1,0:T(2,128)S(1)}, f32[2,2,128]{2,1,0:T(2,128)}, u32[]{:S(2)}) copy-start(f32[2,2,128]{2,1,0:T(2,128)} %param.8) | copy-start | bytes 6148
  0.0 9.6 %copy-start.1 = (f32[3,5,5,2,2,128]{5,4,3,2,1,0:T(2,128)S(1)}, f32[3,5,5,2,2,128]{5,4,3,2,1,0:T(2,128)}, u32[]{:S(2)}) copy-start(f32[3,5,5,2,2,128]{5,4,3,2,1,0:T(2,128)} %param.7) | copy-start | bytes 460804
  1.9 10.0 %collective-permute-start = (f32[5,4,8,128]{3,2,1,0:T(8,128)S(1)}, f32[5,4,8,128]{3,2,1,0:T(8,128)S(1)}, u32[]{:S(2)}, u32[]{:S(2)}) collective-permute-start(f32[5,4,8,128]{3,2,1,0:T(8,128)S(1)} %get-tuple-element.39), channel_id=1, source_target_pairs={{0,28},{4,8},{8,4},{12,16},{16,12},{20,24},{24,20},{28,0},{1,29},{... | collective-permute-start | bytes 245768 | tf_op jit(solution)/shard_map/ppermute | solution.py:647
  8.0 4.4 %collective-permute-start.1 = (f32[5,4,8,128]{3,2,1,0:T(8,128)S(1)}, f32[5,4,8,128]{3,2,1,0:T(8,128)S(1)}, u32[]{:S(2)}, u32[]{:S(2)}) collective-permute-start(f32[5,4,8,128]{3,2,1,0:T(8,128)S(1)} %get-tuple-element.40), channel_id=1, source_target_pairs={{0,4},{4,0},{8,12},{12,8},{16,20},{20,16},{24,28},{28,24},{1,5},{5... | collective-permute-start | bytes 245768 | tf_op jit(solution)/shard_map/ppermute | solution.py:648
  8.0 4.7 %collective-permute-start.2 = (f32[5,4,8,128]{3,2,1,0:T(8,128)S(1)}, f32[5,4,8,128]{3,2,1,0:T(8,128)S(1)}, u32[]{:S(2)}, u32[]{:S(2)}) collective-permute-start(f32[5,4,8,128]{3,2,1,0:T(8,128)S(1)} %get-tuple-element.41), channel_id=1, source_target_pairs={{0,3},{1,2},{2,1},{3,0},{4,7},{5,6},{6,5},{7,4},{8,11},{9,10},{10,... | collective-permute-start | bytes 245768 | tf_op jit(solution)/shard_map/ppermute | solution.py:649
  8.7 4.0 %collective-permute-start.3 = (f32[5,4,8,128]{3,2,1,0:T(8,128)S(1)}, f32[5,4,8,128]{3,2,1,0:T(8,128)S(1)}, u32[]{:S(2)}, u32[]{:S(2)}) collective-permute-start(f32[5,4,8,128]{3,2,1,0:T(8,128)S(1)} %get-tuple-element.42), channel_id=1, source_target_pairs={{0,1},{1,0},{2,3},{3,2},{4,5},{5,4},{6,7},{7,6},{8,9},{9,8},{10,11... | collective-permute-start | bytes 245768 | tf_op jit(solution)/shard_map/ppermute | solution.py:650
  13.3 6.6 %copy-start = (bf16[5,5,2,2,2,2,2,128]{7,6,5,4,3,2,1,0:T(2,128)(2,1)S(1)}, bf16[5,5,2,2,2,2,2,128]{7,6,5,4,3,2,1,0:T(2,128)(2,1)}, u32[]{:S(2)}) copy-start(bf16[5,5,2,2,2,2,2,128]{7,6,5,4,3,2,1,0:T(2,128)(2,1)} %param.11) | copy-start | bytes 614404
  13.3 6.5 %collective-permute-start.4 = (f32[5,8,128]{2,1,0:T(8,128)S(1)}, f32[5,8,128]{2,1,0:T(8,128)S(1)}, u32[]{:S(2)}, u32[]{:S(2)}) collective-permute-start(f32[5,8,128]{2,1,0:T(8,128)S(1)} %get-tuple-element.46), channel_id=1, source_target_pairs={{0,28},{4,8},{8,4},{12,16},{16,12},{20,24},{24,20},{28,0},{1,29},{... | collective-permute-start | bytes 61448 | tf_op jit(solution)/shard_map/ppermute | solution.py:647
  15.9 4.0 %collective-permute-start.5 = (f32[5,8,128]{2,1,0:T(8,128)S(1)}, f32[5,8,128]{2,1,0:T(8,128)S(1)}, u32[]{:S(2)}, u32[]{:S(2)}) collective-permute-start(f32[5,8,128]{2,1,0:T(8,128)S(1)} %get-tuple-element.47), channel_id=1, source_target_pairs={{0,4},{4,0},{8,12},{12,8},{16,20},{20,16},{24,28},{28,24},{1,5},{5... | collective-permute-start | bytes 61448 | tf_op jit(solution)/shard_map/ppermute | solution.py:648
  15.9 4.0 %collective-permute-start.6 = (f32[5,8,128]{2,1,0:T(8,128)S(1)}, f32[5,8,128]{2,1,0:T(8,128)S(1)}, u32[]{:S(2)}, u32[]{:S(2)}) collective-permute-start(f32[5,8,128]{2,1,0:T(8,128)S(1)} %get-tuple-element.48), channel_id=1, source_target_pairs={{0,3},{1,2},{2,1},{3,0},{4,7},{5,6},{6,5},{7,4},{8,11},{9,10},{10,... | collective-permute-start | bytes 61448 | tf_op jit(solution)/shard_map/ppermute | solution.py:649
  15.9 4.0 %collective-permute-start.7 = (f32[5,8,128]{2,1,0:T(8,128)S(1)}, f32[5,8,128]{2,1,0:T(8,128)S(1)}, u32[]{:S(2)}, u32[]{:S(2)}) collective-permute-start(f32[5,8,128]{2,1,0:T(8,128)S(1)} %get-tuple-element.49), channel_id=1, source_target_pairs={{0,1},{1,0},{2,3},{3,2},{4,5},{5,4},{6,7},{7,6},{8,9},{9,8},{10,11... | collective-permute-start | bytes 61448 | tf_op jit(solution)/shard_map/ppermute | solution.py:650
  20.0 6.5 %collective-permute-start.8 = (f32[5,8,128]{2,1,0:T(8,128)S(1)}, f32[5,8,128]{2,1,0:T(8,128)S(1)}, u32[]{:S(2)}, u32[]{:S(2)}) collective-permute-start(f32[5,8,128]{2,1,0:T(8,128)S(1)} %get-tuple-element.52), channel_id=1, source_target_pairs={{0,28},{4,8},{8,4},{12,16},{16,12},{20,24},{24,20},{28,0},{1,29},{... | collective-permute-start | bytes 61448 | tf_op jit(solution)/shard_map/ppermute | solution.py:647
  22.6 4.0 %collective-permute-start.9 = (f32[5,8,128]{2,1,0:T(8,128)S(1)}, f32[5,8,128]{2,1,0:T(8,128)S(1)}, u32[]{:S(2)}, u32[]{:S(2)}) collective-permute-start(f32[5,8,128]{2,1,0:T(8,128)S(1)} %get-tuple-element.53), channel_id=1, source_target_pairs={{0,4},{4,0},{8,12},{12,8},{16,20},{20,16},{24,28},{28,24},{1,5},{5... | collective-permute-start | bytes 61448 | tf_op jit(solution)/shard_map/ppermute | solution.py:648
  22.6 4.0 %collective-permute-start.10 = (f32[5,8,128]{2,1,0:T(8,128)S(1)}, f32[5,8,128]{2,1,0:T(8,128)S(1)}, u32[]{:S(2)}, u32[]{:S(2)}) collective-permute-start(f32[5,8,128]{2,1,0:T(8,128)S(1)} %get-tuple-element.54), channel_id=1, source_target_pairs={{0,3},{1,2},{2,1},{3,0},{4,7},{5,6},{6,5},{7,4},{8,11},{9,10},{10,... | collective-permute-start | bytes 61448 | tf_op jit(solution)/shard_map/ppermute | solution.py:649
  22.6 4.0 %collective-permute-start.11 = (f32[5,8,128]{2,1,0:T(8,128)S(1)}, f32[5,8,128]{2,1,0:T(8,128)S(1)}, u32[]{:S(2)}, u32[]{:S(2)}) collective-permute-start(f32[5,8,128]{2,1,0:T(8,128)S(1)} %get-tuple-element.55), channel_id=1, source_target_pairs={{0,1},{1,0},{2,3},{3,2},{4,5},{5,4},{6,7},{7,6},{8,9},{9,8},{10,11... | collective-permute-start | bytes 61448 | tf_op jit(solution)/shard_map/ppermute | solution.py:650
  26.8 6.5 %collective-permute-start.12 = (f32[5,8,128]{2,1,0:T(8,128)S(1)}, f32[5,8,128]{2,1,0:T(8,128)S(1)}, u32[]{:S(2)}, u32[]{:S(2)}) collective-permute-start(f32[5,8,128]{2,1,0:T(8,128)S(1)} %get-tuple-element.57), channel_id=1, source_target_pairs={{0,28},{4,8},{8,4},{12,16},{16,12},{20,24},{24,20},{28,0},{1,29},{... | collective-permute-start | bytes 61448 | tf_op jit(solution)/shard_map/ppermute | solution.py:647
  29.4 4.0 %collective-permute-start.13 = (f32[5,8,128]{2,1,0:T(8,128)S(1)}, f32[5,8,128]{2,1,0:T(8,128)S(1)}, u32[]{:S(2)}, u32[]{:S(2)}) collective-permute-start(f32[5,8,128]{2,1,0:T(8,128)S(1)} %get-tuple-element.58), channel_id=1, source_target_pairs={{0,4},{4,0},{8,12},{12,8},{16,20},{20,16},{24,28},{28,24},{1,5},{5... | collective-permute-start | bytes 61448 | tf_op jit(solution)/shard_map/ppermute | solution.py:648
  29.4 4.0 %collective-permute-start.14 = (f32[5,8,128]{2,1,0:T(8,128)S(1)}, f32[5,8,128]{2,1,0:T(8,128)S(1)}, u32[]{:S(2)}, u32[]{:S(2)}) collective-permute-start(f32[5,8,128]{2,1,0:T(8,128)S(1)} %get-tuple-element.59), channel_id=1, source_target_pairs={{0,3},{1,2},{2,1},{3,0},{4,7},{5,6},{6,5},{7,4},{8,11},{9,10},{10,... | collective-permute-start | bytes 61448 | tf_op jit(solution)/shard_map/ppermute | solution.py:649
  29.4 4.0 %collective-permute-start.15 = (f32[5,8,128]{2,1,0:T(8,128)S(1)}, f32[5,8,128]{2,1,0:T(8,128)S(1)}, u32[]{:S(2)}, u32[]{:S(2)}) collective-permute-start(f32[5,8,128]{2,1,0:T(8,128)S(1)} %get-tuple-element.60), channel_id=1, source_target_pairs={{0,1},{1,0},{2,3},{3,2},{4,5},{5,4},{6,7},{7,6},{8,9},{9,8},{10,11... | collective-permute-start | bytes 61448 | tf_op jit(solution)/shard_map/ppermute | solution.py:650

commit v3 on v2

--- a/solution.py
+++ b/solution.py
@@ -107,26 +107,24 @@
     return out
 
 
-def parity(axis):
-    return lax.rem(lax.axis_index(axis), 2) == 0
-
-
-def put_pair(even_ref, odd_ref, index, low_face, high_face, is_even):
-    even_ref[index] = jnp.where(is_even, high_face, low_face)
-    odd_ref[index] = jnp.where(is_even, low_face, high_face)
-
-
-def fine_faces(u_ref, flag_ref, xo, xe, yo, ye):
-    even_x, even_y = parity("gx"), parity("gy")
+def is_black():
+    return lax.rem(lax.axis_index("gx") + lax.axis_index("gy"), 2) == 1
+
+
+def received(refs, index):
+    return jnp.where(is_black(), refs[0][index], refs[1][index])
+
+
+def fine_faces(u_ref, flag_ref, x_low_ref, x_high_ref, y_low_ref, y_high_ref):
     fx, fy = flag_ref[0] != 0, flag_ref[1] != 0
     for v in range(5):
         for n in range(4):
-            low = pack_low(u_ref[v, 0, n, 0], u_ref[v, 0, n, 1], 0)
+            x_low_ref[v, n] = pack_low(u_ref[v, 0, n, 0], u_ref[v, 0, n, 1], 0)
             h = [jnp.where(fx, u_ref[v, 3, 3 - n, q], u_ref[v, 3, n, q]) for q in range(2)]
-            put_pair(xe, xo, (v, n), low, pack_high(h[0], h[1], 0), even_x)
-            low = pack_low(u_ref[v, n, 0, 0], u_ref[v, n, 0, 1], 1)
+            x_high_ref[v, n] = pack_high(h[0], h[1], 0)
+            y_low_ref[v, n] = pack_low(u_ref[v, n, 0, 0], u_ref[v, n, 0, 1], 1)
             h = [jnp.where(fy, u_ref[v, 3 - n, 3, q], u_ref[v, n, 3, q]) for q in range(2)]
-            put_pair(ye, yo, (v, n), low, pack_high(h[0], h[1], 1), even_y)
+            y_high_ref[v, n] = pack_high(h[0], h[1], 1)
 
 
 def restrict_c(first, second):
@@ -139,16 +137,16 @@
     return values[0] + NEAR * values[1] + FAR * values[2], values[3] + NEAR * values[2] + FAR * values[1]
 
 
-def put_coarse_faces(v, lows, highs, flag_ref, pairs):
-    for d, axis in ((0, "gx"), (1, "gy")):
+def put_coarse_faces(v, lows, highs, flag_ref, faces):
+    for d in range(2):
         flag = flag_ref[d] != 0
         low, high = lows[d], highs[d]
         turned = [jnp.where(flag, high[1 - m], high[m]) for m in range(2)]
-        even_ref, odd_ref = pairs[d]
-        put_pair(even_ref, odd_ref, v, pack_low(*low, d), pack_high(*turned, d), parity(axis))
-
-
-def restricted_faces(u_ref, flag_ref, xo, xe, yo, ye):
+        faces[2 * d][v] = pack_low(*low, d)
+        faces[2 * d + 1][v] = pack_high(*turned, d)
+
+
+def restricted_faces(u_ref, flag_ref, faces):
     for v in range(5):
         line = {}
         for a in range(4):
@@ -157,12 +155,13 @@
                     line[a, b] = restrict_c(u_ref[v, a, b, 0], u_ref[v, a, b, 1])
         lows = [restrict_four([line[0, n] for n in range(4)]), restrict_four([line[n, 0] for n in range(4)])]
         highs = [restrict_four([line[3, n] for n in range(4)]), restrict_four([line[n, 3] for n in range(4)])]
-        put_coarse_faces(v, lows, highs, flag_ref, ((xe, xo), (ye, yo)))
+        put_coarse_faces(v, lows, highs, flag_ref, faces)
 
 
 def first_kernel(
-    src_hbm, smooth_hbm, orient_hbm, src_ref, smooth_ref, u_ref, flag_ref, xo, xe, yo, ye, sems, orient_ref, orient_sem
+    src_hbm, smooth_hbm, orient_hbm, src_ref, smooth_ref, u_ref, flag_ref, f0, f1, f2, f3, sems, orient_ref, orient_sem
 ):
+    faces = (f0, f1, f2, f3)
     orient_copy = pltpu.make_async_copy(orient_hbm, orient_ref, orient_sem)
     orient_copy.start()
     copies = []
@@ -195,7 +194,7 @@
             return carry
 
         lax.fori_loop(0, 4, one_line, 0)
-    fine_faces(u_ref, flag_ref, xo, xe, yo, ye)
+    fine_faces(u_ref, flag_ref, *faces)
 
 
 def prepare_tables(jac_ref, damp_ref, jac8_ref, damp8_ref, face_ref):
@@ -312,23 +311,27 @@
     volume(src_ref, u_ref, flag_ref, jac8_ref, damp8_ref, acc_ref)
 
 
-def remote_parts(even_refs, odd_refs, flag_ref, face_ref, part_ref):
-    for d, axis in ((0, "gx"), (1, "gy")):
-        is_even = parity(axis)
+def both_colours(refs):
+    return [(refs[k], refs[4 + k]) for k in range(4)], refs[8:]
+
+
+def remote_parts(got, flag_ref, face_ref, part_ref):
+    for d in range(2):
         low, step = axis_low(d)
         flag = flag_ref[d]
         flag = jnp.where(low, sroll(flag, -step), flag) != 0
-        even, odd = even_refs[d], odd_refs[d]
+        from_right, from_left = got[2 * d], got[2 * d + 1]
         matrix = [[face_ref[2 * d, 5 * o + i] for i in range(5)] for o in range(5)]
         for n in range(4):
-            take = lambda v, m: jnp.where(is_even, even[v, m], odd[v, m])
-            right = [jnp.where(flag, take(v, 3 - n), take(v, n)) for v in range(5)]
+            right = [
+                jnp.where(flag, received(from_right, (v, 3 - n)), received(from_right, (v, n))) for v in range(5)
+            ]
             for v, value in enumerate(mix(matrix, right)):
                 part_ref[2 * d, v, n, 0] = jnp.where(low, 0.0, -sroll(value, step))
                 part_ref[2 * d, v, n, 1] = jnp.where(low, 0.0, -value)
         matrix = [[face_ref[2 * d + 1, 5 * o + i] for i in range(5)] for o in range(5)]
         for n in range(4):
-            left = [jnp.where(is_even, odd[v, n], even[v, n]) for v in range(5)]
+            left = [received(from_left, (v, n)) for v in range(5)]
             for v, value in enumerate(mix(matrix, left)):
                 part_ref[2 * d + 1, v, n, 0] = jnp.where(low, value, 0.0)
                 part_ref[2 * d + 1, v, n, 1] = jnp.where(low, sroll(value, -step), 0.0)
@@ -348,9 +351,10 @@
 
 
 def second_kernel(
-    acc_ref, u_ref, smooth_ref, flag_ref, face_ref, rxo, rxe, ryo, rye, out_ref, xo, xe, yo, ye, part_ref
+    acc_ref, u_ref, smooth_ref, flag_ref, face_ref, *refs
 ):
-    remote_parts((rxe, rye), (rxo, ryo), flag_ref, face_ref, part_ref)
+    got, (out_ref, *faces, part_ref) = both_colours(refs)
+    remote_parts(got, flag_ref, face_ref, part_ref)
     for a in range(4):
         for b in range(4):
             left = [[whole(acc_ref, part_ref, v, a, b, q) for q in range(2)] for v in range(5)]
@@ -363,7 +367,7 @@
                         total[q] = term if i == 0 else total[q] + term
                 for q in range(2):
                     out_ref[o, a, b, q] = u_ref[o, a, b, q] + OMEGA * total[q]
-    restricted_faces(out_ref, flag_ref, xo, xe, yo, ye)
+    restricted_faces(out_ref, flag_ref, faces)
 
 
 def coarse_smooth(smooth_ref, fields):
@@ -381,12 +385,12 @@
     return out
 
 
-def coarse_faces(field, flag_ref, xo, xe, yo, ye):
+def coarse_faces(field, flag_ref, faces):
     for v in range(5):
         c = field[v]
         lows = [[c[0][0], c[0][1]], [c[0][0], c[1][0]]]
         highs = [[c[1][0], c[1][1]], [c[0][1], c[1][1]]]
-        put_coarse_faces(v, lows, highs, flag_ref, ((xe, xo), (ye, yo)))
+        put_coarse_faces(v, lows, highs, flag_ref, faces)
 
 
 def restricted_volume_kernel(src_ref, u_ref, flag_ref, jac_ref, damp_ref, acc_ref):
@@ -469,22 +473,21 @@
 
 
 def restrict_kernel(
-    acc_ref, flag_ref, face_ref, smooth_ref, rxo, rxe, ryo, rye, rhs_ref, c_ref, xo, xe, yo, ye
+    acc_ref, flag_ref, face_ref, smooth_ref, *refs
 ):
+    got, (rhs_ref, c_ref, *faces) = both_colours(refs)
     rhs = [[[acc_ref[v, i, j] for j in range(2)] for i in range(2)] for v in range(5)]
-    for d, axis in ((0, "gx"), (1, "gy")):
-        is_even = parity(axis)
+    for d in range(2):
         low, step = axis_low(d)
         flag = flag_ref[d]
         flag = jnp.where(low, sroll(flag, -step), flag) != 0
-        even, odd = ((rxe, rxo), (rye, ryo))[d]
         at = (lambda n, m: (n, m)) if d == 0 else (lambda n, m: (m, n))
         right, left = [], []
         for v in range(5):
-            value = jnp.where(is_even, even[v], odd[v])
+            value = received(got[2 * d], v)
             swapped = jnp.where(low, sroll(value, -step), sroll(value, step))
             right.append(jnp.where(flag, swapped, value))
-            left.append(jnp.where(is_even, odd[v], even[v]))
+            left.append(received(got[2 * d + 1], v))
         upper = [[face_ref[2 * d, 5 * o + i] for i in range(5)] for o in range(5)]
         lower = [[face_ref[2 * d + 1, 5 * o + i] for i in range(5)] for o in range(5)]
         for v, value in enumerate(mix(upper, right)):
@@ -501,24 +504,22 @@
             for j in range(2):
                 rhs_ref[v, i, j] = rhs[v][i][j]
                 c_ref[v, i, j] = c[v][i][j]
-    coarse_faces(c, flag_ref, xo, xe, yo, ye)
-
-
-def coarse_step(c_ref, rhs_ref, smooth_ref, flag_ref, jac_ref, damp_ref, rxo, rxe, ryo, rye):
+    coarse_faces(c, flag_ref, faces)
+
+
+def coarse_step(c_ref, rhs_ref, smooth_ref, flag_ref, jac_ref, damp_ref, got):
     damp = 0.5 * damp_ref[...]
     c = [[[c_ref[v, i, j] for j in range(2)] for i in range(2)] for v in range(5)]
     acc = [[[rhs_ref[v, i, j] - 2.0 * c[v][i][j] for j in range(2)] for i in range(2)] for v in range(5)]
-    for d, axis in ((0, "gx"), (1, "gy")):
-        is_even = parity(axis)
+    for d in range(2):
         low, step = axis_low(d)
         flag = flag_ref[d] != 0
         matrix = [[jac_ref[25 * d + 5 * o + i] for i in range(5)] for o in range(5)]
-        even, odd = ((rxe, rxo), (rye, ryo))[d]
         at = (lambda n, m: (n, m)) if d == 0 else (lambda n, m: (m, n))
         waves = [[[None] * 5, [None] * 5] for _ in range(2)]
         for v in range(5):
-            got_right = jnp.where(is_even, even[v], odd[v])
-            got_left = jnp.where(is_even, odd[v], even[v])
+            got_right = received(got[2 * d], v)
+            got_left = received(got[2 * d + 1], v)
             lo = [c[v][at(0, m)[0]][at(0, m)[1]] for m in range(2)]
             hi = [c[v][at(1, m)[0]][at(1, m)[1]] for m in range(2)]
             right = [
@@ -561,25 +562,23 @@
     return [[[c[v][i][j] + change[v][i][j] for j in range(2)] for i in range(2)] for v in range(5)]
 
 
-def coarse_kernel(
-    c_ref, rhs_ref, smooth_ref, flag_ref, jac_ref, damp_ref, rxo, rxe, ryo, rye, out_ref, xo, xe, yo, ye
-):
-    c = coarse_step(c_ref, rhs_ref, smooth_ref, flag_ref, jac_ref, damp_ref, rxo, rxe, ryo, rye)
+def coarse_kernel(c_ref, rhs_ref, smooth_ref, flag_ref, jac_ref, damp_ref, *refs):
+    got, (out_ref, *faces) = both_colours(refs)
+    c = coarse_step(c_ref, rhs_ref, smooth_ref, flag_ref, jac_ref, damp_ref, got)
     for v in range(5):
         for i in range(2):
             for j in range(2):
                 out_ref[v, i, j] = c[v][i][j]
-    coarse_faces(c, flag_ref, xo, xe, yo, ye)
+    coarse_faces(c, flag_ref, faces)
 
 
 def spread(first, second):
     return first, NEAR * first + FAR * second, FAR * first + NEAR * second, second
 
 
-def last_kernel(
-    c_ref, rhs_ref, smooth_ref, flag_ref, jac_ref, damp_ref, rxo, rxe, ryo, rye, second_ref, out_hbm, out_ref, sems
-):
-    c = coarse_step(c_ref, rhs_ref, smooth_ref, flag_ref, jac_ref, damp_ref, rxo, rxe, ryo, rye)
+def last_kernel(c_ref, rhs_ref, smooth_ref, flag_ref, jac_ref, damp_ref, *refs):
+    got, (second_ref, out_hbm, out_ref, sems) = both_colours(refs)
+    c = coarse_step(c_ref, rhs_ref, smooth_ref, flag_ref, jac_ref, damp_ref, got)
     low = c_low()
     copies = []
     for v in range(5):
@@ -634,21 +633,22 @@
     )(*args)
 
 
-def partners(axis):
-    size = lax.axis_size(axis)
-    even = [(i, i ^ 1) for i in range(size)]
-    odd = [(i, (i - 1) % size if i % 2 == 0 else (i + 1) % size) for i in range(size)]
-    return even, odd
-
-
-def exchange(xo, xe, yo, ye):
-    even_x, odd_x = partners("gx")
-    even_y, odd_y = partners("gy")
-    xo = lax.ppermute(xo, "gx", odd_x)
-    xe = lax.ppermute(xe, "gx", even_x)
-    yo = lax.ppermute(yo, "gy", odd_y)
-    ye = lax.ppermute(ye, "gy", even_y)
-    return xo, xe, yo, ye
+def half_ring(dx, dy, colour):
+    nx, ny = lax.axis_size("gx"), lax.axis_size("gy")
+    return [
+        (i * ny + j, (i + dx) % nx * ny + (j + dy) % ny) for i in range(nx) for j in range(ny) if (i + j) % 2 == colour
+    ]
+
+
+def exchange(*faces):
+    steps = ((-1, 0), (1, 0), (0, -1), (0, 1))
+
+    def send(faces, colour):
+        return [lax.ppermute(face, ("gx", "gy"), half_ring(dx, dy, colour)) for face, (dx, dy) in zip(faces, steps)]
+
+    white = send(faces, 0)
+    *white, f0, f1, f2, f3 = lax.optimization_barrier((*white, *faces))
+    return white + send((f0, f1, f2, f3), 1)
 
 
 def body(source, jacobian, damping, orient, smoother, coarse_smoother):

time: 34.7 us -> 82.9 us (2.39)
  starting transfers between devices: 20.2 us -> 55.8 us
  waiting for transfers between devices: 7.21 us -> 18.9 us
    ppermute x16 -> x32, starting transfers between devices: 20.2 us -> 55.8 us  [send(): lax.ppermute(face, ('gx', 'gy'), half_ring(dx, dy, colour))]
    ppermute x16 -> x32, waiting for transfers between devices: 7.21 us -> 18.9 us  [send(): lax.ppermute(face, ('gx', 'gy'), half_ring(dx, dy, colour))]
  transfers between devices with their start and end apart: 16 -> 32, of which waited for: 5 -> 14; matrix products, arithmetic and copies ran while one was open for 0% -> 0% of each run, Pallas kernels for 8% -> 4%
where the time goes in v3:
time: 82.9 us; the launch traced here: 82.1 us
  starting transfers between devices  55.8 us (67%)
  waiting for transfers between devices  18.9 us (23%)
  Pallas kernels  7.02 us (8%)
    ppermute x32, starting transfers between devices, send(): lax.ppermute(face, ('gx', 'gy'), half_ring(dx, dy, colour))  55.8 us
    ppermute x32, waiting for transfers between devices, send(): lax.ppermute(face, ('gx', 'gy'), half_ring(dx, dy, colour))  18.9 us
    pallas_call x7, Pallas kernels, call(): pl.pallas_call(kernel, out_shape=outs, in_specs=in_specs, out_specs=out_s...  7.02 us
  transfers between devices with their start and end apart: 32, of which 14 were waited for; matrix products, arithmetic and copies ran while one was open for 0% of the time, Pallas kernels for 4%

profile of v3, /device:TPU:0, one launch (start us, length us, event | category | flops | bytes accessed | tf_op | source)
XLA Modules:
  0.0 82.1 jit_solution(1953092417025189593)
XLA Ops:
  0.0 1.9 %shard_map.64 = (f32[5,4,4,2,8,128]{5,4,3,2,1,0:T(8,128)S(1)}, bf16[25,4,4,16,128]{4,3,2,1,0:T(8,128)(2,1)S(1)}, f32[5,4,4,2,8,128]{5,4,3,2,1,0:T(8,128)S(1)}, s...) custom-call(f32[5,4,4,2,8,128]{5,4,3,2,1,0:T(8,128)} %bitcast.13, ...), custom_call_target="tpu_custom_call" | custom-call | flops 1638400 | bytes 4194304 | tf_op jit(solution)/shard_map/pallas_call | solution.py:625
  1.9 7.9 %collective-permute-start = (f32[5,4,8,128]{3,2,1,0:T(8,128)S(1)}, f32[5,4,8,128]{3,2,1,0:T(8,128)S(1)}, u32[]{:S(2)}, u32[]{:S(2)}) collective-permute-start(f32[5,4,8,128]{3,2,1,0:T(8,128)S(1)} %get-tuple-element.79), channel_id=1, source_target_pairs={{0,28},{2,30},{5,1},{7,3},{8,4},{10,6},{13,9},{15,11},{16,12},{18,... | collective-permute-start | bytes 245768 | tf_op jit(solution)/shard_map/ppermute | solution.py:647
  9.8 1.3 %collective-permute-start.1 = (f32[5,4,8,128]{3,2,1,0:T(8,128)S(1)}, f32[5,4,8,128]{3,2,1,0:T(8,128)S(1)}, u32[]{:S(2)}, u32[]{:S(2)}) collective-permute-start(f32[5,4,8,128]{3,2,1,0:T(8,128)S(1)} %get-tuple-element.80), channel_id=1, source_target_pairs={{0,4},{2,6},{5,9},{7,11},{8,12},{10,14},{13,17},{15,19},{16,20},{1... | collective-permute-start | bytes 245768 | tf_op jit(solution)/shard_map/ppermute | solution.py:647
  11.1 1.3 %collective-permute-start.2 = (f32[5,4,8,128]{3,2,1,0:T(8,128)S(1)}, f32[5,4,8,128]{3,2,1,0:T(8,128)S(1)}, u32[]{:S(2)}, u32[]{:S(2)}) collective-permute-start(f32[5,4,8,128]{3,2,1,0:T(8,128)S(1)} %get-tuple-element.81), channel_id=1, source_target_pairs={{0,3},{2,1},{5,4},{7,6},{8,11},{10,9},{13,12},{15,14},{16,19},{18,... | collective-permute-start | bytes 245768 | tf_op jit(solution)/shard_map/ppermute | solution.py:647
  12.4 1.3 %collective-permute-start.3 = (f32[5,4,8,128]{3,2,1,0:T(8,128)S(1)}, f32[5,4,8,128]{3,2,1,0:T(8,128)S(1)}, u32[]{:S(2)}, u32[]{:S(2)}) collective-permute-start(f32[5,4,8,128]{3,2,1,0:T(8,128)S(1)} %get-tuple-element.82), channel_id=1, source_target_pairs={{0,1},{2,3},{5,6},{7,4},{8,9},{10,11},{13,14},{15,12},{16,17},{18,... | collective-permute-start | bytes 245768 | tf_op jit(solution)/shard_map/ppermute | solution.py:647
  13.7 0.0 collective-permute-done.1.refs_1_
  13.7 0.7 collective-permute-done.2.refs_2_
  14.5 0.2 collective-permute-done.3.refs_3_
  14.6 1.3 %collective-permute-start.4 = (f32[5,4,8,128]{3,2,1,0:T(8,128)S(1)}, f32[5,4,8,128]{3,2,1,0:T(8,128)S(1)}, u32[]{:S(2)}, u32[]{:S(2)}) collective-permute-start(f32[5,4,8,128]{3,2,1,0:T(8,128)S(1)} %get-tuple-element.79), channel_id=1, source_target_pairs={{1,29},{3,31},{4,0},{6,2},{9,5},{11,7},{12,8},{14,10},{17,13},{19,... | collective-permute-start | bytes 245768 | tf_op jit(solution)/shard_map/ppermute | solution.py:647
  15.9 1.3 %collective-permute-start.5 = (f32[5,4,8,128]{3,2,1,0:T(8,128)S(1)}, f32[5,4,8,128]{3,2,1,0:T(8,128)S(1)}, u32[]{:S(2)}, u32[]{:S(2)}) collective-permute-start(f32[5,4,8,128]{3,2,1,0:T(8,128)S(1)} %get-tuple-element.80), channel_id=1, source_target_pairs={{1,5},{3,7},{4,8},{6,10},{9,13},{11,15},{12,16},{14,18},{17,21},{1... | collective-permute-start | bytes 245768 | tf_op jit(solution)/shard_map/ppermute | solution.py:647
  17.2 1.3 %collective-permute-start.6 = (f32[5,4,8,128]{3,2,1,0:T(8,128)S(1)}, f32[5,4,8,128]{3,2,1,0:T(8,128)S(1)}, u32[]{:S(2)}, u32[]{:S(2)}) collective-permute-start(f32[5,4,8,128]{3,2,1,0:T(8,128)S(1)} %get-tuple-element.81), channel_id=1, source_target_pairs={{1,0},{3,2},{4,7},{6,5},{9,8},{11,10},{12,15},{14,13},{17,16},{19,... | collective-permute-start | bytes 245768 | tf_op jit(solution)/shard_map/ppermute | solution.py:647
  18.5 1.3 %collective-permute-start.7 = (f32[5,4,8,128]{3,2,1,0:T(8,128)S(1)}, f32[5,4,8,128]{3,2,1,0:T(8,128)S(1)}, u32[]{:S(2)}, u32[]{:S(2)}) collective-permute-start(f32[5,4,8,128]{3,2,1,0:T(8,128)S(1)} %get-tuple-element.82), channel_id=1, source_target_pairs={{1,2},{3,0},{4,5},{6,7},{9,10},{11,8},{12,13},{14,15},{17,18},{19,... | collective-permute-start | bytes 245768 | tf_op jit(solution)/shard_map/ppermute | solution.py:647
  19.8 2.3 %shard_map.65 = (f32[5,4,4,2,8,128]{5,4,3,2,1,0:T(8,128)S(1)}, f32[75,8,128]{2,1,0:T(8,128)S(1)}, f32[8,128]{1,0:T(8,128)S(1)}, f32[4,25,8,128]{3,2,1,0:T(8,128)S(1)}) custom-call(f32[5,4,4,2,8,128]{5,4,3,2,1,0:T(8,128)S(1)} %get-tuple-element.65.src_ref, f32[5,4,4,2,8,128]{5,4,3,2,1,0:T(8,128)S(1)} %get-tuple-element.66.u_ref, ...), custom_call_target="tpu_custom_call" | custom-call | flops 9437184 | bytes 4194304 | tf_op jit(solution)/shard_map/pallas_call | solution.py:625
  22.1 2.8 %collective-permute-done.5.refs_5_ = f32[5,4,8,128]{3,2,1,0:T(8,128)S(1)} collective-permute-done((f32[5,4,8,128]{3,2,1,0:T(8,128)S(1)}, f32[5,4,8,128]{3,2,1,0:T(8,128)S(1)}, u32[]{:S(2)}, u32[]{:S(2)}) %collective-permute-start.5) | collective-permute-done | bytes 81952 | tf_op jit(solution)/shard_map/ppermute | solution.py:647
  24.9 0.6 shard_map.66
  25.6 0.0 copy-start
  25.6 4.6 %collective-permute-start.8 = (f32[5,8,128]{2,1,0:T(8,128)S(1)}, f32[5,8,128]{2,1,0:T(8,128)S(1)}, u32[]{:S(2)}, u32[]{:S(2)}) collective-permute-start(f32[5,8,128]{2,1,0:T(8,128)S(1)} %get-tuple-element.94), channel_id=1, source_target_pairs={{0,28},{2,30},{5,1},{7,3},{8,4},{10,6},{13,9},{15,11},{16,12},{18,... | collective-permute-start | bytes 61448 | tf_op jit(solution)/shard_map/ppermute | solution.py:647
  30.2 1.3 %collective-permute-start.9 = (f32[5,8,128]{2,1,0:T(8,128)S(1)}, f32[5,8,128]{2,1,0:T(8,128)S(1)}, u32[]{:S(2)}, u32[]{:S(2)}) collective-permute-start(f32[5,8,128]{2,1,0:T(8,128)S(1)} %get-tuple-element.95), channel_id=1, source_target_pairs={{0,4},{2,6},{5,9},{7,11},{8,12},{10,14},{13,17},{15,19},{16,20},{1... | collective-permute-start | bytes 61448 | tf_op jit(solution)/shard_map/ppermute | solution.py:647
  31.5 1.3 %collective-permute-start.10 = (f32[5,8,128]{2,1,0:T(8,128)S(1)}, f32[5,8,128]{2,1,0:T(8,128)S(1)}, u32[]{:S(2)}, u32[]{:S(2)}) collective-permute-start(f32[5,8,128]{2,1,0:T(8,128)S(1)} %get-tuple-element.96), channel_id=1, source_target_pairs={{0,3},{2,1},{5,4},{7,6},{8,11},{10,9},{13,12},{15,14},{16,19},{18,... | collective-permute-start | bytes 61448 | tf_op jit(solution)/shard_map/ppermute | solution.py:647
  32.8 1.3 %collective-permute-start.11 = (f32[5,8,128]{2,1,0:T(8,128)S(1)}, f32[5,8,128]{2,1,0:T(8,128)S(1)}, u32[]{:S(2)}, u32[]{:S(2)}) collective-permute-start(f32[5,8,128]{2,1,0:T(8,128)S(1)} %get-tuple-element.97), channel_id=1, source_target_pairs={{0,1},{2,3},{5,6},{7,4},{8,9},{10,11},{13,14},{15,12},{16,17},{18,... | collective-permute-start | bytes 61448 | tf_op jit(solution)/shard_map/ppermute | solution.py:647
  34.1 0.0 collective-permute-done.8.refs_0_
  34.1 0.0 collective-permute-done.9.refs_1_
  34.1 0.1 collective-permute-done.10.refs_2_
  34.3 0.7 collective-permute-done.11.refs_3_
  34.9 1.3 %collective-permute-start.12 = (f32[5,8,128]{2,1,0:T(8,128)S(1)}, f32[5,8,128]{2,1,0:T(8,128)S(1)}, u32[]{:S(2)}, u32[]{:S(2)}) collective-permute-start(f32[5,8,128]{2,1,0:T(8,128)S(1)} %get-tuple-element.94), channel_id=1, source_target_pairs={{1,29},{3,31},{4,0},{6,2},{9,5},{11,7},{12,8},{14,10},{17,13},{19,... | collective-permute-start | bytes 61448 | tf_op jit(solution)/shard_map/ppermute | solution.py:647
  36.2 1.3 %collective-permute-start.13 = (f32[5,8,128]{2,1,0:T(8,128)S(1)}, f32[5,8,128]{2,1,0:T(8,128)S(1)}, u32[]{:S(2)}, u32[]{:S(2)}) collective-permute-start(f32[5,8,128]{2,1,0:T(8,128)S(1)} %get-tuple-element.95), channel_id=1, source_target_pairs={{1,5},{3,7},{4,8},{6,10},{9,13},{11,15},{12,16},{14,18},{17,21},{1... | collective-permute-start | bytes 61448 | tf_op jit(solution)/shard_map/ppermute | solution.py:647
  37.5 1.3 %collective-permute-start.14 = (f32[5,8,128]{2,1,0:T(8,128)S(1)}, f32[5,8,128]{2,1,0:T(8,128)S(1)}, u32[]{:S(2)}, u32[]{:S(2)}) collective-permute-start(f32[5,8,128]{2,1,0:T(8,128)S(1)} %get-tuple-element.96), channel_id=1, source_target_pairs={{1,0},{3,2},{4,7},{6,5},{9,8},{11,10},{12,15},{14,13},{17,16},{19,... | collective-permute-start | bytes 61448 | tf_op jit(solution)/shard_map/ppermute | solution.py:647
  38.8 1.3 %collective-permute-start.15 = (f32[5,8,128]{2,1,0:T(8,128)S(1)}, f32[5,8,128]{2,1,0:T(8,128)S(1)}, u32[]{:S(2)}, u32[]{:S(2)}) collective-permute-start(f32[5,8,128]{2,1,0:T(8,128)S(1)} %get-tuple-element.97), channel_id=1, source_target_pairs={{1,2},{3,0},{4,5},{6,7},{9,10},{11,8},{12,13},{14,15},{17,18},{19,... | collective-permute-start | bytes 61448 | tf_op jit(solution)/shard_map/ppermute | solution.py:647
  40.1 0.6 shard_map.67.acc_ref
  40.8 0.0 collective-permute-done.12.refs_4_
  40.8 3.8 %collective-permute-done.13.refs_5_ = f32[5,8,128]{2,1,0:T(8,128)S(1)} collective-permute-done((f32[5,8,128]{2,1,0:T(8,128)S(1)}, f32[5,8,128]{2,1,0:T(8,128)S(1)}, u32[]{:S(2)}, u32[]{:S(2)}) %collective-permute-start.13) | collective-permute-done | bytes 20512 | tf_op jit(solution)/shard_map/ppermute | solution.py:647
  44.6 0.0 collective-permute-done.14.refs_6_
  44.6 0.0 collective-permute-done.15.refs_7_
  44.6 0.1 shard_map.68
  44.7 3.6 %collective-permute-start.16 = (f32[5,8,128]{2,1,0:T(8,128)S(1)}, f32[5,8,128]{2,1,0:T(8,128)S(1)}, u32[]{:S(2)}, u32[]{:S(2)}) collective-permute-start(f32[5,8,128]{2,1,0:T(8,128)S(1)} %get-tuple-element.108), channel_id=1, source_target_pairs={{0,28},{2,30},{5,1},{7,3},{8,4},{10,6},{13,9},{15,11},{16,12},{18,... | collective-permute-start | bytes 61448 | tf_op jit(solution)/shard_map/ppermute | solution.py:647
  48.3 1.3 %collective-permute-start.17 = (f32[5,8,128]{2,1,0:T(8,128)S(1)}, f32[5,8,128]{2,1,0:T(8,128)S(1)}, u32[]{:S(2)}, u32[]{:S(2)}) collective-permute-start(f32[5,8,128]{2,1,0:T(8,128)S(1)} %get-tuple-element.109), channel_id=1, source_target_pairs={{0,4},{2,6},{5,9},{7,11},{8,12},{10,14},{13,17},{15,19},{16,20},{1... | collective-permute-start | bytes 61448 | tf_op jit(solution)/shard_map/ppermute | solution.py:647
  49.6 1.3 %collective-permute-start.18 = (f32[5,8,128]{2,1,0:T(8,128)S(1)}, f32[5,8,128]{2,1,0:T(8,128)S(1)}, u32[]{:S(2)}, u32[]{:S(2)}) collective-permute-start(f32[5,8,128]{2,1,0:T(8,128)S(1)} %get-tuple-element.110), channel_id=1, source_target_pairs={{0,3},{2,1},{5,4},{7,6},{8,11},{10,9},{13,12},{15,14},{16,19},{18,... | collective-permute-start | bytes 61448 | tf_op jit(solution)/shard_map/ppermute | solution.py:647
  50.9 1.3 %collective-permute-start.19 = (f32[5,8,128]{2,1,0:T(8,128)S(1)}, f32[5,8,128]{2,1,0:T(8,128)S(1)}, u32[]{:S(2)}, u32[]{:S(2)}) collective-permute-start(f32[5,8,128]{2,1,0:T(8,128)S(1)} %get-tuple-element.111), channel_id=1, source_target_pairs={{0,1},{2,3},{5,6},{7,4},{8,9},{10,11},{13,14},{15,12},{16,17},{18,... | collective-permute-start | bytes 61448 | tf_op jit(solution)/shard_map/ppermute | solution.py:647
  52.2 0.0 collective-permute-done.17.refs_1_
  52.2 0.1 collective-permute-done.18.refs_2_
  52.4 0.7 collective-permute-done.19.refs_3_
  53.0 1.3 %collective-permute-start.20 = (f32[5,8,128]{2,1,0:T(8,128)S(1)}, f32[5,8,128]{2,1,0:T(8,128)S(1)}, u32[]{:S(2)}, u32[]{:S(2)}) collective-permute-start(f32[5,8,128]{2,1,0:T(8,128)S(1)} %get-tuple-element.108), channel_id=1, source_target_pairs={{1,29},{3,31},{4,0},{6,2},{9,5},{11,7},{12,8},{14,10},{17,13},{19,... | collective-permute-start | bytes 61448 | tf_op jit(solution)/shard_map/ppermute | solution.py:647
  54.3 1.3 %collective-permute-start.21 = (f32[5,8,128]{2,1,0:T(8,128)S(1)}, f32[5,8,128]{2,1,0:T(8,128)S(1)}, u32[]{:S(2)}, u32[]{:S(2)}) collective-permute-start(f32[5,8,128]{2,1,0:T(8,128)S(1)} %get-tuple-element.109), channel_id=1, source_target_pairs={{1,5},{3,7},{4,8},{6,10},{9,13},{11,15},{12,16},{14,18},{17,21},{1... | collective-permute-start | bytes 61448 | tf_op jit(solution)/shard_map/ppermute | solution.py:647
  55.6 1.3 %collective-permute-start.22 = (f32[5,8,128]{2,1,0:T(8,128)S(1)}, f32[5,8,128]{2,1,0:T(8,128)S(1)}, u32[]{:S(2)}, u32[]{:S(2)}) collective-permute-start(f32[5,8,128]{2,1,0:T(8,128)S(1)} %get-tuple-element.110), channel_id=1, source_target_pairs={{1,0},{3,2},{4,7},{6,5},{9,8},{11,10},{12,15},{14,13},{17,16},{19,... | collective-permute-start | bytes 61448 | tf_op jit(solution)/shard_map/ppermute | solution.py:647
  56.9 1.3 %collective-permute-start.23 = (f32[5,8,128]{2,1,0:T(8,128)S(1)}, f32[5,8,128]{2,1,0:T(8,128)S(1)}, u32[]{:S(2)}, u32[]{:S(2)}) collective-permute-start(f32[5,8,128]{2,1,0:T(8,128)S(1)} %get-tuple-element.111), channel_id=1, source_target_pairs={{1,2},{3,0},{4,5},{6,7},{9,10},{11,8},{12,13},{14,15},{17,18},{19,... | collective-permute-start | bytes 61448 | tf_op jit(solution)/shard_map/ppermute | solution.py:647
  58.2 0.5 collective-permute-done.20.refs_4_
  58.7 4.0 %collective-permute-done.21.refs_5_ = f32[5,8,128]{2,1,0:T(8,128)S(1)} collective-permute-done((f32[5,8,128]{2,1,0:T(8,128)S(1)}, f32[5,8,128]{2,1,0:T(8,128)S(1)}, u32[]{:S(2)}, u32[]{:S(2)}) %collective-permute-start.21) | collective-permute-done | bytes 20512 | tf_op jit(solution)/shard_map/ppermute | solution.py:647
  62.7 0.0 collective-permute-done.22.refs_6_
  62.7 0.0 collective-permute-done.23.refs_7_
  62.7 0.3 shard_map.69
  63.0 3.6 %collective-permute-start.24 = (f32[5,8,128]{2,1,0:T(8,128)S(1)}, f32[5,8,128]{2,1,0:T(8,128)S(1)}, u32[]{:S(2)}, u32[]{:S(2)}) collective-permute-start(f32[5,8,128]{2,1,0:T(8,128)S(1)} %get-tuple-element.121), channel_id=1, source_target_pairs={{0,28},{2,30},{5,1},{7,3},{8,4},{10,6},{13,9},{15,11},{16,12},{18,... | collective-permute-start | bytes 61448 | tf_op jit(solution)/shard_map/ppermute | solution.py:647
  66.6 1.3 %collective-permute-start.25 = (f32[5,8,128]{2,1,0:T(8,128)S(1)}, f32[5,8,128]{2,1,0:T(8,128)S(1)}, u32[]{:S(2)}, u32[]{:S(2)}) collective-permute-start(f32[5,8,128]{2,1,0:T(8,128)S(1)} %get-tuple-element.122), channel_id=1, source_target_pairs={{0,4},{2,6},{5,9},{7,11},{8,12},{10,14},{13,17},{15,19},{16,20},{1... | collective-permute-start | bytes 61448 | tf_op jit(solution)/shard_map/ppermute | solution.py:647
  67.9 1.3 %collective-permute-start.26 = (f32[5,8,128]{2,1,0:T(8,128)S(1)}, f32[5,8,128]{2,1,0:T(8,128)S(1)}, u32[]{:S(2)}, u32[]{:S(2)}) collective-permute-start(f32[5,8,128]{2,1,0:T(8,128)S(1)} %get-tuple-element.123), channel_id=1, source_target_pairs={{0,3},{2,1},{5,4},{7,6},{8,11},{10,9},{13,12},{15,14},{16,19},{18,... | collective-permute-start | bytes 61448 | tf_op jit(solution)/shard_map/ppermute | solution.py:647
  69.2 1.3 %collective-permute-start.27 = (f32[5,8,128]{2,1,0:T(8,128)S(1)}, f32[5,8,128]{2,1,0:T(8,128)S(1)}, u32[]{:S(2)}, u32[]{:S(2)}) collective-permute-start(f32[5,8,128]{2,1,0:T(8,128)S(1)} %get-tuple-element.124), channel_id=1, source_target_pairs={{0,1},{2,3},{5,6},{7,4},{8,9},{10,11},{13,14},{15,12},{16,17},{18,... | collective-permute-start | bytes 61448 | tf_op jit(solution)/shard_map/ppermute | solution.py:647
  70.5 0.0 collective-permute-done.25.refs_1_
  70.5 0.1 collective-permute-done.26.refs_2_
  70.6 0.7 collective-permute-done.27.refs_3_
  71.3 1.3 %collective-permute-start.28 = (f32[5,8,128]{2,1,0:T(8,128)S(1)}, f32[5,8,128]{2,1,0:T(8,128)S(1)}, u32[]{:S(2)}, u32[]{:S(2)}) collective-permute-start(f32[5,8,128]{2,1,0:T(8,128)S(1)} %get-tuple-element.121), channel_id=1, source_target_pairs={{1,29},{3,31},{4,0},{6,2},{9,5},{11,7},{12,8},{14,10},{17,13},{19,... | collective-permute-start | bytes 61448 | tf_op jit(solution)/shard_map/ppermute | solution.py:647
  72.6 1.3 %collective-permute-start.29 = (f32[5,8,128]{2,1,0:T(8,128)S(1)}, f32[5,8,128]{2,1,0:T(8,128)S(1)}, u32[]{:S(2)}, u32[]{:S(2)}) collective-permute-start(f32[5,8,128]{2,1,0:T(8,128)S(1)} %get-tuple-element.122), channel_id=1, source_target_pairs={{1,5},{3,7},{4,8},{6,10},{9,13},{11,15},{12,16},{14,18},{17,21},{1... | collective-permute-start | bytes 61448 | tf_op jit(solution)/shard_map/ppermute | solution.py:647
  73.9 1.3 %collective-permute-start.30 = (f32[5,8,128]{2,1,0:T(8,128)S(1)}, f32[5,8,128]{2,1,0:T(8,128)S(1)}, u32[]{:S(2)}, u32[]{:S(2)}) collective-permute-start(f32[5,8,128]{2,1,0:T(8,128)S(1)} %get-tuple-element.123), channel_id=1, source_target_pairs={{1,0},{3,2},{4,7},{6,5},{9,8},{11,10},{12,15},{14,13},{17,16},{19,... | collective-permute-start | bytes 61448 | tf_op jit(solution)/shard_map/ppermute | solution.py:647
  75.2 1.3 %collective-permute-start.31 = (f32[5,8,128]{2,1,0:T(8,128)S(1)}, f32[5,8,128]{2,1,0:T(8,128)S(1)}, u32[]{:S(2)}, u32[]{:S(2)}) collective-permute-start(f32[5,8,128]{2,1,0:T(8,128)S(1)} %get-tuple-element.124), channel_id=1, source_target_pairs={{1,2},{3,0},{4,5},{6,7},{9,10},{11,8},{12,13},{14,15},{17,18},{19,... | collective-permute-start | bytes 61448 | tf_op jit(solution)/shard_map/ppermute | solution.py:647
  76.5 0.5 collective-permute-done.28.refs_4_
  77.0 4.0 %collective-permute-done.29.refs_5_ = f32[5,8,128]{2,1,0:T(8,128)S(1)} collective-permute-done((f32[5,8,128]{2,1,0:T(8,128)S(1)}, f32[5,8,128]{2,1,0:T(8,128)S(1)}, u32[]{:S(2)}, u32[]{:S(2)}) %collective-permute-start.29) | collective-permute-done | bytes 20512 | tf_op jit(solution)/shard_map/ppermute | solution.py:647
  81.0 1.2 %shard_map.70 = f32[5,4,4,2,8,128]{5,4,3,2,1,0:T(8,128)} custom-call(f32[5,2,2,8,128]{4,3,2,1,0:T(8,128)S(1)} %get-tuple-element.112.c_ref, f32[5,2,2,8,128]{4,3,2,1,0:T(8,128)S(1)} %get-tuple-element.99.rhs_ref, bf16[25,2,16,128]{3,2,1,0:T(8,128)(2,1)S(1)} %bitcast.9, s32[3,8,128]{2,1,0:T(8,128)S(1)} %get-tuple-element.67.flag_ref, ...), custom_call_target="tpu_custom_call" | custom-call | flops 1048576 | bytes 4194304 | tf_op jit(solution)/shard_map/pallas_call | solution.py:625
  (13 shorter events, 0.0 us)
Async XLA Ops:
  0.0 19.8 %copy-start.2 = (f32[2,2,128]{2,1,0:T(2,128)S(1)}, f32[2,2,128]{2,1,0:T(2,128)}, u32[]{:S(2)}) copy-start(f32[2,2,128]{2,1,0:T(2,128)} %param.8) | copy-start | bytes 6148
  0.0 19.8 %copy-start.1 = (f32[3,5,5,2,2,128]{5,4,3,2,1,0:T(2,128)S(1)}, f32[3,5,5,2,2,128]{5,4,3,2,1,0:T(2,128)}, u32[]{:S(2)}) copy-start(f32[3,5,5,2,2,128]{5,4,3,2,1,0:T(2,128)} %param.7) | copy-start | bytes 460804
  1.9 11.8 %collective-permute-start = (f32[5,4,8,128]{3,2,1,0:T(8,128)S(1)}, f32[5,4,8,128]{3,2,1,0:T(8,128)S(1)}, u32[]{:S(2)}, u32[]{:S(2)}) collective-permute-start(f32[5,4,8,128]{3,2,1,0:T(8,128)S(1)} %get-tuple-element.79), channel_id=1, source_target_pairs={{0,28},{2,30},{5,1},{7,3},{8,4},{10,6},{13,9},{15,11},{16,12},{18,... | collective-permute-start | bytes 245768 | tf_op jit(solution)/shard_map/ppermute | solution.py:647
  9.8 3.9 %collective-permute-start.1 = (f32[5,4,8,128]{3,2,1,0:T(8,128)S(1)}, f32[5,4,8,128]{3,2,1,0:T(8,128)S(1)}, u32[]{:S(2)}, u32[]{:S(2)}) collective-permute-start(f32[5,4,8,128]{3,2,1,0:T(8,128)S(1)} %get-tuple-element.80), channel_id=1, source_target_pairs={{0,4},{2,6},{5,9},{7,11},{8,12},{10,14},{13,17},{15,19},{16,20},{1... | collective-permute-start | bytes 245768 | tf_op jit(solution)/shard_map/ppermute | solution.py:647
  11.1 3.3 %collective-permute-start.2 = (f32[5,4,8,128]{3,2,1,0:T(8,128)S(1)}, f32[5,4,8,128]{3,2,1,0:T(8,128)S(1)}, u32[]{:S(2)}, u32[]{:S(2)}) collective-permute-start(f32[5,4,8,128]{3,2,1,0:T(8,128)S(1)} %get-tuple-element.81), channel_id=1, source_target_pairs={{0,3},{2,1},{5,4},{7,6},{8,11},{10,9},{13,12},{15,14},{16,19},{18,... | collective-permute-start | bytes 245768 | tf_op jit(solution)/shard_map/ppermute | solution.py:647
  12.4 2.2 %collective-permute-start.3 = (f32[5,4,8,128]{3,2,1,0:T(8,128)S(1)}, f32[5,4,8,128]{3,2,1,0:T(8,128)S(1)}, u32[]{:S(2)}, u32[]{:S(2)}) collective-permute-start(f32[5,4,8,128]{3,2,1,0:T(8,128)S(1)} %get-tuple-element.82), channel_id=1, source_target_pairs={{0,1},{2,3},{5,6},{7,4},{8,9},{10,11},{13,14},{15,12},{16,17},{18,... | collective-permute-start | bytes 245768 | tf_op jit(solution)/shard_map/ppermute | solution.py:647
  14.6 7.5 %collective-permute-start.4 = (f32[5,4,8,128]{3,2,1,0:T(8,128)S(1)}, f32[5,4,8,128]{3,2,1,0:T(8,128)S(1)}, u32[]{:S(2)}, u32[]{:S(2)}) collective-permute-start(f32[5,4,8,128]{3,2,1,0:T(8,128)S(1)} %get-tuple-element.79), channel_id=1, source_target_pairs={{1,29},{3,31},{4,0},{6,2},{9,5},{11,7},{12,8},{14,10},{17,13},{19,... | collective-permute-start | bytes 245768 | tf_op jit(solution)/shard_map/ppermute | solution.py:647
  15.9 9.0 %collective-permute-start.5 = (f32[5,4,8,128]{3,2,1,0:T(8,128)S(1)}, f32[5,4,8,128]{3,2,1,0:T(8,128)S(1)}, u32[]{:S(2)}, u32[]{:S(2)}) collective-permute-start(f32[5,4,8,128]{3,2,1,0:T(8,128)S(1)} %get-tuple-element.80), channel_id=1, source_target_pairs={{1,5},{3,7},{4,8},{6,10},{9,13},{11,15},{12,16},{14,18},{17,21},{1... | collective-permute-start | bytes 245768 | tf_op jit(solution)/shard_map/ppermute | solution.py:647
  17.2 7.7 %collective-permute-start.6 = (f32[5,4,8,128]{3,2,1,0:T(8,128)S(1)}, f32[5,4,8,128]{3,2,1,0:T(8,128)S(1)}, u32[]{:S(2)}, u32[]{:S(2)}) collective-permute-start(f32[5,4,8,128]{3,2,1,0:T(8,128)S(1)} %get-tuple-element.81), channel_id=1, source_target_pairs={{1,0},{3,2},{4,7},{6,5},{9,8},{11,10},{12,15},{14,13},{17,16},{19,... | collective-permute-start | bytes 245768 | tf_op jit(solution)/shard_map/ppermute | solution.py:647
  18.5 6.4 %collective-permute-start.7 = (f32[5,4,8,128]{3,2,1,0:T(8,128)S(1)}, f32[5,4,8,128]{3,2,1,0:T(8,128)S(1)}, u32[]{:S(2)}, u32[]{:S(2)}) collective-permute-start(f32[5,4,8,128]{3,2,1,0:T(8,128)S(1)} %get-tuple-element.82), channel_id=1, source_target_pairs={{1,2},{3,0},{4,5},{6,7},{9,10},{11,8},{12,13},{14,15},{17,18},{19,... | collective-permute-start | bytes 245768 | tf_op jit(solution)/shard_map/ppermute | solution.py:647
  25.6 19.0 %copy-start = (bf16[5,5,2,2,2,2,2,128]{7,6,5,4,3,2,1,0:T(2,128)(2,1)S(1)}, bf16[5,5,2,2,2,2,2,128]{7,6,5,4,3,2,1,0:T(2,128)(2,1)}, u32[]{:S(2)}) copy-start(bf16[5,5,2,2,2,2,2,128]{7,6,5,4,3,2,1,0:T(2,128)(2,1)} %param.11) | copy-start | bytes 614404
  25.6 8.5 %collective-permute-start.8 = (f32[5,8,128]{2,1,0:T(8,128)S(1)}, f32[5,8,128]{2,1,0:T(8,128)S(1)}, u32[]{:S(2)}, u32[]{:S(2)}) collective-permute-start(f32[5,8,128]{2,1,0:T(8,128)S(1)} %get-tuple-element.94), channel_id=1, source_target_pairs={{0,28},{2,30},{5,1},{7,3},{8,4},{10,6},{13,9},{15,11},{16,12},{18,... | collective-permute-start | bytes 61448 | tf_op jit(solution)/shard_map/ppermute | solution.py:647
  30.2 3.9 %collective-permute-start.9 = (f32[5,8,128]{2,1,0:T(8,128)S(1)}, f32[5,8,128]{2,1,0:T(8,128)S(1)}, u32[]{:S(2)}, u32[]{:S(2)}) collective-permute-start(f32[5,8,128]{2,1,0:T(8,128)S(1)} %get-tuple-element.95), channel_id=1, source_target_pairs={{0,4},{2,6},{5,9},{7,11},{8,12},{10,14},{13,17},{15,19},{16,20},{1... | collective-permute-start | bytes 61448 | tf_op jit(solution)/shard_map/ppermute | solution.py:647
  31.5 2.8 %collective-permute-start.10 = (f32[5,8,128]{2,1,0:T(8,128)S(1)}, f32[5,8,128]{2,1,0:T(8,128)S(1)}, u32[]{:S(2)}, u32[]{:S(2)}) collective-permute-start(f32[5,8,128]{2,1,0:T(8,128)S(1)} %get-tuple-element.96), channel_id=1, source_target_pairs={{0,3},{2,1},{5,4},{7,6},{8,11},{10,9},{13,12},{15,14},{16,19},{18,... | collective-permute-start | bytes 61448 | tf_op jit(solution)/shard_map/ppermute | solution.py:647
  32.8 2.1 %collective-permute-start.11 = (f32[5,8,128]{2,1,0:T(8,128)S(1)}, f32[5,8,128]{2,1,0:T(8,128)S(1)}, u32[]{:S(2)}, u32[]{:S(2)}) collective-permute-start(f32[5,8,128]{2,1,0:T(8,128)S(1)} %get-tuple-element.97), channel_id=1, source_target_pairs={{0,1},{2,3},{5,6},{7,4},{8,9},{10,11},{13,14},{15,12},{16,17},{18,... | collective-permute-start | bytes 61448 | tf_op jit(solution)/shard_map/ppermute | solution.py:647
  34.9 5.8 %collective-permute-start.12 = (f32[5,8,128]{2,1,0:T(8,128)S(1)}, f32[5,8,128]{2,1,0:T(8,128)S(1)}, u32[]{:S(2)}, u32[]{:S(2)}) collective-permute-start(f32[5,8,128]{2,1,0:T(8,128)S(1)} %get-tuple-element.94), channel_id=1, source_target_pairs={{1,29},{3,31},{4,0},{6,2},{9,5},{11,7},{12,8},{14,10},{17,13},{19,... | collective-permute-start | bytes 61448 | tf_op jit(solution)/shard_map/ppermute | solution.py:647
  36.2 8.4 %collective-permute-start.13 = (f32[5,8,128]{2,1,0:T(8,128)S(1)}, f32[5,8,128]{2,1,0:T(8,128)S(1)}, u32[]{:S(2)}, u32[]{:S(2)}) collective-permute-start(f32[5,8,128]{2,1,0:T(8,128)S(1)} %get-tuple-element.95), channel_id=1, source_target_pairs={{1,5},{3,7},{4,8},{6,10},{9,13},{11,15},{12,16},{14,18},{17,21},{1... | collective-permute-start | bytes 61448 | tf_op jit(solution)/shard_map/ppermute | solution.py:647
  37.5 7.1 %collective-permute-start.14 = (f32[5,8,128]{2,1,0:T(8,128)S(1)}, f32[5,8,128]{2,1,0:T(8,128)S(1)}, u32[]{:S(2)}, u32[]{:S(2)}) collective-permute-start(f32[5,8,128]{2,1,0:T(8,128)S(1)} %get-tuple-element.96), channel_id=1, source_target_pairs={{1,0},{3,2},{4,7},{6,5},{9,8},{11,10},{12,15},{14,13},{17,16},{19,... | collective-permute-start | bytes 61448 | tf_op jit(solution)/shard_map/ppermute | solution.py:647
  38.8 5.8 %collective-permute-start.15 = (f32[5,8,128]{2,1,0:T(8,128)S(1)}, f32[5,8,128]{2,1,0:T(8,128)S(1)}, u32[]{:S(2)}, u32[]{:S(2)}) collective-permute-start(f32[5,8,128]{2,1,0:T(8,128)S(1)} %get-tuple-element.97), channel_id=1, source_target_pairs={{1,2},{3,0},{4,5},{6,7},{9,10},{11,8},{12,13},{14,15},{17,18},{19,... | collective-permute-start | bytes 61448 | tf_op jit(solution)/shard_map/ppermute | solution.py:647
  44.7 7.5 %collective-permute-start.16 = (f32[5,8,128]{2,1,0:T(8,128)S(1)}, f32[5,8,128]{2,1,0:T(8,128)S(1)}, u32[]{:S(2)}, u32[]{:S(2)}) collective-permute-start(f32[5,8,128]{2,1,0:T(8,128)S(1)} %get-tuple-element.108), channel_id=1, source_target_pairs={{0,28},{2,30},{5,1},{7,3},{8,4},{10,6},{13,9},{15,11},{16,12},{18,... | collective-permute-start | bytes 61448 | tf_op jit(solution)/shard_map/ppermute | solution.py:647
  48.3 3.9 %collective-permute-start.17 = (f32[5,8,128]{2,1,0:T(8,128)S(1)}, f32[5,8,128]{2,1,0:T(8,128)S(1)}, u32[]{:S(2)}, u32[]{:S(2)}) collective-permute-start(f32[5,8,128]{2,1,0:T(8,128)S(1)} %get-tuple-element.109), channel_id=1, source_target_pairs={{0,4},{2,6},{5,9},{7,11},{8,12},{10,14},{13,17},{15,19},{16,20},{1... | collective-permute-start | bytes 61448 | tf_op jit(solution)/shard_map/ppermute | solution.py:647
  49.6 2.8 %collective-permute-start.18 = (f32[5,8,128]{2,1,0:T(8,128)S(1)}, f32[5,8,128]{2,1,0:T(8,128)S(1)}, u32[]{:S(2)}, u32[]{:S(2)}) collective-permute-start(f32[5,8,128]{2,1,0:T(8,128)S(1)} %get-tuple-element.110), channel_id=1, source_target_pairs={{0,3},{2,1},{5,4},{7,6},{8,11},{10,9},{13,12},{15,14},{16,19},{18,... | collective-permute-start | bytes 61448 | tf_op jit(solution)/shard_map/ppermute | solution.py:647
  50.9 2.1 %collective-permute-start.19 = (f32[5,8,128]{2,1,0:T(8,128)S(1)}, f32[5,8,128]{2,1,0:T(8,128)S(1)}, u32[]{:S(2)}, u32[]{:S(2)}) collective-permute-start(f32[5,8,128]{2,1,0:T(8,128)S(1)} %get-tuple-element.111), channel_id=1, source_target_pairs={{0,1},{2,3},{5,6},{7,4},{8,9},{10,11},{13,14},{15,12},{16,17},{18,... | collective-permute-start | bytes 61448 | tf_op jit(solution)/shard_map/ppermute | solution.py:647
  53.0 5.7 %collective-permute-start.20 = (f32[5,8,128]{2,1,0:T(8,128)S(1)}, f32[5,8,128]{2,1,0:T(8,128)S(1)}, u32[]{:S(2)}, u32[]{:S(2)}) collective-permute-start(f32[5,8,128]{2,1,0:T(8,128)S(1)} %get-tuple-element.108), channel_id=1, source_target_pairs={{1,29},{3,31},{4,0},{6,2},{9,5},{11,7},{12,8},{14,10},{17,13},{19,... | collective-permute-start | bytes 61448 | tf_op jit(solution)/shard_map/ppermute | solution.py:647
  54.3 8.4 %collective-permute-start.21 = (f32[5,8,128]{2,1,0:T(8,128)S(1)}, f32[5,8,128]{2,1,0:T(8,128)S(1)}, u32[]{:S(2)}, u32[]{:S(2)}) collective-permute-start(f32[5,8,128]{2,1,0:T(8,128)S(1)} %get-tuple-element.109), channel_id=1, source_target_pairs={{1,5},{3,7},{4,8},{6,10},{9,13},{11,15},{12,16},{14,18},{17,21},{1... | collective-permute-start | bytes 61448 | tf_op jit(solution)/shard_map/ppermute | solution.py:647
  55.6 7.1 %collective-permute-start.22 = (f32[5,8,128]{2,1,0:T(8,128)S(1)}, f32[5,8,128]{2,1,0:T(8,128)S(1)}, u32[]{:S(2)}, u32[]{:S(2)}) collective-permute-start(f32[5,8,128]{2,1,0:T(8,128)S(1)} %get-tuple-element.110), channel_id=1, source_target_pairs={{1,0},{3,2},{4,7},{6,5},{9,8},{11,10},{12,15},{14,13},{17,16},{19,... | collective-permute-start | bytes 61448 | tf_op jit(solution)/shard_map/ppermute | solution.py:647
  56.9 5.8 %collective-permute-start.23 = (f32[5,8,128]{2,1,0:T(8,128)S(1)}, f32[5,8,128]{2,1,0:T(8,128)S(1)}, u32[]{:S(2)}, u32[]{:S(2)}) collective-permute-start(f32[5,8,128]{2,1,0:T(8,128)S(1)} %get-tuple-element.111), channel_id=1, source_target_pairs={{1,2},{3,0},{4,5},{6,7},{9,10},{11,8},{12,13},{14,15},{17,18},{19,... | collective-permute-start | bytes 61448 | tf_op jit(solution)/shard_map/ppermute | solution.py:647
  63.0 7.5 %collective-permute-start.24 = (f32[5,8,128]{2,1,0:T(8,128)S(1)}, f32[5,8,128]{2,1,0:T(8,128)S(1)}, u32[]{:S(2)}, u32[]{:S(2)}) collective-permute-start(f32[5,8,128]{2,1,0:T(8,128)S(1)} %get-tuple-element.121), channel_id=1, source_target_pairs={{0,28},{2,30},{5,1},{7,3},{8,4},{10,6},{13,9},{15,11},{16,12},{18,... | collective-permute-start | bytes 61448 | tf_op jit(solution)/shard_map/ppermute | solution.py:647
  66.6 3.9 %collective-permute-start.25 = (f32[5,8,128]{2,1,0:T(8,128)S(1)}, f32[5,8,128]{2,1,0:T(8,128)S(1)}, u32[]{:S(2)}, u32[]{:S(2)}) collective-permute-start(f32[5,8,128]{2,1,0:T(8,128)S(1)} %get-tuple-element.122), channel_id=1, source_target_pairs={{0,4},{2,6},{5,9},{7,11},{8,12},{10,14},{13,17},{15,19},{16,20},{1... | collective-permute-start | bytes 61448 | tf_op jit(solution)/shard_map/ppermute | solution.py:647
  67.9 2.8 %collective-permute-start.26 = (f32[5,8,128]{2,1,0:T(8,128)S(1)}, f32[5,8,128]{2,1,0:T(8,128)S(1)}, u32[]{:S(2)}, u32[]{:S(2)}) collective-permute-start(f32[5,8,128]{2,1,0:T(8,128)S(1)} %get-tuple-element.123), channel_id=1, source_target_pairs={{0,3},{2,1},{5,4},{7,6},{8,11},{10,9},{13,12},{15,14},{16,19},{18,... | collective-permute-start | bytes 61448 | tf_op jit(solution)/shard_map/ppermute | solution.py:647
  69.2 2.1 %collective-permute-start.27 = (f32[5,8,128]{2,1,0:T(8,128)S(1)}, f32[5,8,128]{2,1,0:T(8,128)S(1)}, u32[]{:S(2)}, u32[]{:S(2)}) collective-permute-start(f32[5,8,128]{2,1,0:T(8,128)S(1)} %get-tuple-element.124), channel_id=1, source_target_pairs={{0,1},{2,3},{5,6},{7,4},{8,9},{10,11},{13,14},{15,12},{16,17},{18,... | collective-permute-start | bytes 61448 | tf_op jit(solution)/shard_map/ppermute | solution.py:647
  71.3 5.7 %collective-permute-start.28 = (f32[5,8,128]{2,1,0:T(8,128)S(1)}, f32[5,8,128]{2,1,0:T(8,128)S(1)}, u32[]{:S(2)}, u32[]{:S(2)}) collective-permute-start(f32[5,8,128]{2,1,0:T(8,128)S(1)} %get-tuple-element.121), channel_id=1, source_target_pairs={{1,29},{3,31},{4,0},{6,2},{9,5},{11,7},{12,8},{14,10},{17,13},{19,... | collective-permute-start | bytes 61448 | tf_op jit(solution)/shard_map/ppermute | solution.py:647
  72.6 8.4 %collective-permute-start.29 = (f32[5,8,128]{2,1,0:T(8,128)S(1)}, f32[5,8,128]{2,1,0:T(8,128)S(1)}, u32[]{:S(2)}, u32[]{:S(2)}) collective-permute-start(f32[5,8,128]{2,1,0:T(8,128)S(1)} %get-tuple-element.122), channel_id=1, source_target_pairs={{1,5},{3,7},{4,8},{6,10},{9,13},{11,15},{12,16},{14,18},{17,21},{1... | collective-permute-start | bytes 61448 | tf_op jit(solution)/shard_map/ppermute | solution.py:647
  73.9 7.1 %collective-permute-start.30 = (f32[5,8,128]{2,1,0:T(8,128)S(1)}, f32[5,8,128]{2,1,0:T(8,128)S(1)}, u32[]{:S(2)}, u32[]{:S(2)}) collective-permute-start(f32[5,8,128]{2,1,0:T(8,128)S(1)} %get-tuple-element.123), channel_id=1, source_target_pairs={{1,0},{3,2},{4,7},{6,5},{9,8},{11,10},{12,15},{14,13},{17,16},{19,... | collective-permute-start | bytes 61448 | tf_op jit(solution)/shard_map/ppermute | solution.py:647
  75.2 5.8 %collective-permute-start.31 = (f32[5,8,128]{2,1,0:T(8,128)S(1)}, f32[5,8,128]{2,1,0:T(8,128)S(1)}, u32[]{:S(2)}, u32[]{:S(2)}) collective-permute-start(f32[5,8,128]{2,1,0:T(8,128)S(1)} %get-tuple-element.124), channel_id=1, source_target_pairs={{1,2},{3,0},{4,5},{6,7},{9,10},{11,8},{12,13},{14,15},{17,18},{19,... | collective-permute-start | bytes 61448 | tf_op jit(solution)/shard_map/ppermute | solution.py:647

commit v4 on v2

--- a/solution.py
+++ b/solution.py
@@ -114,6 +114,16 @@
 def put_pair(even_ref, odd_ref, index, low_face, high_face, is_even):
     even_ref[index] = jnp.where(is_even, high_face, low_face)
     odd_ref[index] = jnp.where(is_even, low_face, high_face)
+
+
+def block_views(even_ref, odd_ref):
+    x, y = lax.rem(lax.axis_index("gx"), 2), lax.rem(lax.axis_index("gy"), 2)
+    return (
+        odd_ref.at[x + 2 * (1 - y)],
+        even_ref.at[(1 - x) + 2 * y],
+        odd_ref.at[(1 - x) + 2 * y],
+        even_ref.at[x + 2 * (1 - y)],
+    )
 
 
 def fine_faces(u_ref, flag_ref, xo, xe, yo, ye):
@@ -348,7 +358,7 @@
 
 
 def second_kernel(
-    acc_ref, u_ref, smooth_ref, flag_ref, face_ref, rxo, rxe, ryo, rye, out_ref, xo, xe, yo, ye, part_ref
+    acc_ref, u_ref, smooth_ref, flag_ref, face_ref, rxo, rxe, ryo, rye, out_ref, even_ref, odd_ref, part_ref
 ):
     remote_parts((rxe, rye), (rxo, ryo), flag_ref, face_ref, part_ref)
     for a in range(4):
@@ -363,7 +373,7 @@
                         total[q] = term if i == 0 else total[q] + term
                 for q in range(2):
                     out_ref[o, a, b, q] = u_ref[o, a, b, q] + OMEGA * total[q]
-    restricted_faces(out_ref, flag_ref, xo, xe, yo, ye)
+    restricted_faces(out_ref, flag_ref, *block_views(even_ref, odd_ref))
 
 
 def coarse_smooth(smooth_ref, fields):
@@ -469,8 +479,9 @@
 
 
 def restrict_kernel(
-    acc_ref, flag_ref, face_ref, smooth_ref, rxo, rxe, ryo, rye, rhs_ref, c_ref, xo, xe, yo, ye
+    acc_ref, flag_ref, face_ref, smooth_ref, got_even, got_odd, rhs_ref, c_ref, even_ref, odd_ref
 ):
+    rxo, rxe, ryo, rye = block_views(got_even, got_odd)
     rhs = [[[acc_ref[v, i, j] for j in range(2)] for i in range(2)] for v in range(5)]
     for d, axis in ((0, "gx"), (1, "gy")):
         is_even = parity(axis)
@@ -501,7 +512,7 @@
             for j in range(2):
                 rhs_ref[v, i, j] = rhs[v][i][j]
                 c_ref[v, i, j] = c[v][i][j]
-    coarse_faces(c, flag_ref, xo, xe, yo, ye)
+    coarse_faces(c, flag_ref, *block_views(even_ref, odd_ref))
 
 
 def coarse_step(c_ref, rhs_ref, smooth_ref, flag_ref, jac_ref, damp_ref, rxo, rxe, ryo, rye):
@@ -562,14 +573,15 @@
 
 
 def coarse_kernel(
-    c_ref, rhs_ref, smooth_ref, flag_ref, jac_ref, damp_ref, rxo, rxe, ryo, rye, out_ref, xo, xe, yo, ye
+    c_ref, rhs_ref, smooth_ref, flag_ref, jac_ref, damp_ref, got_even, got_odd, out_ref, even_ref, odd_ref
 ):
+    rxo, rxe, ryo, rye = block_views(got_even, got_odd)
     c = coarse_step(c_ref, rhs_ref, smooth_ref, flag_ref, jac_ref, damp_ref, rxo, rxe, ryo, rye)
     for v in range(5):
         for i in range(2):
             for j in range(2):
                 out_ref[v, i, j] = c[v][i][j]
-    coarse_faces(c, flag_ref, xo, xe, yo, ye)
+    coarse_faces(c, flag_ref, *block_views(even_ref, odd_ref))
 
 
 def spread(first, second):
@@ -577,8 +589,9 @@
 
 
 def last_kernel(
-    c_ref, rhs_ref, smooth_ref, flag_ref, jac_ref, damp_ref, rxo, rxe, ryo, rye, second_ref, out_hbm, out_ref, sems
+    c_ref, rhs_ref, smooth_ref, flag_ref, jac_ref, damp_ref, got_even, got_odd, second_ref, out_hbm, out_ref, sems
 ):
+    rxo, rxe, ryo, rye = block_views(got_even, got_odd)
     c = coarse_step(c_ref, rhs_ref, smooth_ref, flag_ref, jac_ref, damp_ref, rxo, rxe, ryo, rye)
     low = c_low()
     copies = []
@@ -604,7 +617,7 @@
 FINE = (5, 4, 4, 2, 8, 128)
 FINE_MESSAGE = (5, 4, 8, 128)
 COARSE = (5, 2, 2, 8, 128)
-COARSE_MESSAGE = (5, 8, 128)
+COARSE_MESSAGE = (4, 5, 8, 128)
 
 
 def vmem(shape, dtype=F32):
@@ -651,6 +664,21 @@
     return xo, xe, yo, ye
 
 
+def blocks(first):
+    nx, ny = lax.axis_size("gx"), lax.axis_size("gy")
+    return [
+        [(i + a) % nx * ny + (j + b) % ny for b in range(2) for a in range(2)]
+        for i in range(first, nx, 2)
+        for j in range(first, ny, 2)
+    ]
+
+
+def block_exchange(even, odd):
+    odd = lax.all_to_all(odd, ("gx", "gy"), 0, 0, axis_index_groups=blocks(1), tiled=True)
+    even = lax.all_to_all(even, ("gx", "gy"), 0, 0, axis_index_groups=blocks(0), tiled=True)
+    return even, odd
+
+
 def body(source, jacobian, damping, orient, smoother, coarse_smoother):
     source = source.reshape(FINE)
     smoother = smoother.reshape(25, 4, 4, 16, 128)
@@ -659,7 +687,7 @@
     damping = damping.reshape(4, 128)
     orient = orient.reshape(3, 4, 128)
     fine_messages = [vmem(FINE_MESSAGE)] * 4
-    coarse_messages = [vmem(COARSE_MESSAGE)] * 4
+    coarse_messages = [vmem(COARSE_MESSAGE)] * 2
 
     source, smoother, first, flag, *sent = call(
         first_kernel,
@@ -683,7 +711,7 @@
         scratch=[pltpu.VMEM((4, 5, 4, 2, 8, 128), F32)],
         flops=3 * 2**20,
     )
-    got = exchange(*sent)
+    got = block_exchange(*sent)
     (acc,) = call(restricted_volume_kernel, (source, second, flag, jac8, damp8), [vmem(COARSE)], flops=4 * 2**20)
     rhs, coarse, *sent = call(
         restrict_kernel,
@@ -691,14 +719,14 @@
         [vmem(COARSE), vmem(COARSE)] + coarse_messages,
         flops=2**20,
     )
-    got = exchange(*sent)
+    got = block_exchange(*sent)
     coarse, *sent = call(
         coarse_kernel,
         (coarse, rhs, coarse_smoother, flag, jac8, damp8, *got),
         [vmem(COARSE)] + coarse_messages,
         flops=2**20,
     )
-    got = exchange(*sent)
+    got = block_exchange(*sent)
     (out,) = call(
         last_kernel,
         (coarse, rhs, coarse_smoother, flag, jac8, damp8, *got, second),

time: 34.7 us -> 63.5 us (1.83)
  blocking collectives: 0 us -> 38.4 us
  starting transfers between devices: 20.2 us -> 14.3 us
  waiting for transfers between devices: 7.21 us -> 2.63 us
    all_to_all x0 -> x5, blocking collectives: none -> 38.4 us  [the longest x3 20.6 us: block_exchange(): lax.all_to_all(even, ('gx', 'gy'), 0, 0, axis_index_groups=blocks(0), til...]
    ppermute x4 -> x1, starting transfers between devices: 13.7 us -> 6.04 us  [exchange(): xo = lax.ppermute(xo, 'gx', odd_x)]
    all_to_all x0 -> x1, starting transfers between devices: none -> 6.61 us  [block_exchange(): lax.all_to_all(odd, ('gx', 'gy'), 0, 0, axis_index_groups=blocks(1), tile...]
    ppermute x4 -> x1, waiting for transfers between devices: 6.46 us -> 0.01 us  [exchange(): xo = lax.ppermute(xo, 'gx', odd_x)]
    ppermute x4 -> x1, starting transfers between devices: 5.85 us -> 0.96 us  [exchange(): ye = lax.ppermute(ye, 'gy', even_y)]
    all_to_all x0 -> x1, waiting for transfers between devices: none -> 1.9 us  [block_exchange(): lax.all_to_all(odd, ('gx', 'gy'), 0, 0, axis_index_groups=blocks(1), tile...]
  transfers between devices with their start and end apart: 16 -> 5, of which waited for: 5 -> 3; matrix products, arithmetic and copies ran while one was open for 0% -> 0% of each run, Pallas kernels for 8% -> 5%
where the time goes in v4:
time: 63.5 us; the launch traced here: 63.1 us
  blocking collectives  38.4 us (60%)
  starting transfers between devices  14.3 us (23%)
  Pallas kernels  7.64 us (12%)
  waiting for transfers between devices  2.63 us (4%)
    all_to_all x3, blocking collectives, block_exchange(): lax.all_to_all(even, ('gx', 'gy'), 0, 0, axis_index_groups=blocks(0), til...  20.6 us
    all_to_all x2, blocking collectives, block_exchange(): lax.all_to_all(odd, ('gx', 'gy'), 0, 0, axis_index_groups=blocks(1), tile...  17.9 us
    pallas_call x7, Pallas kernels, call(): pl.pallas_call(kernel, out_shape=outs, in_specs=in_specs, out_specs=out_s...  7.64 us
    all_to_all x1, starting transfers between devices, block_exchange(): lax.all_to_all(odd, ('gx', 'gy'), 0, 0, axis_index_groups=blocks(1), tile...  6.61 us
    ppermute x1, starting transfers between devices, exchange(): xo = lax.ppermute(xo, 'gx', odd_x)  6.04 us
    all_to_all x1, waiting for transfers between devices, block_exchange(): lax.all_to_all(odd, ('gx', 'gy'), 0, 0, axis_index_groups=blocks(1), tile...  1.9 us
  transfers between devices with their start and end apart: 5, of which 3 were waited for; matrix products, arithmetic and copies ran while one was open for 0% of the time, Pallas kernels for 5%

profile of v4, /device:TPU:0, one launch (start us, length us, event | category | flops | bytes accessed | tf_op | source)
XLA Modules:
  0.0 63.1 jit_solution(15825237239339411207)
XLA Ops:
  0.0 0.0 copy-start.2
  0.0 0.0 copy-start.1
  0.0 1.9 %shard_map.64 = (f32[5,4,4,2,8,128]{5,4,3,2,1,0:T(8,128)S(1)}, bf16[25,4,4,16,128]{4,3,2,1,0:T(8,128)(2,1)S(1)}, f32[5,4,4,2,8,128]{5,4,3,2,1,0:T(8,128)S(1)}, s...) custom-call(f32[5,4,4,2,8,128]{5,4,3,2,1,0:T(8,128)} %bitcast.13, ...), custom_call_target="tpu_custom_call" | custom-call | flops 1638400 | bytes 4194304 | tf_op jit(solution)/shard_map/pallas_call | solution.py:639
  1.9 6.0 %collective-permute-start = (f32[5,4,8,128]{3,2,1,0:T(8,128)S(1)}, f32[5,4,8,128]{3,2,1,0:T(8,128)S(1)}, u32[]{:S(2)}, u32[]{:S(2)}) collective-permute-start(f32[5,4,8,128]{3,2,1,0:T(8,128)S(1)} %get-tuple-element.33), channel_id=1, source_target_pairs={{0,28},{4,8},{8,4},{12,16},{16,12},{20,24},{24,20},{28,0},{1,29},{... | collective-permute-start | bytes 245768 | tf_op jit(solution)/shard_map/ppermute | solution.py:660
  8.0 0.0 collective-permute-start.1
  8.0 0.7 %collective-permute-start.2 = (f32[5,4,8,128]{3,2,1,0:T(8,128)S(1)}, f32[5,4,8,128]{3,2,1,0:T(8,128)S(1)}, u32[]{:S(2)}, u32[]{:S(2)}) collective-permute-start(f32[5,4,8,128]{3,2,1,0:T(8,128)S(1)} %get-tuple-element.35), channel_id=1, source_target_pairs={{0,3},{1,2},{2,1},{3,0},{4,7},{5,6},{6,5},{7,4},{8,11},{9,10},{10,... | collective-permute-start | bytes 245768 | tf_op jit(solution)/shard_map/ppermute | solution.py:662
  8.7 1.0 %collective-permute-start.3 = (f32[5,4,8,128]{3,2,1,0:T(8,128)S(1)}, f32[5,4,8,128]{3,2,1,0:T(8,128)S(1)}, u32[]{:S(2)}, u32[]{:S(2)}) collective-permute-start(f32[5,4,8,128]{3,2,1,0:T(8,128)S(1)} %get-tuple-element.36), channel_id=1, source_target_pairs={{0,1},{1,0},{2,3},{3,2},{4,5},{5,4},{6,7},{7,6},{8,9},{9,8},{10,11... | collective-permute-start | bytes 245768 | tf_op jit(solution)/shard_map/ppermute | solution.py:663
  9.6 0.0 copy-done.2
  9.6 0.0 copy-done.1
  9.6 2.3 %shard_map.65 = (f32[5,4,4,2,8,128]{5,4,3,2,1,0:T(8,128)S(1)}, f32[75,8,128]{2,1,0:T(8,128)S(1)}, f32[8,128]{1,0:T(8,128)S(1)}, f32[4,25,8,128]{3,2,1,0:T(8,128)S(1)}) custom-call(f32[5,4,4,2,8,128]{5,4,3,2,1,0:T(8,128)S(1)} %get-tuple-element.27.src_ref, f32[5,4,4,2,8,128]{5,4,3,2,1,0:T(8,128)S(1)} %get-tuple-element.28.u_ref, ...), custom_call_target="tpu_custom_call" | custom-call | flops 9437184 | bytes 4194304 | tf_op jit(solution)/shard_map/pallas_call | solution.py:639
  11.9 0.0 collective-permute-done.rxo
  11.9 0.5 collective-permute-done.1.rxe
  12.4 0.2 collective-permute-done.2.ryo
  12.7 0.0 collective-permute-done.3.rye
  12.7 1.3 %shard_map.66 = (f32[5,4,4,2,8,128]{5,4,3,2,1,0:T(8,128)S(1)}, f32[4,5,8,128]{3,2,1,0:T(8,128)S(1)}, f32[4,5,8,128]{3,2,1,0:T(8,128)}) custom-call(f32[5,4,4,2,8,128]{5,4,3,2,1,0:T(8,128)S(1)} %get-tuple-element.30.acc_ref, f32[5,4,4,2,8,128]{5,4,3,2,1,0:T(8,128)S(1)} %get-tuple-element.28.u_ref, ...), custom_call_target="tpu_custom_call" | custom-call | flops 3145728 | bytes 4194304 | tf_op jit(solution)/shard_map/pallas_call | solution.py:639
  13.9 0.0 copy-start
  13.9 7.4 %all_to_all.30.got_even = f32[4,5,8,128]{3,2,1,0:T(8,128)S(1)} all-to-all(f32[4,5,8,128]{3,2,1,0:T(8,128)S(1)} %get-tuple-element.40), channel_id=1, replica_groups={{0,4,1,5},{2,6,3,7},{8,12,9,13},{10,14,11,15},{16,20,17,21},{18,22,19,2..., dimensions={0} | all-to-all | bytes 163840 | tf_op jit(solution)/shard_map/all_to_all | solution.py:678
  21.4 6.6 %all-to-all-start.1 = ((f32[4,5,8,128]{3,2,1,0:T(8,128)}), f32[4,5,8,128]{3,2,1,0:T(8,128)S(1)}, u32[]{:S(2)}, u32[]{:S(2)}) async-start(f32[4,5,8,128]{3,2,1,0:T(8,128)} %get-tuple-element.41), calls=%async_computation.1 | async-start | bytes 163840 | tf_op jit(solution)/shard_map/all_to_all | solution.py:677
  28.0 0.6 shard_map.67.acc_ref
  28.6 1.9 %all-to-all-done.1.got_odd = f32[4,5,8,128]{3,2,1,0:T(8,128)S(1)} async-done(((f32[4,5,8,128]{3,2,1,0:T(8,128)}), f32[4,5,8,128]{3,2,1,0:T(8,128)S(1)}, u32[]{:S(2)}, u32[]{:S(2)}) %all-to-all-start.1) | async-done | bytes 81952 | tf_op jit(solution)/shard_map/all_to_all | solution.py:677
  30.5 0.0 copy-done
  30.5 0.1 shard_map.68
  30.6 6.6 %all_to_all.31.got_even = f32[4,5,8,128]{3,2,1,0:T(8,128)S(1)} all-to-all(f32[4,5,8,128]{3,2,1,0:T(8,128)S(1)} %get-tuple-element.44), channel_id=1, replica_groups={{0,4,1,5},{2,6,3,7},{8,12,9,13},{10,14,11,15},{16,20,17,21},{18,22,19,2..., dimensions={0} | all-to-all | bytes 163840 | tf_op jit(solution)/shard_map/all_to_all | solution.py:678
  37.2 8.9 %all_to_all.32.got_odd = f32[4,5,8,128]{3,2,1,0:T(8,128)S(1)} all-to-all(f32[4,5,8,128]{3,2,1,0:T(8,128)S(1)} %get-tuple-element.45), channel_id=1, replica_groups={{5,9,6,10},{7,11,4,8},{13,17,14,18},{15,19,12,16},{21,25,22,26},{23,27,..., dimensions={0} | all-to-all | bytes 163840 | tf_op jit(solution)/shard_map/all_to_all | solution.py:677
  46.1 0.3 shard_map.69
  46.4 6.6 %all_to_all.33.got_even = f32[4,5,8,128]{3,2,1,0:T(8,128)S(1)} all-to-all(f32[4,5,8,128]{3,2,1,0:T(8,128)S(1)} %get-tuple-element.47), channel_id=1, replica_groups={{0,4,1,5},{2,6,3,7},{8,12,9,13},{10,14,11,15},{16,20,17,21},{18,22,19,2..., dimensions={0} | all-to-all | bytes 163840 | tf_op jit(solution)/shard_map/all_to_all | solution.py:678
  53.0 8.9 %all_to_all.34.got_odd = f32[4,5,8,128]{3,2,1,0:T(8,128)S(1)} all-to-all(f32[4,5,8,128]{3,2,1,0:T(8,128)S(1)} %get-tuple-element.48), channel_id=1, replica_groups={{5,9,6,10},{7,11,4,8},{13,17,14,18},{15,19,12,16},{21,25,22,26},{23,27,..., dimensions={0} | all-to-all | bytes 163840 | tf_op jit(solution)/shard_map/all_to_all | solution.py:677
  61.9 1.2 %shard_map.70 = f32[5,4,4,2,8,128]{5,4,3,2,1,0:T(8,128)} custom-call(f32[5,2,2,8,128]{4,3,2,1,0:T(8,128)S(1)} %get-tuple-element.46.c_ref, f32[5,2,2,8,128]{4,3,2,1,0:T(8,128)S(1)} %get-tuple-element.43.rhs_ref, bf16[25,2,16,128]{3,2,1,0:T(8,128)(2,1)S(1)} %bitcast.9, s32[3,8,128]{2,1,0:T(8,128)S(1)} %get-tuple-element.29.flag_ref, ...), custom_call_target="tpu_custom_call" | custom-call | flops 1048576 | bytes 4194304 | tf_op jit(solution)/shard_map/pallas_call | solution.py:639
Async XLA Ops:
  0.0 9.6 %copy-start.2 = (f32[2,2,128]{2,1,0:T(2,128)S(1)}, f32[2,2,128]{2,1,0:T(2,128)}, u32[]{:S(2)}) copy-start(f32[2,2,128]{2,1,0:T(2,128)} %param.8) | copy-start | bytes 6148
  0.0 9.6 %copy-start.1 = (f32[3,5,5,2,2,128]{5,4,3,2,1,0:T(2,128)S(1)}, f32[3,5,5,2,2,128]{5,4,3,2,1,0:T(2,128)}, u32[]{:S(2)}) copy-start(f32[3,5,5,2,2,128]{5,4,3,2,1,0:T(2,128)} %param.7) | copy-start | bytes 460804
  1.9 10.0 %collective-permute-start = (f32[5,4,8,128]{3,2,1,0:T(8,128)S(1)}, f32[5,4,8,128]{3,2,1,0:T(8,128)S(1)}, u32[]{:S(2)}, u32[]{:S(2)}) collective-permute-start(f32[5,4,8,128]{3,2,1,0:T(8,128)S(1)} %get-tuple-element.33), channel_id=1, source_target_pairs={{0,28},{4,8},{8,4},{12,16},{16,12},{20,24},{24,20},{28,0},{1,29},{... | collective-permute-start | bytes 245768 | tf_op jit(solution)/shard_map/ppermute | solution.py:660
  8.0 4.4 %collective-permute-start.1 = (f32[5,4,8,128]{3,2,1,0:T(8,128)S(1)}, f32[5,4,8,128]{3,2,1,0:T(8,128)S(1)}, u32[]{:S(2)}, u32[]{:S(2)}) collective-permute-start(f32[5,4,8,128]{3,2,1,0:T(8,128)S(1)} %get-tuple-element.34), channel_id=1, source_target_pairs={{0,4},{4,0},{8,12},{12,8},{16,20},{20,16},{24,28},{28,24},{1,5},{5... | collective-permute-start | bytes 245768 | tf_op jit(solution)/shard_map/ppermute | solution.py:661
  8.0 4.7 %collective-permute-start.2 = (f32[5,4,8,128]{3,2,1,0:T(8,128)S(1)}, f32[5,4,8,128]{3,2,1,0:T(8,128)S(1)}, u32[]{:S(2)}, u32[]{:S(2)}) collective-permute-start(f32[5,4,8,128]{3,2,1,0:T(8,128)S(1)} %get-tuple-element.35), channel_id=1, source_target_pairs={{0,3},{1,2},{2,1},{3,0},{4,7},{5,6},{6,5},{7,4},{8,11},{9,10},{10,... | collective-permute-start | bytes 245768 | tf_op jit(solution)/shard_map/ppermute | solution.py:662
  8.7 4.0 %collective-permute-start.3 = (f32[5,4,8,128]{3,2,1,0:T(8,128)S(1)}, f32[5,4,8,128]{3,2,1,0:T(8,128)S(1)}, u32[]{:S(2)}, u32[]{:S(2)}) collective-permute-start(f32[5,4,8,128]{3,2,1,0:T(8,128)S(1)} %get-tuple-element.36), channel_id=1, source_target_pairs={{0,1},{1,0},{2,3},{3,2},{4,5},{5,4},{6,7},{7,6},{8,9},{9,8},{10,11... | collective-permute-start | bytes 245768 | tf_op jit(solution)/shard_map/ppermute | solution.py:663
  13.9 16.6 %copy-start = (bf16[5,5,2,2,2,2,2,128]{7,6,5,4,3,2,1,0:T(2,128)(2,1)S(1)}, bf16[5,5,2,2,2,2,2,128]{7,6,5,4,3,2,1,0:T(2,128)(2,1)}, u32[]{:S(2)}) copy-start(bf16[5,5,2,2,2,2,2,128]{7,6,5,4,3,2,1,0:T(2,128)(2,1)} %param.11) | copy-start | bytes 614404
  21.4 9.1 %all-to-all-start.1 = ((f32[4,5,8,128]{3,2,1,0:T(8,128)}), f32[4,5,8,128]{3,2,1,0:T(8,128)S(1)}, u32[]{:S(2)}, u32[]{:S(2)}) async-start(f32[4,5,8,128]{3,2,1,0:T(8,128)} %get-tuple-element.41), calls=%async_computation.1 | async-start | bytes 163840 | tf_op jit(solution)/shard_map/all_to_all | solution.py:677

commit v5 on v2

--- a/solution.py
+++ b/solution.py
@@ -181,7 +181,7 @@
         for one in pair:
             one.wait()
 
-        def one_line(b, carry, a=a):
+        for b in range(4):
             src = [[src_ref[v, a, b, q] for q in range(2)] for v in range(5)]
             for o in range(5):
                 total = [None, None]
@@ -192,9 +192,6 @@
                         total[q] = term if i == 0 else total[q] + term
                 for q in range(2):
                     u_ref[o, a, b, q] = OMEGA * total[q]
-            return carry
-
-        lax.fori_loop(0, 4, one_line, 0)
     fine_faces(u_ref, flag_ref, xo, xe, yo, ye)
 
 
@@ -468,10 +465,7 @@
                     acc_ref[v, i, j] = acc_ref[v, i, j] - value
 
 
-def restrict_kernel(
-    acc_ref, flag_ref, face_ref, smooth_ref, rxo, rxe, ryo, rye, rhs_ref, c_ref, xo, xe, yo, ye
-):
-    rhs = [[[acc_ref[v, i, j] for j in range(2)] for i in range(2)] for v in range(5)]
+def add_remote(field, scale, flag_ref, face_ref, rxo, rxe, ryo, rye):
     for d, axis in ((0, "gx"), (1, "gy")):
         is_even = parity(axis)
         low, step = axis_low(d)
@@ -481,20 +475,27 @@
         at = (lambda n, m: (n, m)) if d == 0 else (lambda n, m: (m, n))
         right, left = [], []
         for v in range(5):
-            value = jnp.where(is_even, even[v], odd[v])
+            value = scale * jnp.where(is_even, even[v], odd[v])
             swapped = jnp.where(low, sroll(value, -step), sroll(value, step))
             right.append(jnp.where(flag, swapped, value))
-            left.append(jnp.where(is_even, odd[v], even[v]))
+            left.append(scale * jnp.where(is_even, odd[v], even[v]))
         upper = [[face_ref[2 * d, 5 * o + i] for i in range(5)] for o in range(5)]
         lower = [[face_ref[2 * d + 1, 5 * o + i] for i in range(5)] for o in range(5)]
         for v, value in enumerate(mix(upper, right)):
             for m, part in enumerate((sroll(value, step), value)):
                 i, j = at(1, m)
-                rhs[v][i][j] = rhs[v][i][j] - jnp.where(low, 0.0, part)
+                field[v][i][j] = field[v][i][j] - jnp.where(low, 0.0, part)
         for v, value in enumerate(mix(lower, left)):
             for m, part in enumerate((value, sroll(value, -step))):
                 i, j = at(0, m)
-                rhs[v][i][j] = rhs[v][i][j] + jnp.where(low, part, 0.0)
+                field[v][i][j] = field[v][i][j] + jnp.where(low, part, 0.0)
+
+
+def restrict_kernel(
+    acc_ref, flag_ref, face_ref, smooth_ref, rxo, rxe, ryo, rye, rhs_ref, c_ref, xo, xe, yo, ye
+):
+    rhs = [[[acc_ref[v, i, j] for j in range(2)] for i in range(2)] for v in range(5)]
+    add_remote(rhs, 1.0, flag_ref, face_ref, rxo, rxe, ryo, rye)
     c = coarse_smooth(smooth_ref, rhs)
     for v in range(5):
         for i in range(2):
@@ -504,37 +505,29 @@
     coarse_faces(c, flag_ref, xo, xe, yo, ye)
 
 
-def coarse_step(c_ref, rhs_ref, smooth_ref, flag_ref, jac_ref, damp_ref, rxo, rxe, ryo, rye):
+def coarse_local_kernel(c_ref, rhs_ref, smooth_ref, flag_ref, jac_ref, damp_ref, out_ref):
     damp = 0.5 * damp_ref[...]
     c = [[[c_ref[v, i, j] for j in range(2)] for i in range(2)] for v in range(5)]
     acc = [[[rhs_ref[v, i, j] - 2.0 * c[v][i][j] for j in range(2)] for i in range(2)] for v in range(5)]
-    for d, axis in ((0, "gx"), (1, "gy")):
-        is_even = parity(axis)
+    for d in range(2):
         low, step = axis_low(d)
         flag = flag_ref[d] != 0
+        flag_before = sroll(flag_ref[d], step) != 0
         matrix = [[jac_ref[25 * d + 5 * o + i] for i in range(5)] for o in range(5)]
-        even, odd = ((rxe, rxo), (rye, ryo))[d]
         at = (lambda n, m: (n, m)) if d == 0 else (lambda n, m: (m, n))
         waves = [[[None] * 5, [None] * 5] for _ in range(2)]
         for v in range(5):
-            got_right = jnp.where(is_even, even[v], odd[v])
-            got_left = jnp.where(is_even, odd[v], even[v])
             lo = [c[v][at(0, m)[0]][at(0, m)[1]] for m in range(2)]
             hi = [c[v][at(1, m)[0]][at(1, m)[1]] for m in range(2)]
-            right = [
-                jnp.where(low, sroll(lo[0], -step), sroll(got_right, step)),
-                jnp.where(low, sroll(lo[1], -step), got_right),
-            ]
-            right = [jnp.where(flag, right[1 - m], right[m]) for m in range(2)]
-            left = [sroll(jnp.where(flag, hi[1 - m], hi[m]), step) for m in range(2)]
-            left = [jnp.where(low, got_left, left[0]), jnp.where(low, sroll(got_left, -step), left[1])]
             for m in range(2):
-                waves[1][m][v] = 0.5 * (right[m] - lo[m])
-                waves[0][m][v] = 0.5 * (hi[m] - left[m])
+                right = jnp.where(low, sroll(jnp.where(flag_before, lo[1 - m], lo[m]), -step), 0.0)
+                left = jnp.where(low, 0.0, sroll(jnp.where(flag, hi[1 - m], hi[m]), step))
+                waves[1][m][v] = 0.5 * (right - lo[m])
+                waves[0][m][v] = 0.5 * (hi[m] - left)
                 i, j = at(1, m)
-                acc[v][i][j] = acc[v][i][j] + damp * (right[m] - hi[m])
+                acc[v][i][j] = acc[v][i][j] + damp * (right - hi[m])
                 i, j = at(0, m)
-                acc[v][i][j] = acc[v][i][j] + damp * (left[m] - lo[m])
+                acc[v][i][j] = acc[v][i][j] + damp * (left - lo[m])
         for n in range(2):
             for m in range(2):
                 i, j = at(n, m)
@@ -558,13 +551,21 @@
             for v, value in enumerate(mix(matrix, wave)):
                 acc[v][i][j] = acc[v][i][j] - value
     change = coarse_smooth(smooth_ref, acc)
-    return [[[c[v][i][j] + change[v][i][j] for j in range(2)] for i in range(2)] for v in range(5)]
-
-
-def coarse_kernel(
-    c_ref, rhs_ref, smooth_ref, flag_ref, jac_ref, damp_ref, rxo, rxe, ryo, rye, out_ref, xo, xe, yo, ye
-):
-    c = coarse_step(c_ref, rhs_ref, smooth_ref, flag_ref, jac_ref, damp_ref, rxo, rxe, ryo, rye)
+    for v in range(5):
+        for i in range(2):
+            for j in range(2):
+                out_ref[v, i, j] = c[v][i][j] + change[v][i][j]
+
+
+def coarse_step(c_ref, smooth_ref, flag_ref, face_ref, rxo, rxe, ryo, rye):
+    rest = [[[0.0, 0.0], [0.0, 0.0]] for _ in range(5)]
+    add_remote(rest, 1.0 / 6.0, flag_ref, face_ref, rxo, rxe, ryo, rye)
+    change = coarse_smooth(smooth_ref, rest)
+    return [[[c_ref[v, i, j] + change[v][i][j] for j in range(2)] for i in range(2)] for v in range(5)]
+
+
+def coarse_kernel(c_ref, smooth_ref, flag_ref, face_ref, rxo, rxe, ryo, rye, out_ref, xo, xe, yo, ye):
+    c = coarse_step(c_ref, smooth_ref, flag_ref, face_ref, rxo, rxe, ryo, rye)
     for v in range(5):
         for i in range(2):
             for j in range(2):
@@ -577,9 +578,9 @@
 
 
 def last_kernel(
-    c_ref, rhs_ref, smooth_ref, flag_ref, jac_ref, damp_ref, rxo, rxe, ryo, rye, second_ref, out_hbm, out_ref, sems
+    c_ref, smooth_ref, flag_ref, face_ref, rxo, rxe, ryo, rye, second_ref, out_hbm, out_ref, sems
 ):
-    c = coarse_step(c_ref, rhs_ref, smooth_ref, flag_ref, jac_ref, damp_ref, rxo, rxe, ryo, rye)
+    c = coarse_step(c_ref, smooth_ref, flag_ref, face_ref, rxo, rxe, ryo, rye)
     low = c_low()
     copies = []
     for v in range(5):
@@ -649,6 +650,11 @@
     yo = lax.ppermute(yo, "gy", odd_y)
     ye = lax.ppermute(ye, "gy", even_y)
     return xo, xe, yo, ye
+
+
+def local_sweep(coarse, *rest):
+    (out,) = call(coarse_local_kernel, (coarse, *rest), [vmem(COARSE)], flops=4 * 2**20)
+    return out
 
 
 def body(source, jacobian, damping, orient, smoother, coarse_smoother):
@@ -692,16 +698,18 @@
         flops=2**20,
     )
     got = exchange(*sent)
+    coarse = local_sweep(coarse, rhs, coarse_smoother, flag, jac8, damp8)
     coarse, *sent = call(
         coarse_kernel,
-        (coarse, rhs, coarse_smoother, flag, jac8, damp8, *got),
+        (coarse, coarse_smoother, flag, face, *got),
         [vmem(COARSE)] + coarse_messages,
         flops=2**20,
     )
     got = exchange(*sent)
+    coarse = local_sweep(coarse, rhs, coarse_smoother, flag, jac8, damp8)
     (out,) = call(
         last_kernel,
-        (coarse, rhs, coarse_smoother, flag, jac8, damp8, *got, second),
+        (coarse, coarse_smoother, flag, face, *got, second),
         [jax.ShapeDtypeStruct(FINE, F32)],
         out_hbm=(0,),
         scratch=[pltpu.VMEM(FINE, F32), pltpu.SemaphoreType.DMA((5,))],

time: 34.7 us -> 34.3 us (0.988)
  waiting for transfers between devices: 7.21 us -> 6.73 us
    ppermute x4, waiting for transfers between devices: 6.46 us -> 5.97 us  [exchange(): xo = lax.ppermute(xo, 'gx', odd_x)]
    pallas_call x7 -> x9, Pallas kernels: 7.04 us -> 7.09 us  [call(): pl.pallas_call(kernel, out_shape=outs, in_specs=in_specs, out_specs=out_s...]
  transfers between devices with their start and end apart: 16 -> 16, of which waited for: 5 -> 5; matrix products, arithmetic and copies ran while one was open for 0% -> 0% of each run, Pallas kernels for 8% -> 10%
where the time goes in v5:
time: 34.3 us; the launch traced here: 34.1 us
  starting transfers between devices  20.2 us (59%)
  Pallas kernels  7.09 us (21%)
  waiting for transfers between devices  6.73 us (20%)
    ppermute x4, starting transfers between devices, exchange(): xo = lax.ppermute(xo, 'gx', odd_x)  13.7 us
    pallas_call x9, Pallas kernels, call(): pl.pallas_call(kernel, out_shape=outs, in_specs=in_specs, out_specs=out_s...  7.09 us
    ppermute x4, waiting for transfers between devices, exchange(): xo = lax.ppermute(xo, 'gx', odd_x)  5.97 us
    ppermute x4, starting transfers between devices, exchange(): ye = lax.ppermute(ye, 'gy', even_y)  5.85 us
    ppermute x4, starting transfers between devices, exchange(): yo = lax.ppermute(yo, 'gy', odd_y)  0.69 us
  transfers between devices with their start and end apart: 16, of which 5 were waited for; matrix products, arithmetic and copies ran while one was open for 0% of the time, Pallas kernels for 10%

profile of v5, /device:TPU:0, one launch (start us, length us, event | category | flops | bytes accessed | tf_op | source)
XLA Modules:
  0.0 34.1 jit_solution(8676520650251614834)
XLA Ops:
  0.0 0.0 copy-start.2
  0.0 0.0 copy-start.1
  0.0 1.8 %shard_map.64 = (f32[5,4,4,2,8,128]{5,4,3,2,1,0:T(8,128)S(1)}, bf16[25,4,4,16,128]{4,3,2,1,0:T(8,128)(2,1)S(1)}, f32[5,4,4,2,8,128]{5,4,3,2,1,0:T(8,128)S(1)}, s...) custom-call(f32[5,4,4,2,8,128]{5,4,3,2,1,0:T(8,128)} %bitcast.15, ...), custom_call_target="tpu_custom_call" | custom-call | flops 1638400 | bytes 4194304 | tf_op jit(solution)/shard_map/pallas_call | solution.py:627
  1.9 6.0 %collective-permute-start = (f32[5,4,8,128]{3,2,1,0:T(8,128)S(1)}, f32[5,4,8,128]{3,2,1,0:T(8,128)S(1)}, u32[]{:S(2)}, u32[]{:S(2)}) collective-permute-start(f32[5,4,8,128]{3,2,1,0:T(8,128)S(1)} %get-tuple-element.39), channel_id=1, source_target_pairs={{0,28},{4,8},{8,4},{12,16},{16,12},{20,24},{24,20},{28,0},{1,29},{... | collective-permute-start | bytes 245768 | tf_op jit(solution)/shard_map/ppermute | solution.py:648
  7.9 0.0 collective-permute-start.1
  7.9 0.7 %collective-permute-start.2 = (f32[5,4,8,128]{3,2,1,0:T(8,128)S(1)}, f32[5,4,8,128]{3,2,1,0:T(8,128)S(1)}, u32[]{:S(2)}, u32[]{:S(2)}) collective-permute-start(f32[5,4,8,128]{3,2,1,0:T(8,128)S(1)} %get-tuple-element.41), channel_id=1, source_target_pairs={{0,3},{1,2},{2,1},{3,0},{4,7},{5,6},{6,5},{7,4},{8,11},{9,10},{10,... | collective-permute-start | bytes 245768 | tf_op jit(solution)/shard_map/ppermute | solution.py:650
  8.6 1.0 %collective-permute-start.3 = (f32[5,4,8,128]{3,2,1,0:T(8,128)S(1)}, f32[5,4,8,128]{3,2,1,0:T(8,128)S(1)}, u32[]{:S(2)}, u32[]{:S(2)}) collective-permute-start(f32[5,4,8,128]{3,2,1,0:T(8,128)S(1)} %get-tuple-element.42), channel_id=1, source_target_pairs={{0,1},{1,0},{2,3},{3,2},{4,5},{5,4},{6,7},{7,6},{8,9},{9,8},{10,11... | collective-permute-start | bytes 245768 | tf_op jit(solution)/shard_map/ppermute | solution.py:651
  9.5 0.0 copy-done.2
  9.5 0.0 copy-done.1
  9.5 2.3 %shard_map.65 = (f32[5,4,4,2,8,128]{5,4,3,2,1,0:T(8,128)S(1)}, f32[75,8,128]{2,1,0:T(8,128)S(1)}, f32[8,128]{1,0:T(8,128)S(1)}, f32[4,25,8,128]{3,2,1,0:T(8,128)S(1)}) custom-call(f32[5,4,4,2,8,128]{5,4,3,2,1,0:T(8,128)S(1)} %get-tuple-element.33.src_ref, f32[5,4,4,2,8,128]{5,4,3,2,1,0:T(8,128)S(1)} %get-tuple-element.34.u_ref, ...), custom_call_target="tpu_custom_call" | custom-call | flops 9437184 | bytes 4194304 | tf_op jit(solution)/shard_map/pallas_call | solution.py:627
  11.8 0.0 collective-permute-done.rxo
  11.8 0.5 %collective-permute-done.1.rxe = f32[5,4,8,128]{3,2,1,0:T(8,128)S(1)} collective-permute-done((f32[5,4,8,128]{3,2,1,0:T(8,128)S(1)}, f32[5,4,8,128]{3,2,1,0:T(8,128)S(1)}, u32[]{:S(2)}, u32[]{:S(2)}) %collective-permute-start.1) | collective-permute-done | bytes 81952 | tf_op jit(solution)/shard_map/ppermute | solution.py:649
  12.3 0.2 collective-permute-done.2.ryo
  12.6 0.0 collective-permute-done.3.rye
  12.6 0.6 %shard_map.66 = (f32[5,4,4,2,8,128]{5,4,3,2,1,0:T(8,128)S(1)}, f32[5,8,128]{2,1,0:T(8,128)S(1)}, f32[5,8,128]{2,1,0:T(8,128)S(1)}, f32[5,8,128]{2,1,0:T(8,128)S(1)}, f32[5,8,128]{2,1,0:T(8,128)S(1)}) custom-call(f32[5,4,4,2,8,128]{5,4,3,2,1,0:T(8,128)S(1)} %get-tuple-element.36.acc_ref, f32[5,4,4,2,8,128]{5,4,3,2,1,0:T(8,128)S(1)} %get-tuple-element.34.u_ref, ...), custom_call_target="tpu_custom_call" | custom-call | flops 3145728 | bytes 4194304 | tf_op jit(solution)/shard_map/pallas_call | solution.py:627
  13.2 0.0 copy-start
  13.2 2.5 %collective-permute-start.4 = (f32[5,8,128]{2,1,0:T(8,128)S(1)}, f32[5,8,128]{2,1,0:T(8,128)S(1)}, u32[]{:S(2)}, u32[]{:S(2)}) collective-permute-start(f32[5,8,128]{2,1,0:T(8,128)S(1)} %get-tuple-element.46), channel_id=1, source_target_pairs={{0,28},{4,8},{8,4},{12,16},{16,12},{20,24},{24,20},{28,0},{1,29},{... | collective-permute-start | bytes 61448 | tf_op jit(solution)/shard_map/ppermute | solution.py:648
  15.8 0.0 collective-permute-start.5
  15.8 0.0 collective-permute-start.6
  15.8 1.6 %collective-permute-start.7 = (f32[5,8,128]{2,1,0:T(8,128)S(1)}, f32[5,8,128]{2,1,0:T(8,128)S(1)}, u32[]{:S(2)}, u32[]{:S(2)}) collective-permute-start(f32[5,8,128]{2,1,0:T(8,128)S(1)} %get-tuple-element.49), channel_id=1, source_target_pairs={{0,1},{1,0},{2,3},{3,2},{4,5},{5,4},{6,7},{7,6},{8,9},{9,8},{10,11... | collective-permute-start | bytes 61448 | tf_op jit(solution)/shard_map/ppermute | solution.py:651
  17.4 0.6 %shard_map.67.acc_ref = f32[5,2,2,8,128]{4,3,2,1,0:T(8,128)S(1)} custom-call(f32[5,4,4,2,8,128]{5,4,3,2,1,0:T(8,128)S(1)} %get-tuple-element.33.src_ref, f32[5,4,4,2,8,128]{5,4,3,2,1,0:T(8,128)S(1)} %get-tuple-element.43.u_ref.second_ref, s32[3,8,128]{2,1,0:T(8,128)S(1)} %get-tuple-element.35.flag_ref, f32[75,8,128]{2,1,0:T(8,128)S(1)} %get-tuple-element.44.jac_ref, ...), custom_call_target="tpu_custom_call" | custom-call | flops 4194304 | bytes 4194304 | tf_op jit(solution)/shard_map/pallas_call | solution.py:627
  18.1 1.7 %collective-permute-done.4.rxo = f32[5,8,128]{2,1,0:T(8,128)S(1)} collective-permute-done((f32[5,8,128]{2,1,0:T(8,128)S(1)}, f32[5,8,128]{2,1,0:T(8,128)S(1)}, u32[]{:S(2)}, u32[]{:S(2)}) %collective-permute-start.4) | collective-permute-done | bytes 20512 | tf_op jit(solution)/shard_map/ppermute | solution.py:648
  19.8 0.0 collective-permute-done.5.rxe
  19.8 0.0 collective-permute-done.6.ryo
  19.8 0.0 collective-permute-done.7.rye
  19.8 0.0 copy-done
  19.8 0.1 shard_map.68
  19.9 2.5 %collective-permute-start.8 = (f32[5,8,128]{2,1,0:T(8,128)S(1)}, f32[5,8,128]{2,1,0:T(8,128)S(1)}, u32[]{:S(2)}, u32[]{:S(2)}) collective-permute-start(f32[5,8,128]{2,1,0:T(8,128)S(1)} %get-tuple-element.52), channel_id=1, source_target_pairs={{0,28},{4,8},{8,4},{12,16},{16,12},{20,24},{24,20},{28,0},{1,29},{... | collective-permute-start | bytes 61448 | tf_op jit(solution)/shard_map/ppermute | solution.py:648
  22.5 0.0 collective-permute-start.9
  22.5 0.0 collective-permute-start.10
  22.5 1.6 %collective-permute-start.11 = (f32[5,8,128]{2,1,0:T(8,128)S(1)}, f32[5,8,128]{2,1,0:T(8,128)S(1)}, u32[]{:S(2)}, u32[]{:S(2)}) collective-permute-start(f32[5,8,128]{2,1,0:T(8,128)S(1)} %get-tuple-element.55), channel_id=1, source_target_pairs={{0,1},{1,0},{2,3},{3,2},{4,5},{5,4},{6,7},{7,6},{8,9},{9,8},{10,11... | collective-permute-start | bytes 61448 | tf_op jit(solution)/shard_map/ppermute | solution.py:651
  24.1 0.2 shard_map.69.c_ref
  24.4 2.1 %collective-permute-done.8.rxo = f32[5,8,128]{2,1,0:T(8,128)S(1)} collective-permute-done((f32[5,8,128]{2,1,0:T(8,128)S(1)}, f32[5,8,128]{2,1,0:T(8,128)S(1)}, u32[]{:S(2)}, u32[]{:S(2)}) %collective-permute-start.8) | collective-permute-done | bytes 20512 | tf_op jit(solution)/shard_map/ppermute | solution.py:648
  26.5 0.0 collective-permute-done.9.rxe
  26.5 0.0 collective-permute-done.10.ryo
  26.5 0.0 collective-permute-done.11.rye
  26.5 0.1 shard_map.70
  26.6 2.5 %collective-permute-start.12 = (f32[5,8,128]{2,1,0:T(8,128)S(1)}, f32[5,8,128]{2,1,0:T(8,128)S(1)}, u32[]{:S(2)}, u32[]{:S(2)}) collective-permute-start(f32[5,8,128]{2,1,0:T(8,128)S(1)} %get-tuple-element.57), channel_id=1, source_target_pairs={{0,28},{4,8},{8,4},{12,16},{16,12},{20,24},{24,20},{28,0},{1,29},{... | collective-permute-start | bytes 61448 | tf_op jit(solution)/shard_map/ppermute | solution.py:648
  29.2 0.0 collective-permute-start.13
  29.2 0.0 collective-permute-start.14
  29.2 1.6 %collective-permute-start.15 = (f32[5,8,128]{2,1,0:T(8,128)S(1)}, f32[5,8,128]{2,1,0:T(8,128)S(1)}, u32[]{:S(2)}, u32[]{:S(2)}) collective-permute-start(f32[5,8,128]{2,1,0:T(8,128)S(1)} %get-tuple-element.60), channel_id=1, source_target_pairs={{0,1},{1,0},{2,3},{3,2},{4,5},{5,4},{6,7},{7,6},{8,9},{9,8},{10,11... | collective-permute-start | bytes 61448 | tf_op jit(solution)/shard_map/ppermute | solution.py:651
  30.8 0.2 shard_map.71.c_ref
  31.0 2.1 %collective-permute-done.12.rxo = f32[5,8,128]{2,1,0:T(8,128)S(1)} collective-permute-done((f32[5,8,128]{2,1,0:T(8,128)S(1)}, f32[5,8,128]{2,1,0:T(8,128)S(1)}, u32[]{:S(2)}, u32[]{:S(2)}) %collective-permute-start.12) | collective-permute-done | bytes 20512 | tf_op jit(solution)/shard_map/ppermute | solution.py:648
  33.2 0.0 collective-permute-done.13.rxe
  33.2 0.0 collective-permute-done.14.ryo
  33.2 0.0 collective-permute-done.15.rye
  33.2 1.0 %shard_map.72 = f32[5,4,4,2,8,128]{5,4,3,2,1,0:T(8,128)} custom-call(f32[5,2,2,8,128]{4,3,2,1,0:T(8,128)S(1)} %shard_map.71.c_ref, bf16[25,2,16,128]{3,2,1,0:T(8,128)(2,1)S(1)} %bitcast.11, s32[3,8,128]{2,1,0:T(8,128)S(1)} %get-tuple-element.35.flag_ref, f32[4,25,8,128]{3,2,1,0:T(8,128)S(1)} %get-tuple-element.38.face_ref, ...), custom_call_target="tpu_custom_call" | custom-call | flops 1048576 | bytes 4194304 | tf_op jit(solution)/shard_map/pallas_call | solution.py:627
Async XLA Ops:
  0.0 9.5 %copy-start.2 = (f32[2,2,128]{2,1,0:T(2,128)S(1)}, f32[2,2,128]{2,1,0:T(2,128)}, u32[]{:S(2)}) copy-start(f32[2,2,128]{2,1,0:T(2,128)} %param.8) | copy-start | bytes 6148
  0.0 9.5 %copy-start.1 = (f32[3,5,5,2,2,128]{5,4,3,2,1,0:T(2,128)S(1)}, f32[3,5,5,2,2,128]{5,4,3,2,1,0:T(2,128)}, u32[]{:S(2)}) copy-start(f32[3,5,5,2,2,128]{5,4,3,2,1,0:T(2,128)} %param.7) | copy-start | bytes 460804
  1.9 10.0 %collective-permute-start = (f32[5,4,8,128]{3,2,1,0:T(8,128)S(1)}, f32[5,4,8,128]{3,2,1,0:T(8,128)S(1)}, u32[]{:S(2)}, u32[]{:S(2)}) collective-permute-start(f32[5,4,8,128]{3,2,1,0:T(8,128)S(1)} %get-tuple-element.39), channel_id=1, source_target_pairs={{0,28},{4,8},{8,4},{12,16},{16,12},{20,24},{24,20},{28,0},{1,29},{... | collective-permute-start | bytes 245768 | tf_op jit(solution)/shard_map/ppermute | solution.py:648
  7.9 4.4 %collective-permute-start.1 = (f32[5,4,8,128]{3,2,1,0:T(8,128)S(1)}, f32[5,4,8,128]{3,2,1,0:T(8,128)S(1)}, u32[]{:S(2)}, u32[]{:S(2)}) collective-permute-start(f32[5,4,8,128]{3,2,1,0:T(8,128)S(1)} %get-tuple-element.40), channel_id=1, source_target_pairs={{0,4},{4,0},{8,12},{12,8},{16,20},{20,16},{24,28},{28,24},{1,5},{5... | collective-permute-start | bytes 245768 | tf_op jit(solution)/shard_map/ppermute | solution.py:649
  7.9 4.7 %collective-permute-start.2 = (f32[5,4,8,128]{3,2,1,0:T(8,128)S(1)}, f32[5,4,8,128]{3,2,1,0:T(8,128)S(1)}, u32[]{:S(2)}, u32[]{:S(2)}) collective-permute-start(f32[5,4,8,128]{3,2,1,0:T(8,128)S(1)} %get-tuple-element.41), channel_id=1, source_target_pairs={{0,3},{1,2},{2,1},{3,0},{4,7},{5,6},{6,5},{7,4},{8,11},{9,10},{10,... | collective-permute-start | bytes 245768 | tf_op jit(solution)/shard_map/ppermute | solution.py:650
  8.6 4.0 %collective-permute-start.3 = (f32[5,4,8,128]{3,2,1,0:T(8,128)S(1)}, f32[5,4,8,128]{3,2,1,0:T(8,128)S(1)}, u32[]{:S(2)}, u32[]{:S(2)}) collective-permute-start(f32[5,4,8,128]{3,2,1,0:T(8,128)S(1)} %get-tuple-element.42), channel_id=1, source_target_pairs={{0,1},{1,0},{2,3},{3,2},{4,5},{5,4},{6,7},{7,6},{8,9},{9,8},{10,11... | collective-permute-start | bytes 245768 | tf_op jit(solution)/shard_map/ppermute | solution.py:651
  13.2 6.6 %copy-start = (bf16[5,5,2,2,2,2,2,128]{7,6,5,4,3,2,1,0:T(2,128)(2,1)S(1)}, bf16[5,5,2,2,2,2,2,128]{7,6,5,4,3,2,1,0:T(2,128)(2,1)}, u32[]{:S(2)}) copy-start(bf16[5,5,2,2,2,2,2,128]{7,6,5,4,3,2,1,0:T(2,128)(2,1)} %param.11) | copy-start | bytes 614404
  13.2 6.5 %collective-permute-start.4 = (f32[5,8,128]{2,1,0:T(8,128)S(1)}, f32[5,8,128]{2,1,0:T(8,128)S(1)}, u32[]{:S(2)}, u32[]{:S(2)}) collective-permute-start(f32[5,8,128]{2,1,0:T(8,128)S(1)} %get-tuple-element.46), channel_id=1, source_target_pairs={{0,28},{4,8},{8,4},{12,16},{16,12},{20,24},{24,20},{28,0},{1,29},{... | collective-permute-start | bytes 61448 | tf_op jit(solution)/shard_map/ppermute | solution.py:648
  15.8 4.0 %collective-permute-start.5 = (f32[5,8,128]{2,1,0:T(8,128)S(1)}, f32[5,8,128]{2,1,0:T(8,128)S(1)}, u32[]{:S(2)}, u32[]{:S(2)}) collective-permute-start(f32[5,8,128]{2,1,0:T(8,128)S(1)} %get-tuple-element.47), channel_id=1, source_target_pairs={{0,4},{4,0},{8,12},{12,8},{16,20},{20,16},{24,28},{28,24},{1,5},{5... | collective-permute-start | bytes 61448 | tf_op jit(solution)/shard_map/ppermute | solution.py:649
  15.8 4.0 %collective-permute-start.6 = (f32[5,8,128]{2,1,0:T(8,128)S(1)}, f32[5,8,128]{2,1,0:T(8,128)S(1)}, u32[]{:S(2)}, u32[]{:S(2)}) collective-permute-start(f32[5,8,128]{2,1,0:T(8,128)S(1)} %get-tuple-element.48), channel_id=1, source_target_pairs={{0,3},{1,2},{2,1},{3,0},{4,7},{5,6},{6,5},{7,4},{8,11},{9,10},{10,... | collective-permute-start | bytes 61448 | tf_op jit(solution)/shard_map/ppermute | solution.py:650
  15.8 4.0 %collective-permute-start.7 = (f32[5,8,128]{2,1,0:T(8,128)S(1)}, f32[5,8,128]{2,1,0:T(8,128)S(1)}, u32[]{:S(2)}, u32[]{:S(2)}) collective-permute-start(f32[5,8,128]{2,1,0:T(8,128)S(1)} %get-tuple-element.49), channel_id=1, source_target_pairs={{0,1},{1,0},{2,3},{3,2},{4,5},{5,4},{6,7},{7,6},{8,9},{9,8},{10,11... | collective-permute-start | bytes 61448 | tf_op jit(solution)/shard_map/ppermute | solution.py:651
  19.9 6.5 %collective-permute-start.8 = (f32[5,8,128]{2,1,0:T(8,128)S(1)}, f32[5,8,128]{2,1,0:T(8,128)S(1)}, u32[]{:S(2)}, u32[]{:S(2)}) collective-permute-start(f32[5,8,128]{2,1,0:T(8,128)S(1)} %get-tuple-element.52), channel_id=1, source_target_pairs={{0,28},{4,8},{8,4},{12,16},{16,12},{20,24},{24,20},{28,0},{1,29},{... | collective-permute-start | bytes 61448 | tf_op jit(solution)/shard_map/ppermute | solution.py:648
  22.5 4.0 %collective-permute-start.9 = (f32[5,8,128]{2,1,0:T(8,128)S(1)}, f32[5,8,128]{2,1,0:T(8,128)S(1)}, u32[]{:S(2)}, u32[]{:S(2)}) collective-permute-start(f32[5,8,128]{2,1,0:T(8,128)S(1)} %get-tuple-element.53), channel_id=1, source_target_pairs={{0,4},{4,0},{8,12},{12,8},{16,20},{20,16},{24,28},{28,24},{1,5},{5... | collective-permute-start | bytes 61448 | tf_op jit(solution)/shard_map/ppermute | solution.py:649
  22.5 4.0 %collective-permute-start.10 = (f32[5,8,128]{2,1,0:T(8,128)S(1)}, f32[5,8,128]{2,1,0:T(8,128)S(1)}, u32[]{:S(2)}, u32[]{:S(2)}) collective-permute-start(f32[5,8,128]{2,1,0:T(8,128)S(1)} %get-tuple-element.54), channel_id=1, source_target_pairs={{0,3},{1,2},{2,1},{3,0},{4,7},{5,6},{6,5},{7,4},{8,11},{9,10},{10,... | collective-permute-start | bytes 61448 | tf_op jit(solution)/shard_map/ppermute | solution.py:650
  22.5 4.0 %collective-permute-start.11 = (f32[5,8,128]{2,1,0:T(8,128)S(1)}, f32[5,8,128]{2,1,0:T(8,128)S(1)}, u32[]{:S(2)}, u32[]{:S(2)}) collective-permute-start(f32[5,8,128]{2,1,0:T(8,128)S(1)} %get-tuple-element.55), channel_id=1, source_target_pairs={{0,1},{1,0},{2,3},{3,2},{4,5},{5,4},{6,7},{7,6},{8,9},{9,8},{10,11... | collective-permute-start | bytes 61448 | tf_op jit(solution)/shard_map/ppermute | solution.py:651
  26.6 6.5 %collective-permute-start.12 = (f32[5,8,128]{2,1,0:T(8,128)S(1)}, f32[5,8,128]{2,1,0:T(8,128)S(1)}, u32[]{:S(2)}, u32[]{:S(2)}) collective-permute-start(f32[5,8,128]{2,1,0:T(8,128)S(1)} %get-tuple-element.57), channel_id=1, source_target_pairs={{0,28},{4,8},{8,4},{12,16},{16,12},{20,24},{24,20},{28,0},{1,29},{... | collective-permute-start | bytes 61448 | tf_op jit(solution)/shard_map/ppermute | solution.py:648
  29.2 4.0 %collective-permute-start.13 = (f32[5,8,128]{2,1,0:T(8,128)S(1)}, f32[5,8,128]{2,1,0:T(8,128)S(1)}, u32[]{:S(2)}, u32[]{:S(2)}) collective-permute-start(f32[5,8,128]{2,1,0:T(8,128)S(1)} %get-tuple-element.58), channel_id=1, source_target_pairs={{0,4},{4,0},{8,12},{12,8},{16,20},{20,16},{24,28},{28,24},{1,5},{5... | collective-permute-start | bytes 61448 | tf_op jit(solution)/shard_map/ppermute | solution.py:649
  29.2 4.0 %collective-permute-start.14 = (f32[5,8,128]{2,1,0:T(8,128)S(1)}, f32[5,8,128]{2,1,0:T(8,128)S(1)}, u32[]{:S(2)}, u32[]{:S(2)}) collective-permute-start(f32[5,8,128]{2,1,0:T(8,128)S(1)} %get-tuple-element.59), channel_id=1, source_target_pairs={{0,3},{1,2},{2,1},{3,0},{4,7},{5,6},{6,5},{7,4},{8,11},{9,10},{10,... | collective-permute-start | bytes 61448 | tf_op jit(solution)/shard_map/ppermute | solution.py:650
  29.2 4.0 %collective-permute-start.15 = (f32[5,8,128]{2,1,0:T(8,128)S(1)}, f32[5,8,128]{2,1,0:T(8,128)S(1)}, u32[]{:S(2)}, u32[]{:S(2)}) collective-permute-start(f32[5,8,128]{2,1,0:T(8,128)S(1)} %get-tuple-element.60), channel_id=1, source_target_pairs={{0,1},{1,0},{2,3},{3,2},{4,5},{5,4},{6,7},{7,6},{8,9},{9,8},{10,11... | collective-permute-start | bytes 61448 | tf_op jit(solution)/shard_map/ppermute | solution.py:651

commit v6 on v5

--- a/solution.py
+++ b/solution.py
@@ -116,14 +116,19 @@
     odd_ref[index] = jnp.where(is_even, low_face, high_face)
 
 
-def fine_faces(u_ref, flag_ref, xo, xe, yo, ye):
-    even_x, even_y = parity("gx"), parity("gy")
-    fx, fy = flag_ref[0] != 0, flag_ref[1] != 0
+def fine_x_faces(u_ref, flag_ref, xo, xe):
+    even_x, fx = parity("gx"), flag_ref[0] != 0
     for v in range(5):
         for n in range(4):
             low = pack_low(u_ref[v, 0, n, 0], u_ref[v, 0, n, 1], 0)
             h = [jnp.where(fx, u_ref[v, 3, 3 - n, q], u_ref[v, 3, n, q]) for q in range(2)]
             put_pair(xe, xo, (v, n), low, pack_high(h[0], h[1], 0), even_x)
+
+
+def fine_y_faces(u_ref, flag_ref, yo, ye):
+    even_y, fy = parity("gy"), flag_ref[1] != 0
+    for v in range(5):
+        for n in range(4):
             low = pack_low(u_ref[v, n, 0, 0], u_ref[v, n, 0, 1], 1)
             h = [jnp.where(fy, u_ref[v, 3 - n, 3, q], u_ref[v, n, 3, q]) for q in range(2)]
             put_pair(ye, yo, (v, n), low, pack_high(h[0], h[1], 1), even_y)
@@ -160,39 +165,56 @@
         put_coarse_faces(v, lows, highs, flag_ref, ((xe, xo), (ye, yo)))
 
 
-def first_kernel(
-    src_hbm, smooth_hbm, orient_hbm, src_ref, smooth_ref, u_ref, flag_ref, xo, xe, yo, ye, sems, orient_ref, orient_sem
+def first_plane(src_ref, smooth_ref, u_ref, a, at):
+    for b in range(4):
+        src = [[src_ref[v, at, b, q] for q in range(2)] for v in range(5)]
+        for o in range(5):
+            total = [None, None]
+            for i in range(5):
+                block = smooth_ref[5 * o + i, at, b].astype(F32)
+                for q in range(2):
+                    term = block[8 * q : 8 * q + 8] * src[i][q]
+                    total[q] = term if i == 0 else total[q] + term
+            for q in range(2):
+                u_ref[o, a, b, q] = OMEGA * total[q]
+
+
+def x_planes_kernel(
+    src_hbm, smooth_hbm, orient_hbm, jac_hbm, damp_hbm,
+    xo, xe, u_ref, flag_ref, jac8_ref, damp8_ref, face_ref,
+    src_ref, smooth_ref, orient_ref, jac_ref, damp_ref, sems, small_sems,
 ):
-    orient_copy = pltpu.make_async_copy(orient_hbm, orient_ref, orient_sem)
-    orient_copy.start()
     copies = []
-    for slot, a in enumerate((0, 3, 1, 2)):
+    for slot, a in enumerate((0, 3)):
         pair = (
-            pltpu.make_async_copy(src_hbm.at[:, a], src_ref.at[:, a], sems.at[0, slot]),
-            pltpu.make_async_copy(smooth_hbm.at[:, a], smooth_ref.at[:, a], sems.at[1, slot]),
+            pltpu.make_async_copy(src_hbm.at[:, a], src_ref.at[:, slot], sems.at[0, slot]),
+            pltpu.make_async_copy(smooth_hbm.at[:, a], smooth_ref.at[:, slot], sems.at[1, slot]),
         )
         for one in pair:
             one.start()
         copies.append((a, pair))
-    orient_copy.wait()
+    small = [
+        pltpu.make_async_copy(hbm, ref, small_sems.at[k])
+        for k, (hbm, ref) in enumerate(((orient_hbm, orient_ref), (damp_hbm, damp_ref), (jac_hbm, jac_ref)))
+    ]
+    for one in small:
+        one.start()
+    for one in small:
+        one.wait()
     for d in range(3):
         flag_ref[d] = twice(orient_ref[d])
-    for a, pair in copies:
+    prepare_tables(jac_ref, damp_ref, jac8_ref, damp8_ref, face_ref)
+    for slot, (a, pair) in enumerate(copies):
         for one in pair:
             one.wait()
-
-        for b in range(4):
-            src = [[src_ref[v, a, b, q] for q in range(2)] for v in range(5)]
-            for o in range(5):
-                total = [None, None]
-                for i in range(5):
-                    block = smooth_ref[5 * o + i, a, b].astype(F32)
-                    for q in range(2):
-                        term = block[8 * q : 8 * q + 8] * src[i][q]
-                        total[q] = term if i == 0 else total[q] + term
-                for q in range(2):
-                    u_ref[o, a, b, q] = OMEGA * total[q]
-    fine_faces(u_ref, flag_ref, xo, xe, yo, ye)
+        first_plane(src_ref, smooth_ref, u_ref, a, slot)
+    fine_x_faces(u_ref, flag_ref, xo, xe)
+
+
+def inner_planes_kernel(src_ref, smooth_ref, outer_ref, flag_ref, yo, ye, u_ref):
+    for a in (1, 2):
+        first_plane(src_ref, smooth_ref, u_ref, a, a)
+    fine_y_faces(u_ref, flag_ref, yo, ye)
 
 
 def prepare_tables(jac_ref, damp_ref, jac8_ref, damp8_ref, face_ref):
@@ -304,8 +326,7 @@
     lax.fori_loop(0, 8, step_z, 0)
 
 
-def first_volume_kernel(src_ref, u_ref, flag_ref, jac_ref, damp_ref, acc_ref, jac8_ref, damp8_ref, face_ref):
-    prepare_tables(jac_ref, damp_ref, jac8_ref, damp8_ref, face_ref)
+def volume_kernel(src_ref, u_ref, flag_ref, jac8_ref, damp8_ref, acc_ref):
     volume(src_ref, u_ref, flag_ref, jac8_ref, damp8_ref, acc_ref)
 
 
@@ -616,7 +637,7 @@
     return pltpu.with_memory_space_constraint(array, pltpu.VMEM)
 
 
-def call(kernel, args, outs, in_hbm=(), out_hbm=(), scratch=(), flops=0):
+def call(kernel, args, outs, in_hbm=(), out_hbm=(), scratch=(), aliases=None, flops=0):
     in_specs = [
         pl.BlockSpec(memory_space=pltpu.HBM if k in in_hbm else pltpu.VMEM) for k in range(len(args))
     ]
@@ -630,6 +651,7 @@
         in_specs=in_specs,
         out_specs=out_specs,
         scratch_shapes=scratch,
+        input_output_aliases=aliases or {},
         compiler_params=pltpu.CompilerParams(vmem_limit_bytes=8 * 2**20),
         cost_estimate=pl.CostEstimate(flops=flops, bytes_accessed=4 * 2**20, transcendentals=0),
     )(*args)
@@ -642,14 +664,18 @@
     return even, odd
 
 
+def exchange_x(xo, xe):
+    even, odd = partners("gx")
+    return lax.ppermute(xo, "gx", odd), lax.ppermute(xe, "gx", even)
+
+
+def exchange_y(yo, ye):
+    even, odd = partners("gy")
+    return lax.ppermute(yo, "gy", odd), lax.ppermute(ye, "gy", even)
+
+
 def exchange(xo, xe, yo, ye):
-    even_x, odd_x = partners("gx")
-    even_y, odd_y = partners("gy")
-    xo = lax.ppermute(xo, "gx", odd_x)
-    xe = lax.ppermute(xe, "gx", even_x)
-    yo = lax.ppermute(yo, "gy", odd_y)
-    ye = lax.ppermute(ye, "gy", even_y)
-    return xo, xe, yo, ye
+    return *exchange_x(xo, xe), *exchange_y(yo, ye)
 
 
 def local_sweep(coarse, *rest):
@@ -664,24 +690,43 @@
     jacobian = jacobian.reshape(75, 4, 128)
     damping = damping.reshape(4, 128)
     orient = orient.reshape(3, 4, 128)
-    fine_messages = [vmem(FINE_MESSAGE)] * 4
+    fine_message = vmem(FINE_MESSAGE)
     coarse_messages = [vmem(COARSE_MESSAGE)] * 4
 
-    source, smoother, first, flag, *sent = call(
-        first_kernel,
-        (source, smoother, orient),
-        [vmem(FINE), vmem(smoother.shape, smoother.dtype), vmem(FINE), vmem((3, 8, 128), jnp.int32)] + fine_messages,
-        in_hbm=(0, 1, 2),
-        scratch=[pltpu.SemaphoreType.DMA((2, 4)), pltpu.VMEM((3, 4, 128), jnp.int32), pltpu.SemaphoreType.DMA],
+    xo, xe, outer, flag, jac8, damp8, face = call(
+        x_planes_kernel,
+        (source, smoother, orient, jacobian, damping),
+        [
+            fine_message,
+            fine_message,
+            vmem(FINE),
+            vmem((3, 8, 128), jnp.int32),
+            vmem((75, 8, 128)),
+            vmem((8, 128)),
+            vmem((4, 25, 8, 128)),
+        ],
+        in_hbm=(0, 1, 2, 3, 4),
+        scratch=[
+            pltpu.VMEM((5, 2, 4, 2, 8, 128), F32),
+            pltpu.VMEM((25, 2, 4, 16, 128), smoother.dtype),
+            pltpu.VMEM((3, 4, 128), jnp.int32),
+            pltpu.VMEM((75, 4, 128), F32),
+            pltpu.VMEM((4, 128), F32),
+            pltpu.SemaphoreType.DMA((2, 2)),
+            pltpu.SemaphoreType.DMA((3,)),
+        ],
         flops=2 * 25 * 64 * 512,
     )
-    got = exchange(*sent)
-    acc, jac8, damp8, face = call(
-        first_volume_kernel,
-        (source, first, flag, jacobian, damping),
-        [vmem(FINE), vmem((75, 8, 128)), vmem((8, 128)), vmem((4, 25, 8, 128))],
-        flops=9 * 2**20,
+    got_x = exchange_x(xo, xe)
+    yo, ye, first = call(
+        inner_planes_kernel,
+        (source, smoother, outer, flag),
+        [fine_message, fine_message, vmem(FINE)],
+        aliases={2: 2},
+        flops=2 * 25 * 64 * 512,
     )
+    got = (*got_x, *exchange_y(yo, ye))
+    (acc,) = call(volume_kernel, (source, first, flag, jac8, damp8), [vmem(FINE)], flops=9 * 2**20)
     second, *sent = call(
         second_kernel,
         (acc, first, smoother, flag, face, *got),

time: 34.3 us -> 34.5 us (level)
  waiting for transfers between devices: 6.73 us -> 7.58 us
  starting transfers between devices: 20.2 us -> 19.5 us
    ppermute x16, waiting for transfers between devices: 6.73 us -> 7.58 us  [the longest x8 7.06 us: exchange_x(): return (lax.ppermute(xo, 'gx', odd), lax.ppermute(xe, 'gx', even))]
    ppermute x16, starting transfers between devices: 20.2 us -> 19.5 us  [the longest x8 13 us: exchange_x(): return (lax.ppermute(xo, 'gx', odd), lax.ppermute(xe, 'gx', even))]
    pallas_call x9 -> x10, Pallas kernels: 7.09 us -> 7.16 us  [call(): pl.pallas_call(kernel, out_shape=outs, in_specs=in_specs, out_specs=out_s...]
where the time goes in v6:
time: 34.5 us; the launch traced here: 34.3 us
  starting transfers between devices  19.5 us (57%)
  waiting for transfers between devices  7.58 us (22%)
  Pallas kernels  7.16 us (21%)
    ppermute x8, starting transfers between devices, exchange_x(): return (lax.ppermute(xo, 'gx', odd), lax.ppermute(xe, 'gx', even))  13 us
    pallas_call x10, Pallas kernels, call(): pl.pallas_call(kernel, out_shape=outs, in_specs=in_specs, out_specs=out_s...  7.16 us
    ppermute x8, waiting for transfers between devices, exchange_x(): return (lax.ppermute(xo, 'gx', odd), lax.ppermute(xe, 'gx', even))  7.06 us
    ppermute x8, starting transfers between devices, exchange_y(): return (lax.ppermute(yo, 'gy', odd), lax.ppermute(ye, 'gy', even))  6.54 us
  transfers between devices with their start and end apart: 16, of which 5 were waited for; matrix products, arithmetic and copies ran while one was open for 0% of the time, Pallas kernels for 10%

profile of v6, /device:TPU:0, one launch (start us, length us, event | category | flops | bytes accessed | tf_op | source)
XLA Modules:
  0.0 34.3 jit_solution(5820056317909552216)
XLA Ops:
  0.0 0.0 copy-start
  0.0 0.0 copy-start.1
  0.0 1.8 %shard_map.64 = (f32[5,4,8,128]{3,2,1,0:T(8,128)S(1)}, f32[5,4,8,128]{3,2,1,0:T(8,128)S(1)}, f32[5,4,4,2,8,128]{5,4,3,2,1,0:T(8,128)S(1)}, s32[3,8,128]{2,1,0:T(...) custom-call(f32[5,4,4,2,8,128]{5,4,3,2,1,0:T(8,128)} %bitcast.10, ...), custom_call_target="tpu_custom_call" | custom-call | flops 1638400 | bytes 4194304 | tf_op jit(solution)/shard_map/pallas_call | solution.py:648
  1.8 6.0 %collective-permute-start = (f32[5,4,8,128]{3,2,1,0:T(8,128)S(1)}, f32[5,4,8,128]{3,2,1,0:T(8,128)S(1)}, u32[]{:S(2)}, u32[]{:S(2)}) collective-permute-start(f32[5,4,8,128]{3,2,1,0:T(8,128)S(1)} %get-tuple-element.37), channel_id=1, source_target_pairs={{0,28},{4,8},{8,4},{12,16},{16,12},{20,24},{24,20},{28,0},{1,29},{... | collective-permute-start | bytes 245768 | tf_op jit(solution)/shard_map/ppermute | solution.py:669
  7.8 0.0 collective-permute-start.1
  7.8 0.0 copy-done
  7.9 0.0 copy-done.1
  7.9 0.2 shard_map.65
  8.1 0.7 %collective-permute-start.2 = (f32[5,4,8,128]{3,2,1,0:T(8,128)S(1)}, f32[5,4,8,128]{3,2,1,0:T(8,128)S(1)}, u32[]{:S(2)}, u32[]{:S(2)}) collective-permute-start(f32[5,4,8,128]{3,2,1,0:T(8,128)S(1)} %get-tuple-element.39), channel_id=1, source_target_pairs={{0,3},{1,2},{2,1},{3,0},{4,7},{5,6},{6,5},{7,4},{8,11},{9,10},{10,... | collective-permute-start | bytes 245768 | tf_op jit(solution)/shard_map/ppermute | solution.py:674
  8.8 1.0 %collective-permute-start.3 = (f32[5,4,8,128]{3,2,1,0:T(8,128)S(1)}, f32[5,4,8,128]{3,2,1,0:T(8,128)S(1)}, u32[]{:S(2)}, u32[]{:S(2)}) collective-permute-start(f32[5,4,8,128]{3,2,1,0:T(8,128)S(1)} %get-tuple-element.40), channel_id=1, source_target_pairs={{0,1},{1,0},{2,3},{3,2},{4,5},{5,4},{6,7},{7,6},{8,9},{9,8},{10,11... | collective-permute-start | bytes 245768 | tf_op jit(solution)/shard_map/ppermute | solution.py:674
  9.8 2.2 %shard_map.66.acc_ref = f32[5,4,4,2,8,128]{5,4,3,2,1,0:T(8,128)S(1)} custom-call(f32[5,4,4,2,8,128]{5,4,3,2,1,0:T(8,128)S(1)} %bitcast.12, f32[5,4,4,2,8,128]{5,4,3,2,1,0:T(8,128)S(1)} %get-tuple-element.33.u_ref, s32[3,8,128]{2,1,0:T(8,128)S(1)} %get-tuple-element.32.flag_ref, f32[75,8,128]{2,1,0:T(8,128)S(1)} %get-tuple-element.34.jac8_ref.jac_ref, ...), custom_call_target="tpu_custom_call" | custom-call | flops 9437184 | bytes 4194304 | tf_op jit(solution)/shard_map/pallas_call | solution.py:648
  12.0 0.0 collective-permute-done.rxo
  12.0 0.3 collective-permute-done.1.rxe
  12.3 0.5 %collective-permute-done.2.ryo = f32[5,4,8,128]{3,2,1,0:T(8,128)S(1)} collective-permute-done((f32[5,4,8,128]{3,2,1,0:T(8,128)S(1)}, f32[5,4,8,128]{3,2,1,0:T(8,128)S(1)}, u32[]{:S(2)}, u32[]{:S(2)}) %collective-permute-start.2) | collective-permute-done | bytes 81952 | tf_op jit(solution)/shard_map/ppermute | solution.py:674
  12.8 0.0 collective-permute-done.3.rye
  12.8 0.6 %shard_map.67 = (f32[5,4,4,2,8,128]{5,4,3,2,1,0:T(8,128)S(1)}, f32[5,8,128]{2,1,0:T(8,128)S(1)}, f32[5,8,128]{2,1,0:T(8,128)S(1)}, f32[5,8,128]{2,1,0:T(8,128)S(1)}, f32[5,8,128]{2,1,0:T(8,128)S(1)}) custom-call(f32[5,4,4,2,8,128]{5,4,3,2,1,0:T(8,128)S(1)} %shard_map.66.acc_ref, f32[5,4,4,2,8,128]{5,4,3,2,1,0:T(8,128)S(1)} %get-tuple-element.33.u_ref, ...), custom_call_target="tpu_custom_call" | custom-call | flops 3145728 | bytes 4194304 | tf_op jit(solution)/shard_map/pallas_call | solution.py:648
  13.4 0.0 copy-start.2
  13.4 2.3 %collective-permute-start.4 = (f32[5,8,128]{2,1,0:T(8,128)S(1)}, f32[5,8,128]{2,1,0:T(8,128)S(1)}, u32[]{:S(2)}, u32[]{:S(2)}) collective-permute-start(f32[5,8,128]{2,1,0:T(8,128)S(1)} %get-tuple-element.42), channel_id=1, source_target_pairs={{0,28},{4,8},{8,4},{12,16},{16,12},{20,24},{24,20},{28,0},{1,29},{... | collective-permute-start | bytes 61448 | tf_op jit(solution)/shard_map/ppermute | solution.py:669
  15.7 0.0 collective-permute-start.5
  15.7 0.0 collective-permute-start.6
  15.7 1.6 %collective-permute-start.7 = (f32[5,8,128]{2,1,0:T(8,128)S(1)}, f32[5,8,128]{2,1,0:T(8,128)S(1)}, u32[]{:S(2)}, u32[]{:S(2)}) collective-permute-start(f32[5,8,128]{2,1,0:T(8,128)S(1)} %get-tuple-element.45), channel_id=1, source_target_pairs={{0,1},{1,0},{2,3},{3,2},{4,5},{5,4},{6,7},{7,6},{8,9},{9,8},{10,11... | collective-permute-start | bytes 61448 | tf_op jit(solution)/shard_map/ppermute | solution.py:674
  17.4 0.6 %shard_map.68.acc_ref = f32[5,2,2,8,128]{4,3,2,1,0:T(8,128)S(1)} custom-call(f32[5,4,4,2,8,128]{5,4,3,2,1,0:T(8,128)S(1)} %bitcast.13, f32[5,4,4,2,8,128]{5,4,3,2,1,0:T(8,128)S(1)} %get-tuple-element.41.u_ref.second_ref, s32[3,8,128]{2,1,0:T(8,128)S(1)} %get-tuple-element.32.flag_ref, f32[75,8,128]{2,1,0:T(8,128)S(1)} %get-tuple-element.34.jac8_ref.jac_ref, ...), custom_call_target="tpu_custom_call" | custom-call | flops 4194304 | bytes 4194304 | tf_op jit(solution)/shard_map/pallas_call | solution.py:648
  18.0 2.0 %collective-permute-done.4.rxo = f32[5,8,128]{2,1,0:T(8,128)S(1)} collective-permute-done((f32[5,8,128]{2,1,0:T(8,128)S(1)}, f32[5,8,128]{2,1,0:T(8,128)S(1)}, u32[]{:S(2)}, u32[]{:S(2)}) %collective-permute-start.4) | collective-permute-done | bytes 20512 | tf_op jit(solution)/shard_map/ppermute | solution.py:669
  20.0 0.0 collective-permute-done.5.rxe
  20.0 0.0 collective-permute-done.6.ryo
  20.0 0.0 collective-permute-done.7.rye
  20.0 0.0 copy-done.2
  20.0 0.1 shard_map.69
  20.1 2.3 %collective-permute-start.8 = (f32[5,8,128]{2,1,0:T(8,128)S(1)}, f32[5,8,128]{2,1,0:T(8,128)S(1)}, u32[]{:S(2)}, u32[]{:S(2)}) collective-permute-start(f32[5,8,128]{2,1,0:T(8,128)S(1)} %get-tuple-element.48), channel_id=1, source_target_pairs={{0,28},{4,8},{8,4},{12,16},{16,12},{20,24},{24,20},{28,0},{1,29},{... | collective-permute-start | bytes 61448 | tf_op jit(solution)/shard_map/ppermute | solution.py:669
  22.4 0.0 collective-permute-start.9
  22.5 0.0 collective-permute-start.10
  22.5 1.6 %collective-permute-start.11 = (f32[5,8,128]{2,1,0:T(8,128)S(1)}, f32[5,8,128]{2,1,0:T(8,128)S(1)}, u32[]{:S(2)}, u32[]{:S(2)}) collective-permute-start(f32[5,8,128]{2,1,0:T(8,128)S(1)} %get-tuple-element.51), channel_id=1, source_target_pairs={{0,1},{1,0},{2,3},{3,2},{4,5},{5,4},{6,7},{7,6},{8,9},{9,8},{10,11... | collective-permute-start | bytes 61448 | tf_op jit(solution)/shard_map/ppermute | solution.py:674
  24.1 0.2 shard_map.70.c_ref
  24.3 2.4 %collective-permute-done.8.rxo = f32[5,8,128]{2,1,0:T(8,128)S(1)} collective-permute-done((f32[5,8,128]{2,1,0:T(8,128)S(1)}, f32[5,8,128]{2,1,0:T(8,128)S(1)}, u32[]{:S(2)}, u32[]{:S(2)}) %collective-permute-start.8) | collective-permute-done | bytes 20512 | tf_op jit(solution)/shard_map/ppermute | solution.py:669
  26.7 0.0 collective-permute-done.9.rxe
  26.7 0.0 collective-permute-done.10.ryo
  26.7 0.0 collective-permute-done.11.rye
  26.7 0.1 shard_map.71
  26.8 2.3 %collective-permute-start.12 = (f32[5,8,128]{2,1,0:T(8,128)S(1)}, f32[5,8,128]{2,1,0:T(8,128)S(1)}, u32[]{:S(2)}, u32[]{:S(2)}) collective-permute-start(f32[5,8,128]{2,1,0:T(8,128)S(1)} %get-tuple-element.53), channel_id=1, source_target_pairs={{0,28},{4,8},{8,4},{12,16},{16,12},{20,24},{24,20},{28,0},{1,29},{... | collective-permute-start | bytes 61448 | tf_op jit(solution)/shard_map/ppermute | solution.py:669
  29.1 0.0 collective-permute-start.13
  29.1 0.0 collective-permute-start.14
  29.1 1.6 %collective-permute-start.15 = (f32[5,8,128]{2,1,0:T(8,128)S(1)}, f32[5,8,128]{2,1,0:T(8,128)S(1)}, u32[]{:S(2)}, u32[]{:S(2)}) collective-permute-start(f32[5,8,128]{2,1,0:T(8,128)S(1)} %get-tuple-element.56), channel_id=1, source_target_pairs={{0,1},{1,0},{2,3},{3,2},{4,5},{5,4},{6,7},{7,6},{8,9},{9,8},{10,11... | collective-permute-start | bytes 61448 | tf_op jit(solution)/shard_map/ppermute | solution.py:674
  30.7 0.2 shard_map.72.c_ref
  31.0 2.4 %collective-permute-done.12.rxo = f32[5,8,128]{2,1,0:T(8,128)S(1)} collective-permute-done((f32[5,8,128]{2,1,0:T(8,128)S(1)}, f32[5,8,128]{2,1,0:T(8,128)S(1)}, u32[]{:S(2)}, u32[]{:S(2)}) %collective-permute-start.12) | collective-permute-done | bytes 20512 | tf_op jit(solution)/shard_map/ppermute | solution.py:669
  33.4 0.0 collective-permute-done.13.rxe
  33.4 0.0 collective-permute-done.14.ryo
  33.4 0.0 collective-permute-done.15.rye
  33.4 1.0 %shard_map.73 = f32[5,4,4,2,8,128]{5,4,3,2,1,0:T(8,128)} custom-call(f32[5,2,2,8,128]{4,3,2,1,0:T(8,128)S(1)} %shard_map.72.c_ref, bf16[25,2,16,128]{3,2,1,0:T(8,128)(2,1)S(1)} %bitcast.18, s32[3,8,128]{2,1,0:T(8,128)S(1)} %get-tuple-element.32.flag_ref, f32[4,25,8,128]{3,2,1,0:T(8,128)S(1)} %get-tuple-element.36.face_ref, ...), custom_call_target="tpu_custom_call" | custom-call | flops 1048576 | bytes 4194304 | tf_op jit(solution)/shard_map/pallas_call | solution.py:648
Async XLA Ops:
  0.0 7.9 %copy-start = (bf16[5,5,4,4,4,2,2,128]{7,6,5,4,3,2,1,0:T(2,128)(2,1)S(1)}, bf16[5,5,4,4,4,2,2,128]{7,6,5,4,3,2,1,0:T(2,128)(2,1)}, u32[]{:S(2)}) copy-start(bf16[5,5,4,4,4,2,2,128]{7,6,5,4,3,2,1,0:T(2,128)(2,1)} %param.10) | copy-start | bytes 4915204
  0.0 7.9 %copy-start.1 = (f32[5,4,4,4,2,2,128]{6,5,4,3,2,1,0:T(2,128)S(1)}, f32[5,4,4,4,2,2,128]{6,5,4,3,2,1,0:T(2,128)}, u32[]{:S(2)}) copy-start(f32[5,4,4,4,2,2,128]{6,5,4,3,2,1,0:T(2,128)} %param.6) | copy-start | bytes 1966084
  1.8 10.2 %collective-permute-start = (f32[5,4,8,128]{3,2,1,0:T(8,128)S(1)}, f32[5,4,8,128]{3,2,1,0:T(8,128)S(1)}, u32[]{:S(2)}, u32[]{:S(2)}) collective-permute-start(f32[5,4,8,128]{3,2,1,0:T(8,128)S(1)} %get-tuple-element.37), channel_id=1, source_target_pairs={{0,28},{4,8},{8,4},{12,16},{16,12},{20,24},{24,20},{28,0},{1,29},{... | collective-permute-start | bytes 245768 | tf_op jit(solution)/shard_map/ppermute | solution.py:669
  7.8 4.4 %collective-permute-start.1 = (f32[5,4,8,128]{3,2,1,0:T(8,128)S(1)}, f32[5,4,8,128]{3,2,1,0:T(8,128)S(1)}, u32[]{:S(2)}, u32[]{:S(2)}) collective-permute-start(f32[5,4,8,128]{3,2,1,0:T(8,128)S(1)} %get-tuple-element.38), channel_id=1, source_target_pairs={{0,4},{4,0},{8,12},{12,8},{16,20},{20,16},{24,28},{28,24},{1,5},{5... | collective-permute-start | bytes 245768 | tf_op jit(solution)/shard_map/ppermute | solution.py:669
  8.1 4.7 %collective-permute-start.2 = (f32[5,4,8,128]{3,2,1,0:T(8,128)S(1)}, f32[5,4,8,128]{3,2,1,0:T(8,128)S(1)}, u32[]{:S(2)}, u32[]{:S(2)}) collective-permute-start(f32[5,4,8,128]{3,2,1,0:T(8,128)S(1)} %get-tuple-element.39), channel_id=1, source_target_pairs={{0,3},{1,2},{2,1},{3,0},{4,7},{5,6},{6,5},{7,4},{8,11},{9,10},{10,... | collective-permute-start | bytes 245768 | tf_op jit(solution)/shard_map/ppermute | solution.py:674
  8.8 4.0 %collective-permute-start.3 = (f32[5,4,8,128]{3,2,1,0:T(8,128)S(1)}, f32[5,4,8,128]{3,2,1,0:T(8,128)S(1)}, u32[]{:S(2)}, u32[]{:S(2)}) collective-permute-start(f32[5,4,8,128]{3,2,1,0:T(8,128)S(1)} %get-tuple-element.40), channel_id=1, source_target_pairs={{0,1},{1,0},{2,3},{3,2},{4,5},{5,4},{6,7},{7,6},{8,9},{9,8},{10,11... | collective-permute-start | bytes 245768 | tf_op jit(solution)/shard_map/ppermute | solution.py:674
  13.4 6.6 %copy-start.2 = (bf16[5,5,2,2,2,2,2,128]{7,6,5,4,3,2,1,0:T(2,128)(2,1)S(1)}, bf16[5,5,2,2,2,2,2,128]{7,6,5,4,3,2,1,0:T(2,128)(2,1)}, u32[]{:S(2)}) copy-start(bf16[5,5,2,2,2,2,2,128]{7,6,5,4,3,2,1,0:T(2,128)(2,1)} %param.11) | copy-start | bytes 614404
  13.4 6.5 %collective-permute-start.4 = (f32[5,8,128]{2,1,0:T(8,128)S(1)}, f32[5,8,128]{2,1,0:T(8,128)S(1)}, u32[]{:S(2)}, u32[]{:S(2)}) collective-permute-start(f32[5,8,128]{2,1,0:T(8,128)S(1)} %get-tuple-element.42), channel_id=1, source_target_pairs={{0,28},{4,8},{8,4},{12,16},{16,12},{20,24},{24,20},{28,0},{1,29},{... | collective-permute-start | bytes 61448 | tf_op jit(solution)/shard_map/ppermute | solution.py:669
  15.7 4.3 %collective-permute-start.5 = (f32[5,8,128]{2,1,0:T(8,128)S(1)}, f32[5,8,128]{2,1,0:T(8,128)S(1)}, u32[]{:S(2)}, u32[]{:S(2)}) collective-permute-start(f32[5,8,128]{2,1,0:T(8,128)S(1)} %get-tuple-element.43), channel_id=1, source_target_pairs={{0,4},{4,0},{8,12},{12,8},{16,20},{20,16},{24,28},{28,24},{1,5},{5... | collective-permute-start | bytes 61448 | tf_op jit(solution)/shard_map/ppermute | solution.py:669
  15.7 4.3 %collective-permute-start.6 = (f32[5,8,128]{2,1,0:T(8,128)S(1)}, f32[5,8,128]{2,1,0:T(8,128)S(1)}, u32[]{:S(2)}, u32[]{:S(2)}) collective-permute-start(f32[5,8,128]{2,1,0:T(8,128)S(1)} %get-tuple-element.44), channel_id=1, source_target_pairs={{0,3},{1,2},{2,1},{3,0},{4,7},{5,6},{6,5},{7,4},{8,11},{9,10},{10,... | collective-permute-start | bytes 61448 | tf_op jit(solution)/shard_map/ppermute | solution.py:674
  15.7 4.3 %collective-permute-start.7 = (f32[5,8,128]{2,1,0:T(8,128)S(1)}, f32[5,8,128]{2,1,0:T(8,128)S(1)}, u32[]{:S(2)}, u32[]{:S(2)}) collective-permute-start(f32[5,8,128]{2,1,0:T(8,128)S(1)} %get-tuple-element.45), channel_id=1, source_target_pairs={{0,1},{1,0},{2,3},{3,2},{4,5},{5,4},{6,7},{7,6},{8,9},{9,8},{10,11... | collective-permute-start | bytes 61448 | tf_op jit(solution)/shard_map/ppermute | solution.py:674
  20.1 6.5 %collective-permute-start.8 = (f32[5,8,128]{2,1,0:T(8,128)S(1)}, f32[5,8,128]{2,1,0:T(8,128)S(1)}, u32[]{:S(2)}, u32[]{:S(2)}) collective-permute-start(f32[5,8,128]{2,1,0:T(8,128)S(1)} %get-tuple-element.48), channel_id=1, source_target_pairs={{0,28},{4,8},{8,4},{12,16},{16,12},{20,24},{24,20},{28,0},{1,29},{... | collective-permute-start | bytes 61448 | tf_op jit(solution)/shard_map/ppermute | solution.py:669
  22.4 4.2 %collective-permute-start.9 = (f32[5,8,128]{2,1,0:T(8,128)S(1)}, f32[5,8,128]{2,1,0:T(8,128)S(1)}, u32[]{:S(2)}, u32[]{:S(2)}) collective-permute-start(f32[5,8,128]{2,1,0:T(8,128)S(1)} %get-tuple-element.49), channel_id=1, source_target_pairs={{0,4},{4,0},{8,12},{12,8},{16,20},{20,16},{24,28},{28,24},{1,5},{5... | collective-permute-start | bytes 61448 | tf_op jit(solution)/shard_map/ppermute | solution.py:669
  22.5 4.2 %collective-permute-start.10 = (f32[5,8,128]{2,1,0:T(8,128)S(1)}, f32[5,8,128]{2,1,0:T(8,128)S(1)}, u32[]{:S(2)}, u32[]{:S(2)}) collective-permute-start(f32[5,8,128]{2,1,0:T(8,128)S(1)} %get-tuple-element.50), channel_id=1, source_target_pairs={{0,3},{1,2},{2,1},{3,0},{4,7},{5,6},{6,5},{7,4},{8,11},{9,10},{10,... | collective-permute-start | bytes 61448 | tf_op jit(solution)/shard_map/ppermute | solution.py:674
  22.5 4.2 %collective-permute-start.11 = (f32[5,8,128]{2,1,0:T(8,128)S(1)}, f32[5,8,128]{2,1,0:T(8,128)S(1)}, u32[]{:S(2)}, u32[]{:S(2)}) collective-permute-start(f32[5,8,128]{2,1,0:T(8,128)S(1)} %get-tuple-element.51), channel_id=1, source_target_pairs={{0,1},{1,0},{2,3},{3,2},{4,5},{5,4},{6,7},{7,6},{8,9},{9,8},{10,11... | collective-permute-start | bytes 61448 | tf_op jit(solution)/shard_map/ppermute | solution.py:674
  26.8 6.5 %collective-permute-start.12 = (f32[5,8,128]{2,1,0:T(8,128)S(1)}, f32[5,8,128]{2,1,0:T(8,128)S(1)}, u32[]{:S(2)}, u32[]{:S(2)}) collective-permute-start(f32[5,8,128]{2,1,0:T(8,128)S(1)} %get-tuple-element.53), channel_id=1, source_target_pairs={{0,28},{4,8},{8,4},{12,16},{16,12},{20,24},{24,20},{28,0},{1,29},{... | collective-permute-start | bytes 61448 | tf_op jit(solution)/shard_map/ppermute | solution.py:669
  29.1 4.2 %collective-permute-start.13 = (f32[5,8,128]{2,1,0:T(8,128)S(1)}, f32[5,8,128]{2,1,0:T(8,128)S(1)}, u32[]{:S(2)}, u32[]{:S(2)}) collective-permute-start(f32[5,8,128]{2,1,0:T(8,128)S(1)} %get-tuple-element.54), channel_id=1, source_target_pairs={{0,4},{4,0},{8,12},{12,8},{16,20},{20,16},{24,28},{28,24},{1,5},{5... | collective-permute-start | bytes 61448 | tf_op jit(solution)/shard_map/ppermute | solution.py:669
  29.1 4.2 %collective-permute-start.14 = (f32[5,8,128]{2,1,0:T(8,128)S(1)}, f32[5,8,128]{2,1,0:T(8,128)S(1)}, u32[]{:S(2)}, u32[]{:S(2)}) collective-permute-start(f32[5,8,128]{2,1,0:T(8,128)S(1)} %get-tuple-element.55), channel_id=1, source_target_pairs={{0,3},{1,2},{2,1},{3,0},{4,7},{5,6},{6,5},{7,4},{8,11},{9,10},{10,... | collective-permute-start | bytes 61448 | tf_op jit(solution)/shard_map/ppermute | solution.py:674
  29.1 4.2 %collective-permute-start.15 = (f32[5,8,128]{2,1,0:T(8,128)S(1)}, f32[5,8,128]{2,1,0:T(8,128)S(1)}, u32[]{:S(2)}, u32[]{:S(2)}) collective-permute-start(f32[5,8,128]{2,1,0:T(8,128)S(1)} %get-tuple-element.56), channel_id=1, source_target_pairs={{0,1},{1,0},{2,3},{3,2},{4,5},{5,4},{6,7},{7,6},{8,9},{9,8},{10,11... | collective-permute-start | bytes 61448 | tf_op jit(solution)/shard_map/ppermute | solution.py:674

commit v7 on v5

--- a/solution.py
+++ b/solution.py
@@ -160,38 +160,54 @@
         put_coarse_faces(v, lows, highs, flag_ref, ((xe, xo), (ye, yo)))
 
 
+def smoothed(smooth_ref, fields, a, b):
+    out = []
+    for o in range(5):
+        total = [None, None]
+        for i in range(5):
+            block = smooth_ref[5 * o + i, a, b].astype(F32)
+            for q in range(2):
+                term = block[8 * q : 8 * q + 8] * fields[i][q]
+                total[q] = term if i == 0 else total[q] + term
+        out.append([OMEGA * total[q] for q in range(2)])
+    return out
+
+
+def first_line(src_ref, smooth_ref, u_ref, a, b):
+    value = smoothed(smooth_ref, [[src_ref[v, a, b, q] for q in range(2)] for v in range(5)], a, b)
+    for v in range(5):
+        for q in range(2):
+            u_ref[v, a, b, q] = value[v][q]
+
+
+def line_copies(src_hbm, smooth_hbm, src_ref, smooth_ref, sems, slot, a, b):
+    return (
+        pltpu.make_async_copy(src_hbm.at[:, a, b], src_ref.at[:, a, b], sems.at[0, slot]),
+        pltpu.make_async_copy(smooth_hbm.at[:, a, b], smooth_ref.at[:, a, b], sems.at[1, slot]),
+    )
+
+
 def first_kernel(
     src_hbm, smooth_hbm, orient_hbm, src_ref, smooth_ref, u_ref, flag_ref, xo, xe, yo, ye, sems, orient_ref, orient_sem
 ):
+    every, inner = slice(0, 4), slice(1, 3)
     orient_copy = pltpu.make_async_copy(orient_hbm, orient_ref, orient_sem)
     orient_copy.start()
     copies = []
-    for slot, a in enumerate((0, 3, 1, 2)):
-        pair = (
-            pltpu.make_async_copy(src_hbm.at[:, a], src_ref.at[:, a], sems.at[0, slot]),
-            pltpu.make_async_copy(smooth_hbm.at[:, a], smooth_ref.at[:, a], sems.at[1, slot]),
-        )
+    for slot, (a, b) in enumerate(((0, every), (3, every), (inner, 0), (inner, 3))):
+        pair = line_copies(src_hbm, smooth_hbm, src_ref, smooth_ref, sems, slot, a, b)
         for one in pair:
             one.start()
-        copies.append((a, pair))
+        copies.append(pair)
     orient_copy.wait()
     for d in range(3):
         flag_ref[d] = twice(orient_ref[d])
-    for a, pair in copies:
+    lines = [[(0, b) for b in range(4)], [(3, b) for b in range(4)], [(1, 0), (2, 0)], [(1, 3), (2, 3)]]
+    for pair, group in zip(copies, lines):
         for one in pair:
             one.wait()
-
-        for b in range(4):
-            src = [[src_ref[v, a, b, q] for q in range(2)] for v in range(5)]
-            for o in range(5):
-                total = [None, None]
-                for i in range(5):
-                    block = smooth_ref[5 * o + i, a, b].astype(F32)
-                    for q in range(2):
-                        term = block[8 * q : 8 * q + 8] * src[i][q]
-                        total[q] = term if i == 0 else total[q] + term
-                for q in range(2):
-                    u_ref[o, a, b, q] = OMEGA * total[q]
+        for a, b in group:
+            first_line(src_ref, smooth_ref, u_ref, a, b)
     fine_faces(u_ref, flag_ref, xo, xe, yo, ye)
 
 
@@ -211,13 +227,13 @@
                 face_ref[2 * d + 1, k] = jnp.where(low, lower, sroll(lower, step))
 
 
-def volume(src_ref, u_ref, flag_ref, jac_ref, damp_ref, acc_ref):
+def volume(src_ref, u_ref, flag_ref, jac_ref, damp_ref, acc_ref, finish_lines):
     damp = H4 * damp_ref[...]
 
     def jacobian(d):
         return [[jac_ref[25 * d + 5 * o + i] for i in range(5)] for o in range(5)]
 
-    def along(direction):
+    def along(direction, others):
         low, step = axis_low(direction)
         flag = flag_ref[direction] != 0
         flag_before = sroll(flag_ref[direction], step) != 0
@@ -226,7 +242,7 @@
             return (v, n, other, q) if direction == 0 else (v, other, n, q)
 
         def step_fn(j, carry):
-            other, q = j // 2, j % 2
+            other, q = others(j // 2), j % 2
             u = [[u_ref[at(v, n, other, q)] for n in range(4)] for v in range(5)]
             waves = []
             jumps = []
@@ -245,7 +261,7 @@
             for n in range(4):
                 flux = mix(matrix, [waves[v][n] for v in range(5)])
                 for v in range(5):
-                    if direction == 0:
+                    if direction == 1:
                         total = src_ref[at(v, n, other, q)] - 2.0 * u[v][n]
                     else:
                         total = acc_ref[at(v, n, other, q)]
@@ -255,10 +271,7 @@
                     acc_ref[at(v, n, other, q)] = total
             return carry
 
-        lax.fori_loop(0, 8, step_fn, 0)
-
-    along(0)
-    along(1)
+        return step_fn
 
     low = c_low()
     flag = jnp.where(low, lroll(flag_ref[2], 1), flag_ref[2]) != 0
@@ -301,12 +314,37 @@
                     acc_ref[v, here[s], b, p] = acc_ref[v, here[s], b, p] - flux[v] + part
         return carry
 
-    lax.fori_loop(0, 8, step_z, 0)
-
-
-def first_volume_kernel(src_ref, u_ref, flag_ref, jac_ref, damp_ref, acc_ref, jac8_ref, damp8_ref, face_ref):
+    lax.fori_loop(0, 4, along(1, lambda k: 3 * k), 0)
+    lax.fori_loop(0, 4, step_z, 0)
+    finish_lines()
+    lax.fori_loop(0, 4, along(1, lambda k: 1 + k), 0)
+    lax.fori_loop(4, 8, step_z, 0)
+    lax.fori_loop(0, 8, along(0, lambda k: k), 0)
+
+
+def first_volume_kernel(
+    src_hbm, smooth_hbm, src_in, smooth_in, u_in, flag_ref, jac_ref, damp_ref,
+    src_ref, smooth_ref, u_ref, acc_ref, jac8_ref, damp8_ref, face_ref, second_ref, sems,
+):
+    inner = slice(1, 3)
+    copies = line_copies(src_hbm, smooth_hbm, src_ref, smooth_ref, sems, 0, inner, inner)
+    for one in copies:
+        one.start()
     prepare_tables(jac_ref, damp_ref, jac8_ref, damp8_ref, face_ref)
-    volume(src_ref, u_ref, flag_ref, jac8_ref, damp8_ref, acc_ref)
+    lines = [(a, b) for a in (1, 2) for b in (1, 2)]
+
+    def finish_lines():
+        for one in copies:
+            one.wait()
+        for a, b in lines:
+            first_line(src_ref, smooth_ref, u_ref, a, b)
+
+    volume(src_ref, u_ref, flag_ref, jac8_ref, damp8_ref, acc_ref, finish_lines)
+    for a, b in lines:
+        change = smoothed(smooth_ref, [[acc_ref[v, a, b, q] for q in range(2)] for v in range(5)], a, b)
+        for v in range(5):
+            for q in range(2):
+                second_ref[v, a, b, q] = u_ref[v, a, b, q] + change[v][q]
 
 
 def remote_parts(even_refs, odd_refs, flag_ref, face_ref, part_ref):
@@ -345,21 +383,18 @@
 
 
 def second_kernel(
-    acc_ref, u_ref, smooth_ref, flag_ref, face_ref, rxo, rxe, ryo, rye, out_ref, xo, xe, yo, ye, part_ref
+    acc_ref, u_ref, smooth_ref, flag_ref, face_ref, rxo, rxe, ryo, rye, inner_ref, out_ref, xo, xe, yo, ye, part_ref
 ):
     remote_parts((rxe, rye), (rxo, ryo), flag_ref, face_ref, part_ref)
     for a in range(4):
         for b in range(4):
+            if a in (1, 2) and b in (1, 2):
+                continue
             left = [[whole(acc_ref, part_ref, v, a, b, q) for q in range(2)] for v in range(5)]
-            for o in range(5):
-                total = [None, None]
-                for i in range(5):
-                    block = smooth_ref[5 * o + i, a, b].astype(F32)
-                    for q in range(2):
-                        term = block[8 * q : 8 * q + 8] * left[i][q]
-                        total[q] = term if i == 0 else total[q] + term
+            change = smoothed(smooth_ref, left, a, b)
+            for v in range(5):
                 for q in range(2):
-                    out_ref[o, a, b, q] = u_ref[o, a, b, q] + OMEGA * total[q]
+                    out_ref[v, a, b, q] = u_ref[v, a, b, q] + change[v][q]
     restricted_faces(out_ref, flag_ref, xo, xe, yo, ye)
 
 
@@ -616,7 +651,7 @@
     return pltpu.with_memory_space_constraint(array, pltpu.VMEM)
 
 
-def call(kernel, args, outs, in_hbm=(), out_hbm=(), scratch=(), flops=0):
+def call(kernel, args, outs, in_hbm=(), out_hbm=(), scratch=(), aliases=None, flops=0):
     in_specs = [
         pl.BlockSpec(memory_space=pltpu.HBM if k in in_hbm else pltpu.VMEM) for k in range(len(args))
     ]
@@ -630,6 +665,7 @@
         in_specs=in_specs,
         out_specs=out_specs,
         scratch_shapes=scratch,
+        input_output_aliases=aliases or {},
         compiler_params=pltpu.CompilerParams(vmem_limit_bytes=8 * 2**20),
         cost_estimate=pl.CostEstimate(flops=flops, bytes_accessed=4 * 2**20, transcendentals=0),
     )(*args)
@@ -667,25 +703,31 @@
     fine_messages = [vmem(FINE_MESSAGE)] * 4
     coarse_messages = [vmem(COARSE_MESSAGE)] * 4
 
+    held = vmem(smoother.shape, smoother.dtype)
+    source_in, smoother_in = source, smoother
     source, smoother, first, flag, *sent = call(
         first_kernel,
-        (source, smoother, orient),
-        [vmem(FINE), vmem(smoother.shape, smoother.dtype), vmem(FINE), vmem((3, 8, 128), jnp.int32)] + fine_messages,
+        (source_in, smoother_in, orient),
+        [vmem(FINE), held, vmem(FINE), vmem((3, 8, 128), jnp.int32)] + fine_messages,
         in_hbm=(0, 1, 2),
         scratch=[pltpu.SemaphoreType.DMA((2, 4)), pltpu.VMEM((3, 4, 128), jnp.int32), pltpu.SemaphoreType.DMA],
         flops=2 * 25 * 64 * 512,
     )
     got = exchange(*sent)
-    acc, jac8, damp8, face = call(
+    source, smoother, first, acc, jac8, damp8, face, second = call(
         first_volume_kernel,
-        (source, first, flag, jacobian, damping),
-        [vmem(FINE), vmem((75, 8, 128)), vmem((8, 128)), vmem((4, 25, 8, 128))],
+        (source_in, smoother_in, source, smoother, first, flag, jacobian, damping),
+        [vmem(FINE), held, vmem(FINE), vmem(FINE), vmem((75, 8, 128)), vmem((8, 128)), vmem((4, 25, 8, 128)), vmem(FINE)],
+        in_hbm=(0, 1),
+        aliases={2: 0, 3: 1, 4: 2},
+        scratch=[pltpu.SemaphoreType.DMA((2, 1))],
         flops=9 * 2**20,
     )
     second, *sent = call(
         second_kernel,
-        (acc, first, smoother, flag, face, *got),
+        (acc, first, smoother, flag, face, *got, second),
         [vmem(FINE)] + coarse_messages,
+        aliases={9: 0},
         scratch=[pltpu.VMEM((4, 5, 4, 2, 8, 128), F32)],
         flops=3 * 2**20,
     )

time: 34.3 us -> 34 us (level)
  waiting for transfers between devices: 6.73 us -> 6.37 us
    ppermute x4, waiting for transfers between devices: 0.51 us -> 0.15 us  [exchange(): xe = lax.ppermute(xe, 'gx', even_x)]
  transfers between devices with their start and end apart: 16 -> 16, of which waited for: 5 -> 5; matrix products, arithmetic and copies ran while one was open for 0% -> 0% of each run, Pallas kernels for 10% -> 11%
where the time goes in v7:
time: 34 us; the launch traced here: 33.9 us
  starting transfers between devices  20.2 us (59%)
  Pallas kernels  7.17 us (21%)
  waiting for transfers between devices  6.37 us (19%)
    ppermute x4, starting transfers between devices, exchange(): xo = lax.ppermute(xo, 'gx', odd_x)  13.7 us
    pallas_call x9, Pallas kernels, call(): pl.pallas_call(kernel, out_shape=outs, in_specs=in_specs, out_specs=out_s...  7.17 us
    ppermute x4, waiting for transfers between devices, exchange(): xo = lax.ppermute(xo, 'gx', odd_x)  5.98 us
    ppermute x4, starting transfers between devices, exchange(): ye = lax.ppermute(ye, 'gy', even_y)  5.85 us
    ppermute x4, starting transfers between devices, exchange(): yo = lax.ppermute(yo, 'gy', odd_y)  0.69 us
  transfers between devices with their start and end apart: 16, of which 5 were waited for; matrix products, arithmetic and copies ran while one was open for 0% of the time, Pallas kernels for 11%

profile of v7, /device:TPU:0, one launch (start us, length us, event | category | flops | bytes accessed | tf_op | source)
XLA Modules:
  0.0 33.9 jit_solution(15152570131162613959)
XLA Ops:
  0.0 0.0 copy-start.2
  0.0 0.0 copy-start.1
  0.0 1.6 %shard_map.64 = (f32[5,4,4,2,8,128]{5,4,3,2,1,0:T(8,128)S(1)}, bf16[25,4,4,16,128]{4,3,2,1,0:T(8,128)(2,1)S(1)}, f32[5,4,4,2,8,128]{5,4,3,2,1,0:T(8,128)S(1)}, s...) custom-call(f32[5,4,4,2,8,128]{5,4,3,2,1,0:T(8,128)} %bitcast.16, ...), custom_call_target="tpu_custom_call" | custom-call | flops 1638400 | bytes 4194304 | tf_op jit(solution)/shard_map/pallas_call | solution.py:662
  1.7 6.1 %collective-permute-start = (f32[5,4,8,128]{3,2,1,0:T(8,128)S(1)}, f32[5,4,8,128]{3,2,1,0:T(8,128)S(1)}, u32[]{:S(2)}, u32[]{:S(2)}) collective-permute-start(f32[5,4,8,128]{3,2,1,0:T(8,128)S(1)} %get-tuple-element.46), channel_id=1, source_target_pairs={{0,28},{4,8},{8,4},{12,16},{16,12},{20,24},{24,20},{28,0},{1,29},{... | collective-permute-start | bytes 245768 | tf_op jit(solution)/shard_map/ppermute | solution.py:684
  7.7 0.0 collective-permute-start.1
  7.7 0.7 %collective-permute-start.2 = (f32[5,4,8,128]{3,2,1,0:T(8,128)S(1)}, f32[5,4,8,128]{3,2,1,0:T(8,128)S(1)}, u32[]{:S(2)}, u32[]{:S(2)}) collective-permute-start(f32[5,4,8,128]{3,2,1,0:T(8,128)S(1)} %get-tuple-element.48), channel_id=1, source_target_pairs={{0,3},{1,2},{2,1},{3,0},{4,7},{5,6},{6,5},{7,4},{8,11},{9,10},{10,... | collective-permute-start | bytes 245768 | tf_op jit(solution)/shard_map/ppermute | solution.py:686
  8.4 1.0 %collective-permute-start.3 = (f32[5,4,8,128]{3,2,1,0:T(8,128)S(1)}, f32[5,4,8,128]{3,2,1,0:T(8,128)S(1)}, u32[]{:S(2)}, u32[]{:S(2)}) collective-permute-start(f32[5,4,8,128]{3,2,1,0:T(8,128)S(1)} %get-tuple-element.49), channel_id=1, source_target_pairs={{0,1},{1,0},{2,3},{3,2},{4,5},{5,4},{6,7},{7,6},{8,9},{9,8},{10,11... | collective-permute-start | bytes 245768 | tf_op jit(solution)/shard_map/ppermute | solution.py:687
  9.4 0.0 copy-done.2
  9.4 0.0 copy-done.1
  9.4 2.6 %shard_map.65 = (f32[5,4,4,2,8,128]{5,4,3,2,1,0:T(8,128)S(1)}, bf16[25,4,4,16,128]{4,3,2,1,0:T(8,128)(2,1)S(1)}, f32[5,4,4,2,8,128]{5,4,3,2,1,0:T(8,128)S(1)}, f...) custom-call(f32[5,4,4,2,8,128]{5,4,3,2,1,0:T(8,128)} %bitcast.17, ...), custom_call_target="tpu_custom_call", output_to_operand_aliasing={{0}: (2, {}), {1}: (3, {}), {2}: (4, {})} | custom-call | flops 9437184 | bytes 4194304 | tf_op jit(solution)/shard_map/pallas_call | solution.py:662
  12.0 0.0 collective-permute-done.rxo
  12.0 0.1 collective-permute-done.1.rxe
  12.2 0.2 collective-permute-done.2.ryo
  12.4 0.0 collective-permute-done.3.rye
  12.4 0.6 %shard_map.66 = (f32[5,4,4,2,8,128]{5,4,3,2,1,0:T(8,128)S(1)}, f32[5,8,128]{2,1,0:T(8,128)S(1)}, f32[5,8,128]{2,1,0:T(8,128)S(1)}, f32[5,8,128]{2,1,0:T(8,128)S(1)}, f32[5,8,128]{2,1,0:T(8,128)S(1)}) custom-call(f32[5,4,4,2,8,128]{5,4,3,2,1,0:T(8,128)S(1)} %get-tuple-element.42.acc_ref, ...), custom_call_target="tpu_custom_call", output_to_operand_aliasing={{0}: (9, {})} | custom-call | flops 3145728 | bytes 4194304 | tf_op jit(solution)/shard_map/pallas_call | solution.py:662
  13.0 0.0 copy-start
  13.0 2.5 %collective-permute-start.4 = (f32[5,8,128]{2,1,0:T(8,128)S(1)}, f32[5,8,128]{2,1,0:T(8,128)S(1)}, u32[]{:S(2)}, u32[]{:S(2)}) collective-permute-start(f32[5,8,128]{2,1,0:T(8,128)S(1)} %get-tuple-element.54), channel_id=1, source_target_pairs={{0,28},{4,8},{8,4},{12,16},{16,12},{20,24},{24,20},{28,0},{1,29},{... | collective-permute-start | bytes 61448 | tf_op jit(solution)/shard_map/ppermute | solution.py:684
  15.5 0.0 collective-permute-start.5
  15.5 0.0 collective-permute-start.6
  15.5 1.6 %collective-permute-start.7 = (f32[5,8,128]{2,1,0:T(8,128)S(1)}, f32[5,8,128]{2,1,0:T(8,128)S(1)}, u32[]{:S(2)}, u32[]{:S(2)}) collective-permute-start(f32[5,8,128]{2,1,0:T(8,128)S(1)} %get-tuple-element.57), channel_id=1, source_target_pairs={{0,1},{1,0},{2,3},{3,2},{4,5},{5,4},{6,7},{7,6},{8,9},{9,8},{10,11... | collective-permute-start | bytes 61448 | tf_op jit(solution)/shard_map/ppermute | solution.py:687
  17.2 0.6 %shard_map.67.acc_ref = f32[5,2,2,8,128]{4,3,2,1,0:T(8,128)S(1)} custom-call(f32[5,4,4,2,8,128]{5,4,3,2,1,0:T(8,128)S(1)} %get-tuple-element.41.src_ref, f32[5,4,4,2,8,128]{5,4,3,2,1,0:T(8,128)S(1)} %get-tuple-element.51.u_ref.second_ref, s32[3,8,128]{2,1,0:T(8,128)S(1)} %get-tuple-element.40.flag_ref, f32[75,8,128]{2,1,0:T(8,128)S(1)} %get-tuple-element.52.jac_ref, ...), custom_call_target="tpu_custom_call" | custom-call | flops 4194304 | bytes 4194304 | tf_op jit(solution)/shard_map/pallas_call | solution.py:662
  17.8 1.7 %collective-permute-done.4.rxo = f32[5,8,128]{2,1,0:T(8,128)S(1)} collective-permute-done((f32[5,8,128]{2,1,0:T(8,128)S(1)}, f32[5,8,128]{2,1,0:T(8,128)S(1)}, u32[]{:S(2)}, u32[]{:S(2)}) %collective-permute-start.4) | collective-permute-done | bytes 20512 | tf_op jit(solution)/shard_map/ppermute | solution.py:684
  19.5 0.0 collective-permute-done.5.rxe
  19.5 0.0 collective-permute-done.6.ryo
  19.5 0.0 collective-permute-done.7.rye
  19.5 0.0 copy-done
  19.5 0.1 shard_map.68
  19.7 2.5 %collective-permute-start.8 = (f32[5,8,128]{2,1,0:T(8,128)S(1)}, f32[5,8,128]{2,1,0:T(8,128)S(1)}, u32[]{:S(2)}, u32[]{:S(2)}) collective-permute-start(f32[5,8,128]{2,1,0:T(8,128)S(1)} %get-tuple-element.60), channel_id=1, source_target_pairs={{0,28},{4,8},{8,4},{12,16},{16,12},{20,24},{24,20},{28,0},{1,29},{... | collective-permute-start | bytes 61448 | tf_op jit(solution)/shard_map/ppermute | solution.py:684
  22.2 0.0 collective-permute-start.9
  22.2 0.0 collective-permute-start.10
  22.2 1.6 %collective-permute-start.11 = (f32[5,8,128]{2,1,0:T(8,128)S(1)}, f32[5,8,128]{2,1,0:T(8,128)S(1)}, u32[]{:S(2)}, u32[]{:S(2)}) collective-permute-start(f32[5,8,128]{2,1,0:T(8,128)S(1)} %get-tuple-element.63), channel_id=1, source_target_pairs={{0,1},{1,0},{2,3},{3,2},{4,5},{5,4},{6,7},{7,6},{8,9},{9,8},{10,11... | collective-permute-start | bytes 61448 | tf_op jit(solution)/shard_map/ppermute | solution.py:687
  23.9 0.2 shard_map.69.c_ref
  24.1 2.1 %collective-permute-done.8.rxo = f32[5,8,128]{2,1,0:T(8,128)S(1)} collective-permute-done((f32[5,8,128]{2,1,0:T(8,128)S(1)}, f32[5,8,128]{2,1,0:T(8,128)S(1)}, u32[]{:S(2)}, u32[]{:S(2)}) %collective-permute-start.8) | collective-permute-done | bytes 20512 | tf_op jit(solution)/shard_map/ppermute | solution.py:684
  26.2 0.0 collective-permute-done.9.rxe
  26.2 0.0 collective-permute-done.10.ryo
  26.2 0.0 collective-permute-done.11.rye
  26.2 0.1 shard_map.70
  26.4 2.5 %collective-permute-start.12 = (f32[5,8,128]{2,1,0:T(8,128)S(1)}, f32[5,8,128]{2,1,0:T(8,128)S(1)}, u32[]{:S(2)}, u32[]{:S(2)}) collective-permute-start(f32[5,8,128]{2,1,0:T(8,128)S(1)} %get-tuple-element.65), channel_id=1, source_target_pairs={{0,28},{4,8},{8,4},{12,16},{16,12},{20,24},{24,20},{28,0},{1,29},{... | collective-permute-start | bytes 61448 | tf_op jit(solution)/shard_map/ppermute | solution.py:684
  28.9 0.0 collective-permute-start.13
  28.9 0.0 collective-permute-start.14
  28.9 1.6 %collective-permute-start.15 = (f32[5,8,128]{2,1,0:T(8,128)S(1)}, f32[5,8,128]{2,1,0:T(8,128)S(1)}, u32[]{:S(2)}, u32[]{:S(2)}) collective-permute-start(f32[5,8,128]{2,1,0:T(8,128)S(1)} %get-tuple-element.68), channel_id=1, source_target_pairs={{0,1},{1,0},{2,3},{3,2},{4,5},{5,4},{6,7},{7,6},{8,9},{9,8},{10,11... | collective-permute-start | bytes 61448 | tf_op jit(solution)/shard_map/ppermute | solution.py:687
  30.5 0.2 shard_map.71.c_ref
  30.8 2.1 %collective-permute-done.12.rxo = f32[5,8,128]{2,1,0:T(8,128)S(1)} collective-permute-done((f32[5,8,128]{2,1,0:T(8,128)S(1)}, f32[5,8,128]{2,1,0:T(8,128)S(1)}, u32[]{:S(2)}, u32[]{:S(2)}) %collective-permute-start.12) | collective-permute-done | bytes 20512 | tf_op jit(solution)/shard_map/ppermute | solution.py:684
  32.9 0.0 collective-permute-done.13.rxe
  32.9 0.0 collective-permute-done.14.ryo
  32.9 0.0 collective-permute-done.15.rye
  32.9 1.0 %shard_map.72 = f32[5,4,4,2,8,128]{5,4,3,2,1,0:T(8,128)} custom-call(f32[5,2,2,8,128]{4,3,2,1,0:T(8,128)S(1)} %shard_map.71.c_ref, bf16[25,2,16,128]{3,2,1,0:T(8,128)(2,1)S(1)} %bitcast.11, s32[3,8,128]{2,1,0:T(8,128)S(1)} %get-tuple-element.40.flag_ref, f32[4,25,8,128]{3,2,1,0:T(8,128)S(1)} %get-tuple-element.45.face_ref, ...), custom_call_target="tpu_custom_call" | custom-call | flops 1048576 | bytes 4194304 | tf_op jit(solution)/shard_map/pallas_call | solution.py:662
Async XLA Ops:
  0.0 9.4 %copy-start.2 = (f32[2,2,128]{2,1,0:T(2,128)S(1)}, f32[2,2,128]{2,1,0:T(2,128)}, u32[]{:S(2)}) copy-start(f32[2,2,128]{2,1,0:T(2,128)} %param.8) | copy-start | bytes 6148
  0.0 9.4 %copy-start.1 = (f32[3,5,5,2,2,128]{5,4,3,2,1,0:T(2,128)S(1)}, f32[3,5,5,2,2,128]{5,4,3,2,1,0:T(2,128)}, u32[]{:S(2)}) copy-start(f32[3,5,5,2,2,128]{5,4,3,2,1,0:T(2,128)} %param.7) | copy-start | bytes 460804
  1.7 10.4 %collective-permute-start = (f32[5,4,8,128]{3,2,1,0:T(8,128)S(1)}, f32[5,4,8,128]{3,2,1,0:T(8,128)S(1)}, u32[]{:S(2)}, u32[]{:S(2)}) collective-permute-start(f32[5,4,8,128]{3,2,1,0:T(8,128)S(1)} %get-tuple-element.46), channel_id=1, source_target_pairs={{0,28},{4,8},{8,4},{12,16},{16,12},{20,24},{24,20},{28,0},{1,29},{... | collective-permute-start | bytes 245768 | tf_op jit(solution)/shard_map/ppermute | solution.py:684
  7.7 4.4 %collective-permute-start.1 = (f32[5,4,8,128]{3,2,1,0:T(8,128)S(1)}, f32[5,4,8,128]{3,2,1,0:T(8,128)S(1)}, u32[]{:S(2)}, u32[]{:S(2)}) collective-permute-start(f32[5,4,8,128]{3,2,1,0:T(8,128)S(1)} %get-tuple-element.47), channel_id=1, source_target_pairs={{0,4},{4,0},{8,12},{12,8},{16,20},{20,16},{24,28},{28,24},{1,5},{5... | collective-permute-start | bytes 245768 | tf_op jit(solution)/shard_map/ppermute | solution.py:685
  7.7 4.7 %collective-permute-start.2 = (f32[5,4,8,128]{3,2,1,0:T(8,128)S(1)}, f32[5,4,8,128]{3,2,1,0:T(8,128)S(1)}, u32[]{:S(2)}, u32[]{:S(2)}) collective-permute-start(f32[5,4,8,128]{3,2,1,0:T(8,128)S(1)} %get-tuple-element.48), channel_id=1, source_target_pairs={{0,3},{1,2},{2,1},{3,0},{4,7},{5,6},{6,5},{7,4},{8,11},{9,10},{10,... | collective-permute-start | bytes 245768 | tf_op jit(solution)/shard_map/ppermute | solution.py:686
  8.4 4.0 %collective-permute-start.3 = (f32[5,4,8,128]{3,2,1,0:T(8,128)S(1)}, f32[5,4,8,128]{3,2,1,0:T(8,128)S(1)}, u32[]{:S(2)}, u32[]{:S(2)}) collective-permute-start(f32[5,4,8,128]{3,2,1,0:T(8,128)S(1)} %get-tuple-element.49), channel_id=1, source_target_pairs={{0,1},{1,0},{2,3},{3,2},{4,5},{5,4},{6,7},{7,6},{8,9},{9,8},{10,11... | collective-permute-start | bytes 245768 | tf_op jit(solution)/shard_map/ppermute | solution.py:687
  13.0 6.6 %copy-start = (bf16[5,5,2,2,2,2,2,128]{7,6,5,4,3,2,1,0:T(2,128)(2,1)S(1)}, bf16[5,5,2,2,2,2,2,128]{7,6,5,4,3,2,1,0:T(2,128)(2,1)}, u32[]{:S(2)}) copy-start(bf16[5,5,2,2,2,2,2,128]{7,6,5,4,3,2,1,0:T(2,128)(2,1)} %param.11) | copy-start | bytes 614404
  13.0 6.5 %collective-permute-start.4 = (f32[5,8,128]{2,1,0:T(8,128)S(1)}, f32[5,8,128]{2,1,0:T(8,128)S(1)}, u32[]{:S(2)}, u32[]{:S(2)}) collective-permute-start(f32[5,8,128]{2,1,0:T(8,128)S(1)} %get-tuple-element.54), channel_id=1, source_target_pairs={{0,28},{4,8},{8,4},{12,16},{16,12},{20,24},{24,20},{28,0},{1,29},{... | collective-permute-start | bytes 61448 | tf_op jit(solution)/shard_map/ppermute | solution.py:684
  15.5 4.0 %collective-permute-start.5 = (f32[5,8,128]{2,1,0:T(8,128)S(1)}, f32[5,8,128]{2,1,0:T(8,128)S(1)}, u32[]{:S(2)}, u32[]{:S(2)}) collective-permute-start(f32[5,8,128]{2,1,0:T(8,128)S(1)} %get-tuple-element.55), channel_id=1, source_target_pairs={{0,4},{4,0},{8,12},{12,8},{16,20},{20,16},{24,28},{28,24},{1,5},{5... | collective-permute-start | bytes 61448 | tf_op jit(solution)/shard_map/ppermute | solution.py:685
  15.5 4.0 %collective-permute-start.6 = (f32[5,8,128]{2,1,0:T(8,128)S(1)}, f32[5,8,128]{2,1,0:T(8,128)S(1)}, u32[]{:S(2)}, u32[]{:S(2)}) collective-permute-start(f32[5,8,128]{2,1,0:T(8,128)S(1)} %get-tuple-element.56), channel_id=1, source_target_pairs={{0,3},{1,2},{2,1},{3,0},{4,7},{5,6},{6,5},{7,4},{8,11},{9,10},{10,... | collective-permute-start | bytes 61448 | tf_op jit(solution)/shard_map/ppermute | solution.py:686
  15.5 4.0 %collective-permute-start.7 = (f32[5,8,128]{2,1,0:T(8,128)S(1)}, f32[5,8,128]{2,1,0:T(8,128)S(1)}, u32[]{:S(2)}, u32[]{:S(2)}) collective-permute-start(f32[5,8,128]{2,1,0:T(8,128)S(1)} %get-tuple-element.57), channel_id=1, source_target_pairs={{0,1},{1,0},{2,3},{3,2},{4,5},{5,4},{6,7},{7,6},{8,9},{9,8},{10,11... | collective-permute-start | bytes 61448 | tf_op jit(solution)/shard_map/ppermute | solution.py:687
  19.7 6.5 %collective-permute-start.8 = (f32[5,8,128]{2,1,0:T(8,128)S(1)}, f32[5,8,128]{2,1,0:T(8,128)S(1)}, u32[]{:S(2)}, u32[]{:S(2)}) collective-permute-start(f32[5,8,128]{2,1,0:T(8,128)S(1)} %get-tuple-element.60), channel_id=1, source_target_pairs={{0,28},{4,8},{8,4},{12,16},{16,12},{20,24},{24,20},{28,0},{1,29},{... | collective-permute-start | bytes 61448 | tf_op jit(solution)/shard_map/ppermute | solution.py:684
  22.2 4.0 %collective-permute-start.9 = (f32[5,8,128]{2,1,0:T(8,128)S(1)}, f32[5,8,128]{2,1,0:T(8,128)S(1)}, u32[]{:S(2)}, u32[]{:S(2)}) collective-permute-start(f32[5,8,128]{2,1,0:T(8,128)S(1)} %get-tuple-element.61), channel_id=1, source_target_pairs={{0,4},{4,0},{8,12},{12,8},{16,20},{20,16},{24,28},{28,24},{1,5},{5... | collective-permute-start | bytes 61448 | tf_op jit(solution)/shard_map/ppermute | solution.py:685
  22.2 4.0 %collective-permute-start.10 = (f32[5,8,128]{2,1,0:T(8,128)S(1)}, f32[5,8,128]{2,1,0:T(8,128)S(1)}, u32[]{:S(2)}, u32[]{:S(2)}) collective-permute-start(f32[5,8,128]{2,1,0:T(8,128)S(1)} %get-tuple-element.62), channel_id=1, source_target_pairs={{0,3},{1,2},{2,1},{3,0},{4,7},{5,6},{6,5},{7,4},{8,11},{9,10},{10,... | collective-permute-start | bytes 61448 | tf_op jit(solution)/shard_map/ppermute | solution.py:686
  22.2 4.0 %collective-permute-start.11 = (f32[5,8,128]{2,1,0:T(8,128)S(1)}, f32[5,8,128]{2,1,0:T(8,128)S(1)}, u32[]{:S(2)}, u32[]{:S(2)}) collective-permute-start(f32[5,8,128]{2,1,0:T(8,128)S(1)} %get-tuple-element.63), channel_id=1, source_target_pairs={{0,1},{1,0},{2,3},{3,2},{4,5},{5,4},{6,7},{7,6},{8,9},{9,8},{10,11... | collective-permute-start | bytes 61448 | tf_op jit(solution)/shard_map/ppermute | solution.py:687
  26.4 6.5 %collective-permute-start.12 = (f32[5,8,128]{2,1,0:T(8,128)S(1)}, f32[5,8,128]{2,1,0:T(8,128)S(1)}, u32[]{:S(2)}, u32[]{:S(2)}) collective-permute-start(f32[5,8,128]{2,1,0:T(8,128)S(1)} %get-tuple-element.65), channel_id=1, source_target_pairs={{0,28},{4,8},{8,4},{12,16},{16,12},{20,24},{24,20},{28,0},{1,29},{... | collective-permute-start | bytes 61448 | tf_op jit(solution)/shard_map/ppermute | solution.py:684
  28.9 4.0 %collective-permute-start.13 = (f32[5,8,128]{2,1,0:T(8,128)S(1)}, f32[5,8,128]{2,1,0:T(8,128)S(1)}, u32[]{:S(2)}, u32[]{:S(2)}) collective-permute-start(f32[5,8,128]{2,1,0:T(8,128)S(1)} %get-tuple-element.66), channel_id=1, source_target_pairs={{0,4},{4,0},{8,12},{12,8},{16,20},{20,16},{24,28},{28,24},{1,5},{5... | collective-permute-start | bytes 61448 | tf_op jit(solution)/shard_map/ppermute | solution.py:685
  28.9 4.0 %collective-permute-start.14 = (f32[5,8,128]{2,1,0:T(8,128)S(1)}, f32[5,8,128]{2,1,0:T(8,128)S(1)}, u32[]{:S(2)}, u32[]{:S(2)}) collective-permute-start(f32[5,8,128]{2,1,0:T(8,128)S(1)} %get-tuple-element.67), channel_id=1, source_target_pairs={{0,3},{1,2},{2,1},{3,0},{4,7},{5,6},{6,5},{7,4},{8,11},{9,10},{10,... | collective-permute-start | bytes 61448 | tf_op jit(solution)/shard_map/ppermute | solution.py:686
  28.9 4.0 %collective-permute-start.15 = (f32[5,8,128]{2,1,0:T(8,128)S(1)}, f32[5,8,128]{2,1,0:T(8,128)S(1)}, u32[]{:S(2)}, u32[]{:S(2)}) collective-permute-start(f32[5,8,128]{2,1,0:T(8,128)S(1)} %get-tuple-element.68), channel_id=1, source_target_pairs={{0,1},{1,0},{2,3},{3,2},{4,5},{5,4},{6,7},{7,6},{8,9},{9,8},{10,11... | collective-permute-start | bytes 61448 | tf_op jit(solution)/shard_map/ppermute | solution.py:687

commit v8 on v5

--- a/solution.py
+++ b/solution.py
@@ -160,38 +160,46 @@
         put_coarse_faces(v, lows, highs, flag_ref, ((xe, xo), (ye, yo)))
 
 
+def smoothed(smooth_ref, fields, a, b):
+    out = []
+    for o in range(5):
+        total = [None, None]
+        for i in range(5):
+            block = smooth_ref[5 * o + i, a, b].astype(F32)
+            for q in range(2):
+                term = block[8 * q : 8 * q + 8] * fields[i][q]
+                total[q] = term if i == 0 else total[q] + term
+        out.append([OMEGA * total[q] for q in range(2)])
+    return out
+
+
 def first_kernel(
-    src_hbm, smooth_hbm, orient_hbm, src_ref, smooth_ref, u_ref, flag_ref, xo, xe, yo, ye, sems, orient_ref, orient_sem
+    src_hbm, smooth_hbm, orient_hbm, src_ref, smooth_ref, u_ref, flag_ref, xo, xe, yo, ye,
+    src_sems, smooth_sems, orient_ref, orient_sem,
 ):
     orient_copy = pltpu.make_async_copy(orient_hbm, orient_ref, orient_sem)
-    orient_copy.start()
-    copies = []
-    for slot, a in enumerate((0, 3, 1, 2)):
-        pair = (
-            pltpu.make_async_copy(src_hbm.at[:, a], src_ref.at[:, a], sems.at[0, slot]),
-            pltpu.make_async_copy(smooth_hbm.at[:, a], smooth_ref.at[:, a], sems.at[1, slot]),
-        )
-        for one in pair:
-            one.start()
-        copies.append((a, pair))
-    orient_copy.wait()
-    for d in range(3):
-        flag_ref[d] = twice(orient_ref[d])
-    for a, pair in copies:
-        for one in pair:
+    src_copies = [pltpu.make_async_copy(src_hbm.at[v], src_ref.at[v], src_sems.at[v]) for v in range(5)]
+    smooth_copies = [pltpu.make_async_copy(smooth_hbm.at[k], smooth_ref.at[k], smooth_sems.at[k]) for k in range(25)]
+    for one in (*src_copies, *smooth_copies, orient_copy):
+        one.start()
+    for one in src_copies:
+        one.wait()
+    for o in range(5):
+        for one in smooth_copies[5 * o : 5 * o + 5]:
             one.wait()
-
-        for b in range(4):
-            src = [[src_ref[v, a, b, q] for q in range(2)] for v in range(5)]
-            for o in range(5):
+        for a in range(4):
+            for b in range(4):
                 total = [None, None]
                 for i in range(5):
                     block = smooth_ref[5 * o + i, a, b].astype(F32)
                     for q in range(2):
-                        term = block[8 * q : 8 * q + 8] * src[i][q]
+                        term = block[8 * q : 8 * q + 8] * src_ref[i, a, b, q]
                         total[q] = term if i == 0 else total[q] + term
                 for q in range(2):
                     u_ref[o, a, b, q] = OMEGA * total[q]
+    orient_copy.wait()
+    for d in range(3):
+        flag_ref[d] = twice(orient_ref[d])
     fine_faces(u_ref, flag_ref, xo, xe, yo, ye)
 
 
@@ -245,7 +253,7 @@
             for n in range(4):
                 flux = mix(matrix, [waves[v][n] for v in range(5)])
                 for v in range(5):
-                    if direction == 0:
+                    if direction == 1:
                         total = src_ref[at(v, n, other, q)] - 2.0 * u[v][n]
                     else:
                         total = acc_ref[at(v, n, other, q)]
@@ -255,10 +263,7 @@
                     acc_ref[at(v, n, other, q)] = total
             return carry
 
-        lax.fori_loop(0, 8, step_fn, 0)
-
-    along(0)
-    along(1)
+        return step_fn
 
     low = c_low()
     flag = jnp.where(low, lroll(flag_ref[2], 1), flag_ref[2]) != 0
@@ -301,12 +306,22 @@
                     acc_ref[v, here[s], b, p] = acc_ref[v, here[s], b, p] - flux[v] + part
         return carry
 
+    lax.fori_loop(0, 8, along(1), 0)
     lax.fori_loop(0, 8, step_z, 0)
-
-
-def first_volume_kernel(src_ref, u_ref, flag_ref, jac_ref, damp_ref, acc_ref, jac8_ref, damp8_ref, face_ref):
+    lax.fori_loop(0, 8, along(0), 0)
+
+
+def first_volume_kernel(
+    src_ref, smooth_ref, u_ref, flag_ref, jac_ref, damp_ref, acc_ref, jac8_ref, damp8_ref, face_ref, second_ref
+):
     prepare_tables(jac_ref, damp_ref, jac8_ref, damp8_ref, face_ref)
     volume(src_ref, u_ref, flag_ref, jac8_ref, damp8_ref, acc_ref)
+    for a in (1, 2):
+        for b in (1, 2):
+            change = smoothed(smooth_ref, [[acc_ref[v, a, b, q] for q in range(2)] for v in range(5)], a, b)
+            for v in range(5):
+                for q in range(2):
+                    second_ref[v, a, b, q] = u_ref[v, a, b, q] + change[v][q]
 
 
 def remote_parts(even_refs, odd_refs, flag_ref, face_ref, part_ref):
@@ -345,21 +360,18 @@
 
 
 def second_kernel(
-    acc_ref, u_ref, smooth_ref, flag_ref, face_ref, rxo, rxe, ryo, rye, out_ref, xo, xe, yo, ye, part_ref
+    acc_ref, u_ref, smooth_ref, flag_ref, face_ref, rxo, rxe, ryo, rye, inner_ref, out_ref, xo, xe, yo, ye, part_ref
 ):
     remote_parts((rxe, rye), (rxo, ryo), flag_ref, face_ref, part_ref)
     for a in range(4):
         for b in range(4):
+            if a in (1, 2) and b in (1, 2):
+                continue
             left = [[whole(acc_ref, part_ref, v, a, b, q) for q in range(2)] for v in range(5)]
-            for o in range(5):
-                total = [None, None]
-                for i in range(5):
-                    block = smooth_ref[5 * o + i, a, b].astype(F32)
-                    for q in range(2):
-                        term = block[8 * q : 8 * q + 8] * left[i][q]
-                        total[q] = term if i == 0 else total[q] + term
+            change = smoothed(smooth_ref, left, a, b)
+            for v in range(5):
                 for q in range(2):
-                    out_ref[o, a, b, q] = u_ref[o, a, b, q] + OMEGA * total[q]
+                    out_ref[v, a, b, q] = u_ref[v, a, b, q] + change[v][q]
     restricted_faces(out_ref, flag_ref, xo, xe, yo, ye)
 
 
@@ -616,7 +628,7 @@
     return pltpu.with_memory_space_constraint(array, pltpu.VMEM)
 
 
-def call(kernel, args, outs, in_hbm=(), out_hbm=(), scratch=(), flops=0):
+def call(kernel, args, outs, in_hbm=(), out_hbm=(), scratch=(), aliases=None, flops=0):
     in_specs = [
         pl.BlockSpec(memory_space=pltpu.HBM if k in in_hbm else pltpu.VMEM) for k in range(len(args))
     ]
@@ -630,6 +642,7 @@
         in_specs=in_specs,
         out_specs=out_specs,
         scratch_shapes=scratch,
+        input_output_aliases=aliases or {},
         compiler_params=pltpu.CompilerParams(vmem_limit_bytes=8 * 2**20),
         cost_estimate=pl.CostEstimate(flops=flops, bytes_accessed=4 * 2**20, transcendentals=0),
     )(*args)
@@ -672,20 +685,26 @@
         (source, smoother, orient),
         [vmem(FINE), vmem(smoother.shape, smoother.dtype), vmem(FINE), vmem((3, 8, 128), jnp.int32)] + fine_messages,
         in_hbm=(0, 1, 2),
-        scratch=[pltpu.SemaphoreType.DMA((2, 4)), pltpu.VMEM((3, 4, 128), jnp.int32), pltpu.SemaphoreType.DMA],
+        scratch=[
+            pltpu.SemaphoreType.DMA((5,)),
+            pltpu.SemaphoreType.DMA((25,)),
+            pltpu.VMEM((3, 4, 128), jnp.int32),
+            pltpu.SemaphoreType.DMA,
+        ],
         flops=2 * 25 * 64 * 512,
     )
     got = exchange(*sent)
-    acc, jac8, damp8, face = call(
+    acc, jac8, damp8, face, second = call(
         first_volume_kernel,
-        (source, first, flag, jacobian, damping),
-        [vmem(FINE), vmem((75, 8, 128)), vmem((8, 128)), vmem((4, 25, 8, 128))],
+        (source, smoother, first, flag, jacobian, damping),
+        [vmem(FINE), vmem((75, 8, 128)), vmem((8, 128)), vmem((4, 25, 8, 128)), vmem(FINE)],
         flops=9 * 2**20,
     )
     second, *sent = call(
         second_kernel,
-        (acc, first, smoother, flag, face, *got),
+        (acc, first, smoother, flag, face, *got, second),
         [vmem(FINE)] + coarse_messages,
+        aliases={9: 0},
         scratch=[pltpu.VMEM((4, 5, 4, 2, 8, 128), F32)],
         flops=3 * 2**20,
     )

time: 34.3 us -> 34.7 us (1.012)
  Pallas kernels: 7.09 us -> 7.59 us
    pallas_call x9, Pallas kernels: 7.09 us -> 7.59 us  [call(): pl.pallas_call(kernel, out_shape=outs, in_specs=in_specs, out_specs=out_s...]
where the time goes in v8:
time: 34.7 us; the launch traced here: 34.6 us
  starting transfers between devices  20.2 us (58%)
  Pallas kernels  7.59 us (22%)
  waiting for transfers between devices  6.69 us (19%)
    ppermute x4, starting transfers between devices, exchange(): xo = lax.ppermute(xo, 'gx', odd_x)  13.7 us
    pallas_call x9, Pallas kernels, call(): pl.pallas_call(kernel, out_shape=outs, in_specs=in_specs, out_specs=out_s...  7.59 us
    ppermute x4, waiting for transfers between devices, exchange(): xo = lax.ppermute(xo, 'gx', odd_x)  5.98 us
    ppermute x4, starting transfers between devices, exchange(): ye = lax.ppermute(ye, 'gy', even_y)  5.85 us
  transfers between devices with their start and end apart: 16, of which 5 were waited for; matrix products, arithmetic and copies ran while one was open for 0% of the time, Pallas kernels for 10%

profile of v8, /device:TPU:0, one launch (start us, length us, event | category | flops | bytes accessed | tf_op | source)
XLA Modules:
  0.0 34.6 jit_solution(7573640158116558747)
XLA Ops:
  0.0 0.0 copy-start.2
  0.0 0.0 copy-start.1
  0.0 2.4 %shard_map.64 = (f32[5,4,4,2,8,128]{5,4,3,2,1,0:T(8,128)S(1)}, bf16[25,4,4,16,128]{4,3,2,1,0:T(8,128)(2,1)S(1)}, f32[5,4,4,2,8,128]{5,4,3,2,1,0:T(8,128)S(1)}, s...) custom-call(f32[5,4,4,2,8,128]{5,4,3,2,1,0:T(8,128)} %bitcast.15, ...), custom_call_target="tpu_custom_call" | custom-call | flops 1638400 | bytes 4194304 | tf_op jit(solution)/shard_map/pallas_call | solution.py:639
  2.4 6.0 %collective-permute-start = (f32[5,4,8,128]{3,2,1,0:T(8,128)S(1)}, f32[5,4,8,128]{3,2,1,0:T(8,128)S(1)}, u32[]{:S(2)}, u32[]{:S(2)}) collective-permute-start(f32[5,4,8,128]{3,2,1,0:T(8,128)S(1)} %get-tuple-element.40), channel_id=1, source_target_pairs={{0,28},{4,8},{8,4},{12,16},{16,12},{20,24},{24,20},{28,0},{1,29},{... | collective-permute-start | bytes 245768 | tf_op jit(solution)/shard_map/ppermute | solution.py:661
  8.4 0.0 collective-permute-start.1
  8.4 0.7 %collective-permute-start.2 = (f32[5,4,8,128]{3,2,1,0:T(8,128)S(1)}, f32[5,4,8,128]{3,2,1,0:T(8,128)S(1)}, u32[]{:S(2)}, u32[]{:S(2)}) collective-permute-start(f32[5,4,8,128]{3,2,1,0:T(8,128)S(1)} %get-tuple-element.42), channel_id=1, source_target_pairs={{0,3},{1,2},{2,1},{3,0},{4,7},{5,6},{6,5},{7,4},{8,11},{9,10},{10,... | collective-permute-start | bytes 245768 | tf_op jit(solution)/shard_map/ppermute | solution.py:663
  9.1 1.0 %collective-permute-start.3 = (f32[5,4,8,128]{3,2,1,0:T(8,128)S(1)}, f32[5,4,8,128]{3,2,1,0:T(8,128)S(1)}, u32[]{:S(2)}, u32[]{:S(2)}) collective-permute-start(f32[5,4,8,128]{3,2,1,0:T(8,128)S(1)} %get-tuple-element.43), channel_id=1, source_target_pairs={{0,1},{1,0},{2,3},{3,2},{4,5},{5,4},{6,7},{7,6},{8,9},{9,8},{10,11... | collective-permute-start | bytes 245768 | tf_op jit(solution)/shard_map/ppermute | solution.py:664
  10.1 0.0 copy-done.2
  10.1 0.0 copy-done.1
  10.1 2.3 %shard_map.65 = (f32[5,4,4,2,8,128]{5,4,3,2,1,0:T(8,128)S(1)}, f32[75,8,128]{2,1,0:T(8,128)S(1)}, f32[8,128]{1,0:T(8,128)S(1)}, f32[4,25,8,128]{3,2,1,0:T(8,128)S(1)}, f32[5,4,4,2,8,128]{5,4,3,2,1,0:T(8,128)S(1)}) custom-call(f32[5,4,4,2,8,128]{5,4,3,2,1,0:T(8,128)S(1)} %get-tuple-element.34.src_ref, ...), custom_call_target="tpu_custom_call" | custom-call | flops 9437184 | bytes 4194304 | tf_op jit(solution)/shard_map/pallas_call | solution.py:639
  12.4 0.0 collective-permute-done.rxo
  12.4 0.5 %collective-permute-done.1.rxe = f32[5,4,8,128]{3,2,1,0:T(8,128)S(1)} collective-permute-done((f32[5,4,8,128]{3,2,1,0:T(8,128)S(1)}, f32[5,4,8,128]{3,2,1,0:T(8,128)S(1)}, u32[]{:S(2)}, u32[]{:S(2)}) %collective-permute-start.1) | collective-permute-done | bytes 81952 | tf_op jit(solution)/shard_map/ppermute | solution.py:662
  12.9 0.2 collective-permute-done.2.ryo
  13.1 0.0 collective-permute-done.3.rye
  13.1 0.6 %shard_map.66 = (f32[5,4,4,2,8,128]{5,4,3,2,1,0:T(8,128)S(1)}, f32[5,8,128]{2,1,0:T(8,128)S(1)}, f32[5,8,128]{2,1,0:T(8,128)S(1)}, f32[5,8,128]{2,1,0:T(8,128)S(1)}, f32[5,8,128]{2,1,0:T(8,128)S(1)}) custom-call(f32[5,4,4,2,8,128]{5,4,3,2,1,0:T(8,128)S(1)} %get-tuple-element.38.acc_ref, ...), custom_call_target="tpu_custom_call", output_to_operand_aliasing={{0}: (9, {})} | custom-call | flops 3145728 | bytes 4194304 | tf_op jit(solution)/shard_map/pallas_call | solution.py:639
  13.7 0.0 copy-start
  13.7 2.5 %collective-permute-start.4 = (f32[5,8,128]{2,1,0:T(8,128)S(1)}, f32[5,8,128]{2,1,0:T(8,128)S(1)}, u32[]{:S(2)}, u32[]{:S(2)}) collective-permute-start(f32[5,8,128]{2,1,0:T(8,128)S(1)} %get-tuple-element.48), channel_id=1, source_target_pairs={{0,28},{4,8},{8,4},{12,16},{16,12},{20,24},{24,20},{28,0},{1,29},{... | collective-permute-start | bytes 61448 | tf_op jit(solution)/shard_map/ppermute | solution.py:661
  16.2 0.0 collective-permute-start.5
  16.2 0.0 collective-permute-start.6
  16.2 1.6 %collective-permute-start.7 = (f32[5,8,128]{2,1,0:T(8,128)S(1)}, f32[5,8,128]{2,1,0:T(8,128)S(1)}, u32[]{:S(2)}, u32[]{:S(2)}) collective-permute-start(f32[5,8,128]{2,1,0:T(8,128)S(1)} %get-tuple-element.51), channel_id=1, source_target_pairs={{0,1},{1,0},{2,3},{3,2},{4,5},{5,4},{6,7},{7,6},{8,9},{9,8},{10,11... | collective-permute-start | bytes 61448 | tf_op jit(solution)/shard_map/ppermute | solution.py:664
  17.9 0.6 %shard_map.67.acc_ref = f32[5,2,2,8,128]{4,3,2,1,0:T(8,128)S(1)} custom-call(f32[5,4,4,2,8,128]{5,4,3,2,1,0:T(8,128)S(1)} %get-tuple-element.34.src_ref, f32[5,4,4,2,8,128]{5,4,3,2,1,0:T(8,128)S(1)} %get-tuple-element.45.u_ref.second_ref, s32[3,8,128]{2,1,0:T(8,128)S(1)} %get-tuple-element.37.flag_ref, f32[75,8,128]{2,1,0:T(8,128)S(1)} %get-tuple-element.46.jac_ref, ...), custom_call_target="tpu_custom_call" | custom-call | flops 4194304 | bytes 4194304 | tf_op jit(solution)/shard_map/pallas_call | solution.py:639
  18.5 1.7 %collective-permute-done.4.rxo = f32[5,8,128]{2,1,0:T(8,128)S(1)} collective-permute-done((f32[5,8,128]{2,1,0:T(8,128)S(1)}, f32[5,8,128]{2,1,0:T(8,128)S(1)}, u32[]{:S(2)}, u32[]{:S(2)}) %collective-permute-start.4) | collective-permute-done | bytes 20512 | tf_op jit(solution)/shard_map/ppermute | solution.py:661
  20.2 0.0 collective-permute-done.5.rxe
  20.2 0.0 collective-permute-done.6.ryo
  20.2 0.0 collective-permute-done.7.rye
  20.3 0.0 copy-done
  20.3 0.1 shard_map.68
  20.4 2.5 %collective-permute-start.8 = (f32[5,8,128]{2,1,0:T(8,128)S(1)}, f32[5,8,128]{2,1,0:T(8,128)S(1)}, u32[]{:S(2)}, u32[]{:S(2)}) collective-permute-start(f32[5,8,128]{2,1,0:T(8,128)S(1)} %get-tuple-element.54), channel_id=1, source_target_pairs={{0,28},{4,8},{8,4},{12,16},{16,12},{20,24},{24,20},{28,0},{1,29},{... | collective-permute-start | bytes 61448 | tf_op jit(solution)/shard_map/ppermute | solution.py:661
  22.9 0.0 collective-permute-start.9
  22.9 0.0 collective-permute-start.10
  22.9 1.6 %collective-permute-start.11 = (f32[5,8,128]{2,1,0:T(8,128)S(1)}, f32[5,8,128]{2,1,0:T(8,128)S(1)}, u32[]{:S(2)}, u32[]{:S(2)}) collective-permute-start(f32[5,8,128]{2,1,0:T(8,128)S(1)} %get-tuple-element.57), channel_id=1, source_target_pairs={{0,1},{1,0},{2,3},{3,2},{4,5},{5,4},{6,7},{7,6},{8,9},{9,8},{10,11... | collective-permute-start | bytes 61448 | tf_op jit(solution)/shard_map/ppermute | solution.py:664
  24.6 0.2 shard_map.69.c_ref
  24.8 2.1 %collective-permute-done.8.rxo = f32[5,8,128]{2,1,0:T(8,128)S(1)} collective-permute-done((f32[5,8,128]{2,1,0:T(8,128)S(1)}, f32[5,8,128]{2,1,0:T(8,128)S(1)}, u32[]{:S(2)}, u32[]{:S(2)}) %collective-permute-start.8) | collective-permute-done | bytes 20512 | tf_op jit(solution)/shard_map/ppermute | solution.py:661
  26.9 0.0 collective-permute-done.9.rxe
  26.9 0.0 collective-permute-done.10.ryo
  26.9 0.0 collective-permute-done.11.rye
  27.0 0.1 shard_map.70
  27.1 2.5 %collective-permute-start.12 = (f32[5,8,128]{2,1,0:T(8,128)S(1)}, f32[5,8,128]{2,1,0:T(8,128)S(1)}, u32[]{:S(2)}, u32[]{:S(2)}) collective-permute-start(f32[5,8,128]{2,1,0:T(8,128)S(1)} %get-tuple-element.59), channel_id=1, source_target_pairs={{0,28},{4,8},{8,4},{12,16},{16,12},{20,24},{24,20},{28,0},{1,29},{... | collective-permute-start | bytes 61448 | tf_op jit(solution)/shard_map/ppermute | solution.py:661
  29.6 0.0 collective-permute-start.13
  29.6 0.0 collective-permute-start.14
  29.6 1.6 %collective-permute-start.15 = (f32[5,8,128]{2,1,0:T(8,128)S(1)}, f32[5,8,128]{2,1,0:T(8,128)S(1)}, u32[]{:S(2)}, u32[]{:S(2)}) collective-permute-start(f32[5,8,128]{2,1,0:T(8,128)S(1)} %get-tuple-element.62), channel_id=1, source_target_pairs={{0,1},{1,0},{2,3},{3,2},{4,5},{5,4},{6,7},{7,6},{8,9},{9,8},{10,11... | collective-permute-start | bytes 61448 | tf_op jit(solution)/shard_map/ppermute | solution.py:664
  31.3 0.2 shard_map.71.c_ref
  31.5 2.1 %collective-permute-done.12.rxo = f32[5,8,128]{2,1,0:T(8,128)S(1)} collective-permute-done((f32[5,8,128]{2,1,0:T(8,128)S(1)}, f32[5,8,128]{2,1,0:T(8,128)S(1)}, u32[]{:S(2)}, u32[]{:S(2)}) %collective-permute-start.12) | collective-permute-done | bytes 20512 | tf_op jit(solution)/shard_map/ppermute | solution.py:661
  33.6 0.0 collective-permute-done.13.rxe
  33.6 0.0 collective-permute-done.14.ryo
  33.6 0.0 collective-permute-done.15.rye
  33.6 1.0 %shard_map.72 = f32[5,4,4,2,8,128]{5,4,3,2,1,0:T(8,128)} custom-call(f32[5,2,2,8,128]{4,3,2,1,0:T(8,128)S(1)} %shard_map.71.c_ref, bf16[25,2,16,128]{3,2,1,0:T(8,128)(2,1)S(1)} %bitcast.11, s32[3,8,128]{2,1,0:T(8,128)S(1)} %get-tuple-element.37.flag_ref, f32[4,25,8,128]{3,2,1,0:T(8,128)S(1)} %get-tuple-element.39.face_ref, ...), custom_call_target="tpu_custom_call" | custom-call | flops 1048576 | bytes 4194304 | tf_op jit(solution)/shard_map/pallas_call | solution.py:639
Async XLA Ops:
  0.0 10.1 %copy-start.2 = (f32[2,2,128]{2,1,0:T(2,128)S(1)}, f32[2,2,128]{2,1,0:T(2,128)}, u32[]{:S(2)}) copy-start(f32[2,2,128]{2,1,0:T(2,128)} %param.8) | copy-start | bytes 6148
  0.0 10.1 %copy-start.1 = (f32[3,5,5,2,2,128]{5,4,3,2,1,0:T(2,128)S(1)}, f32[3,5,5,2,2,128]{5,4,3,2,1,0:T(2,128)}, u32[]{:S(2)}) copy-start(f32[3,5,5,2,2,128]{5,4,3,2,1,0:T(2,128)} %param.7) | copy-start | bytes 460804
  2.4 10.0 %collective-permute-start = (f32[5,4,8,128]{3,2,1,0:T(8,128)S(1)}, f32[5,4,8,128]{3,2,1,0:T(8,128)S(1)}, u32[]{:S(2)}, u32[]{:S(2)}) collective-permute-start(f32[5,4,8,128]{3,2,1,0:T(8,128)S(1)} %get-tuple-element.40), channel_id=1, source_target_pairs={{0,28},{4,8},{8,4},{12,16},{16,12},{20,24},{24,20},{28,0},{1,29},{... | collective-permute-start | bytes 245768 | tf_op jit(solution)/shard_map/ppermute | solution.py:661
  8.4 4.4 %collective-permute-start.1 = (f32[5,4,8,128]{3,2,1,0:T(8,128)S(1)}, f32[5,4,8,128]{3,2,1,0:T(8,128)S(1)}, u32[]{:S(2)}, u32[]{:S(2)}) collective-permute-start(f32[5,4,8,128]{3,2,1,0:T(8,128)S(1)} %get-tuple-element.41), channel_id=1, source_target_pairs={{0,4},{4,0},{8,12},{12,8},{16,20},{20,16},{24,28},{28,24},{1,5},{5... | collective-permute-start | bytes 245768 | tf_op jit(solution)/shard_map/ppermute | solution.py:662
  8.4 4.7 %collective-permute-start.2 = (f32[5,4,8,128]{3,2,1,0:T(8,128)S(1)}, f32[5,4,8,128]{3,2,1,0:T(8,128)S(1)}, u32[]{:S(2)}, u32[]{:S(2)}) collective-permute-start(f32[5,4,8,128]{3,2,1,0:T(8,128)S(1)} %get-tuple-element.42), channel_id=1, source_target_pairs={{0,3},{1,2},{2,1},{3,0},{4,7},{5,6},{6,5},{7,4},{8,11},{9,10},{10,... | collective-permute-start | bytes 245768 | tf_op jit(solution)/shard_map/ppermute | solution.py:663
  9.1 4.0 %collective-permute-start.3 = (f32[5,4,8,128]{3,2,1,0:T(8,128)S(1)}, f32[5,4,8,128]{3,2,1,0:T(8,128)S(1)}, u32[]{:S(2)}, u32[]{:S(2)}) collective-permute-start(f32[5,4,8,128]{3,2,1,0:T(8,128)S(1)} %get-tuple-element.43), channel_id=1, source_target_pairs={{0,1},{1,0},{2,3},{3,2},{4,5},{5,4},{6,7},{7,6},{8,9},{9,8},{10,11... | collective-permute-start | bytes 245768 | tf_op jit(solution)/shard_map/ppermute | solution.py:664
  13.7 6.6 %copy-start = (bf16[5,5,2,2,2,2,2,128]{7,6,5,4,3,2,1,0:T(2,128)(2,1)S(1)}, bf16[5,5,2,2,2,2,2,128]{7,6,5,4,3,2,1,0:T(2,128)(2,1)}, u32[]{:S(2)}) copy-start(bf16[5,5,2,2,2,2,2,128]{7,6,5,4,3,2,1,0:T(2,128)(2,1)} %param.11) | copy-start | bytes 614404
  13.7 6.5 %collective-permute-start.4 = (f32[5,8,128]{2,1,0:T(8,128)S(1)}, f32[5,8,128]{2,1,0:T(8,128)S(1)}, u32[]{:S(2)}, u32[]{:S(2)}) collective-permute-start(f32[5,8,128]{2,1,0:T(8,128)S(1)} %get-tuple-element.48), channel_id=1, source_target_pairs={{0,28},{4,8},{8,4},{12,16},{16,12},{20,24},{24,20},{28,0},{1,29},{... | collective-permute-start | bytes 61448 | tf_op jit(solution)/shard_map/ppermute | solution.py:661
  16.2 4.0 %collective-permute-start.5 = (f32[5,8,128]{2,1,0:T(8,128)S(1)}, f32[5,8,128]{2,1,0:T(8,128)S(1)}, u32[]{:S(2)}, u32[]{:S(2)}) collective-permute-start(f32[5,8,128]{2,1,0:T(8,128)S(1)} %get-tuple-element.49), channel_id=1, source_target_pairs={{0,4},{4,0},{8,12},{12,8},{16,20},{20,16},{24,28},{28,24},{1,5},{5... | collective-permute-start | bytes 61448 | tf_op jit(solution)/shard_map/ppermute | solution.py:662
  16.2 4.0 %collective-permute-start.6 = (f32[5,8,128]{2,1,0:T(8,128)S(1)}, f32[5,8,128]{2,1,0:T(8,128)S(1)}, u32[]{:S(2)}, u32[]{:S(2)}) collective-permute-start(f32[5,8,128]{2,1,0:T(8,128)S(1)} %get-tuple-element.50), channel_id=1, source_target_pairs={{0,3},{1,2},{2,1},{3,0},{4,7},{5,6},{6,5},{7,4},{8,11},{9,10},{10,... | collective-permute-start | bytes 61448 | tf_op jit(solution)/shard_map/ppermute | solution.py:663
  16.2 4.0 %collective-permute-start.7 = (f32[5,8,128]{2,1,0:T(8,128)S(1)}, f32[5,8,128]{2,1,0:T(8,128)S(1)}, u32[]{:S(2)}, u32[]{:S(2)}) collective-permute-start(f32[5,8,128]{2,1,0:T(8,128)S(1)} %get-tuple-element.51), channel_id=1, source_target_pairs={{0,1},{1,0},{2,3},{3,2},{4,5},{5,4},{6,7},{7,6},{8,9},{9,8},{10,11... | collective-permute-start | bytes 61448 | tf_op jit(solution)/shard_map/ppermute | solution.py:664
  20.4 6.5 %collective-permute-start.8 = (f32[5,8,128]{2,1,0:T(8,128)S(1)}, f32[5,8,128]{2,1,0:T(8,128)S(1)}, u32[]{:S(2)}, u32[]{:S(2)}) collective-permute-start(f32[5,8,128]{2,1,0:T(8,128)S(1)} %get-tuple-element.54), channel_id=1, source_target_pairs={{0,28},{4,8},{8,4},{12,16},{16,12},{20,24},{24,20},{28,0},{1,29},{... | collective-permute-start | bytes 61448 | tf_op jit(solution)/shard_map/ppermute | solution.py:661
  22.9 4.0 %collective-permute-start.9 = (f32[5,8,128]{2,1,0:T(8,128)S(1)}, f32[5,8,128]{2,1,0:T(8,128)S(1)}, u32[]{:S(2)}, u32[]{:S(2)}) collective-permute-start(f32[5,8,128]{2,1,0:T(8,128)S(1)} %get-tuple-element.55), channel_id=1, source_target_pairs={{0,4},{4,0},{8,12},{12,8},{16,20},{20,16},{24,28},{28,24},{1,5},{5... | collective-permute-start | bytes 61448 | tf_op jit(solution)/shard_map/ppermute | solution.py:662
  22.9 4.0 %collective-permute-start.10 = (f32[5,8,128]{2,1,0:T(8,128)S(1)}, f32[5,8,128]{2,1,0:T(8,128)S(1)}, u32[]{:S(2)}, u32[]{:S(2)}) collective-permute-start(f32[5,8,128]{2,1,0:T(8,128)S(1)} %get-tuple-element.56), channel_id=1, source_target_pairs={{0,3},{1,2},{2,1},{3,0},{4,7},{5,6},{6,5},{7,4},{8,11},{9,10},{10,... | collective-permute-start | bytes 61448 | tf_op jit(solution)/shard_map/ppermute | solution.py:663
  22.9 4.0 %collective-permute-start.11 = (f32[5,8,128]{2,1,0:T(8,128)S(1)}, f32[5,8,128]{2,1,0:T(8,128)S(1)}, u32[]{:S(2)}, u32[]{:S(2)}) collective-permute-start(f32[5,8,128]{2,1,0:T(8,128)S(1)} %get-tuple-element.57), channel_id=1, source_target_pairs={{0,1},{1,0},{2,3},{3,2},{4,5},{5,4},{6,7},{7,6},{8,9},{9,8},{10,11... | collective-permute-start | bytes 61448 | tf_op jit(solution)/shard_map/ppermute | solution.py:664
  27.1 6.5 %collective-permute-start.12 = (f32[5,8,128]{2,1,0:T(8,128)S(1)}, f32[5,8,128]{2,1,0:T(8,128)S(1)}, u32[]{:S(2)}, u32[]{:S(2)}) collective-permute-start(f32[5,8,128]{2,1,0:T(8,128)S(1)} %get-tuple-element.59), channel_id=1, source_target_pairs={{0,28},{4,8},{8,4},{12,16},{16,12},{20,24},{24,20},{28,0},{1,29},{... | collective-permute-start | bytes 61448 | tf_op jit(solution)/shard_map/ppermute | solution.py:661
  29.6 4.0 %collective-permute-start.13 = (f32[5,8,128]{2,1,0:T(8,128)S(1)}, f32[5,8,128]{2,1,0:T(8,128)S(1)}, u32[]{:S(2)}, u32[]{:S(2)}) collective-permute-start(f32[5,8,128]{2,1,0:T(8,128)S(1)} %get-tuple-element.60), channel_id=1, source_target_pairs={{0,4},{4,0},{8,12},{12,8},{16,20},{20,16},{24,28},{28,24},{1,5},{5... | collective-permute-start | bytes 61448 | tf_op jit(solution)/shard_map/ppermute | solution.py:662
  29.6 4.0 %collective-permute-start.14 = (f32[5,8,128]{2,1,0:T(8,128)S(1)}, f32[5,8,128]{2,1,0:T(8,128)S(1)}, u32[]{:S(2)}, u32[]{:S(2)}) collective-permute-start(f32[5,8,128]{2,1,0:T(8,128)S(1)} %get-tuple-element.61), channel_id=1, source_target_pairs={{0,3},{1,2},{2,1},{3,0},{4,7},{5,6},{6,5},{7,4},{8,11},{9,10},{10,... | collective-permute-start | bytes 61448 | tf_op jit(solution)/shard_map/ppermute | solution.py:663
  29.6 4.0 %collective-permute-start.15 = (f32[5,8,128]{2,1,0:T(8,128)S(1)}, f32[5,8,128]{2,1,0:T(8,128)S(1)}, u32[]{:S(2)}, u32[]{:S(2)}) collective-permute-start(f32[5,8,128]{2,1,0:T(8,128)S(1)} %get-tuple-element.62), channel_id=1, source_target_pairs={{0,1},{1,0},{2,3},{3,2},{4,5},{5,4},{6,7},{7,6},{8,9},{9,8},{10,11... | collective-permute-start | bytes 61448 | tf_op jit(solution)/shard_map/ppermute | solution.py:664

commit v9 on v7

--- a/solution.py
+++ b/solution.py
@@ -180,32 +180,31 @@
             u_ref[v, a, b, q] = value[v][q]
 
 
-def line_copies(src_hbm, smooth_hbm, src_ref, smooth_ref, sems, slot, a, b):
-    return (
-        pltpu.make_async_copy(src_hbm.at[:, a, b], src_ref.at[:, a, b], sems.at[0, slot]),
-        pltpu.make_async_copy(smooth_hbm.at[:, a, b], smooth_ref.at[:, a, b], sems.at[1, slot]),
-    )
+def line_copy(smooth_hbm, smooth_ref, sem, a, b):
+    return pltpu.make_async_copy(smooth_hbm.at[:, a, b], smooth_ref.at[:, a, b], sem)
 
 
 def first_kernel(
     src_hbm, smooth_hbm, orient_hbm, src_ref, smooth_ref, u_ref, flag_ref, xo, xe, yo, ye, sems, orient_ref, orient_sem
 ):
     every, inner = slice(0, 4), slice(1, 3)
+    src_copy = pltpu.make_async_copy(src_hbm, src_ref, sems.at[4])
+    src_copy.start()
+    copies = [
+        line_copy(smooth_hbm, smooth_ref, sems.at[slot], a, b)
+        for slot, (a, b) in enumerate(((0, every), (3, every), (inner, 0), (inner, 3)))
+    ]
+    for one in copies:
+        one.start()
     orient_copy = pltpu.make_async_copy(orient_hbm, orient_ref, orient_sem)
     orient_copy.start()
-    copies = []
-    for slot, (a, b) in enumerate(((0, every), (3, every), (inner, 0), (inner, 3))):
-        pair = line_copies(src_hbm, smooth_hbm, src_ref, smooth_ref, sems, slot, a, b)
-        for one in pair:
-            one.start()
-        copies.append(pair)
     orient_copy.wait()
     for d in range(3):
         flag_ref[d] = twice(orient_ref[d])
     lines = [[(0, b) for b in range(4)], [(3, b) for b in range(4)], [(1, 0), (2, 0)], [(1, 3), (2, 3)]]
-    for pair, group in zip(copies, lines):
-        for one in pair:
-            one.wait()
+    src_copy.wait()
+    for one, group in zip(copies, lines):
+        one.wait()
         for a, b in group:
             first_line(src_ref, smooth_ref, u_ref, a, b)
     fine_faces(u_ref, flag_ref, xo, xe, yo, ye)
@@ -323,19 +322,17 @@
 
 
 def first_volume_kernel(
-    src_hbm, smooth_hbm, src_in, smooth_in, u_in, flag_ref, jac_ref, damp_ref,
-    src_ref, smooth_ref, u_ref, acc_ref, jac8_ref, damp8_ref, face_ref, second_ref, sems,
+    smooth_hbm, src_ref, smooth_in, u_in, flag_ref, jac_ref, damp_ref,
+    smooth_ref, u_ref, acc_ref, jac8_ref, damp8_ref, face_ref, second_ref, sem,
 ):
     inner = slice(1, 3)
-    copies = line_copies(src_hbm, smooth_hbm, src_ref, smooth_ref, sems, 0, inner, inner)
-    for one in copies:
-        one.start()
+    copy = line_copy(smooth_hbm, smooth_ref, sem, inner, inner)
+    copy.start()
     prepare_tables(jac_ref, damp_ref, jac8_ref, damp8_ref, face_ref)
     lines = [(a, b) for a in (1, 2) for b in (1, 2)]
 
     def finish_lines():
-        for one in copies:
-            one.wait()
+        copy.wait()
         for a, b in lines:
             first_line(src_ref, smooth_ref, u_ref, a, b)
 
@@ -704,23 +701,23 @@
     coarse_messages = [vmem(COARSE_MESSAGE)] * 4
 
     held = vmem(smoother.shape, smoother.dtype)
-    source_in, smoother_in = source, smoother
+    smoother_in = smoother
     source, smoother, first, flag, *sent = call(
         first_kernel,
-        (source_in, smoother_in, orient),
+        (source, smoother_in, orient),
         [vmem(FINE), held, vmem(FINE), vmem((3, 8, 128), jnp.int32)] + fine_messages,
         in_hbm=(0, 1, 2),
-        scratch=[pltpu.SemaphoreType.DMA((2, 4)), pltpu.VMEM((3, 4, 128), jnp.int32), pltpu.SemaphoreType.DMA],
+        scratch=[pltpu.SemaphoreType.DMA((5,)), pltpu.VMEM((3, 4, 128), jnp.int32), pltpu.SemaphoreType.DMA],
         flops=2 * 25 * 64 * 512,
     )
     got = exchange(*sent)
-    source, smoother, first, acc, jac8, damp8, face, second = call(
+    smoother, first, acc, jac8, damp8, face, second = call(
         first_volume_kernel,
-        (source_in, smoother_in, source, smoother, first, flag, jacobian, damping),
-        [vmem(FINE), held, vmem(FINE), vmem(FINE), vmem((75, 8, 128)), vmem((8, 128)), vmem((4, 25, 8, 128)), vmem(FINE)],
-        in_hbm=(0, 1),
-        aliases={2: 0, 3: 1, 4: 2},
-        scratch=[pltpu.SemaphoreType.DMA((2, 1))],
+        (smoother_in, source, smoother, first, flag, jacobian, damping),
+        [held, vmem(FINE), vmem(FINE), vmem((75, 8, 128)), vmem((8, 128)), vmem((4, 25, 8, 128)), vmem(FINE)],
+        in_hbm=(0,),
+        aliases={2: 0, 3: 1},
+        scratch=[pltpu.SemaphoreType.DMA],
         flops=9 * 2**20,
     )
     second, *sent = call(

time: 34 us -> 34.1 us (level)
  no operation moved by 1% of the time
where the time goes in v9:
time: 34.1 us; the launch traced here: 33.9 us
  starting transfers between devices  20.2 us (59%)
  Pallas kernels  7.1 us (21%)
  waiting for transfers between devices  6.47 us (19%)
    ppermute x4, starting transfers between devices, exchange(): xo = lax.ppermute(xo, 'gx', odd_x)  13.7 us
    pallas_call x9, Pallas kernels, call(): pl.pallas_call(kernel, out_shape=outs, in_specs=in_specs, out_specs=out_s...  7.1 us
    ppermute x4, waiting for transfers between devices, exchange(): xo = lax.ppermute(xo, 'gx', odd_x)  5.98 us
    ppermute x4, starting transfers between devices, exchange(): ye = lax.ppermute(ye, 'gy', even_y)  5.85 us
    ppermute x4, starting transfers between devices, exchange(): yo = lax.ppermute(yo, 'gy', odd_y)  0.69 us
  transfers between devices with their start and end apart: 16, of which 5 were waited for; matrix products, arithmetic and copies ran while one was open for 0% of the time, Pallas kernels for 11%

profile of v9, /device:TPU:0, one launch (start us, length us, event | category | flops | bytes accessed | tf_op | source)
XLA Modules:
  0.0 33.9 jit_solution(13546477975042120885)
XLA Ops:
  0.0 0.0 copy-start.2
  0.0 0.0 copy-start.1
  0.0 1.7 %shard_map.64 = (f32[5,4,4,2,8,128]{5,4,3,2,1,0:T(8,128)S(1)}, bf16[25,4,4,16,128]{4,3,2,1,0:T(8,128)(2,1)S(1)}, f32[5,4,4,2,8,128]{5,4,3,2,1,0:T(8,128)S(1)}, s...) custom-call(f32[5,4,4,2,8,128]{5,4,3,2,1,0:T(8,128)} %bitcast.16, ...), custom_call_target="tpu_custom_call" | custom-call | flops 1638400 | bytes 4194304 | tf_op jit(solution)/shard_map/pallas_call | solution.py:659
  1.7 6.0 %collective-permute-start = (f32[5,4,8,128]{3,2,1,0:T(8,128)S(1)}, f32[5,4,8,128]{3,2,1,0:T(8,128)S(1)}, u32[]{:S(2)}, u32[]{:S(2)}) collective-permute-start(f32[5,4,8,128]{3,2,1,0:T(8,128)S(1)} %get-tuple-element.44), channel_id=1, source_target_pairs={{0,28},{4,8},{8,4},{12,16},{16,12},{20,24},{24,20},{28,0},{1,29},{... | collective-permute-start | bytes 245768 | tf_op jit(solution)/shard_map/ppermute | solution.py:681
  7.7 0.0 collective-permute-start.1
  7.7 0.7 %collective-permute-start.2 = (f32[5,4,8,128]{3,2,1,0:T(8,128)S(1)}, f32[5,4,8,128]{3,2,1,0:T(8,128)S(1)}, u32[]{:S(2)}, u32[]{:S(2)}) collective-permute-start(f32[5,4,8,128]{3,2,1,0:T(8,128)S(1)} %get-tuple-element.46), channel_id=1, source_target_pairs={{0,3},{1,2},{2,1},{3,0},{4,7},{5,6},{6,5},{7,4},{8,11},{9,10},{10,... | collective-permute-start | bytes 245768 | tf_op jit(solution)/shard_map/ppermute | solution.py:683
  8.4 1.0 %collective-permute-start.3 = (f32[5,4,8,128]{3,2,1,0:T(8,128)S(1)}, f32[5,4,8,128]{3,2,1,0:T(8,128)S(1)}, u32[]{:S(2)}, u32[]{:S(2)}) collective-permute-start(f32[5,4,8,128]{3,2,1,0:T(8,128)S(1)} %get-tuple-element.47), channel_id=1, source_target_pairs={{0,1},{1,0},{2,3},{3,2},{4,5},{5,4},{6,7},{7,6},{8,9},{9,8},{10,11... | collective-permute-start | bytes 245768 | tf_op jit(solution)/shard_map/ppermute | solution.py:684
  9.4 0.0 copy-done.2
  9.4 0.0 copy-done.1
  9.4 2.5 %shard_map.65 = (bf16[25,4,4,16,128]{4,3,2,1,0:T(8,128)(2,1)S(1)}, f32[5,4,4,2,8,128]{5,4,3,2,1,0:T(8,128)S(1)}, f32[5,4,4,2,8,128]{5,4,3,2,1,0:T(8,128)S(1)}, f...) custom-call(bf16[25,4,4,16,128]{4,3,2,1,0:T(8,128)(2,1)} %bitcast.15, ...), custom_call_target="tpu_custom_call", output_to_operand_aliasing={{0}: (2, {}), {1}: (3, {})} | custom-call | flops 9437184 | bytes 4194304 | tf_op jit(solution)/shard_map/pallas_call | solution.py:659
  11.9 0.0 collective-permute-done.rxo
  11.9 0.2 collective-permute-done.1.rxe
  12.2 0.2 collective-permute-done.2.ryo
  12.4 0.0 collective-permute-done.3.rye
  12.4 0.6 %shard_map.66 = (f32[5,4,4,2,8,128]{5,4,3,2,1,0:T(8,128)S(1)}, f32[5,8,128]{2,1,0:T(8,128)S(1)}, f32[5,8,128]{2,1,0:T(8,128)S(1)}, f32[5,8,128]{2,1,0:T(8,128)S(1)}, f32[5,8,128]{2,1,0:T(8,128)S(1)}) custom-call(f32[5,4,4,2,8,128]{5,4,3,2,1,0:T(8,128)S(1)} %get-tuple-element.40.acc_ref, ...), custom_call_target="tpu_custom_call", output_to_operand_aliasing={{0}: (9, {})} | custom-call | flops 3145728 | bytes 4194304 | tf_op jit(solution)/shard_map/pallas_call | solution.py:659
  13.0 0.0 copy-start
  13.0 2.5 %collective-permute-start.4 = (f32[5,8,128]{2,1,0:T(8,128)S(1)}, f32[5,8,128]{2,1,0:T(8,128)S(1)}, u32[]{:S(2)}, u32[]{:S(2)}) collective-permute-start(f32[5,8,128]{2,1,0:T(8,128)S(1)} %get-tuple-element.52), channel_id=1, source_target_pairs={{0,28},{4,8},{8,4},{12,16},{16,12},{20,24},{24,20},{28,0},{1,29},{... | collective-permute-start | bytes 61448 | tf_op jit(solution)/shard_map/ppermute | solution.py:681
  15.5 0.0 collective-permute-start.5
  15.5 0.0 collective-permute-start.6
  15.5 1.6 %collective-permute-start.7 = (f32[5,8,128]{2,1,0:T(8,128)S(1)}, f32[5,8,128]{2,1,0:T(8,128)S(1)}, u32[]{:S(2)}, u32[]{:S(2)}) collective-permute-start(f32[5,8,128]{2,1,0:T(8,128)S(1)} %get-tuple-element.55), channel_id=1, source_target_pairs={{0,1},{1,0},{2,3},{3,2},{4,5},{5,4},{6,7},{7,6},{8,9},{9,8},{10,11... | collective-permute-start | bytes 61448 | tf_op jit(solution)/shard_map/ppermute | solution.py:684
  17.2 0.6 %shard_map.67.acc_ref = f32[5,2,2,8,128]{4,3,2,1,0:T(8,128)S(1)} custom-call(f32[5,4,4,2,8,128]{5,4,3,2,1,0:T(8,128)S(1)} %get-tuple-element.36.src_ref, f32[5,4,4,2,8,128]{5,4,3,2,1,0:T(8,128)S(1)} %get-tuple-element.49.u_ref.second_ref, s32[3,8,128]{2,1,0:T(8,128)S(1)} %get-tuple-element.39.flag_ref, f32[75,8,128]{2,1,0:T(8,128)S(1)} %get-tuple-element.50.jac_ref, ...), custom_call_target="tpu_custom_call" | custom-call | flops 4194304 | bytes 4194304 | tf_op jit(solution)/shard_map/pallas_call | solution.py:659
  17.8 1.7 %collective-permute-done.4.rxo = f32[5,8,128]{2,1,0:T(8,128)S(1)} collective-permute-done((f32[5,8,128]{2,1,0:T(8,128)S(1)}, f32[5,8,128]{2,1,0:T(8,128)S(1)}, u32[]{:S(2)}, u32[]{:S(2)}) %collective-permute-start.4) | collective-permute-done | bytes 20512 | tf_op jit(solution)/shard_map/ppermute | solution.py:681
  19.5 0.0 collective-permute-done.5.rxe
  19.5 0.0 collective-permute-done.6.ryo
  19.5 0.0 collective-permute-done.7.rye
  19.5 0.0 copy-done
  19.6 0.1 shard_map.68
  19.7 2.5 %collective-permute-start.8 = (f32[5,8,128]{2,1,0:T(8,128)S(1)}, f32[5,8,128]{2,1,0:T(8,128)S(1)}, u32[]{:S(2)}, u32[]{:S(2)}) collective-permute-start(f32[5,8,128]{2,1,0:T(8,128)S(1)} %get-tuple-element.58), channel_id=1, source_target_pairs={{0,28},{4,8},{8,4},{12,16},{16,12},{20,24},{24,20},{28,0},{1,29},{... | collective-permute-start | bytes 61448 | tf_op jit(solution)/shard_map/ppermute | solution.py:681
  22.2 0.0 collective-permute-start.9
  22.2 0.0 collective-permute-start.10
  22.2 1.6 %collective-permute-start.11 = (f32[5,8,128]{2,1,0:T(8,128)S(1)}, f32[5,8,128]{2,1,0:T(8,128)S(1)}, u32[]{:S(2)}, u32[]{:S(2)}) collective-permute-start(f32[5,8,128]{2,1,0:T(8,128)S(1)} %get-tuple-element.61), channel_id=1, source_target_pairs={{0,1},{1,0},{2,3},{3,2},{4,5},{5,4},{6,7},{7,6},{8,9},{9,8},{10,11... | collective-permute-start | bytes 61448 | tf_op jit(solution)/shard_map/ppermute | solution.py:684
  23.9 0.2 shard_map.69.c_ref
  24.1 2.1 %collective-permute-done.8.rxo = f32[5,8,128]{2,1,0:T(8,128)S(1)} collective-permute-done((f32[5,8,128]{2,1,0:T(8,128)S(1)}, f32[5,8,128]{2,1,0:T(8,128)S(1)}, u32[]{:S(2)}, u32[]{:S(2)}) %collective-permute-start.8) | collective-permute-done | bytes 20512 | tf_op jit(solution)/shard_map/ppermute | solution.py:681
  26.2 0.0 collective-permute-done.9.rxe
  26.2 0.0 collective-permute-done.10.ryo
  26.2 0.0 collective-permute-done.11.rye
  26.2 0.1 shard_map.70
  26.4 2.5 %collective-permute-start.12 = (f32[5,8,128]{2,1,0:T(8,128)S(1)}, f32[5,8,128]{2,1,0:T(8,128)S(1)}, u32[]{:S(2)}, u32[]{:S(2)}) collective-permute-start(f32[5,8,128]{2,1,0:T(8,128)S(1)} %get-tuple-element.63), channel_id=1, source_target_pairs={{0,28},{4,8},{8,4},{12,16},{16,12},{20,24},{24,20},{28,0},{1,29},{... | collective-permute-start | bytes 61448 | tf_op jit(solution)/shard_map/ppermute | solution.py:681
  28.9 0.0 collective-permute-start.13
  28.9 0.0 collective-permute-start.14
  28.9 1.6 %collective-permute-start.15 = (f32[5,8,128]{2,1,0:T(8,128)S(1)}, f32[5,8,128]{2,1,0:T(8,128)S(1)}, u32[]{:S(2)}, u32[]{:S(2)}) collective-permute-start(f32[5,8,128]{2,1,0:T(8,128)S(1)} %get-tuple-element.66), channel_id=1, source_target_pairs={{0,1},{1,0},{2,3},{3,2},{4,5},{5,4},{6,7},{7,6},{8,9},{9,8},{10,11... | collective-permute-start | bytes 61448 | tf_op jit(solution)/shard_map/ppermute | solution.py:684
  30.5 0.2 shard_map.71.c_ref
  30.8 2.1 %collective-permute-done.12.rxo = f32[5,8,128]{2,1,0:T(8,128)S(1)} collective-permute-done((f32[5,8,128]{2,1,0:T(8,128)S(1)}, f32[5,8,128]{2,1,0:T(8,128)S(1)}, u32[]{:S(2)}, u32[]{:S(2)}) %collective-permute-start.12) | collective-permute-done | bytes 20512 | tf_op jit(solution)/shard_map/ppermute | solution.py:681
  32.9 0.0 collective-permute-done.13.rxe
  32.9 0.0 collective-permute-done.14.ryo
  32.9 0.0 collective-permute-done.15.rye
  32.9 1.0 %shard_map.72 = f32[5,4,4,2,8,128]{5,4,3,2,1,0:T(8,128)} custom-call(f32[5,2,2,8,128]{4,3,2,1,0:T(8,128)S(1)} %shard_map.71.c_ref, bf16[25,2,16,128]{3,2,1,0:T(8,128)(2,1)S(1)} %bitcast.11, s32[3,8,128]{2,1,0:T(8,128)S(1)} %get-tuple-element.39.flag_ref, f32[4,25,8,128]{3,2,1,0:T(8,128)S(1)} %get-tuple-element.43.face_ref, ...), custom_call_target="tpu_custom_call" | custom-call | flops 1048576 | bytes 4194304 | tf_op jit(solution)/shard_map/pallas_call | solution.py:659
Async XLA Ops:
  0.0 9.4 %copy-start.2 = (f32[2,2,128]{2,1,0:T(2,128)S(1)}, f32[2,2,128]{2,1,0:T(2,128)}, u32[]{:S(2)}) copy-start(f32[2,2,128]{2,1,0:T(2,128)} %param.8) | copy-start | bytes 6148
  0.0 9.4 %copy-start.1 = (f32[3,5,5,2,2,128]{5,4,3,2,1,0:T(2,128)S(1)}, f32[3,5,5,2,2,128]{5,4,3,2,1,0:T(2,128)}, u32[]{:S(2)}) copy-start(f32[3,5,5,2,2,128]{5,4,3,2,1,0:T(2,128)} %param.7) | copy-start | bytes 460804
  1.7 10.2 %collective-permute-start = (f32[5,4,8,128]{3,2,1,0:T(8,128)S(1)}, f32[5,4,8,128]{3,2,1,0:T(8,128)S(1)}, u32[]{:S(2)}, u32[]{:S(2)}) collective-permute-start(f32[5,4,8,128]{3,2,1,0:T(8,128)S(1)} %get-tuple-element.44), channel_id=1, source_target_pairs={{0,28},{4,8},{8,4},{12,16},{16,12},{20,24},{24,20},{28,0},{1,29},{... | collective-permute-start | bytes 245768 | tf_op jit(solution)/shard_map/ppermute | solution.py:681
  7.7 4.4 %collective-permute-start.1 = (f32[5,4,8,128]{3,2,1,0:T(8,128)S(1)}, f32[5,4,8,128]{3,2,1,0:T(8,128)S(1)}, u32[]{:S(2)}, u32[]{:S(2)}) collective-permute-start(f32[5,4,8,128]{3,2,1,0:T(8,128)S(1)} %get-tuple-element.45), channel_id=1, source_target_pairs={{0,4},{4,0},{8,12},{12,8},{16,20},{20,16},{24,28},{28,24},{1,5},{5... | collective-permute-start | bytes 245768 | tf_op jit(solution)/shard_map/ppermute | solution.py:682
  7.7 4.7 %collective-permute-start.2 = (f32[5,4,8,128]{3,2,1,0:T(8,128)S(1)}, f32[5,4,8,128]{3,2,1,0:T(8,128)S(1)}, u32[]{:S(2)}, u32[]{:S(2)}) collective-permute-start(f32[5,4,8,128]{3,2,1,0:T(8,128)S(1)} %get-tuple-element.46), channel_id=1, source_target_pairs={{0,3},{1,2},{2,1},{3,0},{4,7},{5,6},{6,5},{7,4},{8,11},{9,10},{10,... | collective-permute-start | bytes 245768 | tf_op jit(solution)/shard_map/ppermute | solution.py:683
  8.4 4.0 %collective-permute-start.3 = (f32[5,4,8,128]{3,2,1,0:T(8,128)S(1)}, f32[5,4,8,128]{3,2,1,0:T(8,128)S(1)}, u32[]{:S(2)}, u32[]{:S(2)}) collective-permute-start(f32[5,4,8,128]{3,2,1,0:T(8,128)S(1)} %get-tuple-element.47), channel_id=1, source_target_pairs={{0,1},{1,0},{2,3},{3,2},{4,5},{5,4},{6,7},{7,6},{8,9},{9,8},{10,11... | collective-permute-start | bytes 245768 | tf_op jit(solution)/shard_map/ppermute | solution.py:684
  13.0 6.6 %copy-start = (bf16[5,5,2,2,2,2,2,128]{7,6,5,4,3,2,1,0:T(2,128)(2,1)S(1)}, bf16[5,5,2,2,2,2,2,128]{7,6,5,4,3,2,1,0:T(2,128)(2,1)}, u32[]{:S(2)}) copy-start(bf16[5,5,2,2,2,2,2,128]{7,6,5,4,3,2,1,0:T(2,128)(2,1)} %param.11) | copy-start | bytes 614404
  13.0 6.5 %collective-permute-start.4 = (f32[5,8,128]{2,1,0:T(8,128)S(1)}, f32[5,8,128]{2,1,0:T(8,128)S(1)}, u32[]{:S(2)}, u32[]{:S(2)}) collective-permute-start(f32[5,8,128]{2,1,0:T(8,128)S(1)} %get-tuple-element.52), channel_id=1, source_target_pairs={{0,28},{4,8},{8,4},{12,16},{16,12},{20,24},{24,20},{28,0},{1,29},{... | collective-permute-start | bytes 61448 | tf_op jit(solution)/shard_map/ppermute | solution.py:681
  15.5 4.0 %collective-permute-start.5 = (f32[5,8,128]{2,1,0:T(8,128)S(1)}, f32[5,8,128]{2,1,0:T(8,128)S(1)}, u32[]{:S(2)}, u32[]{:S(2)}) collective-permute-start(f32[5,8,128]{2,1,0:T(8,128)S(1)} %get-tuple-element.53), channel_id=1, source_target_pairs={{0,4},{4,0},{8,12},{12,8},{16,20},{20,16},{24,28},{28,24},{1,5},{5... | collective-permute-start | bytes 61448 | tf_op jit(solution)/shard_map/ppermute | solution.py:682
  15.5 4.0 %collective-permute-start.6 = (f32[5,8,128]{2,1,0:T(8,128)S(1)}, f32[5,8,128]{2,1,0:T(8,128)S(1)}, u32[]{:S(2)}, u32[]{:S(2)}) collective-permute-start(f32[5,8,128]{2,1,0:T(8,128)S(1)} %get-tuple-element.54), channel_id=1, source_target_pairs={{0,3},{1,2},{2,1},{3,0},{4,7},{5,6},{6,5},{7,4},{8,11},{9,10},{10,... | collective-permute-start | bytes 61448 | tf_op jit(solution)/shard_map/ppermute | solution.py:683
  15.5 4.0 %collective-permute-start.7 = (f32[5,8,128]{2,1,0:T(8,128)S(1)}, f32[5,8,128]{2,1,0:T(8,128)S(1)}, u32[]{:S(2)}, u32[]{:S(2)}) collective-permute-start(f32[5,8,128]{2,1,0:T(8,128)S(1)} %get-tuple-element.55), channel_id=1, source_target_pairs={{0,1},{1,0},{2,3},{3,2},{4,5},{5,4},{6,7},{7,6},{8,9},{9,8},{10,11... | collective-permute-start | bytes 61448 | tf_op jit(solution)/shard_map/ppermute | solution.py:684
  19.7 6.5 %collective-permute-start.8 = (f32[5,8,128]{2,1,0:T(8,128)S(1)}, f32[5,8,128]{2,1,0:T(8,128)S(1)}, u32[]{:S(2)}, u32[]{:S(2)}) collective-permute-start(f32[5,8,128]{2,1,0:T(8,128)S(1)} %get-tuple-element.58), channel_id=1, source_target_pairs={{0,28},{4,8},{8,4},{12,16},{16,12},{20,24},{24,20},{28,0},{1,29},{... | collective-permute-start | bytes 61448 | tf_op jit(solution)/shard_map/ppermute | solution.py:681
  22.2 4.0 %collective-permute-start.9 = (f32[5,8,128]{2,1,0:T(8,128)S(1)}, f32[5,8,128]{2,1,0:T(8,128)S(1)}, u32[]{:S(2)}, u32[]{:S(2)}) collective-permute-start(f32[5,8,128]{2,1,0:T(8,128)S(1)} %get-tuple-element.59), channel_id=1, source_target_pairs={{0,4},{4,0},{8,12},{12,8},{16,20},{20,16},{24,28},{28,24},{1,5},{5... | collective-permute-start | bytes 61448 | tf_op jit(solution)/shard_map/ppermute | solution.py:682
  22.2 4.0 %collective-permute-start.10 = (f32[5,8,128]{2,1,0:T(8,128)S(1)}, f32[5,8,128]{2,1,0:T(8,128)S(1)}, u32[]{:S(2)}, u32[]{:S(2)}) collective-permute-start(f32[5,8,128]{2,1,0:T(8,128)S(1)} %get-tuple-element.60), channel_id=1, source_target_pairs={{0,3},{1,2},{2,1},{3,0},{4,7},{5,6},{6,5},{7,4},{8,11},{9,10},{10,... | collective-permute-start | bytes 61448 | tf_op jit(solution)/shard_map/ppermute | solution.py:683
  22.2 4.0 %collective-permute-start.11 = (f32[5,8,128]{2,1,0:T(8,128)S(1)}, f32[5,8,128]{2,1,0:T(8,128)S(1)}, u32[]{:S(2)}, u32[]{:S(2)}) collective-permute-start(f32[5,8,128]{2,1,0:T(8,128)S(1)} %get-tuple-element.61), channel_id=1, source_target_pairs={{0,1},{1,0},{2,3},{3,2},{4,5},{5,4},{6,7},{7,6},{8,9},{9,8},{10,11... | collective-permute-start | bytes 61448 | tf_op jit(solution)/shard_map/ppermute | solution.py:684
  26.4 6.5 %collective-permute-start.12 = (f32[5,8,128]{2,1,0:T(8,128)S(1)}, f32[5,8,128]{2,1,0:T(8,128)S(1)}, u32[]{:S(2)}, u32[]{:S(2)}) collective-permute-start(f32[5,8,128]{2,1,0:T(8,128)S(1)} %get-tuple-element.63), channel_id=1, source_target_pairs={{0,28},{4,8},{8,4},{12,16},{16,12},{20,24},{24,20},{28,0},{1,29},{... | collective-permute-start | bytes 61448 | tf_op jit(solution)/shard_map/ppermute | solution.py:681
  28.9 4.0 %collective-permute-start.13 = (f32[5,8,128]{2,1,0:T(8,128)S(1)}, f32[5,8,128]{2,1,0:T(8,128)S(1)}, u32[]{:S(2)}, u32[]{:S(2)}) collective-permute-start(f32[5,8,128]{2,1,0:T(8,128)S(1)} %get-tuple-element.64), channel_id=1, source_target_pairs={{0,4},{4,0},{8,12},{12,8},{16,20},{20,16},{24,28},{28,24},{1,5},{5... | collective-permute-start | bytes 61448 | tf_op jit(solution)/shard_map/ppermute | solution.py:682
  28.9 4.0 %collective-permute-start.14 = (f32[5,8,128]{2,1,0:T(8,128)S(1)}, f32[5,8,128]{2,1,0:T(8,128)S(1)}, u32[]{:S(2)}, u32[]{:S(2)}) collective-permute-start(f32[5,8,128]{2,1,0:T(8,128)S(1)} %get-tuple-element.65), channel_id=1, source_target_pairs={{0,3},{1,2},{2,1},{3,0},{4,7},{5,6},{6,5},{7,4},{8,11},{9,10},{10,... | collective-permute-start | bytes 61448 | tf_op jit(solution)/shard_map/ppermute | solution.py:683
  28.9 4.0 %collective-permute-start.15 = (f32[5,8,128]{2,1,0:T(8,128)S(1)}, f32[5,8,128]{2,1,0:T(8,128)S(1)}, u32[]{:S(2)}, u32[]{:S(2)}) collective-permute-start(f32[5,8,128]{2,1,0:T(8,128)S(1)} %get-tuple-element.66), channel_id=1, source_target_pairs={{0,1},{1,0},{2,3},{3,2},{4,5},{5,4},{6,7},{7,6},{8,9},{9,8},{10,11... | collective-permute-start | bytes 61448 | tf_op jit(solution)/shard_map/ppermute | solution.py:684

commit v10 on v9

--- a/solution.py
+++ b/solution.py
@@ -185,7 +185,7 @@
 
 
 def first_kernel(
-    src_hbm, smooth_hbm, orient_hbm, src_ref, smooth_ref, u_ref, flag_ref, xo, xe, yo, ye, sems, orient_ref, orient_sem
+    src_hbm, smooth_hbm, orient_hbm, src_ref, smooth_ref, u_ref, flag_ref, xo, yo, xe, ye, sems, orient_ref, orient_sem
 ):
     every, inner = slice(0, 4), slice(1, 3)
     src_copy = pltpu.make_async_copy(src_hbm, src_ref, sems.at[4])
@@ -702,7 +702,7 @@
 
     held = vmem(smoother.shape, smoother.dtype)
     smoother_in = smoother
-    source, smoother, first, flag, *sent = call(
+    source, smoother, first, flag, xo, yo, xe, ye = call(
         first_kernel,
         (source, smoother_in, orient),
         [vmem(FINE), held, vmem(FINE), vmem((3, 8, 128), jnp.int32)] + fine_messages,
@@ -710,7 +710,7 @@
         scratch=[pltpu.SemaphoreType.DMA((5,)), pltpu.VMEM((3, 4, 128), jnp.int32), pltpu.SemaphoreType.DMA],
         flops=2 * 25 * 64 * 512,
     )
-    got = exchange(*sent)
+    got = exchange(xo, xe, yo, ye)
     smoother, first, acc, jac8, damp8, face, second = call(
         first_volume_kernel,
         (smoother_in, source, smoother, first, flag, jacobian, damping),

time: 34.1 us -> 34.1 us (level)
  no operation moved by 1% of the time
where the time goes in v10:
time: 34.1 us; the launch traced here: 33.9 us
  starting transfers between devices  20.2 us (59%)
  Pallas kernels  7.1 us (21%)
  waiting for transfers between devices  6.47 us (19%)
    ppermute x4, starting transfers between devices, exchange(): xo = lax.ppermute(xo, 'gx', odd_x)  13.7 us
    pallas_call x9, Pallas kernels, call(): pl.pallas_call(kernel, out_shape=outs, in_specs=in_specs, out_specs=out_s...  7.1 us
    ppermute x4, waiting for transfers between devices, exchange(): xo = lax.ppermute(xo, 'gx', odd_x)  5.98 us
    ppermute x4, starting transfers between devices, exchange(): ye = lax.ppermute(ye, 'gy', even_y)  5.85 us
    ppermute x4, starting transfers between devices, exchange(): yo = lax.ppermute(yo, 'gy', odd_y)  0.69 us
  transfers between devices with their start and end apart: 16, of which 5 were waited for; matrix products, arithmetic and copies ran while one was open for 0% of the time, Pallas kernels for 11%

profile of v10, /device:TPU:0, one launch (start us, length us, event | category | flops | bytes accessed | tf_op | source)
XLA Modules:
  0.0 33.9 jit_solution(13753728670668802978)
XLA Ops:
  0.0 0.0 copy-start.2
  0.0 0.0 copy-start.1
  0.0 1.7 %shard_map.64 = (f32[5,4,4,2,8,128]{5,4,3,2,1,0:T(8,128)S(1)}, bf16[25,4,4,16,128]{4,3,2,1,0:T(8,128)(2,1)S(1)}, f32[5,4,4,2,8,128]{5,4,3,2,1,0:T(8,128)S(1)}, s...) custom-call(f32[5,4,4,2,8,128]{5,4,3,2,1,0:T(8,128)} %bitcast.16, ...), custom_call_target="tpu_custom_call" | custom-call | flops 1638400 | bytes 4194304 | tf_op jit(solution)/shard_map/pallas_call | solution.py:659
  1.7 6.0 %collective-permute-start = (f32[5,4,8,128]{3,2,1,0:T(8,128)S(1)}, f32[5,4,8,128]{3,2,1,0:T(8,128)S(1)}, u32[]{:S(2)}, u32[]{:S(2)}) collective-permute-start(f32[5,4,8,128]{3,2,1,0:T(8,128)S(1)} %get-tuple-element.44), channel_id=1, source_target_pairs={{0,28},{4,8},{8,4},{12,16},{16,12},{20,24},{24,20},{28,0},{1,29},{... | collective-permute-start | bytes 245768 | tf_op jit(solution)/shard_map/ppermute | solution.py:681
  7.7 0.0 collective-permute-start.1
  7.7 0.7 %collective-permute-start.2 = (f32[5,4,8,128]{3,2,1,0:T(8,128)S(1)}, f32[5,4,8,128]{3,2,1,0:T(8,128)S(1)}, u32[]{:S(2)}, u32[]{:S(2)}) collective-permute-start(f32[5,4,8,128]{3,2,1,0:T(8,128)S(1)} %get-tuple-element.46), channel_id=1, source_target_pairs={{0,3},{1,2},{2,1},{3,0},{4,7},{5,6},{6,5},{7,4},{8,11},{9,10},{10,... | collective-permute-start | bytes 245768 | tf_op jit(solution)/shard_map/ppermute | solution.py:683
  8.4 1.0 %collective-permute-start.3 = (f32[5,4,8,128]{3,2,1,0:T(8,128)S(1)}, f32[5,4,8,128]{3,2,1,0:T(8,128)S(1)}, u32[]{:S(2)}, u32[]{:S(2)}) collective-permute-start(f32[5,4,8,128]{3,2,1,0:T(8,128)S(1)} %get-tuple-element.47), channel_id=1, source_target_pairs={{0,1},{1,0},{2,3},{3,2},{4,5},{5,4},{6,7},{7,6},{8,9},{9,8},{10,11... | collective-permute-start | bytes 245768 | tf_op jit(solution)/shard_map/ppermute | solution.py:684
  9.4 0.0 copy-done.2
  9.4 0.0 copy-done.1
  9.4 2.5 %shard_map.65 = (bf16[25,4,4,16,128]{4,3,2,1,0:T(8,128)(2,1)S(1)}, f32[5,4,4,2,8,128]{5,4,3,2,1,0:T(8,128)S(1)}, f32[5,4,4,2,8,128]{5,4,3,2,1,0:T(8,128)S(1)}, f...) custom-call(bf16[25,4,4,16,128]{4,3,2,1,0:T(8,128)(2,1)} %bitcast.15, ...), custom_call_target="tpu_custom_call", output_to_operand_aliasing={{0}: (2, {}), {1}: (3, {})} | custom-call | flops 9437184 | bytes 4194304 | tf_op jit(solution)/shard_map/pallas_call | solution.py:659
  11.9 0.0 collective-permute-done.rxo
  11.9 0.2 collective-permute-done.1.rxe
  12.2 0.2 collective-permute-done.2.ryo
  12.4 0.0 collective-permute-done.3.rye
  12.4 0.6 %shard_map.66 = (f32[5,4,4,2,8,128]{5,4,3,2,1,0:T(8,128)S(1)}, f32[5,8,128]{2,1,0:T(8,128)S(1)}, f32[5,8,128]{2,1,0:T(8,128)S(1)}, f32[5,8,128]{2,1,0:T(8,128)S(1)}, f32[5,8,128]{2,1,0:T(8,128)S(1)}) custom-call(f32[5,4,4,2,8,128]{5,4,3,2,1,0:T(8,128)S(1)} %get-tuple-element.40.acc_ref, ...), custom_call_target="tpu_custom_call", output_to_operand_aliasing={{0}: (9, {})} | custom-call | flops 3145728 | bytes 4194304 | tf_op jit(solution)/shard_map/pallas_call | solution.py:659
  13.0 0.0 copy-start
  13.0 2.5 %collective-permute-start.4 = (f32[5,8,128]{2,1,0:T(8,128)S(1)}, f32[5,8,128]{2,1,0:T(8,128)S(1)}, u32[]{:S(2)}, u32[]{:S(2)}) collective-permute-start(f32[5,8,128]{2,1,0:T(8,128)S(1)} %get-tuple-element.52), channel_id=1, source_target_pairs={{0,28},{4,8},{8,4},{12,16},{16,12},{20,24},{24,20},{28,0},{1,29},{... | collective-permute-start | bytes 61448 | tf_op jit(solution)/shard_map/ppermute | solution.py:681
  15.5 0.0 collective-permute-start.5
  15.5 0.0 collective-permute-start.6
  15.5 1.6 %collective-permute-start.7 = (f32[5,8,128]{2,1,0:T(8,128)S(1)}, f32[5,8,128]{2,1,0:T(8,128)S(1)}, u32[]{:S(2)}, u32[]{:S(2)}) collective-permute-start(f32[5,8,128]{2,1,0:T(8,128)S(1)} %get-tuple-element.55), channel_id=1, source_target_pairs={{0,1},{1,0},{2,3},{3,2},{4,5},{5,4},{6,7},{7,6},{8,9},{9,8},{10,11... | collective-permute-start | bytes 61448 | tf_op jit(solution)/shard_map/ppermute | solution.py:684
  17.2 0.6 %shard_map.67.acc_ref = f32[5,2,2,8,128]{4,3,2,1,0:T(8,128)S(1)} custom-call(f32[5,4,4,2,8,128]{5,4,3,2,1,0:T(8,128)S(1)} %get-tuple-element.36.src_ref, f32[5,4,4,2,8,128]{5,4,3,2,1,0:T(8,128)S(1)} %get-tuple-element.49.u_ref.second_ref, s32[3,8,128]{2,1,0:T(8,128)S(1)} %get-tuple-element.39.flag_ref, f32[75,8,128]{2,1,0:T(8,128)S(1)} %get-tuple-element.50.jac_ref, ...), custom_call_target="tpu_custom_call" | custom-call | flops 4194304 | bytes 4194304 | tf_op jit(solution)/shard_map/pallas_call | solution.py:659
  17.8 1.7 %collective-permute-done.4.rxo = f32[5,8,128]{2,1,0:T(8,128)S(1)} collective-permute-done((f32[5,8,128]{2,1,0:T(8,128)S(1)}, f32[5,8,128]{2,1,0:T(8,128)S(1)}, u32[]{:S(2)}, u32[]{:S(2)}) %collective-permute-start.4) | collective-permute-done | bytes 20512 | tf_op jit(solution)/shard_map/ppermute | solution.py:681
  19.5 0.0 collective-permute-done.5.rxe
  19.5 0.0 collective-permute-done.6.ryo
  19.5 0.0 collective-permute-done.7.rye
  19.5 0.0 copy-done
  19.6 0.1 shard_map.68
  19.7 2.5 %collective-permute-start.8 = (f32[5,8,128]{2,1,0:T(8,128)S(1)}, f32[5,8,128]{2,1,0:T(8,128)S(1)}, u32[]{:S(2)}, u32[]{:S(2)}) collective-permute-start(f32[5,8,128]{2,1,0:T(8,128)S(1)} %get-tuple-element.58), channel_id=1, source_target_pairs={{0,28},{4,8},{8,4},{12,16},{16,12},{20,24},{24,20},{28,0},{1,29},{... | collective-permute-start | bytes 61448 | tf_op jit(solution)/shard_map/ppermute | solution.py:681
  22.2 0.0 collective-permute-start.9
  22.2 0.0 collective-permute-start.10
  22.2 1.6 %collective-permute-start.11 = (f32[5,8,128]{2,1,0:T(8,128)S(1)}, f32[5,8,128]{2,1,0:T(8,128)S(1)}, u32[]{:S(2)}, u32[]{:S(2)}) collective-permute-start(f32[5,8,128]{2,1,0:T(8,128)S(1)} %get-tuple-element.61), channel_id=1, source_target_pairs={{0,1},{1,0},{2,3},{3,2},{4,5},{5,4},{6,7},{7,6},{8,9},{9,8},{10,11... | collective-permute-start | bytes 61448 | tf_op jit(solution)/shard_map/ppermute | solution.py:684
  23.9 0.2 shard_map.69.c_ref
  24.1 2.1 %collective-permute-done.8.rxo = f32[5,8,128]{2,1,0:T(8,128)S(1)} collective-permute-done((f32[5,8,128]{2,1,0:T(8,128)S(1)}, f32[5,8,128]{2,1,0:T(8,128)S(1)}, u32[]{:S(2)}, u32[]{:S(2)}) %collective-permute-start.8) | collective-permute-done | bytes 20512 | tf_op jit(solution)/shard_map/ppermute | solution.py:681
  26.2 0.0 collective-permute-done.9.rxe
  26.2 0.0 collective-permute-done.10.ryo
  26.2 0.0 collective-permute-done.11.rye
  26.2 0.1 shard_map.70
  26.4 2.5 %collective-permute-start.12 = (f32[5,8,128]{2,1,0:T(8,128)S(1)}, f32[5,8,128]{2,1,0:T(8,128)S(1)}, u32[]{:S(2)}, u32[]{:S(2)}) collective-permute-start(f32[5,8,128]{2,1,0:T(8,128)S(1)} %get-tuple-element.63), channel_id=1, source_target_pairs={{0,28},{4,8},{8,4},{12,16},{16,12},{20,24},{24,20},{28,0},{1,29},{... | collective-permute-start | bytes 61448 | tf_op jit(solution)/shard_map/ppermute | solution.py:681
  28.9 0.0 collective-permute-start.13
  28.9 0.0 collective-permute-start.14
  28.9 1.6 %collective-permute-start.15 = (f32[5,8,128]{2,1,0:T(8,128)S(1)}, f32[5,8,128]{2,1,0:T(8,128)S(1)}, u32[]{:S(2)}, u32[]{:S(2)}) collective-permute-start(f32[5,8,128]{2,1,0:T(8,128)S(1)} %get-tuple-element.66), channel_id=1, source_target_pairs={{0,1},{1,0},{2,3},{3,2},{4,5},{5,4},{6,7},{7,6},{8,9},{9,8},{10,11... | collective-permute-start | bytes 61448 | tf_op jit(solution)/shard_map/ppermute | solution.py:684
  30.5 0.2 shard_map.71.c_ref
  30.8 2.1 %collective-permute-done.12.rxo = f32[5,8,128]{2,1,0:T(8,128)S(1)} collective-permute-done((f32[5,8,128]{2,1,0:T(8,128)S(1)}, f32[5,8,128]{2,1,0:T(8,128)S(1)}, u32[]{:S(2)}, u32[]{:S(2)}) %collective-permute-start.12) | collective-permute-done | bytes 20512 | tf_op jit(solution)/shard_map/ppermute | solution.py:681
  32.9 0.0 collective-permute-done.13.rxe
  32.9 0.0 collective-permute-done.14.ryo
  32.9 0.0 collective-permute-done.15.rye
  32.9 1.0 %shard_map.72 = f32[5,4,4,2,8,128]{5,4,3,2,1,0:T(8,128)} custom-call(f32[5,2,2,8,128]{4,3,2,1,0:T(8,128)S(1)} %shard_map.71.c_ref, bf16[25,2,16,128]{3,2,1,0:T(8,128)(2,1)S(1)} %bitcast.11, s32[3,8,128]{2,1,0:T(8,128)S(1)} %get-tuple-element.39.flag_ref, f32[4,25,8,128]{3,2,1,0:T(8,128)S(1)} %get-tuple-element.43.face_ref, ...), custom_call_target="tpu_custom_call" | custom-call | flops 1048576 | bytes 4194304 | tf_op jit(solution)/shard_map/pallas_call | solution.py:659
Async XLA Ops:
  0.0 9.4 %copy-start.2 = (f32[2,2,128]{2,1,0:T(2,128)S(1)}, f32[2,2,128]{2,1,0:T(2,128)}, u32[]{:S(2)}) copy-start(f32[2,2,128]{2,1,0:T(2,128)} %param.8) | copy-start | bytes 6148
  0.0 9.4 %copy-start.1 = (f32[3,5,5,2,2,128]{5,4,3,2,1,0:T(2,128)S(1)}, f32[3,5,5,2,2,128]{5,4,3,2,1,0:T(2,128)}, u32[]{:S(2)}) copy-start(f32[3,5,5,2,2,128]{5,4,3,2,1,0:T(2,128)} %param.7) | copy-start | bytes 460804
  1.7 10.2 %collective-permute-start = (f32[5,4,8,128]{3,2,1,0:T(8,128)S(1)}, f32[5,4,8,128]{3,2,1,0:T(8,128)S(1)}, u32[]{:S(2)}, u32[]{:S(2)}) collective-permute-start(f32[5,4,8,128]{3,2,1,0:T(8,128)S(1)} %get-tuple-element.44), channel_id=1, source_target_pairs={{0,28},{4,8},{8,4},{12,16},{16,12},{20,24},{24,20},{28,0},{1,29},{... | collective-permute-start | bytes 245768 | tf_op jit(solution)/shard_map/ppermute | solution.py:681
  7.7 4.4 %collective-permute-start.1 = (f32[5,4,8,128]{3,2,1,0:T(8,128)S(1)}, f32[5,4,8,128]{3,2,1,0:T(8,128)S(1)}, u32[]{:S(2)}, u32[]{:S(2)}) collective-permute-start(f32[5,4,8,128]{3,2,1,0:T(8,128)S(1)} %get-tuple-element.45), channel_id=1, source_target_pairs={{0,4},{4,0},{8,12},{12,8},{16,20},{20,16},{24,28},{28,24},{1,5},{5... | collective-permute-start | bytes 245768 | tf_op jit(solution)/shard_map/ppermute | solution.py:682
  7.7 4.7 %collective-permute-start.2 = (f32[5,4,8,128]{3,2,1,0:T(8,128)S(1)}, f32[5,4,8,128]{3,2,1,0:T(8,128)S(1)}, u32[]{:S(2)}, u32[]{:S(2)}) collective-permute-start(f32[5,4,8,128]{3,2,1,0:T(8,128)S(1)} %get-tuple-element.46), channel_id=1, source_target_pairs={{0,3},{1,2},{2,1},{3,0},{4,7},{5,6},{6,5},{7,4},{8,11},{9,10},{10,... | collective-permute-start | bytes 245768 | tf_op jit(solution)/shard_map/ppermute | solution.py:683
  8.4 4.0 %collective-permute-start.3 = (f32[5,4,8,128]{3,2,1,0:T(8,128)S(1)}, f32[5,4,8,128]{3,2,1,0:T(8,128)S(1)}, u32[]{:S(2)}, u32[]{:S(2)}) collective-permute-start(f32[5,4,8,128]{3,2,1,0:T(8,128)S(1)} %get-tuple-element.47), channel_id=1, source_target_pairs={{0,1},{1,0},{2,3},{3,2},{4,5},{5,4},{6,7},{7,6},{8,9},{9,8},{10,11... | collective-permute-start | bytes 245768 | tf_op jit(solution)/shard_map/ppermute | solution.py:684
  13.0 6.6 %copy-start = (bf16[5,5,2,2,2,2,2,128]{7,6,5,4,3,2,1,0:T(2,128)(2,1)S(1)}, bf16[5,5,2,2,2,2,2,128]{7,6,5,4,3,2,1,0:T(2,128)(2,1)}, u32[]{:S(2)}) copy-start(bf16[5,5,2,2,2,2,2,128]{7,6,5,4,3,2,1,0:T(2,128)(2,1)} %param.11) | copy-start | bytes 614404
  13.0 6.5 %collective-permute-start.4 = (f32[5,8,128]{2,1,0:T(8,128)S(1)}, f32[5,8,128]{2,1,0:T(8,128)S(1)}, u32[]{:S(2)}, u32[]{:S(2)}) collective-permute-start(f32[5,8,128]{2,1,0:T(8,128)S(1)} %get-tuple-element.52), channel_id=1, source_target_pairs={{0,28},{4,8},{8,4},{12,16},{16,12},{20,24},{24,20},{28,0},{1,29},{... | collective-permute-start | bytes 61448 | tf_op jit(solution)/shard_map/ppermute | solution.py:681
  15.5 4.0 %collective-permute-start.5 = (f32[5,8,128]{2,1,0:T(8,128)S(1)}, f32[5,8,128]{2,1,0:T(8,128)S(1)}, u32[]{:S(2)}, u32[]{:S(2)}) collective-permute-start(f32[5,8,128]{2,1,0:T(8,128)S(1)} %get-tuple-element.53), channel_id=1, source_target_pairs={{0,4},{4,0},{8,12},{12,8},{16,20},{20,16},{24,28},{28,24},{1,5},{5... | collective-permute-start | bytes 61448 | tf_op jit(solution)/shard_map/ppermute | solution.py:682
  15.5 4.0 %collective-permute-start.6 = (f32[5,8,128]{2,1,0:T(8,128)S(1)}, f32[5,8,128]{2,1,0:T(8,128)S(1)}, u32[]{:S(2)}, u32[]{:S(2)}) collective-permute-start(f32[5,8,128]{2,1,0:T(8,128)S(1)} %get-tuple-element.54), channel_id=1, source_target_pairs={{0,3},{1,2},{2,1},{3,0},{4,7},{5,6},{6,5},{7,4},{8,11},{9,10},{10,... | collective-permute-start | bytes 61448 | tf_op jit(solution)/shard_map/ppermute | solution.py:683
  15.5 4.0 %collective-permute-start.7 = (f32[5,8,128]{2,1,0:T(8,128)S(1)}, f32[5,8,128]{2,1,0:T(8,128)S(1)}, u32[]{:S(2)}, u32[]{:S(2)}) collective-permute-start(f32[5,8,128]{2,1,0:T(8,128)S(1)} %get-tuple-element.55), channel_id=1, source_target_pairs={{0,1},{1,0},{2,3},{3,2},{4,5},{5,4},{6,7},{7,6},{8,9},{9,8},{10,11... | collective-permute-start | bytes 61448 | tf_op jit(solution)/shard_map/ppermute | solution.py:684
  19.7 6.5 %collective-permute-start.8 = (f32[5,8,128]{2,1,0:T(8,128)S(1)}, f32[5,8,128]{2,1,0:T(8,128)S(1)}, u32[]{:S(2)}, u32[]{:S(2)}) collective-permute-start(f32[5,8,128]{2,1,0:T(8,128)S(1)} %get-tuple-element.58), channel_id=1, source_target_pairs={{0,28},{4,8},{8,4},{12,16},{16,12},{20,24},{24,20},{28,0},{1,29},{... | collective-permute-start | bytes 61448 | tf_op jit(solution)/shard_map/ppermute | solution.py:681
  22.2 4.0 %collective-permute-start.9 = (f32[5,8,128]{2,1,0:T(8,128)S(1)}, f32[5,8,128]{2,1,0:T(8,128)S(1)}, u32[]{:S(2)}, u32[]{:S(2)}) collective-permute-start(f32[5,8,128]{2,1,0:T(8,128)S(1)} %get-tuple-element.59), channel_id=1, source_target_pairs={{0,4},{4,0},{8,12},{12,8},{16,20},{20,16},{24,28},{28,24},{1,5},{5... | collective-permute-start | bytes 61448 | tf_op jit(solution)/shard_map/ppermute | solution.py:682
  22.2 4.0 %collective-permute-start.10 = (f32[5,8,128]{2,1,0:T(8,128)S(1)}, f32[5,8,128]{2,1,0:T(8,128)S(1)}, u32[]{:S(2)}, u32[]{:S(2)}) collective-permute-start(f32[5,8,128]{2,1,0:T(8,128)S(1)} %get-tuple-element.60), channel_id=1, source_target_pairs={{0,3},{1,2},{2,1},{3,0},{4,7},{5,6},{6,5},{7,4},{8,11},{9,10},{10,... | collective-permute-start | bytes 61448 | tf_op jit(solution)/shard_map/ppermute | solution.py:683
  22.2 4.0 %collective-permute-start.11 = (f32[5,8,128]{2,1,0:T(8,128)S(1)}, f32[5,8,128]{2,1,0:T(8,128)S(1)}, u32[]{:S(2)}, u32[]{:S(2)}) collective-permute-start(f32[5,8,128]{2,1,0:T(8,128)S(1)} %get-tuple-element.61), channel_id=1, source_target_pairs={{0,1},{1,0},{2,3},{3,2},{4,5},{5,4},{6,7},{7,6},{8,9},{9,8},{10,11... | collective-permute-start | bytes 61448 | tf_op jit(solution)/shard_map/ppermute | solution.py:684
  26.4 6.5 %collective-permute-start.12 = (f32[5,8,128]{2,1,0:T(8,128)S(1)}, f32[5,8,128]{2,1,0:T(8,128)S(1)}, u32[]{:S(2)}, u32[]{:S(2)}) collective-permute-start(f32[5,8,128]{2,1,0:T(8,128)S(1)} %get-tuple-element.63), channel_id=1, source_target_pairs={{0,28},{4,8},{8,4},{12,16},{16,12},{20,24},{24,20},{28,0},{1,29},{... | collective-permute-start | bytes 61448 | tf_op jit(solution)/shard_map/ppermute | solution.py:681
  28.9 4.0 %collective-permute-start.13 = (f32[5,8,128]{2,1,0:T(8,128)S(1)}, f32[5,8,128]{2,1,0:T(8,128)S(1)}, u32[]{:S(2)}, u32[]{:S(2)}) collective-permute-start(f32[5,8,128]{2,1,0:T(8,128)S(1)} %get-tuple-element.64), channel_id=1, source_target_pairs={{0,4},{4,0},{8,12},{12,8},{16,20},{20,16},{24,28},{28,24},{1,5},{5... | collective-permute-start | bytes 61448 | tf_op jit(solution)/shard_map/ppermute | solution.py:682
  28.9 4.0 %collective-permute-start.14 = (f32[5,8,128]{2,1,0:T(8,128)S(1)}, f32[5,8,128]{2,1,0:T(8,128)S(1)}, u32[]{:S(2)}, u32[]{:S(2)}) collective-permute-start(f32[5,8,128]{2,1,0:T(8,128)S(1)} %get-tuple-element.65), channel_id=1, source_target_pairs={{0,3},{1,2},{2,1},{3,0},{4,7},{5,6},{6,5},{7,4},{8,11},{9,10},{10,... | collective-permute-start | bytes 61448 | tf_op jit(solution)/shard_map/ppermute | solution.py:683
  28.9 4.0 %collective-permute-start.15 = (f32[5,8,128]{2,1,0:T(8,128)S(1)}, f32[5,8,128]{2,1,0:T(8,128)S(1)}, u32[]{:S(2)}, u32[]{:S(2)}) collective-permute-start(f32[5,8,128]{2,1,0:T(8,128)S(1)} %get-tuple-element.66), channel_id=1, source_target_pairs={{0,1},{1,0},{2,3},{3,2},{4,5},{5,4},{6,7},{7,6},{8,9},{9,8},{10,11... | collective-permute-start | bytes 61448 | tf_op jit(solution)/shard_map/ppermute | solution.py:684

commit v11 on v9

--- a/solution.py
+++ b/solution.py
@@ -380,7 +380,7 @@
 
 
 def second_kernel(
-    acc_ref, u_ref, smooth_ref, flag_ref, face_ref, rxo, rxe, ryo, rye, inner_ref, out_ref, xo, xe, yo, ye, part_ref
+    acc_ref, u_ref, smooth_ref, flag_ref, face_ref, rxo, ryo, rxe, rye, inner_ref, out_ref, xo, xe, yo, ye, part_ref
 ):
     remote_parts((rxe, rye), (rxo, ryo), flag_ref, face_ref, part_ref)
     for a in range(4):
@@ -710,7 +710,7 @@
         scratch=[pltpu.SemaphoreType.DMA((5,)), pltpu.VMEM((3, 4, 128), jnp.int32), pltpu.SemaphoreType.DMA],
         flops=2 * 25 * 64 * 512,
     )
-    got = exchange(*sent)
+    rxo, rxe, ryo, rye = exchange(*sent)
     smoother, first, acc, jac8, damp8, face, second = call(
         first_volume_kernel,
         (smoother_in, source, smoother, first, flag, jacobian, damping),
@@ -722,7 +722,7 @@
     )
     second, *sent = call(
         second_kernel,
-        (acc, first, smoother, flag, face, *got, second),
+        (acc, first, smoother, flag, face, rxo, ryo, rxe, rye, second),
         [vmem(FINE)] + coarse_messages,
         aliases={9: 0},
         scratch=[pltpu.VMEM((4, 5, 4, 2, 8, 128), F32)],

time: 34.1 us -> 35.4 us (1.038)
  waiting for transfers between devices: 6.47 us -> 11.6 us
  starting transfers between devices: 20.2 us -> 16.4 us
    ppermute x4, waiting for transfers between devices: 5.98 us -> 9.78 us  [exchange(): xo = lax.ppermute(xo, 'gx', odd_x)]
    ppermute x4, starting transfers between devices: 5.85 us -> 3.13 us  [exchange(): ye = lax.ppermute(ye, 'gy', even_y)]
    ppermute x4, starting transfers between devices: 13.7 us -> 12.6 us  [exchange(): xo = lax.ppermute(xo, 'gx', odd_x)]
    ppermute x4, waiting for transfers between devices: 0.24 us -> 1.32 us  [exchange(): xe = lax.ppermute(xe, 'gx', even_x)]
  transfers between devices with their start and end apart: 16 -> 16, of which waited for: 5 -> 5; matrix products, arithmetic and copies ran while one was open for 0% -> 0% of each run, Pallas kernels for 11% -> 10%
where the time goes in v11:
time: 35.4 us; the launch traced here: 35.2 us
  starting transfers between devices  16.4 us (46%)
  waiting for transfers between devices  11.6 us (33%)
  Pallas kernels  7.09 us (20%)
    ppermute x4, starting transfers between devices, exchange(): xo = lax.ppermute(xo, 'gx', odd_x)  12.6 us
    ppermute x4, waiting for transfers between devices, exchange(): xo = lax.ppermute(xo, 'gx', odd_x)  9.78 us
    pallas_call x9, Pallas kernels, call(): pl.pallas_call(kernel, out_shape=outs, in_specs=in_specs, out_specs=out_s...  7.09 us
    ppermute x4, starting transfers between devices, exchange(): ye = lax.ppermute(ye, 'gy', even_y)  3.13 us
    ppermute x4, waiting for transfers between devices, exchange(): xe = lax.ppermute(xe, 'gx', even_x)  1.32 us
  transfers between devices with their start and end apart: 16, of which 5 were waited for; matrix products, arithmetic and copies ran while one was open for 0% of the time, Pallas kernels for 10%

profile of v11, /device:TPU:0, one launch (start us, length us, event | category | flops | bytes accessed | tf_op | source)
XLA Modules:
  0.0 35.2 jit_solution(1480877775486472203)
XLA Ops:
  0.0 0.0 copy-start.2
  0.0 0.0 copy-start.1
  0.0 1.7 %shard_map.64 = (f32[5,4,4,2,8,128]{5,4,3,2,1,0:T(8,128)S(1)}, bf16[25,4,4,16,128]{4,3,2,1,0:T(8,128)(2,1)S(1)}, f32[5,4,4,2,8,128]{5,4,3,2,1,0:T(8,128)S(1)}, s...) custom-call(f32[5,4,4,2,8,128]{5,4,3,2,1,0:T(8,128)} %bitcast.16, ...), custom_call_target="tpu_custom_call" | custom-call | flops 1638400 | bytes 4194304 | tf_op jit(solution)/shard_map/pallas_call | solution.py:659
  1.7 6.0 %collective-permute-start = (f32[5,4,8,128]{3,2,1,0:T(8,128)S(1)}, f32[5,4,8,128]{3,2,1,0:T(8,128)S(1)}, u32[]{:S(2)}, u32[]{:S(2)}) collective-permute-start(f32[5,4,8,128]{3,2,1,0:T(8,128)S(1)} %get-tuple-element.44), channel_id=1, source_target_pairs={{0,28},{4,8},{8,4},{12,16},{16,12},{20,24},{24,20},{28,0},{1,29},{... | collective-permute-start | bytes 245768 | tf_op jit(solution)/shard_map/ppermute | solution.py:681
  7.7 0.7 %collective-permute-start.1 = (f32[5,4,8,128]{3,2,1,0:T(8,128)S(1)}, f32[5,4,8,128]{3,2,1,0:T(8,128)S(1)}, u32[]{:S(2)}, u32[]{:S(2)}) collective-permute-start(f32[5,4,8,128]{3,2,1,0:T(8,128)S(1)} %get-tuple-element.45), channel_id=1, source_target_pairs={{0,3},{1,2},{2,1},{3,0},{4,7},{5,6},{6,5},{7,4},{8,11},{9,10},{10,... | collective-permute-start | bytes 245768 | tf_op jit(solution)/shard_map/ppermute | solution.py:683
  8.4 0.0 collective-permute-start.2
  8.4 1.0 %collective-permute-start.3 = (f32[5,4,8,128]{3,2,1,0:T(8,128)S(1)}, f32[5,4,8,128]{3,2,1,0:T(8,128)S(1)}, u32[]{:S(2)}, u32[]{:S(2)}) collective-permute-start(f32[5,4,8,128]{3,2,1,0:T(8,128)S(1)} %get-tuple-element.47), channel_id=1, source_target_pairs={{0,1},{1,0},{2,3},{3,2},{4,5},{5,4},{6,7},{7,6},{8,9},{9,8},{10,11... | collective-permute-start | bytes 245768 | tf_op jit(solution)/shard_map/ppermute | solution.py:684
  9.4 0.0 copy-done.2
  9.4 0.0 copy-done.1
  9.4 2.5 %shard_map.65 = (bf16[25,4,4,16,128]{4,3,2,1,0:T(8,128)(2,1)S(1)}, f32[5,4,4,2,8,128]{5,4,3,2,1,0:T(8,128)S(1)}, f32[5,4,4,2,8,128]{5,4,3,2,1,0:T(8,128)S(1)}, f...) custom-call(bf16[25,4,4,16,128]{4,3,2,1,0:T(8,128)(2,1)} %bitcast.15, ...), custom_call_target="tpu_custom_call", output_to_operand_aliasing={{0}: (2, {}), {1}: (3, {})} | custom-call | flops 9437184 | bytes 4194304 | tf_op jit(solution)/shard_map/pallas_call | solution.py:659
  11.9 0.0 collective-permute-done.rxo
  11.9 0.5 %collective-permute-done.1.ryo = f32[5,4,8,128]{3,2,1,0:T(8,128)S(1)} collective-permute-done((f32[5,4,8,128]{3,2,1,0:T(8,128)S(1)}, f32[5,4,8,128]{3,2,1,0:T(8,128)S(1)}, u32[]{:S(2)}, u32[]{:S(2)}) %collective-permute-start.1) | collective-permute-done | bytes 81952 | tf_op jit(solution)/shard_map/ppermute | solution.py:683
  12.4 1.3 %collective-permute-done.2.rxe = f32[5,4,8,128]{3,2,1,0:T(8,128)S(1)} collective-permute-done((f32[5,4,8,128]{3,2,1,0:T(8,128)S(1)}, f32[5,4,8,128]{3,2,1,0:T(8,128)S(1)}, u32[]{:S(2)}, u32[]{:S(2)}) %collective-permute-start.2) | collective-permute-done | bytes 81952 | tf_op jit(solution)/shard_map/ppermute | solution.py:682
  13.7 0.0 collective-permute-done.3.rye
  13.7 0.6 %shard_map.66 = (f32[5,4,4,2,8,128]{5,4,3,2,1,0:T(8,128)S(1)}, f32[5,8,128]{2,1,0:T(8,128)S(1)}, f32[5,8,128]{2,1,0:T(8,128)S(1)}, f32[5,8,128]{2,1,0:T(8,128)S(1)}, f32[5,8,128]{2,1,0:T(8,128)S(1)}) custom-call(f32[5,4,4,2,8,128]{5,4,3,2,1,0:T(8,128)S(1)} %get-tuple-element.40.acc_ref, ...), custom_call_target="tpu_custom_call", output_to_operand_aliasing={{0}: (9, {})} | custom-call | flops 3145728 | bytes 4194304 | tf_op jit(solution)/shard_map/pallas_call | solution.py:659
  14.3 0.0 copy-start
  14.3 2.0 %collective-permute-start.4 = (f32[5,8,128]{2,1,0:T(8,128)S(1)}, f32[5,8,128]{2,1,0:T(8,128)S(1)}, u32[]{:S(2)}, u32[]{:S(2)}) collective-permute-start(f32[5,8,128]{2,1,0:T(8,128)S(1)} %get-tuple-element.52), channel_id=1, source_target_pairs={{0,28},{4,8},{8,4},{12,16},{16,12},{20,24},{24,20},{28,0},{1,29},{... | collective-permute-start | bytes 61448 | tf_op jit(solution)/shard_map/ppermute | solution.py:681
  16.3 0.0 collective-permute-start.5
  16.3 0.0 collective-permute-start.6
  16.3 0.9 %collective-permute-start.7 = (f32[5,8,128]{2,1,0:T(8,128)S(1)}, f32[5,8,128]{2,1,0:T(8,128)S(1)}, u32[]{:S(2)}, u32[]{:S(2)}) collective-permute-start(f32[5,8,128]{2,1,0:T(8,128)S(1)} %get-tuple-element.55), channel_id=1, source_target_pairs={{0,1},{1,0},{2,3},{3,2},{4,5},{5,4},{6,7},{7,6},{8,9},{9,8},{10,11... | collective-permute-start | bytes 61448 | tf_op jit(solution)/shard_map/ppermute | solution.py:684
  17.2 0.6 %shard_map.67.acc_ref = f32[5,2,2,8,128]{4,3,2,1,0:T(8,128)S(1)} custom-call(f32[5,4,4,2,8,128]{5,4,3,2,1,0:T(8,128)S(1)} %get-tuple-element.36.src_ref, f32[5,4,4,2,8,128]{5,4,3,2,1,0:T(8,128)S(1)} %get-tuple-element.49.u_ref.second_ref, s32[3,8,128]{2,1,0:T(8,128)S(1)} %get-tuple-element.39.flag_ref, f32[75,8,128]{2,1,0:T(8,128)S(1)} %get-tuple-element.50.jac_ref, ...), custom_call_target="tpu_custom_call" | custom-call | flops 4194304 | bytes 4194304 | tf_op jit(solution)/shard_map/pallas_call | solution.py:659
  17.8 3.0 %collective-permute-done.4.rxo = f32[5,8,128]{2,1,0:T(8,128)S(1)} collective-permute-done((f32[5,8,128]{2,1,0:T(8,128)S(1)}, f32[5,8,128]{2,1,0:T(8,128)S(1)}, u32[]{:S(2)}, u32[]{:S(2)}) %collective-permute-start.4) | collective-permute-done | bytes 20512 | tf_op jit(solution)/shard_map/ppermute | solution.py:681
  20.8 0.0 collective-permute-done.5.rxe
  20.8 0.0 collective-permute-done.6.ryo
  20.8 0.0 collective-permute-done.7.rye
  20.9 0.0 copy-done
  20.9 0.1 shard_map.68
  21.0 2.2 %collective-permute-start.8 = (f32[5,8,128]{2,1,0:T(8,128)S(1)}, f32[5,8,128]{2,1,0:T(8,128)S(1)}, u32[]{:S(2)}, u32[]{:S(2)}) collective-permute-start(f32[5,8,128]{2,1,0:T(8,128)S(1)} %get-tuple-element.58), channel_id=1, source_target_pairs={{0,28},{4,8},{8,4},{12,16},{16,12},{20,24},{24,20},{28,0},{1,29},{... | collective-permute-start | bytes 61448 | tf_op jit(solution)/shard_map/ppermute | solution.py:681
  23.2 0.0 collective-permute-start.9
  23.2 0.0 collective-permute-start.10
  23.2 0.7 %collective-permute-start.11 = (f32[5,8,128]{2,1,0:T(8,128)S(1)}, f32[5,8,128]{2,1,0:T(8,128)S(1)}, u32[]{:S(2)}, u32[]{:S(2)}) collective-permute-start(f32[5,8,128]{2,1,0:T(8,128)S(1)} %get-tuple-element.61), channel_id=1, source_target_pairs={{0,1},{1,0},{2,3},{3,2},{4,5},{5,4},{6,7},{7,6},{8,9},{9,8},{10,11... | collective-permute-start | bytes 61448 | tf_op jit(solution)/shard_map/ppermute | solution.py:684
  23.9 0.2 shard_map.69.c_ref
  24.2 3.4 %collective-permute-done.8.rxo = f32[5,8,128]{2,1,0:T(8,128)S(1)} collective-permute-done((f32[5,8,128]{2,1,0:T(8,128)S(1)}, f32[5,8,128]{2,1,0:T(8,128)S(1)}, u32[]{:S(2)}, u32[]{:S(2)}) %collective-permute-start.8) | collective-permute-done | bytes 20512 | tf_op jit(solution)/shard_map/ppermute | solution.py:681
  27.5 0.0 collective-permute-done.9.rxe
  27.5 0.0 collective-permute-done.10.ryo
  27.5 0.0 collective-permute-done.11.rye
  27.5 0.1 shard_map.70
  27.7 2.3 %collective-permute-start.12 = (f32[5,8,128]{2,1,0:T(8,128)S(1)}, f32[5,8,128]{2,1,0:T(8,128)S(1)}, u32[]{:S(2)}, u32[]{:S(2)}) collective-permute-start(f32[5,8,128]{2,1,0:T(8,128)S(1)} %get-tuple-element.63), channel_id=1, source_target_pairs={{0,28},{4,8},{8,4},{12,16},{16,12},{20,24},{24,20},{28,0},{1,29},{... | collective-permute-start | bytes 61448 | tf_op jit(solution)/shard_map/ppermute | solution.py:681
  30.0 0.0 collective-permute-start.13
  30.0 0.0 collective-permute-start.14
  30.0 0.6 %collective-permute-start.15 = (f32[5,8,128]{2,1,0:T(8,128)S(1)}, f32[5,8,128]{2,1,0:T(8,128)S(1)}, u32[]{:S(2)}, u32[]{:S(2)}) collective-permute-start(f32[5,8,128]{2,1,0:T(8,128)S(1)} %get-tuple-element.66), channel_id=1, source_target_pairs={{0,1},{1,0},{2,3},{3,2},{4,5},{5,4},{6,7},{7,6},{8,9},{9,8},{10,11... | collective-permute-start | bytes 61448 | tf_op jit(solution)/shard_map/ppermute | solution.py:684
  30.6 0.2 shard_map.71.c_ref
  30.9 3.4 %collective-permute-done.12.rxo = f32[5,8,128]{2,1,0:T(8,128)S(1)} collective-permute-done((f32[5,8,128]{2,1,0:T(8,128)S(1)}, f32[5,8,128]{2,1,0:T(8,128)S(1)}, u32[]{:S(2)}, u32[]{:S(2)}) %collective-permute-start.12) | collective-permute-done | bytes 20512 | tf_op jit(solution)/shard_map/ppermute | solution.py:681
  34.2 0.0 collective-permute-done.13.rxe
  34.2 0.0 collective-permute-done.14.ryo
  34.2 0.0 collective-permute-done.15.rye
  34.2 1.0 %shard_map.72 = f32[5,4,4,2,8,128]{5,4,3,2,1,0:T(8,128)} custom-call(f32[5,2,2,8,128]{4,3,2,1,0:T(8,128)S(1)} %shard_map.71.c_ref, bf16[25,2,16,128]{3,2,1,0:T(8,128)(2,1)S(1)} %bitcast.11, s32[3,8,128]{2,1,0:T(8,128)S(1)} %get-tuple-element.39.flag_ref, f32[4,25,8,128]{3,2,1,0:T(8,128)S(1)} %get-tuple-element.43.face_ref, ...), custom_call_target="tpu_custom_call" | custom-call | flops 1048576 | bytes 4194304 | tf_op jit(solution)/shard_map/pallas_call | solution.py:659
Async XLA Ops:
  0.0 9.4 %copy-start.2 = (f32[2,2,128]{2,1,0:T(2,128)S(1)}, f32[2,2,128]{2,1,0:T(2,128)}, u32[]{:S(2)}) copy-start(f32[2,2,128]{2,1,0:T(2,128)} %param.8) | copy-start | bytes 6148
  0.0 9.4 %copy-start.1 = (f32[3,5,5,2,2,128]{5,4,3,2,1,0:T(2,128)S(1)}, f32[3,5,5,2,2,128]{5,4,3,2,1,0:T(2,128)}, u32[]{:S(2)}) copy-start(f32[3,5,5,2,2,128]{5,4,3,2,1,0:T(2,128)} %param.7) | copy-start | bytes 460804
  1.7 10.2 %collective-permute-start = (f32[5,4,8,128]{3,2,1,0:T(8,128)S(1)}, f32[5,4,8,128]{3,2,1,0:T(8,128)S(1)}, u32[]{:S(2)}, u32[]{:S(2)}) collective-permute-start(f32[5,4,8,128]{3,2,1,0:T(8,128)S(1)} %get-tuple-element.44), channel_id=1, source_target_pairs={{0,28},{4,8},{8,4},{12,16},{16,12},{20,24},{24,20},{28,0},{1,29},{... | collective-permute-start | bytes 245768 | tf_op jit(solution)/shard_map/ppermute | solution.py:681
  7.7 4.7 %collective-permute-start.1 = (f32[5,4,8,128]{3,2,1,0:T(8,128)S(1)}, f32[5,4,8,128]{3,2,1,0:T(8,128)S(1)}, u32[]{:S(2)}, u32[]{:S(2)}) collective-permute-start(f32[5,4,8,128]{3,2,1,0:T(8,128)S(1)} %get-tuple-element.45), channel_id=1, source_target_pairs={{0,3},{1,2},{2,1},{3,0},{4,7},{5,6},{6,5},{7,4},{8,11},{9,10},{10,... | collective-permute-start | bytes 245768 | tf_op jit(solution)/shard_map/ppermute | solution.py:683
  8.4 5.3 %collective-permute-start.2 = (f32[5,4,8,128]{3,2,1,0:T(8,128)S(1)}, f32[5,4,8,128]{3,2,1,0:T(8,128)S(1)}, u32[]{:S(2)}, u32[]{:S(2)}) collective-permute-start(f32[5,4,8,128]{3,2,1,0:T(8,128)S(1)} %get-tuple-element.46), channel_id=1, source_target_pairs={{0,4},{4,0},{8,12},{12,8},{16,20},{20,16},{24,28},{28,24},{1,5},{5... | collective-permute-start | bytes 245768 | tf_op jit(solution)/shard_map/ppermute | solution.py:682
  8.4 5.3 %collective-permute-start.3 = (f32[5,4,8,128]{3,2,1,0:T(8,128)S(1)}, f32[5,4,8,128]{3,2,1,0:T(8,128)S(1)}, u32[]{:S(2)}, u32[]{:S(2)}) collective-permute-start(f32[5,4,8,128]{3,2,1,0:T(8,128)S(1)} %get-tuple-element.47), channel_id=1, source_target_pairs={{0,1},{1,0},{2,3},{3,2},{4,5},{5,4},{6,7},{7,6},{8,9},{9,8},{10,11... | collective-permute-start | bytes 245768 | tf_op jit(solution)/shard_map/ppermute | solution.py:684
  14.3 6.6 %copy-start = (bf16[5,5,2,2,2,2,2,128]{7,6,5,4,3,2,1,0:T(2,128)(2,1)S(1)}, bf16[5,5,2,2,2,2,2,128]{7,6,5,4,3,2,1,0:T(2,128)(2,1)}, u32[]{:S(2)}) copy-start(bf16[5,5,2,2,2,2,2,128]{7,6,5,4,3,2,1,0:T(2,128)(2,1)} %param.11) | copy-start | bytes 614404
  14.3 6.5 %collective-permute-start.4 = (f32[5,8,128]{2,1,0:T(8,128)S(1)}, f32[5,8,128]{2,1,0:T(8,128)S(1)}, u32[]{:S(2)}, u32[]{:S(2)}) collective-permute-start(f32[5,8,128]{2,1,0:T(8,128)S(1)} %get-tuple-element.52), channel_id=1, source_target_pairs={{0,28},{4,8},{8,4},{12,16},{16,12},{20,24},{24,20},{28,0},{1,29},{... | collective-permute-start | bytes 61448 | tf_op jit(solution)/shard_map/ppermute | solution.py:681
  16.3 4.5 %collective-permute-start.5 = (f32[5,8,128]{2,1,0:T(8,128)S(1)}, f32[5,8,128]{2,1,0:T(8,128)S(1)}, u32[]{:S(2)}, u32[]{:S(2)}) collective-permute-start(f32[5,8,128]{2,1,0:T(8,128)S(1)} %get-tuple-element.53), channel_id=1, source_target_pairs={{0,4},{4,0},{8,12},{12,8},{16,20},{20,16},{24,28},{28,24},{1,5},{5... | collective-permute-start | bytes 61448 | tf_op jit(solution)/shard_map/ppermute | solution.py:682
  16.3 4.5 %collective-permute-start.6 = (f32[5,8,128]{2,1,0:T(8,128)S(1)}, f32[5,8,128]{2,1,0:T(8,128)S(1)}, u32[]{:S(2)}, u32[]{:S(2)}) collective-permute-start(f32[5,8,128]{2,1,0:T(8,128)S(1)} %get-tuple-element.54), channel_id=1, source_target_pairs={{0,3},{1,2},{2,1},{3,0},{4,7},{5,6},{6,5},{7,4},{8,11},{9,10},{10,... | collective-permute-start | bytes 61448 | tf_op jit(solution)/shard_map/ppermute | solution.py:683
  16.3 4.5 %collective-permute-start.7 = (f32[5,8,128]{2,1,0:T(8,128)S(1)}, f32[5,8,128]{2,1,0:T(8,128)S(1)}, u32[]{:S(2)}, u32[]{:S(2)}) collective-permute-start(f32[5,8,128]{2,1,0:T(8,128)S(1)} %get-tuple-element.55), channel_id=1, source_target_pairs={{0,1},{1,0},{2,3},{3,2},{4,5},{5,4},{6,7},{7,6},{8,9},{9,8},{10,11... | collective-permute-start | bytes 61448 | tf_op jit(solution)/shard_map/ppermute | solution.py:684
  21.0 6.5 %collective-permute-start.8 = (f32[5,8,128]{2,1,0:T(8,128)S(1)}, f32[5,8,128]{2,1,0:T(8,128)S(1)}, u32[]{:S(2)}, u32[]{:S(2)}) collective-permute-start(f32[5,8,128]{2,1,0:T(8,128)S(1)} %get-tuple-element.58), channel_id=1, source_target_pairs={{0,28},{4,8},{8,4},{12,16},{16,12},{20,24},{24,20},{28,0},{1,29},{... | collective-permute-start | bytes 61448 | tf_op jit(solution)/shard_map/ppermute | solution.py:681
  23.2 4.3 %collective-permute-start.9 = (f32[5,8,128]{2,1,0:T(8,128)S(1)}, f32[5,8,128]{2,1,0:T(8,128)S(1)}, u32[]{:S(2)}, u32[]{:S(2)}) collective-permute-start(f32[5,8,128]{2,1,0:T(8,128)S(1)} %get-tuple-element.59), channel_id=1, source_target_pairs={{0,4},{4,0},{8,12},{12,8},{16,20},{20,16},{24,28},{28,24},{1,5},{5... | collective-permute-start | bytes 61448 | tf_op jit(solution)/shard_map/ppermute | solution.py:682
  23.2 4.3 %collective-permute-start.10 = (f32[5,8,128]{2,1,0:T(8,128)S(1)}, f32[5,8,128]{2,1,0:T(8,128)S(1)}, u32[]{:S(2)}, u32[]{:S(2)}) collective-permute-start(f32[5,8,128]{2,1,0:T(8,128)S(1)} %get-tuple-element.60), channel_id=1, source_target_pairs={{0,3},{1,2},{2,1},{3,0},{4,7},{5,6},{6,5},{7,4},{8,11},{9,10},{10,... | collective-permute-start | bytes 61448 | tf_op jit(solution)/shard_map/ppermute | solution.py:683
  23.2 4.3 %collective-permute-start.11 = (f32[5,8,128]{2,1,0:T(8,128)S(1)}, f32[5,8,128]{2,1,0:T(8,128)S(1)}, u32[]{:S(2)}, u32[]{:S(2)}) collective-permute-start(f32[5,8,128]{2,1,0:T(8,128)S(1)} %get-tuple-element.61), channel_id=1, source_target_pairs={{0,1},{1,0},{2,3},{3,2},{4,5},{5,4},{6,7},{7,6},{8,9},{9,8},{10,11... | collective-permute-start | bytes 61448 | tf_op jit(solution)/shard_map/ppermute | solution.py:684
  27.7 6.5 %collective-permute-start.12 = (f32[5,8,128]{2,1,0:T(8,128)S(1)}, f32[5,8,128]{2,1,0:T(8,128)S(1)}, u32[]{:S(2)}, u32[]{:S(2)}) collective-permute-start(f32[5,8,128]{2,1,0:T(8,128)S(1)} %get-tuple-element.63), channel_id=1, source_target_pairs={{0,28},{4,8},{8,4},{12,16},{16,12},{20,24},{24,20},{28,0},{1,29},{... | collective-permute-start | bytes 61448 | tf_op jit(solution)/shard_map/ppermute | solution.py:681
  30.0 4.2 %collective-permute-start.13 = (f32[5,8,128]{2,1,0:T(8,128)S(1)}, f32[5,8,128]{2,1,0:T(8,128)S(1)}, u32[]{:S(2)}, u32[]{:S(2)}) collective-permute-start(f32[5,8,128]{2,1,0:T(8,128)S(1)} %get-tuple-element.64), channel_id=1, source_target_pairs={{0,4},{4,0},{8,12},{12,8},{16,20},{20,16},{24,28},{28,24},{1,5},{5... | collective-permute-start | bytes 61448 | tf_op jit(solution)/shard_map/ppermute | solution.py:682
  30.0 4.2 %collective-permute-start.14 = (f32[5,8,128]{2,1,0:T(8,128)S(1)}, f32[5,8,128]{2,1,0:T(8,128)S(1)}, u32[]{:S(2)}, u32[]{:S(2)}) collective-permute-start(f32[5,8,128]{2,1,0:T(8,128)S(1)} %get-tuple-element.65), channel_id=1, source_target_pairs={{0,3},{1,2},{2,1},{3,0},{4,7},{5,6},{6,5},{7,4},{8,11},{9,10},{10,... | collective-permute-start | bytes 61448 | tf_op jit(solution)/shard_map/ppermute | solution.py:683
  30.0 4.2 %collective-permute-start.15 = (f32[5,8,128]{2,1,0:T(8,128)S(1)}, f32[5,8,128]{2,1,0:T(8,128)S(1)}, u32[]{:S(2)}, u32[]{:S(2)}) collective-permute-start(f32[5,8,128]{2,1,0:T(8,128)S(1)} %get-tuple-element.66), channel_id=1, source_target_pairs={{0,1},{1,0},{2,3},{3,2},{4,5},{5,4},{6,7},{7,6},{8,9},{9,8},{10,11... | collective-permute-start | bytes 61448 | tf_op jit(solution)/shard_map/ppermute | solution.py:684

commit v12 on v10

--- a/solution.py
+++ b/solution.py
@@ -116,14 +116,19 @@
     odd_ref[index] = jnp.where(is_even, low_face, high_face)
 
 
-def fine_faces(u_ref, flag_ref, xo, xe, yo, ye):
-    even_x, even_y = parity("gx"), parity("gy")
-    fx, fy = flag_ref[0] != 0, flag_ref[1] != 0
+def fine_x_faces(u_ref, flag_ref, xo, xe):
+    even_x, fx = parity("gx"), flag_ref[0] != 0
     for v in range(5):
         for n in range(4):
             low = pack_low(u_ref[v, 0, n, 0], u_ref[v, 0, n, 1], 0)
             h = [jnp.where(fx, u_ref[v, 3, 3 - n, q], u_ref[v, 3, n, q]) for q in range(2)]
             put_pair(xe, xo, (v, n), low, pack_high(h[0], h[1], 0), even_x)
+
+
+def fine_y_faces(u_ref, flag_ref, yo, ye):
+    even_y, fy = parity("gy"), flag_ref[1] != 0
+    for v in range(5):
+        for n in range(4):
             low = pack_low(u_ref[v, n, 0, 0], u_ref[v, n, 0, 1], 1)
             h = [jnp.where(fy, u_ref[v, 3 - n, 3, q], u_ref[v, n, 3, q]) for q in range(2)]
             put_pair(ye, yo, (v, n), low, pack_high(h[0], h[1], 1), even_y)
@@ -185,7 +190,7 @@
 
 
 def first_kernel(
-    src_hbm, smooth_hbm, orient_hbm, src_ref, smooth_ref, u_ref, flag_ref, xo, yo, xe, ye, sems, orient_ref, orient_sem
+    src_hbm, smooth_hbm, orient_hbm, src_ref, smooth_ref, u_ref, flag_ref, xo, xe, sems, orient_ref, orient_sem
 ):
     every, inner = slice(0, 4), slice(1, 3)
     src_copy = pltpu.make_async_copy(src_hbm, src_ref, sems.at[4])
@@ -201,13 +206,21 @@
     orient_copy.wait()
     for d in range(3):
         flag_ref[d] = twice(orient_ref[d])
-    lines = [[(0, b) for b in range(4)], [(3, b) for b in range(4)], [(1, 0), (2, 0)], [(1, 3), (2, 3)]]
     src_copy.wait()
-    for one, group in zip(copies, lines):
+    for one, a in zip(copies, (0, 3)):
         one.wait()
-        for a, b in group:
+        for b in range(4):
             first_line(src_ref, smooth_ref, u_ref, a, b)
-    fine_faces(u_ref, flag_ref, xo, xe, yo, ye)
+    fine_x_faces(u_ref, flag_ref, xo, xe)
+    for one in copies[2:]:
+        one.wait()
+
+
+def first_y_kernel(src_ref, smooth_ref, x_lines_ref, flag_ref, u_ref, yo, ye):
+    for a in (1, 2):
+        for b in (0, 3):
+            first_line(src_ref, smooth_ref, u_ref, a, b)
+    fine_y_faces(u_ref, flag_ref, yo, ye)
 
 
 def prepare_tables(jac_ref, damp_ref, jac8_ref, damp8_ref, face_ref):
@@ -675,14 +688,18 @@
     return even, odd
 
 
+def exchange_x(xo, xe):
+    even, odd = partners("gx")
+    return lax.ppermute(xo, "gx", odd), lax.ppermute(xe, "gx", even)
+
+
+def exchange_y(yo, ye):
+    even, odd = partners("gy")
+    return lax.ppermute(yo, "gy", odd), lax.ppermute(ye, "gy", even)
+
+
 def exchange(xo, xe, yo, ye):
-    even_x, odd_x = partners("gx")
-    even_y, odd_y = partners("gy")
-    xo = lax.ppermute(xo, "gx", odd_x)
-    xe = lax.ppermute(xe, "gx", even_x)
-    yo = lax.ppermute(yo, "gy", odd_y)
-    ye = lax.ppermute(ye, "gy", even_y)
-    return xo, xe, yo, ye
+    return *exchange_x(xo, xe), *exchange_y(yo, ye)
 
 
 def local_sweep(coarse, *rest):
@@ -702,15 +719,23 @@
 
     held = vmem(smoother.shape, smoother.dtype)
     smoother_in = smoother
-    source, smoother, first, flag, xo, yo, xe, ye = call(
+    source, smoother, first, flag, xo, xe = call(
         first_kernel,
         (source, smoother_in, orient),
-        [vmem(FINE), held, vmem(FINE), vmem((3, 8, 128), jnp.int32)] + fine_messages,
+        [vmem(FINE), held, vmem(FINE), vmem((3, 8, 128), jnp.int32)] + fine_messages[:2],
         in_hbm=(0, 1, 2),
         scratch=[pltpu.SemaphoreType.DMA((5,)), pltpu.VMEM((3, 4, 128), jnp.int32), pltpu.SemaphoreType.DMA],
         flops=2 * 25 * 64 * 512,
     )
-    got = exchange(xo, xe, yo, ye)
+    got_x = exchange_x(xo, xe)
+    first, yo, ye = call(
+        first_y_kernel,
+        (source, smoother, first, flag),
+        [vmem(FINE)] + fine_messages[:2],
+        aliases={2: 0},
+        flops=25 * 64 * 512,
+    )
+    got = (*got_x, *exchange_y(yo, ye))
     smoother, first, acc, jac8, damp8, face, second = call(
         first_volume_kernel,
         (smoother_in, source, smoother, first, flag, jacobian, damping),

time: 34.1 us -> 34.1 us (level)
  waiting for transfers between devices: 6.47 us -> 7 us
  starting transfers between devices: 20.2 us -> 19.8 us
    ppermute x16, waiting for transfers between devices: 6.47 us -> 7 us  [the longest x8 6.57 us: exchange_x(): return (lax.ppermute(xo, 'gx', odd), lax.ppermute(xe, 'gx', even))]
    ppermute x16, starting transfers between devices: 20.2 us -> 19.8 us  [the longest x8 13.2 us: exchange_x(): return (lax.ppermute(xo, 'gx', odd), lax.ppermute(xe, 'gx', even))]
    pallas_call x9 -> x10, Pallas kernels: 7.1 us -> 7.02 us  [call(): pl.pallas_call(kernel, out_shape=outs, in_specs=in_specs, out_specs=out_s...]
where the time goes in v12:
time: 34.1 us; the launch traced here: 33.9 us
  starting transfers between devices  19.8 us (58%)
  Pallas kernels  7.02 us (21%)
  waiting for transfers between devices  7 us (21%)
    ppermute x8, starting transfers between devices, exchange_x(): return (lax.ppermute(xo, 'gx', odd), lax.ppermute(xe, 'gx', even))  13.2 us
    pallas_call x10, Pallas kernels, call(): pl.pallas_call(kernel, out_shape=outs, in_specs=in_specs, out_specs=out_s...  7.02 us
    ppermute x8, starting transfers between devices, exchange_y(): return (lax.ppermute(yo, 'gy', odd), lax.ppermute(ye, 'gy', even))  6.6 us
    ppermute x8, waiting for transfers between devices, exchange_x(): return (lax.ppermute(xo, 'gx', odd), lax.ppermute(xe, 'gx', even))  6.57 us
  transfers between devices with their start and end apart: 16, of which 5 were waited for; matrix products, arithmetic and copies ran while one was open for 0% of the time, Pallas kernels for 11%

profile of v12, /device:TPU:0, one launch (start us, length us, event | category | flops | bytes accessed | tf_op | source)
XLA Modules:
  0.0 33.9 jit_solution(15768798862620930687)
XLA Ops:
  0.0 1.5 %shard_map.64 = (f32[5,4,4,2,8,128]{5,4,3,2,1,0:T(8,128)S(1)}, bf16[25,4,4,16,128]{4,3,2,1,0:T(8,128)(2,1)S(1)}, f32[5,4,4,2,8,128]{5,4,3,2,1,0:T(8,128)S(1)}, s...) custom-call(f32[5,4,4,2,8,128]{5,4,3,2,1,0:T(8,128)} %bitcast.16, ...), custom_call_target="tpu_custom_call" | custom-call | flops 1638400 | bytes 4194304 | tf_op jit(solution)/shard_map/pallas_call | solution.py:672
  1.5 0.0 copy-start.1
  1.5 0.0 copy-start.2
  1.6 6.0 %collective-permute-start = (f32[5,4,8,128]{3,2,1,0:T(8,128)S(1)}, f32[5,4,8,128]{3,2,1,0:T(8,128)S(1)}, u32[]{:S(2)}, u32[]{:S(2)}) collective-permute-start(f32[5,4,8,128]{3,2,1,0:T(8,128)S(1)} %get-tuple-element.46), channel_id=1, source_target_pairs={{0,28},{4,8},{8,4},{12,16},{16,12},{20,24},{24,20},{28,0},{1,29},{... | collective-permute-start | bytes 245768 | tf_op jit(solution)/shard_map/ppermute | solution.py:693
  7.6 0.0 collective-permute-start.1
  7.6 0.1 shard_map.65
  7.7 0.7 %collective-permute-start.2 = (f32[5,4,8,128]{3,2,1,0:T(8,128)S(1)}, f32[5,4,8,128]{3,2,1,0:T(8,128)S(1)}, u32[]{:S(2)}, u32[]{:S(2)}) collective-permute-start(f32[5,4,8,128]{3,2,1,0:T(8,128)S(1)} %get-tuple-element.48), channel_id=1, source_target_pairs={{0,3},{1,2},{2,1},{3,0},{4,7},{5,6},{6,5},{7,4},{8,11},{9,10},{10,... | collective-permute-start | bytes 245768 | tf_op jit(solution)/shard_map/ppermute | solution.py:698
  8.5 1.0 %collective-permute-start.3 = (f32[5,4,8,128]{3,2,1,0:T(8,128)S(1)}, f32[5,4,8,128]{3,2,1,0:T(8,128)S(1)}, u32[]{:S(2)}, u32[]{:S(2)}) collective-permute-start(f32[5,4,8,128]{3,2,1,0:T(8,128)S(1)} %get-tuple-element.49), channel_id=1, source_target_pairs={{0,1},{1,0},{2,3},{3,2},{4,5},{5,4},{6,7},{7,6},{8,9},{9,8},{10,11... | collective-permute-start | bytes 245768 | tf_op jit(solution)/shard_map/ppermute | solution.py:698
  9.4 0.0 copy-done.1
  9.4 0.0 copy-done.2
  9.4 2.5 %shard_map.66 = (bf16[25,4,4,16,128]{4,3,2,1,0:T(8,128)(2,1)S(1)}, f32[5,4,4,2,8,128]{5,4,3,2,1,0:T(8,128)S(1)}, f32[5,4,4,2,8,128]{5,4,3,2,1,0:T(8,128)S(1)}, f...) custom-call(bf16[25,4,4,16,128]{4,3,2,1,0:T(8,128)(2,1)} %bitcast.15, ...), custom_call_target="tpu_custom_call", output_to_operand_aliasing={{0}: (2, {}), {1}: (3, {})} | custom-call | flops 9437184 | bytes 4194304 | tf_op jit(solution)/shard_map/pallas_call | solution.py:672
  12.0 0.0 collective-permute-done.rxo
  12.0 0.1 collective-permute-done.1.rxe
  12.0 0.4 %collective-permute-done.2.ryo = f32[5,4,8,128]{3,2,1,0:T(8,128)S(1)} collective-permute-done((f32[5,4,8,128]{3,2,1,0:T(8,128)S(1)}, f32[5,4,8,128]{3,2,1,0:T(8,128)S(1)}, u32[]{:S(2)}, u32[]{:S(2)}) %collective-permute-start.2) | collective-permute-done | bytes 81952 | tf_op jit(solution)/shard_map/ppermute | solution.py:698
  12.4 0.0 collective-permute-done.3.rye
  12.4 0.6 %shard_map.67 = (f32[5,4,4,2,8,128]{5,4,3,2,1,0:T(8,128)S(1)}, f32[5,8,128]{2,1,0:T(8,128)S(1)}, f32[5,8,128]{2,1,0:T(8,128)S(1)}, f32[5,8,128]{2,1,0:T(8,128)S(1)}, f32[5,8,128]{2,1,0:T(8,128)S(1)}) custom-call(f32[5,4,4,2,8,128]{5,4,3,2,1,0:T(8,128)S(1)} %get-tuple-element.42.acc_ref, ...), custom_call_target="tpu_custom_call", output_to_operand_aliasing={{0}: (9, {})} | custom-call | flops 3145728 | bytes 4194304 | tf_op jit(solution)/shard_map/pallas_call | solution.py:672
  13.0 0.0 copy-start
  13.0 2.4 %collective-permute-start.4 = (f32[5,8,128]{2,1,0:T(8,128)S(1)}, f32[5,8,128]{2,1,0:T(8,128)S(1)}, u32[]{:S(2)}, u32[]{:S(2)}) collective-permute-start(f32[5,8,128]{2,1,0:T(8,128)S(1)} %get-tuple-element.54), channel_id=1, source_target_pairs={{0,28},{4,8},{8,4},{12,16},{16,12},{20,24},{24,20},{28,0},{1,29},{... | collective-permute-start | bytes 61448 | tf_op jit(solution)/shard_map/ppermute | solution.py:693
  15.4 0.0 collective-permute-start.5
  15.4 0.0 collective-permute-start.6
  15.4 1.6 %collective-permute-start.7 = (f32[5,8,128]{2,1,0:T(8,128)S(1)}, f32[5,8,128]{2,1,0:T(8,128)S(1)}, u32[]{:S(2)}, u32[]{:S(2)}) collective-permute-start(f32[5,8,128]{2,1,0:T(8,128)S(1)} %get-tuple-element.57), channel_id=1, source_target_pairs={{0,1},{1,0},{2,3},{3,2},{4,5},{5,4},{6,7},{7,6},{8,9},{9,8},{10,11... | collective-permute-start | bytes 61448 | tf_op jit(solution)/shard_map/ppermute | solution.py:698
  17.0 0.6 %shard_map.68.acc_ref = f32[5,2,2,8,128]{4,3,2,1,0:T(8,128)S(1)} custom-call(f32[5,4,4,2,8,128]{5,4,3,2,1,0:T(8,128)S(1)} %get-tuple-element.37.src_ref, f32[5,4,4,2,8,128]{5,4,3,2,1,0:T(8,128)S(1)} %get-tuple-element.51.u_ref.second_ref, s32[3,8,128]{2,1,0:T(8,128)S(1)} %get-tuple-element.40.flag_ref, f32[75,8,128]{2,1,0:T(8,128)S(1)} %get-tuple-element.52.jac_ref, ...), custom_call_target="tpu_custom_call" | custom-call | flops 4194304 | bytes 4194304 | tf_op jit(solution)/shard_map/pallas_call | solution.py:672
  17.7 1.9 %collective-permute-done.4.rxo = f32[5,8,128]{2,1,0:T(8,128)S(1)} collective-permute-done((f32[5,8,128]{2,1,0:T(8,128)S(1)}, f32[5,8,128]{2,1,0:T(8,128)S(1)}, u32[]{:S(2)}, u32[]{:S(2)}) %collective-permute-start.4) | collective-permute-done | bytes 20512 | tf_op jit(solution)/shard_map/ppermute | solution.py:693
  19.6 0.0 collective-permute-done.5.rxe
  19.6 0.0 collective-permute-done.6.ryo
  19.6 0.0 collective-permute-done.7.rye
  19.6 0.0 copy-done
  19.6 0.1 shard_map.69
  19.7 2.4 %collective-permute-start.8 = (f32[5,8,128]{2,1,0:T(8,128)S(1)}, f32[5,8,128]{2,1,0:T(8,128)S(1)}, u32[]{:S(2)}, u32[]{:S(2)}) collective-permute-start(f32[5,8,128]{2,1,0:T(8,128)S(1)} %get-tuple-element.60), channel_id=1, source_target_pairs={{0,28},{4,8},{8,4},{12,16},{16,12},{20,24},{24,20},{28,0},{1,29},{... | collective-permute-start | bytes 61448 | tf_op jit(solution)/shard_map/ppermute | solution.py:693
  22.1 0.0 collective-permute-start.9
  22.1 0.0 collective-permute-start.10
  22.1 1.6 %collective-permute-start.11 = (f32[5,8,128]{2,1,0:T(8,128)S(1)}, f32[5,8,128]{2,1,0:T(8,128)S(1)}, u32[]{:S(2)}, u32[]{:S(2)}) collective-permute-start(f32[5,8,128]{2,1,0:T(8,128)S(1)} %get-tuple-element.63), channel_id=1, source_target_pairs={{0,1},{1,0},{2,3},{3,2},{4,5},{5,4},{6,7},{7,6},{8,9},{9,8},{10,11... | collective-permute-start | bytes 61448 | tf_op jit(solution)/shard_map/ppermute | solution.py:698
  23.7 0.2 shard_map.70.c_ref
  24.0 2.3 %collective-permute-done.8.rxo = f32[5,8,128]{2,1,0:T(8,128)S(1)} collective-permute-done((f32[5,8,128]{2,1,0:T(8,128)S(1)}, f32[5,8,128]{2,1,0:T(8,128)S(1)}, u32[]{:S(2)}, u32[]{:S(2)}) %collective-permute-start.8) | collective-permute-done | bytes 20512 | tf_op jit(solution)/shard_map/ppermute | solution.py:693
  26.3 0.0 collective-permute-done.9.rxe
  26.3 0.0 collective-permute-done.10.ryo
  26.3 0.0 collective-permute-done.11.rye
  26.3 0.1 shard_map.71
  26.4 2.4 %collective-permute-start.12 = (f32[5,8,128]{2,1,0:T(8,128)S(1)}, f32[5,8,128]{2,1,0:T(8,128)S(1)}, u32[]{:S(2)}, u32[]{:S(2)}) collective-permute-start(f32[5,8,128]{2,1,0:T(8,128)S(1)} %get-tuple-element.65), channel_id=1, source_target_pairs={{0,28},{4,8},{8,4},{12,16},{16,12},{20,24},{24,20},{28,0},{1,29},{... | collective-permute-start | bytes 61448 | tf_op jit(solution)/shard_map/ppermute | solution.py:693
  28.8 0.0 collective-permute-start.13
  28.8 0.0 collective-permute-start.14
  28.8 1.6 %collective-permute-start.15 = (f32[5,8,128]{2,1,0:T(8,128)S(1)}, f32[5,8,128]{2,1,0:T(8,128)S(1)}, u32[]{:S(2)}, u32[]{:S(2)}) collective-permute-start(f32[5,8,128]{2,1,0:T(8,128)S(1)} %get-tuple-element.68), channel_id=1, source_target_pairs={{0,1},{1,0},{2,3},{3,2},{4,5},{5,4},{6,7},{7,6},{8,9},{9,8},{10,11... | collective-permute-start | bytes 61448 | tf_op jit(solution)/shard_map/ppermute | solution.py:698
  30.4 0.2 shard_map.72.c_ref
  30.6 2.3 %collective-permute-done.12.rxo = f32[5,8,128]{2,1,0:T(8,128)S(1)} collective-permute-done((f32[5,8,128]{2,1,0:T(8,128)S(1)}, f32[5,8,128]{2,1,0:T(8,128)S(1)}, u32[]{:S(2)}, u32[]{:S(2)}) %collective-permute-start.12) | collective-permute-done | bytes 20512 | tf_op jit(solution)/shard_map/ppermute | solution.py:693
  32.9 0.0 collective-permute-done.13.rxe
  32.9 0.0 collective-permute-done.14.ryo
  32.9 0.0 collective-permute-done.15.rye
  33.0 1.0 %shard_map.73 = f32[5,4,4,2,8,128]{5,4,3,2,1,0:T(8,128)} custom-call(f32[5,2,2,8,128]{4,3,2,1,0:T(8,128)S(1)} %shard_map.72.c_ref, bf16[25,2,16,128]{3,2,1,0:T(8,128)(2,1)S(1)} %bitcast.11, s32[3,8,128]{2,1,0:T(8,128)S(1)} %get-tuple-element.40.flag_ref, f32[4,25,8,128]{3,2,1,0:T(8,128)S(1)} %get-tuple-element.45.face_ref, ...), custom_call_target="tpu_custom_call" | custom-call | flops 1048576 | bytes 4194304 | tf_op jit(solution)/shard_map/pallas_call | solution.py:672
Async XLA Ops:
  1.5 7.9 %copy-start.1 = (f32[3,5,5,2,2,128]{5,4,3,2,1,0:T(2,128)S(1)}, f32[3,5,5,2,2,128]{5,4,3,2,1,0:T(2,128)}, u32[]{:S(2)}) copy-start(f32[3,5,5,2,2,128]{5,4,3,2,1,0:T(2,128)} %param.7) | copy-start | bytes 460804
  1.5 7.9 %copy-start.2 = (f32[2,2,128]{2,1,0:T(2,128)S(1)}, f32[2,2,128]{2,1,0:T(2,128)}, u32[]{:S(2)}) copy-start(f32[2,2,128]{2,1,0:T(2,128)} %param.8) | copy-start | bytes 6148
  1.6 10.4 %collective-permute-start = (f32[5,4,8,128]{3,2,1,0:T(8,128)S(1)}, f32[5,4,8,128]{3,2,1,0:T(8,128)S(1)}, u32[]{:S(2)}, u32[]{:S(2)}) collective-permute-start(f32[5,4,8,128]{3,2,1,0:T(8,128)S(1)} %get-tuple-element.46), channel_id=1, source_target_pairs={{0,28},{4,8},{8,4},{12,16},{16,12},{20,24},{24,20},{28,0},{1,29},{... | collective-permute-start | bytes 245768 | tf_op jit(solution)/shard_map/ppermute | solution.py:693
  7.6 4.4 %collective-permute-start.1 = (f32[5,4,8,128]{3,2,1,0:T(8,128)S(1)}, f32[5,4,8,128]{3,2,1,0:T(8,128)S(1)}, u32[]{:S(2)}, u32[]{:S(2)}) collective-permute-start(f32[5,4,8,128]{3,2,1,0:T(8,128)S(1)} %get-tuple-element.47), channel_id=1, source_target_pairs={{0,4},{4,0},{8,12},{12,8},{16,20},{20,16},{24,28},{28,24},{1,5},{5... | collective-permute-start | bytes 245768 | tf_op jit(solution)/shard_map/ppermute | solution.py:693
  7.7 4.7 %collective-permute-start.2 = (f32[5,4,8,128]{3,2,1,0:T(8,128)S(1)}, f32[5,4,8,128]{3,2,1,0:T(8,128)S(1)}, u32[]{:S(2)}, u32[]{:S(2)}) collective-permute-start(f32[5,4,8,128]{3,2,1,0:T(8,128)S(1)} %get-tuple-element.48), channel_id=1, source_target_pairs={{0,3},{1,2},{2,1},{3,0},{4,7},{5,6},{6,5},{7,4},{8,11},{9,10},{10,... | collective-permute-start | bytes 245768 | tf_op jit(solution)/shard_map/ppermute | solution.py:698
  8.5 4.0 %collective-permute-start.3 = (f32[5,4,8,128]{3,2,1,0:T(8,128)S(1)}, f32[5,4,8,128]{3,2,1,0:T(8,128)S(1)}, u32[]{:S(2)}, u32[]{:S(2)}) collective-permute-start(f32[5,4,8,128]{3,2,1,0:T(8,128)S(1)} %get-tuple-element.49), channel_id=1, source_target_pairs={{0,1},{1,0},{2,3},{3,2},{4,5},{5,4},{6,7},{7,6},{8,9},{9,8},{10,11... | collective-permute-start | bytes 245768 | tf_op jit(solution)/shard_map/ppermute | solution.py:698
  13.0 6.6 %copy-start = (bf16[5,5,2,2,2,2,2,128]{7,6,5,4,3,2,1,0:T(2,128)(2,1)S(1)}, bf16[5,5,2,2,2,2,2,128]{7,6,5,4,3,2,1,0:T(2,128)(2,1)}, u32[]{:S(2)}) copy-start(bf16[5,5,2,2,2,2,2,128]{7,6,5,4,3,2,1,0:T(2,128)(2,1)} %param.11) | copy-start | bytes 614404
  13.0 6.5 %collective-permute-start.4 = (f32[5,8,128]{2,1,0:T(8,128)S(1)}, f32[5,8,128]{2,1,0:T(8,128)S(1)}, u32[]{:S(2)}, u32[]{:S(2)}) collective-permute-start(f32[5,8,128]{2,1,0:T(8,128)S(1)} %get-tuple-element.54), channel_id=1, source_target_pairs={{0,28},{4,8},{8,4},{12,16},{16,12},{20,24},{24,20},{28,0},{1,29},{... | collective-permute-start | bytes 61448 | tf_op jit(solution)/shard_map/ppermute | solution.py:693
  15.4 4.2 %collective-permute-start.5 = (f32[5,8,128]{2,1,0:T(8,128)S(1)}, f32[5,8,128]{2,1,0:T(8,128)S(1)}, u32[]{:S(2)}, u32[]{:S(2)}) collective-permute-start(f32[5,8,128]{2,1,0:T(8,128)S(1)} %get-tuple-element.55), channel_id=1, source_target_pairs={{0,4},{4,0},{8,12},{12,8},{16,20},{20,16},{24,28},{28,24},{1,5},{5... | collective-permute-start | bytes 61448 | tf_op jit(solution)/shard_map/ppermute | solution.py:693
  15.4 4.2 %collective-permute-start.6 = (f32[5,8,128]{2,1,0:T(8,128)S(1)}, f32[5,8,128]{2,1,0:T(8,128)S(1)}, u32[]{:S(2)}, u32[]{:S(2)}) collective-permute-start(f32[5,8,128]{2,1,0:T(8,128)S(1)} %get-tuple-element.56), channel_id=1, source_target_pairs={{0,3},{1,2},{2,1},{3,0},{4,7},{5,6},{6,5},{7,4},{8,11},{9,10},{10,... | collective-permute-start | bytes 61448 | tf_op jit(solution)/shard_map/ppermute | solution.py:698
  15.4 4.2 %collective-permute-start.7 = (f32[5,8,128]{2,1,0:T(8,128)S(1)}, f32[5,8,128]{2,1,0:T(8,128)S(1)}, u32[]{:S(2)}, u32[]{:S(2)}) collective-permute-start(f32[5,8,128]{2,1,0:T(8,128)S(1)} %get-tuple-element.57), channel_id=1, source_target_pairs={{0,1},{1,0},{2,3},{3,2},{4,5},{5,4},{6,7},{7,6},{8,9},{9,8},{10,11... | collective-permute-start | bytes 61448 | tf_op jit(solution)/shard_map/ppermute | solution.py:698
  19.7 6.5 %collective-permute-start.8 = (f32[5,8,128]{2,1,0:T(8,128)S(1)}, f32[5,8,128]{2,1,0:T(8,128)S(1)}, u32[]{:S(2)}, u32[]{:S(2)}) collective-permute-start(f32[5,8,128]{2,1,0:T(8,128)S(1)} %get-tuple-element.60), channel_id=1, source_target_pairs={{0,28},{4,8},{8,4},{12,16},{16,12},{20,24},{24,20},{28,0},{1,29},{... | collective-permute-start | bytes 61448 | tf_op jit(solution)/shard_map/ppermute | solution.py:693
  22.1 4.2 %collective-permute-start.9 = (f32[5,8,128]{2,1,0:T(8,128)S(1)}, f32[5,8,128]{2,1,0:T(8,128)S(1)}, u32[]{:S(2)}, u32[]{:S(2)}) collective-permute-start(f32[5,8,128]{2,1,0:T(8,128)S(1)} %get-tuple-element.61), channel_id=1, source_target_pairs={{0,4},{4,0},{8,12},{12,8},{16,20},{20,16},{24,28},{28,24},{1,5},{5... | collective-permute-start | bytes 61448 | tf_op jit(solution)/shard_map/ppermute | solution.py:693
  22.1 4.2 %collective-permute-start.10 = (f32[5,8,128]{2,1,0:T(8,128)S(1)}, f32[5,8,128]{2,1,0:T(8,128)S(1)}, u32[]{:S(2)}, u32[]{:S(2)}) collective-permute-start(f32[5,8,128]{2,1,0:T(8,128)S(1)} %get-tuple-element.62), channel_id=1, source_target_pairs={{0,3},{1,2},{2,1},{3,0},{4,7},{5,6},{6,5},{7,4},{8,11},{9,10},{10,... | collective-permute-start | bytes 61448 | tf_op jit(solution)/shard_map/ppermute | solution.py:698
  22.1 4.2 %collective-permute-start.11 = (f32[5,8,128]{2,1,0:T(8,128)S(1)}, f32[5,8,128]{2,1,0:T(8,128)S(1)}, u32[]{:S(2)}, u32[]{:S(2)}) collective-permute-start(f32[5,8,128]{2,1,0:T(8,128)S(1)} %get-tuple-element.63), channel_id=1, source_target_pairs={{0,1},{1,0},{2,3},{3,2},{4,5},{5,4},{6,7},{7,6},{8,9},{9,8},{10,11... | collective-permute-start | bytes 61448 | tf_op jit(solution)/shard_map/ppermute | solution.py:698
  26.4 6.5 %collective-permute-start.12 = (f32[5,8,128]{2,1,0:T(8,128)S(1)}, f32[5,8,128]{2,1,0:T(8,128)S(1)}, u32[]{:S(2)}, u32[]{:S(2)}) collective-permute-start(f32[5,8,128]{2,1,0:T(8,128)S(1)} %get-tuple-element.65), channel_id=1, source_target_pairs={{0,28},{4,8},{8,4},{12,16},{16,12},{20,24},{24,20},{28,0},{1,29},{... | collective-permute-start | bytes 61448 | tf_op jit(solution)/shard_map/ppermute | solution.py:693
  28.8 4.2 %collective-permute-start.13 = (f32[5,8,128]{2,1,0:T(8,128)S(1)}, f32[5,8,128]{2,1,0:T(8,128)S(1)}, u32[]{:S(2)}, u32[]{:S(2)}) collective-permute-start(f32[5,8,128]{2,1,0:T(8,128)S(1)} %get-tuple-element.66), channel_id=1, source_target_pairs={{0,4},{4,0},{8,12},{12,8},{16,20},{20,16},{24,28},{28,24},{1,5},{5... | collective-permute-start | bytes 61448 | tf_op jit(solution)/shard_map/ppermute | solution.py:693
  28.8 4.2 %collective-permute-start.14 = (f32[5,8,128]{2,1,0:T(8,128)S(1)}, f32[5,8,128]{2,1,0:T(8,128)S(1)}, u32[]{:S(2)}, u32[]{:S(2)}) collective-permute-start(f32[5,8,128]{2,1,0:T(8,128)S(1)} %get-tuple-element.67), channel_id=1, source_target_pairs={{0,3},{1,2},{2,1},{3,0},{4,7},{5,6},{6,5},{7,4},{8,11},{9,10},{10,... | collective-permute-start | bytes 61448 | tf_op jit(solution)/shard_map/ppermute | solution.py:698
  28.8 4.2 %collective-permute-start.15 = (f32[5,8,128]{2,1,0:T(8,128)S(1)}, f32[5,8,128]{2,1,0:T(8,128)S(1)}, u32[]{:S(2)}, u32[]{:S(2)}) collective-permute-start(f32[5,8,128]{2,1,0:T(8,128)S(1)} %get-tuple-element.68), channel_id=1, source_target_pairs={{0,1},{1,0},{2,3},{3,2},{4,5},{5,4},{6,7},{7,6},{8,9},{9,8},{10,11... | collective-permute-start | bytes 61448 | tf_op jit(solution)/shard_map/ppermute | solution.py:698

commit v13 on v9

--- a/solution.py
+++ b/solution.py
@@ -12,6 +12,7 @@
 
 F32 = jnp.float32
 OMEGA = 0.8
+FACE_LINES = [(a, b) for a in range(4) for b in range(4) if a in (0, 3) or b in (0, 3)]
 H4 = 3.0
 ROOT = 1.0 / math.sqrt(5.0)
 NEAR = (1.0 + ROOT) / 2.0
@@ -323,7 +324,7 @@
 
 def first_volume_kernel(
     smooth_hbm, src_ref, smooth_in, u_in, flag_ref, jac_ref, damp_ref,
-    smooth_ref, u_ref, acc_ref, jac8_ref, damp8_ref, face_ref, second_ref, sem,
+    smooth_ref, u_ref, acc_ref, jac8_ref, damp8_ref, face_ref, second_ref, scaled_ref, sem,
 ):
     inner = slice(1, 3)
     copy = line_copy(smooth_hbm, smooth_ref, sem, inner, inner)
@@ -342,6 +343,11 @@
         for v in range(5):
             for q in range(2):
                 second_ref[v, a, b, q] = u_ref[v, a, b, q] + change[v][q]
+    for line, (a, b) in enumerate(FACE_LINES):
+        for k in range(25):
+            block = OMEGA * smooth_ref[k, a, b].astype(F32)
+            for q in range(2):
+                scaled_ref[line, k, q] = block[8 * q : 8 * q + 8]
 
 
 def remote_parts(even_refs, odd_refs, flag_ref, face_ref, part_ref):
@@ -380,18 +386,15 @@
 
 
 def second_kernel(
-    acc_ref, u_ref, smooth_ref, flag_ref, face_ref, rxo, rxe, ryo, rye, inner_ref, out_ref, xo, xe, yo, ye, part_ref
+    acc_ref, u_ref, scaled_ref, flag_ref, face_ref, rxo, rxe, ryo, rye, inner_ref, out_ref, xo, xe, yo, ye, part_ref
 ):
     remote_parts((rxe, rye), (rxo, ryo), flag_ref, face_ref, part_ref)
-    for a in range(4):
-        for b in range(4):
-            if a in (1, 2) and b in (1, 2):
-                continue
-            left = [[whole(acc_ref, part_ref, v, a, b, q) for q in range(2)] for v in range(5)]
-            change = smoothed(smooth_ref, left, a, b)
-            for v in range(5):
-                for q in range(2):
-                    out_ref[v, a, b, q] = u_ref[v, a, b, q] + change[v][q]
+    for line, (a, b) in enumerate(FACE_LINES):
+        for q in range(2):
+            left = [whole(acc_ref, part_ref, v, a, b, q) for v in range(5)]
+            matrix = [[scaled_ref[line, 5 * o + i, q] for i in range(5)] for o in range(5)]
+            for v, value in enumerate(mix(matrix, left)):
+                out_ref[v, a, b, q] = u_ref[v, a, b, q] + value
     restricted_faces(out_ref, flag_ref, xo, xe, yo, ye)
 
 
@@ -418,7 +421,29 @@
         put_coarse_faces(v, lows, highs, flag_ref, ((xe, xo), (ye, yo)))
 
 
-def restricted_volume_kernel(src_ref, u_ref, flag_ref, jac_ref, damp_ref, acc_ref):
+def response_kernel(smooth_ref, face_ref, response_ref):
+    packed = []
+    for k in range(25):
+        by_i = [smooth_ref[k, i].astype(F32) for i in range(2)]
+        node = [[by_i[i][8 * j : 8 * j + 8] for j in range(2)] for i in range(2)]
+        packed.append(
+            (
+                pack_high(node[1][0], node[1][1], 0),
+                pack_low(node[0][0], node[0][1], 0),
+                pack_high(node[0][1], node[1][1], 1),
+                pack_low(node[0][0], node[1][0], 1),
+            )
+        )
+    for f in range(4):
+        for o in range(5):
+            for i in range(5):
+                total = packed[5 * o][f] * face_ref[f, i]
+                for k in range(1, 5):
+                    total = total + packed[5 * o + k][f] * face_ref[f, 5 * k + i]
+                response_ref[f, 5 * o + i] = (OMEGA / 6.0) * total
+
+
+def restricted_volume_kernel(src_ref, u_ref, flag_ref, jac_ref, damp_ref, smooth_ref, acc_ref, c_ref):
     damp = H4 * damp_ref[...]
     low_c = c_low()
     slope = [
@@ -495,6 +520,19 @@
             for j in range(2):
                 for v, value in enumerate(mix(matrix, waves[d][i][j])):
                     acc_ref[v, i, j] = acc_ref[v, i, j] - value
+    c = coarse_smooth(smooth_ref, [[[acc_ref[v, i, j] for j in range(2)] for i in range(2)] for v in range(5)])
+    put_field(c_ref, c)
+
+
+def put_field(out_ref, c):
+    for v in range(5):
+        for i in range(2):
+            for j in range(2):
+                out_ref[v, i, j] = c[v][i][j]
+
+
+def get_field(ref):
+    return [[[ref[v, i, j] for j in range(2)] for i in range(2)] for v in range(5)]
 
 
 def add_remote(field, scale, flag_ref, face_ref, rxo, rxe, ryo, rye):
@@ -523,18 +561,20 @@
                 field[v][i][j] = field[v][i][j] + jnp.where(low, part, 0.0)
 
 
-def restrict_kernel(
-    acc_ref, flag_ref, face_ref, smooth_ref, rxo, rxe, ryo, rye, rhs_ref, c_ref, xo, xe, yo, ye
+def restrict_kernel(local_ref, flag_ref, response_ref, rxo, rxe, ryo, rye, c_ref, xo, xe, yo, ye):
+    c = get_field(local_ref)
+    add_remote(c, 6.0, flag_ref, response_ref, rxo, rxe, ryo, rye)
+    put_field(c_ref, c)
+    coarse_faces(c, flag_ref, xo, xe, yo, ye)
+
+
+def first_local_kernel(
+    c_ref, acc_ref, smooth_ref, flag_ref, jac_ref, damp_ref, face_ref, rxo, rxe, ryo, rye, out_ref, rhs_ref
 ):
-    rhs = [[[acc_ref[v, i, j] for j in range(2)] for i in range(2)] for v in range(5)]
+    rhs = get_field(acc_ref)
     add_remote(rhs, 1.0, flag_ref, face_ref, rxo, rxe, ryo, rye)
-    c = coarse_smooth(smooth_ref, rhs)
-    for v in range(5):
-        for i in range(2):
-            for j in range(2):
-                rhs_ref[v, i, j] = rhs[v][i][j]
-                c_ref[v, i, j] = c[v][i][j]
-    coarse_faces(c, flag_ref, xo, xe, yo, ye)
+    put_field(rhs_ref, rhs)
+    coarse_local_kernel(c_ref, rhs_ref, smooth_ref, flag_ref, jac_ref, damp_ref, out_ref)
 
 
 def coarse_local_kernel(c_ref, rhs_ref, smooth_ref, flag_ref, jac_ref, damp_ref, out_ref):
@@ -589,19 +629,10 @@
                 out_ref[v, i, j] = c[v][i][j] + change[v][i][j]
 
 
-def coarse_step(c_ref, smooth_ref, flag_ref, face_ref, rxo, rxe, ryo, rye):
-    rest = [[[0.0, 0.0], [0.0, 0.0]] for _ in range(5)]
-    add_remote(rest, 1.0 / 6.0, flag_ref, face_ref, rxo, rxe, ryo, rye)
-    change = coarse_smooth(smooth_ref, rest)
-    return [[[c_ref[v, i, j] + change[v][i][j] for j in range(2)] for i in range(2)] for v in range(5)]
-
-
-def coarse_kernel(c_ref, smooth_ref, flag_ref, face_ref, rxo, rxe, ryo, rye, out_ref, xo, xe, yo, ye):
-    c = coarse_step(c_ref, smooth_ref, flag_ref, face_ref, rxo, rxe, ryo, rye)
-    for v in range(5):
-        for i in range(2):
-            for j in range(2):
-                out_ref[v, i, j] = c[v][i][j]
+def coarse_kernel(c_ref, flag_ref, response_ref, rxo, rxe, ryo, rye, out_ref, xo, xe, yo, ye):
+    c = get_field(c_ref)
+    add_remote(c, 1.0, flag_ref, response_ref, rxo, rxe, ryo, rye)
+    put_field(out_ref, c)
     coarse_faces(c, flag_ref, xo, xe, yo, ye)
 
 
@@ -610,9 +641,10 @@
 
 
 def last_kernel(
-    c_ref, smooth_ref, flag_ref, face_ref, rxo, rxe, ryo, rye, second_ref, out_hbm, out_ref, sems
+    c_ref, flag_ref, response_ref, rxo, rxe, ryo, rye, second_ref, out_hbm, out_ref, sems
 ):
-    c = coarse_step(c_ref, smooth_ref, flag_ref, face_ref, rxo, rxe, ryo, rye)
+    c = get_field(c_ref)
+    add_remote(c, 1.0, flag_ref, response_ref, rxo, rxe, ryo, rye)
     low = c_low()
     copies = []
     for v in range(5):
@@ -685,11 +717,6 @@
     return xo, xe, yo, ye
 
 
-def local_sweep(coarse, *rest):
-    (out,) = call(coarse_local_kernel, (coarse, *rest), [vmem(COARSE)], flops=4 * 2**20)
-    return out
-
-
 def body(source, jacobian, damping, orient, smoother, coarse_smoother):
     source = source.reshape(FINE)
     smoother = smoother.reshape(25, 4, 4, 16, 128)
@@ -711,10 +738,10 @@
         flops=2 * 25 * 64 * 512,
     )
     got = exchange(*sent)
-    smoother, first, acc, jac8, damp8, face, second = call(
+    _, first, acc, jac8, damp8, face, second, scaled = call(
         first_volume_kernel,
         (smoother_in, source, smoother, first, flag, jacobian, damping),
-        [held, vmem(FINE), vmem(FINE), vmem((75, 8, 128)), vmem((8, 128)), vmem((4, 25, 8, 128)), vmem(FINE)],
+        [held, vmem(FINE), vmem(FINE), vmem((75, 8, 128)), vmem((8, 128)), vmem((4, 25, 8, 128)), vmem(FINE), vmem((12, 25, 2, 8, 128))],
         in_hbm=(0,),
         aliases={2: 0, 3: 1},
         scratch=[pltpu.SemaphoreType.DMA],
@@ -722,33 +749,40 @@
     )
     second, *sent = call(
         second_kernel,
-        (acc, first, smoother, flag, face, *got, second),
+        (acc, first, scaled, flag, face, *got, second),
         [vmem(FINE)] + coarse_messages,
         aliases={9: 0},
         scratch=[pltpu.VMEM((4, 5, 4, 2, 8, 128), F32)],
         flops=3 * 2**20,
     )
     got = exchange(*sent)
-    (acc,) = call(restricted_volume_kernel, (source, second, flag, jac8, damp8), [vmem(COARSE)], flops=4 * 2**20)
-    rhs, coarse, *sent = call(
-        restrict_kernel,
-        (acc, flag, face, coarse_smoother, *got),
-        [vmem(COARSE), vmem(COARSE)] + coarse_messages,
-        flops=2**20,
+    (response,) = call(response_kernel, (coarse_smoother, face), [vmem((4, 25, 8, 128))], flops=2**20)
+    acc, coarse = call(
+        restricted_volume_kernel,
+        (source, second, flag, jac8, damp8, coarse_smoother),
+        [vmem(COARSE), vmem(COARSE)],
+        flops=4 * 2**20,
+    )
+    coarse, *sent = call(
+        restrict_kernel, (coarse, flag, response, *got), [vmem(COARSE)] + coarse_messages, flops=2**20
+    )
+    second_got, got = got, exchange(*sent)
+    coarse, rhs = call(
+        first_local_kernel,
+        (coarse, acc, coarse_smoother, flag, jac8, damp8, face, *second_got),
+        [vmem(COARSE), vmem(COARSE)],
+        flops=4 * 2**20,
+    )
+    coarse, *sent = call(
+        coarse_kernel, (coarse, flag, response, *got), [vmem(COARSE)] + coarse_messages, flops=2**20
     )
     got = exchange(*sent)
-    coarse = local_sweep(coarse, rhs, coarse_smoother, flag, jac8, damp8)
-    coarse, *sent = call(
-        coarse_kernel,
-        (coarse, coarse_smoother, flag, face, *got),
-        [vmem(COARSE)] + coarse_messages,
-        flops=2**20,
-    )
-    got = exchange(*sent)
-    coarse = local_sweep(coarse, rhs, coarse_smoother, flag, jac8, damp8)
+    (coarse,) = call(
+        coarse_local_kernel, (coarse, rhs, coarse_smoother, flag, jac8, damp8), [vmem(COARSE)], flops=4 * 2**20
+    )
     (out,) = call(
         last_kernel,
-        (coarse, coarse_smoother, flag, face, *got, second),
+        (coarse, flag, response, *got, second),
         [jax.ShapeDtypeStruct(FINE, F32)],
         out_hbm=(0,),
         scratch=[pltpu.VMEM(FINE, F32), pltpu.SemaphoreType.DMA((5,))],

time: 34.1 us -> 33.9 us (level)
  waiting for transfers between devices: 6.47 us -> 6.01 us
    pallas_call x9 -> x10, Pallas kernels: 7.1 us -> 7.39 us  [call(): pl.pallas_call(kernel, out_shape=outs, in_specs=in_specs, out_specs=out_s...]
  transfers between devices with their start and end apart: 16 -> 16, of which waited for: 5 -> 4; matrix products, arithmetic and copies ran while one was open for 0% -> 0% of each run, Pallas kernels for 11% -> 12%
where the time goes in v13:
time: 33.9 us; the launch traced here: 33.7 us
  starting transfers between devices  20.2 us (60%)
  Pallas kernels  7.39 us (22%)
  waiting for transfers between devices  6.01 us (18%)
    ppermute x4, starting transfers between devices, exchange(): xo = lax.ppermute(xo, 'gx', odd_x)  13.7 us
    pallas_call x10, Pallas kernels, call(): pl.pallas_call(kernel, out_shape=outs, in_specs=in_specs, out_specs=out_s...  7.39 us
    ppermute x4, starting transfers between devices, exchange(): ye = lax.ppermute(ye, 'gy', even_y)  5.85 us
    ppermute x4, waiting for transfers between devices, exchange(): xo = lax.ppermute(xo, 'gx', odd_x)  5.71 us
    ppermute x4, starting transfers between devices, exchange(): yo = lax.ppermute(yo, 'gy', odd_y)  0.69 us
  transfers between devices with their start and end apart: 16, of which 4 were waited for; matrix products, arithmetic and copies ran while one was open for 0% of the time, Pallas kernels for 12%

profile of v13, /device:TPU:0, one launch (start us, length us, event | category | flops | bytes accessed | tf_op | source)
XLA Modules:
  0.0 33.7 jit_solution(13838816815262128035)
XLA Ops:
  0.0 0.0 copy-start.2
  0.0 0.0 copy-start.1
  0.0 1.7 %shard_map.64 = (f32[5,4,4,2,8,128]{5,4,3,2,1,0:T(8,128)S(1)}, bf16[25,4,4,16,128]{4,3,2,1,0:T(8,128)(2,1)S(1)}, f32[5,4,4,2,8,128]{5,4,3,2,1,0:T(8,128)S(1)}, s...) custom-call(f32[5,4,4,2,8,128]{5,4,3,2,1,0:T(8,128)} %bitcast.15, ...), custom_call_target="tpu_custom_call" | custom-call | flops 1638400 | bytes 4194304 | tf_op jit(solution)/shard_map/pallas_call | solution.py:691
  1.7 6.0 %collective-permute-start = (f32[5,4,8,128]{3,2,1,0:T(8,128)S(1)}, f32[5,4,8,128]{3,2,1,0:T(8,128)S(1)}, u32[]{:S(2)}, u32[]{:S(2)}) collective-permute-start(f32[5,4,8,128]{3,2,1,0:T(8,128)S(1)} %get-tuple-element.47), channel_id=1, source_target_pairs={{0,28},{4,8},{8,4},{12,16},{16,12},{20,24},{24,20},{28,0},{1,29},{... | collective-permute-start | bytes 245768 | tf_op jit(solution)/shard_map/ppermute | solution.py:713
  7.7 0.0 collective-permute-start.1
  7.7 0.7 %collective-permute-start.2 = (f32[5,4,8,128]{3,2,1,0:T(8,128)S(1)}, f32[5,4,8,128]{3,2,1,0:T(8,128)S(1)}, u32[]{:S(2)}, u32[]{:S(2)}) collective-permute-start(f32[5,4,8,128]{3,2,1,0:T(8,128)S(1)} %get-tuple-element.49), channel_id=1, source_target_pairs={{0,3},{1,2},{2,1},{3,0},{4,7},{5,6},{6,5},{7,4},{8,11},{9,10},{10,... | collective-permute-start | bytes 245768 | tf_op jit(solution)/shard_map/ppermute | solution.py:715
  8.4 1.0 %collective-permute-start.3 = (f32[5,4,8,128]{3,2,1,0:T(8,128)S(1)}, f32[5,4,8,128]{3,2,1,0:T(8,128)S(1)}, u32[]{:S(2)}, u32[]{:S(2)}) collective-permute-start(f32[5,4,8,128]{3,2,1,0:T(8,128)S(1)} %get-tuple-element.50), channel_id=1, source_target_pairs={{0,1},{1,0},{2,3},{3,2},{4,5},{5,4},{6,7},{7,6},{8,9},{9,8},{10,11... | collective-permute-start | bytes 245768 | tf_op jit(solution)/shard_map/ppermute | solution.py:716
  9.4 0.0 copy-done.2
  9.4 0.0 copy-done.1
  9.4 2.7 %shard_map.65 = (bf16[25,4,4,16,128]{4,3,2,1,0:T(8,128)(2,1)S(1)}, f32[5,4,4,2,8,128]{5,4,3,2,1,0:T(8,128)S(1)}, f32[5,4,4,2,8,128]{5,4,3,2,1,0:T(8,128)S(1)}, f...) custom-call(bf16[25,4,4,16,128]{4,3,2,1,0:T(8,128)(2,1)} %bitcast.14, ...), custom_call_target="tpu_custom_call", output_to_operand_aliasing={{0}: (2, {}), {1}: (3, {})} | custom-call | flops 9437184 | bytes 4194304 | tf_op jit(solution)/shard_map/pallas_call | solution.py:691
  12.1 0.0 collective-permute-done.rxo
  12.1 0.0 collective-permute-done.1.rxe
  12.2 0.2 collective-permute-done.2.ryo
  12.4 0.0 collective-permute-done.3.rye
  12.4 0.0 copy-start
  12.4 0.5 %shard_map.66 = (f32[5,4,4,2,8,128]{5,4,3,2,1,0:T(8,128)S(1)}, f32[5,8,128]{2,1,0:T(8,128)S(1)}, f32[5,8,128]{2,1,0:T(8,128)S(1)}, f32[5,8,128]{2,1,0:T(8,128)S(1)}, f32[5,8,128]{2,1,0:T(8,128)S(1)}) custom-call(f32[5,4,4,2,8,128]{5,4,3,2,1,0:T(8,128)S(1)} %get-tuple-element.43.acc_ref, ...), custom_call_target="tpu_custom_call", output_to_operand_aliasing={{0}: (9, {})} | custom-call | flops 3145728 | bytes 4194304 | tf_op jit(solution)/shard_map/pallas_call | solution.py:691
  12.9 2.6 %collective-permute-start.4 = (f32[5,8,128]{2,1,0:T(8,128)S(1)}, f32[5,8,128]{2,1,0:T(8,128)S(1)}, u32[]{:S(2)}, u32[]{:S(2)}) collective-permute-start(f32[5,8,128]{2,1,0:T(8,128)S(1)} %get-tuple-element.56), channel_id=1, source_target_pairs={{0,28},{4,8},{8,4},{12,16},{16,12},{20,24},{24,20},{28,0},{1,29},{... | collective-permute-start | bytes 61448 | tf_op jit(solution)/shard_map/ppermute | solution.py:713
  15.5 0.0 collective-permute-start.5
  15.5 0.0 collective-permute-start.6
  15.5 1.6 %collective-permute-start.7 = (f32[5,8,128]{2,1,0:T(8,128)S(1)}, f32[5,8,128]{2,1,0:T(8,128)S(1)}, u32[]{:S(2)}, u32[]{:S(2)}) collective-permute-start(f32[5,8,128]{2,1,0:T(8,128)S(1)} %get-tuple-element.59), channel_id=1, source_target_pairs={{0,1},{1,0},{2,3},{3,2},{4,5},{5,4},{6,7},{7,6},{8,9},{9,8},{10,11... | collective-permute-start | bytes 61448 | tf_op jit(solution)/shard_map/ppermute | solution.py:716
  17.1 0.0 copy-done
  17.1 0.2 shard_map.68.response_ref
  17.3 0.6 %shard_map.67 = (f32[5,2,2,8,128]{4,3,2,1,0:T(8,128)S(1)}, f32[5,2,2,8,128]{4,3,2,1,0:T(8,128)S(1)}) custom-call(f32[5,4,4,2,8,128]{5,4,3,2,1,0:T(8,128)S(1)} %get-tuple-element.39.src_ref, f32[5,4,4,2,8,128]{5,4,3,2,1,0:T(8,128)S(1)} %get-tuple-element.52.u_ref.second_ref, s32[3,8,128]{2,1,0:T(8,128)S(1)} %get-tuple-element.42.flag_ref, ...), custom_call_target="tpu_custom_call" | custom-call | flops 4194304 | bytes 4194304 | tf_op jit(solution)/shard_map/pallas_call | solution.py:691
  18.0 1.5 %collective-permute-done.4.rxo = f32[5,8,128]{2,1,0:T(8,128)S(1)} collective-permute-done((f32[5,8,128]{2,1,0:T(8,128)S(1)}, f32[5,8,128]{2,1,0:T(8,128)S(1)}, u32[]{:S(2)}, u32[]{:S(2)}) %collective-permute-start.4) | collective-permute-done | bytes 20512 | tf_op jit(solution)/shard_map/ppermute | solution.py:713
  19.5 0.0 collective-permute-done.5.rxe
  19.5 0.0 collective-permute-done.6.ryo
  19.5 0.0 collective-permute-done.7.rye
  19.5 0.1 shard_map.69
  19.6 2.5 %collective-permute-start.8 = (f32[5,8,128]{2,1,0:T(8,128)S(1)}, f32[5,8,128]{2,1,0:T(8,128)S(1)}, u32[]{:S(2)}, u32[]{:S(2)}) collective-permute-start(f32[5,8,128]{2,1,0:T(8,128)S(1)} %get-tuple-element.63), channel_id=1, source_target_pairs={{0,28},{4,8},{8,4},{12,16},{16,12},{20,24},{24,20},{28,0},{1,29},{... | collective-permute-start | bytes 61448 | tf_op jit(solution)/shard_map/ppermute | solution.py:713
  22.1 0.0 collective-permute-start.9
  22.1 0.0 collective-permute-start.10
  22.1 1.6 %collective-permute-start.11 = (f32[5,8,128]{2,1,0:T(8,128)S(1)}, f32[5,8,128]{2,1,0:T(8,128)S(1)}, u32[]{:S(2)}, u32[]{:S(2)}) collective-permute-start(f32[5,8,128]{2,1,0:T(8,128)S(1)} %get-tuple-element.66), channel_id=1, source_target_pairs={{0,1},{1,0},{2,3},{3,2},{4,5},{5,4},{6,7},{7,6},{8,9},{9,8},{10,11... | collective-permute-start | bytes 61448 | tf_op jit(solution)/shard_map/ppermute | solution.py:716
  23.8 0.3 shard_map.70
  24.1 2.1 %collective-permute-done.8.rxo = f32[5,8,128]{2,1,0:T(8,128)S(1)} collective-permute-done((f32[5,8,128]{2,1,0:T(8,128)S(1)}, f32[5,8,128]{2,1,0:T(8,128)S(1)}, u32[]{:S(2)}, u32[]{:S(2)}) %collective-permute-start.8) | collective-permute-done | bytes 20512 | tf_op jit(solution)/shard_map/ppermute | solution.py:713
  26.1 0.0 collective-permute-done.9.rxe
  26.1 0.0 collective-permute-done.10.ryo
  26.1 0.0 collective-permute-done.11.rye
  26.2 0.1 shard_map.71
  26.2 2.5 %collective-permute-start.12 = (f32[5,8,128]{2,1,0:T(8,128)S(1)}, f32[5,8,128]{2,1,0:T(8,128)S(1)}, u32[]{:S(2)}, u32[]{:S(2)}) collective-permute-start(f32[5,8,128]{2,1,0:T(8,128)S(1)} %get-tuple-element.69), channel_id=1, source_target_pairs={{0,28},{4,8},{8,4},{12,16},{16,12},{20,24},{24,20},{28,0},{1,29},{... | collective-permute-start | bytes 61448 | tf_op jit(solution)/shard_map/ppermute | solution.py:713
  28.8 0.0 collective-permute-start.13
  28.8 0.0 collective-permute-start.14
  28.8 1.6 %collective-permute-start.15 = (f32[5,8,128]{2,1,0:T(8,128)S(1)}, f32[5,8,128]{2,1,0:T(8,128)S(1)}, u32[]{:S(2)}, u32[]{:S(2)}) collective-permute-start(f32[5,8,128]{2,1,0:T(8,128)S(1)} %get-tuple-element.72), channel_id=1, source_target_pairs={{0,1},{1,0},{2,3},{3,2},{4,5},{5,4},{6,7},{7,6},{8,9},{9,8},{10,11... | collective-permute-start | bytes 61448 | tf_op jit(solution)/shard_map/ppermute | solution.py:716
  30.4 0.2 shard_map.72.c_ref
  30.7 2.1 %collective-permute-done.12.rxo = f32[5,8,128]{2,1,0:T(8,128)S(1)} collective-permute-done((f32[5,8,128]{2,1,0:T(8,128)S(1)}, f32[5,8,128]{2,1,0:T(8,128)S(1)}, u32[]{:S(2)}, u32[]{:S(2)}) %collective-permute-start.12) | collective-permute-done | bytes 20512 | tf_op jit(solution)/shard_map/ppermute | solution.py:713
  32.8 0.0 collective-permute-done.13.rxe
  32.8 0.0 collective-permute-done.14.ryo
  32.8 0.0 collective-permute-done.15.rye
  32.8 0.9 %shard_map.73 = f32[5,4,4,2,8,128]{5,4,3,2,1,0:T(8,128)} custom-call(f32[5,2,2,8,128]{4,3,2,1,0:T(8,128)S(1)} %shard_map.72.c_ref, s32[3,8,128]{2,1,0:T(8,128)S(1)} %get-tuple-element.42.flag_ref, f32[4,25,8,128]{3,2,1,0:T(8,128)S(1)} %shard_map.68.response_ref, f32[5,8,128]{2,1,0:T(8,128)S(1)} %collective-permute-done.12.rxo, ...), custom_call_target="tpu_custom_call" | custom-call | flops 1048576 | bytes 4194304 | tf_op jit(solution)/shard_map/pallas_call | solution.py:691
Async XLA Ops:
  0.0 9.4 %copy-start.2 = (f32[2,2,128]{2,1,0:T(2,128)S(1)}, f32[2,2,128]{2,1,0:T(2,128)}, u32[]{:S(2)}) copy-start(f32[2,2,128]{2,1,0:T(2,128)} %param.8) | copy-start | bytes 6148
  0.0 9.4 %copy-start.1 = (f32[3,5,5,2,2,128]{5,4,3,2,1,0:T(2,128)S(1)}, f32[3,5,5,2,2,128]{5,4,3,2,1,0:T(2,128)}, u32[]{:S(2)}) copy-start(f32[3,5,5,2,2,128]{5,4,3,2,1,0:T(2,128)} %param.7) | copy-start | bytes 460804
  1.7 10.4 %collective-permute-start = (f32[5,4,8,128]{3,2,1,0:T(8,128)S(1)}, f32[5,4,8,128]{3,2,1,0:T(8,128)S(1)}, u32[]{:S(2)}, u32[]{:S(2)}) collective-permute-start(f32[5,4,8,128]{3,2,1,0:T(8,128)S(1)} %get-tuple-element.47), channel_id=1, source_target_pairs={{0,28},{4,8},{8,4},{12,16},{16,12},{20,24},{24,20},{28,0},{1,29},{... | collective-permute-start | bytes 245768 | tf_op jit(solution)/shard_map/ppermute | solution.py:713
  7.7 4.4 %collective-permute-start.1 = (f32[5,4,8,128]{3,2,1,0:T(8,128)S(1)}, f32[5,4,8,128]{3,2,1,0:T(8,128)S(1)}, u32[]{:S(2)}, u32[]{:S(2)}) collective-permute-start(f32[5,4,8,128]{3,2,1,0:T(8,128)S(1)} %get-tuple-element.48), channel_id=1, source_target_pairs={{0,4},{4,0},{8,12},{12,8},{16,20},{20,16},{24,28},{28,24},{1,5},{5... | collective-permute-start | bytes 245768 | tf_op jit(solution)/shard_map/ppermute | solution.py:714
  7.7 4.7 %collective-permute-start.2 = (f32[5,4,8,128]{3,2,1,0:T(8,128)S(1)}, f32[5,4,8,128]{3,2,1,0:T(8,128)S(1)}, u32[]{:S(2)}, u32[]{:S(2)}) collective-permute-start(f32[5,4,8,128]{3,2,1,0:T(8,128)S(1)} %get-tuple-element.49), channel_id=1, source_target_pairs={{0,3},{1,2},{2,1},{3,0},{4,7},{5,6},{6,5},{7,4},{8,11},{9,10},{10,... | collective-permute-start | bytes 245768 | tf_op jit(solution)/shard_map/ppermute | solution.py:715
  8.4 4.0 %collective-permute-start.3 = (f32[5,4,8,128]{3,2,1,0:T(8,128)S(1)}, f32[5,4,8,128]{3,2,1,0:T(8,128)S(1)}, u32[]{:S(2)}, u32[]{:S(2)}) collective-permute-start(f32[5,4,8,128]{3,2,1,0:T(8,128)S(1)} %get-tuple-element.50), channel_id=1, source_target_pairs={{0,1},{1,0},{2,3},{3,2},{4,5},{5,4},{6,7},{7,6},{8,9},{9,8},{10,11... | collective-permute-start | bytes 245768 | tf_op jit(solution)/shard_map/ppermute | solution.py:716
  12.4 4.7 %copy-start = (bf16[5,5,2,2,2,2,2,128]{7,6,5,4,3,2,1,0:T(2,128)(2,1)S(1)}, bf16[5,5,2,2,2,2,2,128]{7,6,5,4,3,2,1,0:T(2,128)(2,1)}, u32[]{:S(2)}) copy-start(bf16[5,5,2,2,2,2,2,128]{7,6,5,4,3,2,1,0:T(2,128)(2,1)} %param.11) | copy-start | bytes 614404
  12.9 6.6 %collective-permute-start.4 = (f32[5,8,128]{2,1,0:T(8,128)S(1)}, f32[5,8,128]{2,1,0:T(8,128)S(1)}, u32[]{:S(2)}, u32[]{:S(2)}) collective-permute-start(f32[5,8,128]{2,1,0:T(8,128)S(1)} %get-tuple-element.56), channel_id=1, source_target_pairs={{0,28},{4,8},{8,4},{12,16},{16,12},{20,24},{24,20},{28,0},{1,29},{... | collective-permute-start | bytes 61448 | tf_op jit(solution)/shard_map/ppermute | solution.py:713
  15.5 4.0 %collective-permute-start.5 = (f32[5,8,128]{2,1,0:T(8,128)S(1)}, f32[5,8,128]{2,1,0:T(8,128)S(1)}, u32[]{:S(2)}, u32[]{:S(2)}) collective-permute-start(f32[5,8,128]{2,1,0:T(8,128)S(1)} %get-tuple-element.57), channel_id=1, source_target_pairs={{0,4},{4,0},{8,12},{12,8},{16,20},{20,16},{24,28},{28,24},{1,5},{5... | collective-permute-start | bytes 61448 | tf_op jit(solution)/shard_map/ppermute | solution.py:714
  15.5 4.0 %collective-permute-start.6 = (f32[5,8,128]{2,1,0:T(8,128)S(1)}, f32[5,8,128]{2,1,0:T(8,128)S(1)}, u32[]{:S(2)}, u32[]{:S(2)}) collective-permute-start(f32[5,8,128]{2,1,0:T(8,128)S(1)} %get-tuple-element.58), channel_id=1, source_target_pairs={{0,3},{1,2},{2,1},{3,0},{4,7},{5,6},{6,5},{7,4},{8,11},{9,10},{10,... | collective-permute-start | bytes 61448 | tf_op jit(solution)/shard_map/ppermute | solution.py:715
  15.5 4.0 %collective-permute-start.7 = (f32[5,8,128]{2,1,0:T(8,128)S(1)}, f32[5,8,128]{2,1,0:T(8,128)S(1)}, u32[]{:S(2)}, u32[]{:S(2)}) collective-permute-start(f32[5,8,128]{2,1,0:T(8,128)S(1)} %get-tuple-element.59), channel_id=1, source_target_pairs={{0,1},{1,0},{2,3},{3,2},{4,5},{5,4},{6,7},{7,6},{8,9},{9,8},{10,11... | collective-permute-start | bytes 61448 | tf_op jit(solution)/shard_map/ppermute | solution.py:716
  19.6 6.5 %collective-permute-start.8 = (f32[5,8,128]{2,1,0:T(8,128)S(1)}, f32[5,8,128]{2,1,0:T(8,128)S(1)}, u32[]{:S(2)}, u32[]{:S(2)}) collective-permute-start(f32[5,8,128]{2,1,0:T(8,128)S(1)} %get-tuple-element.63), channel_id=1, source_target_pairs={{0,28},{4,8},{8,4},{12,16},{16,12},{20,24},{24,20},{28,0},{1,29},{... | collective-permute-start | bytes 61448 | tf_op jit(solution)/shard_map/ppermute | solution.py:713
  22.1 4.0 %collective-permute-start.9 = (f32[5,8,128]{2,1,0:T(8,128)S(1)}, f32[5,8,128]{2,1,0:T(8,128)S(1)}, u32[]{:S(2)}, u32[]{:S(2)}) collective-permute-start(f32[5,8,128]{2,1,0:T(8,128)S(1)} %get-tuple-element.64), channel_id=1, source_target_pairs={{0,4},{4,0},{8,12},{12,8},{16,20},{20,16},{24,28},{28,24},{1,5},{5... | collective-permute-start | bytes 61448 | tf_op jit(solution)/shard_map/ppermute | solution.py:714
  22.1 4.0 %collective-permute-start.10 = (f32[5,8,128]{2,1,0:T(8,128)S(1)}, f32[5,8,128]{2,1,0:T(8,128)S(1)}, u32[]{:S(2)}, u32[]{:S(2)}) collective-permute-start(f32[5,8,128]{2,1,0:T(8,128)S(1)} %get-tuple-element.65), channel_id=1, source_target_pairs={{0,3},{1,2},{2,1},{3,0},{4,7},{5,6},{6,5},{7,4},{8,11},{9,10},{10,... | collective-permute-start | bytes 61448 | tf_op jit(solution)/shard_map/ppermute | solution.py:715
  22.1 4.0 %collective-permute-start.11 = (f32[5,8,128]{2,1,0:T(8,128)S(1)}, f32[5,8,128]{2,1,0:T(8,128)S(1)}, u32[]{:S(2)}, u32[]{:S(2)}) collective-permute-start(f32[5,8,128]{2,1,0:T(8,128)S(1)} %get-tuple-element.66), channel_id=1, source_target_pairs={{0,1},{1,0},{2,3},{3,2},{4,5},{5,4},{6,7},{7,6},{8,9},{9,8},{10,11... | collective-permute-start | bytes 61448 | tf_op jit(solution)/shard_map/ppermute | solution.py:716
  26.2 6.5 %collective-permute-start.12 = (f32[5,8,128]{2,1,0:T(8,128)S(1)}, f32[5,8,128]{2,1,0:T(8,128)S(1)}, u32[]{:S(2)}, u32[]{:S(2)}) collective-permute-start(f32[5,8,128]{2,1,0:T(8,128)S(1)} %get-tuple-element.69), channel_id=1, source_target_pairs={{0,28},{4,8},{8,4},{12,16},{16,12},{20,24},{24,20},{28,0},{1,29},{... | collective-permute-start | bytes 61448 | tf_op jit(solution)/shard_map/ppermute | solution.py:713
  28.8 4.0 %collective-permute-start.13 = (f32[5,8,128]{2,1,0:T(8,128)S(1)}, f32[5,8,128]{2,1,0:T(8,128)S(1)}, u32[]{:S(2)}, u32[]{:S(2)}) collective-permute-start(f32[5,8,128]{2,1,0:T(8,128)S(1)} %get-tuple-element.70), channel_id=1, source_target_pairs={{0,4},{4,0},{8,12},{12,8},{16,20},{20,16},{24,28},{28,24},{1,5},{5... | collective-permute-start | bytes 61448 | tf_op jit(solution)/shard_map/ppermute | solution.py:714
  28.8 4.0 %collective-permute-start.14 = (f32[5,8,128]{2,1,0:T(8,128)S(1)}, f32[5,8,128]{2,1,0:T(8,128)S(1)}, u32[]{:S(2)}, u32[]{:S(2)}) collective-permute-start(f32[5,8,128]{2,1,0:T(8,128)S(1)} %get-tuple-element.71), channel_id=1, source_target_pairs={{0,3},{1,2},{2,1},{3,0},{4,7},{5,6},{6,5},{7,4},{8,11},{9,10},{10,... | collective-permute-start | bytes 61448 | tf_op jit(solution)/shard_map/ppermute | solution.py:715
  28.8 4.0 %collective-permute-start.15 = (f32[5,8,128]{2,1,0:T(8,128)S(1)}, f32[5,8,128]{2,1,0:T(8,128)S(1)}, u32[]{:S(2)}, u32[]{:S(2)}) collective-permute-start(f32[5,8,128]{2,1,0:T(8,128)S(1)} %get-tuple-element.72), channel_id=1, source_target_pairs={{0,1},{1,0},{2,3},{3,2},{4,5},{5,4},{6,7},{7,6},{8,9},{9,8},{10,11... | collective-permute-start | bytes 61448 | tf_op jit(solution)/shard_map/ppermute | solution.py:716

commit v14 on v13

--- a/solution.py
+++ b/solution.py
@@ -350,51 +350,55 @@
                 scaled_ref[line, k, q] = block[8 * q : 8 * q + 8]
 
 
-def remote_parts(even_refs, odd_refs, flag_ref, face_ref, part_ref):
-    for d, axis in ((0, "gx"), (1, "gy")):
-        is_even = parity(axis)
-        low, step = axis_low(d)
-        flag = flag_ref[d]
-        flag = jnp.where(low, sroll(flag, -step), flag) != 0
-        even, odd = even_refs[d], odd_refs[d]
-        matrix = [[face_ref[2 * d, 5 * o + i] for i in range(5)] for o in range(5)]
-        for n in range(4):
-            take = lambda v, m: jnp.where(is_even, even[v, m], odd[v, m])
-            right = [jnp.where(flag, take(v, 3 - n), take(v, n)) for v in range(5)]
-            for v, value in enumerate(mix(matrix, right)):
-                part_ref[2 * d, v, n, 0] = jnp.where(low, 0.0, -sroll(value, step))
-                part_ref[2 * d, v, n, 1] = jnp.where(low, 0.0, -value)
-        matrix = [[face_ref[2 * d + 1, 5 * o + i] for i in range(5)] for o in range(5)]
-        for n in range(4):
-            left = [jnp.where(is_even, odd[v, n], even[v, n]) for v in range(5)]
-            for v, value in enumerate(mix(matrix, left)):
-                part_ref[2 * d + 1, v, n, 0] = jnp.where(low, value, 0.0)
-                part_ref[2 * d + 1, v, n, 1] = jnp.where(low, sroll(value, -step), 0.0)
-
-
-def whole(acc_ref, part_ref, v, a, b, q):
-    total = acc_ref[v, a, b, q]
-    if a == 3:
-        total = total + part_ref[0, v, b, q]
-    if a == 0:
-        total = total + part_ref[1, v, b, q]
-    if b == 3:
-        total = total + part_ref[2, v, a, q]
-    if b == 0:
-        total = total + part_ref[3, v, a, q]
-    return total
-
-
-def second_kernel(
-    acc_ref, u_ref, scaled_ref, flag_ref, face_ref, rxo, rxe, ryo, rye, inner_ref, out_ref, xo, xe, yo, ye, part_ref
-):
-    remote_parts((rxe, rye), (rxo, ryo), flag_ref, face_ref, part_ref)
-    for line, (a, b) in enumerate(FACE_LINES):
+def remote_parts(d, odd, even, flag_ref, face_ref, part_ref):
+    is_even = parity(("gx", "gy")[d])
+    low, step = axis_low(d)
+    flag = flag_ref[d]
+    flag = jnp.where(low, sroll(flag, -step), flag) != 0
+    matrix = [[face_ref[2 * d, 5 * o + i] for i in range(5)] for o in range(5)]
+    for n in range(4):
+        take = lambda v, m: jnp.where(is_even, even[v, m], odd[v, m])
+        right = [jnp.where(flag, take(v, 3 - n), take(v, n)) for v in range(5)]
+        for v, value in enumerate(mix(matrix, right)):
+            part_ref[0, v, n, 0] = jnp.where(low, 0.0, -sroll(value, step))
+            part_ref[0, v, n, 1] = jnp.where(low, 0.0, -value)
+    matrix = [[face_ref[2 * d + 1, 5 * o + i] for i in range(5)] for o in range(5)]
+    for n in range(4):
+        left = [jnp.where(is_even, odd[v, n], even[v, n]) for v in range(5)]
+        for v, value in enumerate(mix(matrix, left)):
+            part_ref[1, v, n, 0] = jnp.where(low, value, 0.0)
+            part_ref[1, v, n, 1] = jnp.where(low, sroll(value, -step), 0.0)
+
+
+def second_lines(lines, acc_ref, x_part_ref, y_part_ref, scaled_ref, u_ref, out_ref):
+    for a, b in lines:
+        line = FACE_LINES.index((a, b))
         for q in range(2):
-            left = [whole(acc_ref, part_ref, v, a, b, q) for v in range(5)]
+            left = [acc_ref[v, a, b, q] for v in range(5)]
+            for v in range(5):
+                if a in (0, 3):
+                    left[v] = left[v] + x_part_ref[0 if a == 3 else 1, v, b, q]
+                if b in (0, 3):
+                    left[v] = left[v] + y_part_ref[0 if b == 3 else 1, v, a, q]
             matrix = [[scaled_ref[line, 5 * o + i, q] for i in range(5)] for o in range(5)]
             for v, value in enumerate(mix(matrix, left)):
                 out_ref[v, a, b, q] = u_ref[v, a, b, q] + value
+
+
+X_LINES = [(a, b) for a in (0, 3) for b in (1, 2)]
+
+
+def second_x_kernel(acc_ref, u_ref, scaled_ref, flag_ref, face_ref, rxo, rxe, inner_ref, out_ref, part_ref):
+    remote_parts(0, rxo, rxe, flag_ref, face_ref, part_ref)
+    second_lines(X_LINES, acc_ref, part_ref, None, scaled_ref, u_ref, out_ref)
+
+
+def second_kernel(
+    acc_ref, u_ref, scaled_ref, flag_ref, face_ref, ryo, rye, x_part_ref, held_ref, out_ref, xo, xe, yo, ye, part_ref
+):
+    remote_parts(1, ryo, rye, flag_ref, face_ref, part_ref)
+    lines = [line for line in FACE_LINES if line not in X_LINES]
+    second_lines(lines, acc_ref, x_part_ref, part_ref, scaled_ref, u_ref, out_ref)
     restricted_faces(out_ref, flag_ref, xo, xe, yo, ye)
 
 
@@ -747,13 +751,21 @@
         scratch=[pltpu.SemaphoreType.DMA],
         flops=9 * 2**20,
     )
+    part = vmem((2, 5, 4, 2, 8, 128))
+    second, x_part = call(
+        second_x_kernel,
+        (acc, first, scaled, flag, face, *got[:2], second),
+        [vmem(FINE), part],
+        aliases={7: 0},
+        flops=2**20,
+    )
     second, *sent = call(
         second_kernel,
-        (acc, first, scaled, flag, face, *got, second),
+        (acc, first, scaled, flag, face, *got[2:], x_part, second),
         [vmem(FINE)] + coarse_messages,
-        aliases={9: 0},
-        scratch=[pltpu.VMEM((4, 5, 4, 2, 8, 128), F32)],
-        flops=3 * 2**20,
+        aliases={8: 0},
+        scratch=[pltpu.VMEM((2, 5, 4, 2, 8, 128), F32)],
+        flops=2 * 2**20,
     )
     got = exchange(*sent)
     (response,) = call(response_kernel, (coarse_smoother, face), [vmem((4, 25, 8, 128))], flops=2**20)

time: 33.9 us -> 33.9 us (level)
    pallas_call x10 -> x11, Pallas kernels: 7.39 us -> 7.35 us  [call(): pl.pallas_call(kernel, out_shape=outs, in_specs=in_specs, out_specs=out_s...]
  transfers between devices with their start and end apart: 16 -> 16, of which waited for: 4 -> 6; matrix products, arithmetic and copies ran while one was open for 0% -> 0% of each run, Pallas kernels for 12% -> 13%
where the time goes in v14:
time: 33.9 us; the launch traced here: 33.7 us
  starting transfers between devices  20.4 us (60%)
  Pallas kernels  7.35 us (22%)
  waiting for transfers between devices  5.85 us (17%)
    ppermute x4, starting transfers between devices, exchange(): xo = lax.ppermute(xo, 'gx', odd_x)  13.9 us
    pallas_call x11, Pallas kernels, call(): pl.pallas_call(kernel, out_shape=outs, in_specs=in_specs, out_specs=out_s...  7.35 us
    ppermute x4, starting transfers between devices, exchange(): ye = lax.ppermute(ye, 'gy', even_y)  5.85 us
    ppermute x4, waiting for transfers between devices, exchange(): xo = lax.ppermute(xo, 'gx', odd_x)  5.62 us
    ppermute x4, starting transfers between devices, exchange(): yo = lax.ppermute(yo, 'gy', odd_y)  0.69 us
  transfers between devices with their start and end apart: 16, of which 6 were waited for; matrix products, arithmetic and copies ran while one was open for 0% of the time, Pallas kernels for 13%

profile of v14, /device:TPU:0, one launch (start us, length us, event | category | flops | bytes accessed | tf_op | source)
XLA Modules:
  0.0 33.7 jit_solution(5416003161390589386)
XLA Ops:
  0.0 0.0 copy-start.2
  0.0 0.0 copy-start.1
  0.0 1.7 %shard_map.64 = (f32[5,4,4,2,8,128]{5,4,3,2,1,0:T(8,128)S(1)}, bf16[25,4,4,16,128]{4,3,2,1,0:T(8,128)(2,1)S(1)}, f32[5,4,4,2,8,128]{5,4,3,2,1,0:T(8,128)S(1)}, s...) custom-call(f32[5,4,4,2,8,128]{5,4,3,2,1,0:T(8,128)} %bitcast.15, ...), custom_call_target="tpu_custom_call" | custom-call | flops 1638400 | bytes 4194304 | tf_op jit(solution)/shard_map/pallas_call | solution.py:695
  1.7 6.0 %collective-permute-start.2 = (f32[5,4,8,128]{3,2,1,0:T(8,128)S(1)}, f32[5,4,8,128]{3,2,1,0:T(8,128)S(1)}, u32[]{:S(2)}, u32[]{:S(2)}) collective-permute-start(f32[5,4,8,128]{3,2,1,0:T(8,128)S(1)} %get-tuple-element.51), channel_id=1, source_target_pairs={{0,28},{4,8},{8,4},{12,16},{16,12},{20,24},{24,20},{28,0},{1,29},{... | collective-permute-start | bytes 245768 | tf_op jit(solution)/shard_map/ppermute | solution.py:717
  7.7 0.0 collective-permute-start.3
  7.7 0.7 %collective-permute-start = (f32[5,4,8,128]{3,2,1,0:T(8,128)S(1)}, f32[5,4,8,128]{3,2,1,0:T(8,128)S(1)}, u32[]{:S(2)}, u32[]{:S(2)}) collective-permute-start(f32[5,4,8,128]{3,2,1,0:T(8,128)S(1)} %get-tuple-element.49), channel_id=1, source_target_pairs={{0,3},{1,2},{2,1},{3,0},{4,7},{5,6},{6,5},{7,4},{8,11},{9,10},{10,... | collective-permute-start | bytes 245768 | tf_op jit(solution)/shard_map/ppermute | solution.py:719
  8.4 1.0 %collective-permute-start.1 = (f32[5,4,8,128]{3,2,1,0:T(8,128)S(1)}, f32[5,4,8,128]{3,2,1,0:T(8,128)S(1)}, u32[]{:S(2)}, u32[]{:S(2)}) collective-permute-start(f32[5,4,8,128]{3,2,1,0:T(8,128)S(1)} %get-tuple-element.50), channel_id=1, source_target_pairs={{0,1},{1,0},{2,3},{3,2},{4,5},{5,4},{6,7},{7,6},{8,9},{9,8},{10,11... | collective-permute-start | bytes 245768 | tf_op jit(solution)/shard_map/ppermute | solution.py:720
  9.4 0.0 copy-done.2
  9.4 0.0 copy-done.1
  9.4 2.7 %shard_map.65 = (bf16[25,4,4,16,128]{4,3,2,1,0:T(8,128)(2,1)S(1)}, f32[5,4,4,2,8,128]{5,4,3,2,1,0:T(8,128)S(1)}, f32[5,4,4,2,8,128]{5,4,3,2,1,0:T(8,128)S(1)}, f...) custom-call(bf16[25,4,4,16,128]{4,3,2,1,0:T(8,128)(2,1)} %bitcast.14, ...), custom_call_target="tpu_custom_call", output_to_operand_aliasing={{0}: (2, {}), {1}: (3, {})} | custom-call | flops 9437184 | bytes 4194304 | tf_op jit(solution)/shard_map/pallas_call | solution.py:695
  12.1 0.0 collective-permute-done.2.rxo
  12.1 0.1 collective-permute-done.3.rxe
  12.2 0.2 shard_map.66
  12.3 0.1 collective-permute-done.ryo
  12.4 0.0 collective-permute-done.1.rye
  12.4 0.0 copy-start
  12.4 0.3 shard_map.67
  12.8 2.7 %collective-permute-start.4 = (f32[5,8,128]{2,1,0:T(8,128)S(1)}, f32[5,8,128]{2,1,0:T(8,128)S(1)}, u32[]{:S(2)}, u32[]{:S(2)}) collective-permute-start(f32[5,8,128]{2,1,0:T(8,128)S(1)} %get-tuple-element.60), channel_id=1, source_target_pairs={{0,28},{4,8},{8,4},{12,16},{16,12},{20,24},{24,20},{28,0},{1,29},{... | collective-permute-start | bytes 61448 | tf_op jit(solution)/shard_map/ppermute | solution.py:717
  15.5 0.0 collective-permute-start.5
  15.5 0.0 collective-permute-start.6
  15.5 1.6 %collective-permute-start.7 = (f32[5,8,128]{2,1,0:T(8,128)S(1)}, f32[5,8,128]{2,1,0:T(8,128)S(1)}, u32[]{:S(2)}, u32[]{:S(2)}) collective-permute-start(f32[5,8,128]{2,1,0:T(8,128)S(1)} %get-tuple-element.63), channel_id=1, source_target_pairs={{0,1},{1,0},{2,3},{3,2},{4,5},{5,4},{6,7},{7,6},{8,9},{9,8},{10,11... | collective-permute-start | bytes 61448 | tf_op jit(solution)/shard_map/ppermute | solution.py:720
  17.1 0.0 copy-done
  17.1 0.2 shard_map.69.response_ref
  17.3 0.6 %shard_map.68 = (f32[5,2,2,8,128]{4,3,2,1,0:T(8,128)S(1)}, f32[5,2,2,8,128]{4,3,2,1,0:T(8,128)S(1)}) custom-call(f32[5,4,4,2,8,128]{5,4,3,2,1,0:T(8,128)S(1)} %get-tuple-element.41.src_ref, f32[5,4,4,2,8,128]{5,4,3,2,1,0:T(8,128)S(1)} %get-tuple-element.56.u_ref.second_ref, s32[3,8,128]{2,1,0:T(8,128)S(1)} %get-tuple-element.44.flag_ref, ...), custom_call_target="tpu_custom_call" | custom-call | flops 4194304 | bytes 4194304 | tf_op jit(solution)/shard_map/pallas_call | solution.py:695
  18.0 1.4 %collective-permute-done.4.rxo = f32[5,8,128]{2,1,0:T(8,128)S(1)} collective-permute-done((f32[5,8,128]{2,1,0:T(8,128)S(1)}, f32[5,8,128]{2,1,0:T(8,128)S(1)}, u32[]{:S(2)}, u32[]{:S(2)}) %collective-permute-start.4) | collective-permute-done | bytes 20512 | tf_op jit(solution)/shard_map/ppermute | solution.py:717
  19.4 0.1 collective-permute-done.5.rxe
  19.5 0.0 collective-permute-done.6.ryo
  19.5 0.0 collective-permute-done.7.rye
  19.5 0.1 shard_map.70
  19.6 2.6 %collective-permute-start.8 = (f32[5,8,128]{2,1,0:T(8,128)S(1)}, f32[5,8,128]{2,1,0:T(8,128)S(1)}, u32[]{:S(2)}, u32[]{:S(2)}) collective-permute-start(f32[5,8,128]{2,1,0:T(8,128)S(1)} %get-tuple-element.67), channel_id=1, source_target_pairs={{0,28},{4,8},{8,4},{12,16},{16,12},{20,24},{24,20},{28,0},{1,29},{... | collective-permute-start | bytes 61448 | tf_op jit(solution)/shard_map/ppermute | solution.py:717
  22.1 0.0 collective-permute-start.9
  22.1 0.0 collective-permute-start.10
  22.1 1.6 %collective-permute-start.11 = (f32[5,8,128]{2,1,0:T(8,128)S(1)}, f32[5,8,128]{2,1,0:T(8,128)S(1)}, u32[]{:S(2)}, u32[]{:S(2)}) collective-permute-start(f32[5,8,128]{2,1,0:T(8,128)S(1)} %get-tuple-element.70), channel_id=1, source_target_pairs={{0,1},{1,0},{2,3},{3,2},{4,5},{5,4},{6,7},{7,6},{8,9},{9,8},{10,11... | collective-permute-start | bytes 61448 | tf_op jit(solution)/shard_map/ppermute | solution.py:720
  23.8 0.3 shard_map.71
  24.1 2.1 %collective-permute-done.8.rxo = f32[5,8,128]{2,1,0:T(8,128)S(1)} collective-permute-done((f32[5,8,128]{2,1,0:T(8,128)S(1)}, f32[5,8,128]{2,1,0:T(8,128)S(1)}, u32[]{:S(2)}, u32[]{:S(2)}) %collective-permute-start.8) | collective-permute-done | bytes 20512 | tf_op jit(solution)/shard_map/ppermute | solution.py:717
  26.1 0.0 collective-permute-done.9.rxe
  26.1 0.0 collective-permute-done.10.ryo
  26.1 0.0 collective-permute-done.11.rye
  26.1 0.1 shard_map.72
  26.2 2.5 %collective-permute-start.12 = (f32[5,8,128]{2,1,0:T(8,128)S(1)}, f32[5,8,128]{2,1,0:T(8,128)S(1)}, u32[]{:S(2)}, u32[]{:S(2)}) collective-permute-start(f32[5,8,128]{2,1,0:T(8,128)S(1)} %get-tuple-element.73), channel_id=1, source_target_pairs={{0,28},{4,8},{8,4},{12,16},{16,12},{20,24},{24,20},{28,0},{1,29},{... | collective-permute-start | bytes 61448 | tf_op jit(solution)/shard_map/ppermute | solution.py:717
  28.8 0.0 collective-permute-start.13
  28.8 0.0 collective-permute-start.14
  28.8 1.6 %collective-permute-start.15 = (f32[5,8,128]{2,1,0:T(8,128)S(1)}, f32[5,8,128]{2,1,0:T(8,128)S(1)}, u32[]{:S(2)}, u32[]{:S(2)}) collective-permute-start(f32[5,8,128]{2,1,0:T(8,128)S(1)} %get-tuple-element.76), channel_id=1, source_target_pairs={{0,1},{1,0},{2,3},{3,2},{4,5},{5,4},{6,7},{7,6},{8,9},{9,8},{10,11... | collective-permute-start | bytes 61448 | tf_op jit(solution)/shard_map/ppermute | solution.py:720
  30.4 0.2 shard_map.73.c_ref
  30.6 2.1 %collective-permute-done.12.rxo = f32[5,8,128]{2,1,0:T(8,128)S(1)} collective-permute-done((f32[5,8,128]{2,1,0:T(8,128)S(1)}, f32[5,8,128]{2,1,0:T(8,128)S(1)}, u32[]{:S(2)}, u32[]{:S(2)}) %collective-permute-start.12) | collective-permute-done | bytes 20512 | tf_op jit(solution)/shard_map/ppermute | solution.py:717
  32.8 0.0 collective-permute-done.13.rxe
  32.8 0.0 collective-permute-done.14.ryo
  32.8 0.0 collective-permute-done.15.rye
  32.8 0.9 %shard_map.74 = f32[5,4,4,2,8,128]{5,4,3,2,1,0:T(8,128)} custom-call(f32[5,2,2,8,128]{4,3,2,1,0:T(8,128)S(1)} %shard_map.73.c_ref, s32[3,8,128]{2,1,0:T(8,128)S(1)} %get-tuple-element.44.flag_ref, f32[4,25,8,128]{3,2,1,0:T(8,128)S(1)} %shard_map.69.response_ref, f32[5,8,128]{2,1,0:T(8,128)S(1)} %collective-permute-done.12.rxo, ...), custom_call_target="tpu_custom_call" | custom-call | flops 1048576 | bytes 4194304 | tf_op jit(solution)/shard_map/pallas_call | solution.py:695
Async XLA Ops:
  0.0 9.4 %copy-start.2 = (f32[2,2,128]{2,1,0:T(2,128)S(1)}, f32[2,2,128]{2,1,0:T(2,128)}, u32[]{:S(2)}) copy-start(f32[2,2,128]{2,1,0:T(2,128)} %param.8) | copy-start | bytes 6148
  0.0 9.4 %copy-start.1 = (f32[3,5,5,2,2,128]{5,4,3,2,1,0:T(2,128)S(1)}, f32[3,5,5,2,2,128]{5,4,3,2,1,0:T(2,128)}, u32[]{:S(2)}) copy-start(f32[3,5,5,2,2,128]{5,4,3,2,1,0:T(2,128)} %param.7) | copy-start | bytes 460804
  1.7 10.4 %collective-permute-start.2 = (f32[5,4,8,128]{3,2,1,0:T(8,128)S(1)}, f32[5,4,8,128]{3,2,1,0:T(8,128)S(1)}, u32[]{:S(2)}, u32[]{:S(2)}) collective-permute-start(f32[5,4,8,128]{3,2,1,0:T(8,128)S(1)} %get-tuple-element.51), channel_id=1, source_target_pairs={{0,28},{4,8},{8,4},{12,16},{16,12},{20,24},{24,20},{28,0},{1,29},{... | collective-permute-start | bytes 245768 | tf_op jit(solution)/shard_map/ppermute | solution.py:717
  7.7 4.4 %collective-permute-start.3 = (f32[5,4,8,128]{3,2,1,0:T(8,128)S(1)}, f32[5,4,8,128]{3,2,1,0:T(8,128)S(1)}, u32[]{:S(2)}, u32[]{:S(2)}) collective-permute-start(f32[5,4,8,128]{3,2,1,0:T(8,128)S(1)} %get-tuple-element.52), channel_id=1, source_target_pairs={{0,4},{4,0},{8,12},{12,8},{16,20},{20,16},{24,28},{28,24},{1,5},{5... | collective-permute-start | bytes 245768 | tf_op jit(solution)/shard_map/ppermute | solution.py:718
  7.7 4.7 %collective-permute-start = (f32[5,4,8,128]{3,2,1,0:T(8,128)S(1)}, f32[5,4,8,128]{3,2,1,0:T(8,128)S(1)}, u32[]{:S(2)}, u32[]{:S(2)}) collective-permute-start(f32[5,4,8,128]{3,2,1,0:T(8,128)S(1)} %get-tuple-element.49), channel_id=1, source_target_pairs={{0,3},{1,2},{2,1},{3,0},{4,7},{5,6},{6,5},{7,4},{8,11},{9,10},{10,... | collective-permute-start | bytes 245768 | tf_op jit(solution)/shard_map/ppermute | solution.py:719
  8.4 4.0 %collective-permute-start.1 = (f32[5,4,8,128]{3,2,1,0:T(8,128)S(1)}, f32[5,4,8,128]{3,2,1,0:T(8,128)S(1)}, u32[]{:S(2)}, u32[]{:S(2)}) collective-permute-start(f32[5,4,8,128]{3,2,1,0:T(8,128)S(1)} %get-tuple-element.50), channel_id=1, source_target_pairs={{0,1},{1,0},{2,3},{3,2},{4,5},{5,4},{6,7},{7,6},{8,9},{9,8},{10,11... | collective-permute-start | bytes 245768 | tf_op jit(solution)/shard_map/ppermute | solution.py:720
  12.4 4.7 %copy-start = (bf16[5,5,2,2,2,2,2,128]{7,6,5,4,3,2,1,0:T(2,128)(2,1)S(1)}, bf16[5,5,2,2,2,2,2,128]{7,6,5,4,3,2,1,0:T(2,128)(2,1)}, u32[]{:S(2)}) copy-start(bf16[5,5,2,2,2,2,2,128]{7,6,5,4,3,2,1,0:T(2,128)(2,1)} %param.11) | copy-start | bytes 614404
  12.8 6.7 %collective-permute-start.4 = (f32[5,8,128]{2,1,0:T(8,128)S(1)}, f32[5,8,128]{2,1,0:T(8,128)S(1)}, u32[]{:S(2)}, u32[]{:S(2)}) collective-permute-start(f32[5,8,128]{2,1,0:T(8,128)S(1)} %get-tuple-element.60), channel_id=1, source_target_pairs={{0,28},{4,8},{8,4},{12,16},{16,12},{20,24},{24,20},{28,0},{1,29},{... | collective-permute-start | bytes 61448 | tf_op jit(solution)/shard_map/ppermute | solution.py:717
  15.5 4.0 %collective-permute-start.5 = (f32[5,8,128]{2,1,0:T(8,128)S(1)}, f32[5,8,128]{2,1,0:T(8,128)S(1)}, u32[]{:S(2)}, u32[]{:S(2)}) collective-permute-start(f32[5,8,128]{2,1,0:T(8,128)S(1)} %get-tuple-element.61), channel_id=1, source_target_pairs={{0,4},{4,0},{8,12},{12,8},{16,20},{20,16},{24,28},{28,24},{1,5},{5... | collective-permute-start | bytes 61448 | tf_op jit(solution)/shard_map/ppermute | solution.py:718
  15.5 4.0 %collective-permute-start.6 = (f32[5,8,128]{2,1,0:T(8,128)S(1)}, f32[5,8,128]{2,1,0:T(8,128)S(1)}, u32[]{:S(2)}, u32[]{:S(2)}) collective-permute-start(f32[5,8,128]{2,1,0:T(8,128)S(1)} %get-tuple-element.62), channel_id=1, source_target_pairs={{0,3},{1,2},{2,1},{3,0},{4,7},{5,6},{6,5},{7,4},{8,11},{9,10},{10,... | collective-permute-start | bytes 61448 | tf_op jit(solution)/shard_map/ppermute | solution.py:719
  15.5 4.0 %collective-permute-start.7 = (f32[5,8,128]{2,1,0:T(8,128)S(1)}, f32[5,8,128]{2,1,0:T(8,128)S(1)}, u32[]{:S(2)}, u32[]{:S(2)}) collective-permute-start(f32[5,8,128]{2,1,0:T(8,128)S(1)} %get-tuple-element.63), channel_id=1, source_target_pairs={{0,1},{1,0},{2,3},{3,2},{4,5},{5,4},{6,7},{7,6},{8,9},{9,8},{10,11... | collective-permute-start | bytes 61448 | tf_op jit(solution)/shard_map/ppermute | solution.py:720
  19.6 6.6 %collective-permute-start.8 = (f32[5,8,128]{2,1,0:T(8,128)S(1)}, f32[5,8,128]{2,1,0:T(8,128)S(1)}, u32[]{:S(2)}, u32[]{:S(2)}) collective-permute-start(f32[5,8,128]{2,1,0:T(8,128)S(1)} %get-tuple-element.67), channel_id=1, source_target_pairs={{0,28},{4,8},{8,4},{12,16},{16,12},{20,24},{24,20},{28,0},{1,29},{... | collective-permute-start | bytes 61448 | tf_op jit(solution)/shard_map/ppermute | solution.py:717
  22.1 4.0 %collective-permute-start.9 = (f32[5,8,128]{2,1,0:T(8,128)S(1)}, f32[5,8,128]{2,1,0:T(8,128)S(1)}, u32[]{:S(2)}, u32[]{:S(2)}) collective-permute-start(f32[5,8,128]{2,1,0:T(8,128)S(1)} %get-tuple-element.68), channel_id=1, source_target_pairs={{0,4},{4,0},{8,12},{12,8},{16,20},{20,16},{24,28},{28,24},{1,5},{5... | collective-permute-start | bytes 61448 | tf_op jit(solution)/shard_map/ppermute | solution.py:718
  22.1 4.0 %collective-permute-start.10 = (f32[5,8,128]{2,1,0:T(8,128)S(1)}, f32[5,8,128]{2,1,0:T(8,128)S(1)}, u32[]{:S(2)}, u32[]{:S(2)}) collective-permute-start(f32[5,8,128]{2,1,0:T(8,128)S(1)} %get-tuple-element.69), channel_id=1, source_target_pairs={{0,3},{1,2},{2,1},{3,0},{4,7},{5,6},{6,5},{7,4},{8,11},{9,10},{10,... | collective-permute-start | bytes 61448 | tf_op jit(solution)/shard_map/ppermute | solution.py:719
  22.1 4.0 %collective-permute-start.11 = (f32[5,8,128]{2,1,0:T(8,128)S(1)}, f32[5,8,128]{2,1,0:T(8,128)S(1)}, u32[]{:S(2)}, u32[]{:S(2)}) collective-permute-start(f32[5,8,128]{2,1,0:T(8,128)S(1)} %get-tuple-element.70), channel_id=1, source_target_pairs={{0,1},{1,0},{2,3},{3,2},{4,5},{5,4},{6,7},{7,6},{8,9},{9,8},{10,11... | collective-permute-start | bytes 61448 | tf_op jit(solution)/shard_map/ppermute | solution.py:720
  26.2 6.5 %collective-permute-start.12 = (f32[5,8,128]{2,1,0:T(8,128)S(1)}, f32[5,8,128]{2,1,0:T(8,128)S(1)}, u32[]{:S(2)}, u32[]{:S(2)}) collective-permute-start(f32[5,8,128]{2,1,0:T(8,128)S(1)} %get-tuple-element.73), channel_id=1, source_target_pairs={{0,28},{4,8},{8,4},{12,16},{16,12},{20,24},{24,20},{28,0},{1,29},{... | collective-permute-start | bytes 61448 | tf_op jit(solution)/shard_map/ppermute | solution.py:717
  28.8 4.0 %collective-permute-start.13 = (f32[5,8,128]{2,1,0:T(8,128)S(1)}, f32[5,8,128]{2,1,0:T(8,128)S(1)}, u32[]{:S(2)}, u32[]{:S(2)}) collective-permute-start(f32[5,8,128]{2,1,0:T(8,128)S(1)} %get-tuple-element.74), channel_id=1, source_target_pairs={{0,4},{4,0},{8,12},{12,8},{16,20},{20,16},{24,28},{28,24},{1,5},{5... | collective-permute-start | bytes 61448 | tf_op jit(solution)/shard_map/ppermute | solution.py:718
  28.8 4.0 %collective-permute-start.14 = (f32[5,8,128]{2,1,0:T(8,128)S(1)}, f32[5,8,128]{2,1,0:T(8,128)S(1)}, u32[]{:S(2)}, u32[]{:S(2)}) collective-permute-start(f32[5,8,128]{2,1,0:T(8,128)S(1)} %get-tuple-element.75), channel_id=1, source_target_pairs={{0,3},{1,2},{2,1},{3,0},{4,7},{5,6},{6,5},{7,4},{8,11},{9,10},{10,... | collective-permute-start | bytes 61448 | tf_op jit(solution)/shard_map/ppermute | solution.py:719
  28.8 4.0 %collective-permute-start.15 = (f32[5,8,128]{2,1,0:T(8,128)S(1)}, f32[5,8,128]{2,1,0:T(8,128)S(1)}, u32[]{:S(2)}, u32[]{:S(2)}) collective-permute-start(f32[5,8,128]{2,1,0:T(8,128)S(1)} %get-tuple-element.76), channel_id=1, source_target_pairs={{0,1},{1,0},{2,3},{3,2},{4,5},{5,4},{6,7},{7,6},{8,9},{9,8},{10,11... | collective-permute-start | bytes 61448 | tf_op jit(solution)/shard_map/ppermute | solution.py:720

commit v15 on v14

--- a/solution.py
+++ b/solution.py
@@ -191,23 +191,23 @@
     every, inner = slice(0, 4), slice(1, 3)
     src_copy = pltpu.make_async_copy(src_hbm, src_ref, sems.at[4])
     src_copy.start()
+    orient_copy = pltpu.make_async_copy(orient_hbm, orient_ref, orient_sem)
+    orient_copy.start()
     copies = [
         line_copy(smooth_hbm, smooth_ref, sems.at[slot], a, b)
         for slot, (a, b) in enumerate(((0, every), (3, every), (inner, 0), (inner, 3)))
     ]
     for one in copies:
         one.start()
-    orient_copy = pltpu.make_async_copy(orient_hbm, orient_ref, orient_sem)
-    orient_copy.start()
-    orient_copy.wait()
-    for d in range(3):
-        flag_ref[d] = twice(orient_ref[d])
     lines = [[(0, b) for b in range(4)], [(3, b) for b in range(4)], [(1, 0), (2, 0)], [(1, 3), (2, 3)]]
     src_copy.wait()
     for one, group in zip(copies, lines):
         one.wait()
         for a, b in group:
             first_line(src_ref, smooth_ref, u_ref, a, b)
+    orient_copy.wait()
+    for d in range(3):
+        flag_ref[d] = twice(orient_ref[d])
     fine_faces(u_ref, flag_ref, xo, xe, yo, ye)
 
 

time: 33.9 us -> 33.9 us (level)
  no operation moved by 1% of the time
where the time goes in v15:
time: 33.9 us; the launch traced here: 33.7 us
  starting transfers between devices  20.4 us (60%)
  Pallas kernels  7.34 us (22%)
  waiting for transfers between devices  5.85 us (17%)
    ppermute x4, starting transfers between devices, exchange(): xo = lax.ppermute(xo, 'gx', odd_x)  13.9 us
    pallas_call x11, Pallas kernels, call(): pl.pallas_call(kernel, out_shape=outs, in_specs=in_specs, out_specs=out_s...  7.34 us
    ppermute x4, starting transfers between devices, exchange(): ye = lax.ppermute(ye, 'gy', even_y)  5.85 us
    ppermute x4, waiting for transfers between devices, exchange(): xo = lax.ppermute(xo, 'gx', odd_x)  5.62 us
    ppermute x4, starting transfers between devices, exchange(): yo = lax.ppermute(yo, 'gy', odd_y)  0.69 us
  transfers between devices with their start and end apart: 16, of which 6 were waited for; matrix products, arithmetic and copies ran while one was open for 0% of the time, Pallas kernels for 13%

profile of v15, /device:TPU:0, one launch (start us, length us, event | category | flops | bytes accessed | tf_op | source)
XLA Modules:
  0.0 33.7 jit_solution(368944920101794216)
XLA Ops:
  0.0 0.0 copy-start.2
  0.0 0.0 copy-start.1
  0.0 1.7 %shard_map.64 = (f32[5,4,4,2,8,128]{5,4,3,2,1,0:T(8,128)S(1)}, bf16[25,4,4,16,128]{4,3,2,1,0:T(8,128)(2,1)S(1)}, f32[5,4,4,2,8,128]{5,4,3,2,1,0:T(8,128)S(1)}, s...) custom-call(f32[5,4,4,2,8,128]{5,4,3,2,1,0:T(8,128)} %bitcast.15, ...), custom_call_target="tpu_custom_call" | custom-call | flops 1638400 | bytes 4194304 | tf_op jit(solution)/shard_map/pallas_call | solution.py:695
  1.7 6.0 %collective-permute-start.2 = (f32[5,4,8,128]{3,2,1,0:T(8,128)S(1)}, f32[5,4,8,128]{3,2,1,0:T(8,128)S(1)}, u32[]{:S(2)}, u32[]{:S(2)}) collective-permute-start(f32[5,4,8,128]{3,2,1,0:T(8,128)S(1)} %get-tuple-element.51), channel_id=1, source_target_pairs={{0,28},{4,8},{8,4},{12,16},{16,12},{20,24},{24,20},{28,0},{1,29},{... | collective-permute-start | bytes 245768 | tf_op jit(solution)/shard_map/ppermute | solution.py:717
  7.7 0.0 collective-permute-start.3
  7.7 0.7 %collective-permute-start = (f32[5,4,8,128]{3,2,1,0:T(8,128)S(1)}, f32[5,4,8,128]{3,2,1,0:T(8,128)S(1)}, u32[]{:S(2)}, u32[]{:S(2)}) collective-permute-start(f32[5,4,8,128]{3,2,1,0:T(8,128)S(1)} %get-tuple-element.49), channel_id=1, source_target_pairs={{0,3},{1,2},{2,1},{3,0},{4,7},{5,6},{6,5},{7,4},{8,11},{9,10},{10,... | collective-permute-start | bytes 245768 | tf_op jit(solution)/shard_map/ppermute | solution.py:719
  8.4 1.0 %collective-permute-start.1 = (f32[5,4,8,128]{3,2,1,0:T(8,128)S(1)}, f32[5,4,8,128]{3,2,1,0:T(8,128)S(1)}, u32[]{:S(2)}, u32[]{:S(2)}) collective-permute-start(f32[5,4,8,128]{3,2,1,0:T(8,128)S(1)} %get-tuple-element.50), channel_id=1, source_target_pairs={{0,1},{1,0},{2,3},{3,2},{4,5},{5,4},{6,7},{7,6},{8,9},{9,8},{10,11... | collective-permute-start | bytes 245768 | tf_op jit(solution)/shard_map/ppermute | solution.py:720
  9.4 0.0 copy-done.2
  9.4 0.0 copy-done.1
  9.4 2.7 %shard_map.65 = (bf16[25,4,4,16,128]{4,3,2,1,0:T(8,128)(2,1)S(1)}, f32[5,4,4,2,8,128]{5,4,3,2,1,0:T(8,128)S(1)}, f32[5,4,4,2,8,128]{5,4,3,2,1,0:T(8,128)S(1)}, f...) custom-call(bf16[25,4,4,16,128]{4,3,2,1,0:T(8,128)(2,1)} %bitcast.14, ...), custom_call_target="tpu_custom_call", output_to_operand_aliasing={{0}: (2, {}), {1}: (3, {})} | custom-call | flops 9437184 | bytes 4194304 | tf_op jit(solution)/shard_map/pallas_call | solution.py:695
  12.1 0.0 collective-permute-done.2.rxo
  12.1 0.1 collective-permute-done.3.rxe
  12.2 0.2 shard_map.66
  12.3 0.1 collective-permute-done.ryo
  12.4 0.0 collective-permute-done.1.rye
  12.4 0.0 copy-start
  12.4 0.3 shard_map.67
  12.7 2.7 %collective-permute-start.4 = (f32[5,8,128]{2,1,0:T(8,128)S(1)}, f32[5,8,128]{2,1,0:T(8,128)S(1)}, u32[]{:S(2)}, u32[]{:S(2)}) collective-permute-start(f32[5,8,128]{2,1,0:T(8,128)S(1)} %get-tuple-element.60), channel_id=1, source_target_pairs={{0,28},{4,8},{8,4},{12,16},{16,12},{20,24},{24,20},{28,0},{1,29},{... | collective-permute-start | bytes 61448 | tf_op jit(solution)/shard_map/ppermute | solution.py:717
  15.5 0.0 collective-permute-start.5
  15.5 0.0 collective-permute-start.6
  15.5 1.6 %collective-permute-start.7 = (f32[5,8,128]{2,1,0:T(8,128)S(1)}, f32[5,8,128]{2,1,0:T(8,128)S(1)}, u32[]{:S(2)}, u32[]{:S(2)}) collective-permute-start(f32[5,8,128]{2,1,0:T(8,128)S(1)} %get-tuple-element.63), channel_id=1, source_target_pairs={{0,1},{1,0},{2,3},{3,2},{4,5},{5,4},{6,7},{7,6},{8,9},{9,8},{10,11... | collective-permute-start | bytes 61448 | tf_op jit(solution)/shard_map/ppermute | solution.py:720
  17.1 0.0 copy-done
  17.1 0.2 shard_map.69.response_ref
  17.3 0.6 %shard_map.68 = (f32[5,2,2,8,128]{4,3,2,1,0:T(8,128)S(1)}, f32[5,2,2,8,128]{4,3,2,1,0:T(8,128)S(1)}) custom-call(f32[5,4,4,2,8,128]{5,4,3,2,1,0:T(8,128)S(1)} %get-tuple-element.41.src_ref, f32[5,4,4,2,8,128]{5,4,3,2,1,0:T(8,128)S(1)} %get-tuple-element.56.u_ref.second_ref, s32[3,8,128]{2,1,0:T(8,128)S(1)} %get-tuple-element.44.flag_ref, ...), custom_call_target="tpu_custom_call" | custom-call | flops 4194304 | bytes 4194304 | tf_op jit(solution)/shard_map/pallas_call | solution.py:695
  17.9 1.4 %collective-permute-done.4.rxo = f32[5,8,128]{2,1,0:T(8,128)S(1)} collective-permute-done((f32[5,8,128]{2,1,0:T(8,128)S(1)}, f32[5,8,128]{2,1,0:T(8,128)S(1)}, u32[]{:S(2)}, u32[]{:S(2)}) %collective-permute-start.4) | collective-permute-done | bytes 20512 | tf_op jit(solution)/shard_map/ppermute | solution.py:717
  19.4 0.1 collective-permute-done.5.rxe
  19.5 0.0 collective-permute-done.6.ryo
  19.5 0.0 collective-permute-done.7.rye
  19.5 0.1 shard_map.70
  19.6 2.6 %collective-permute-start.8 = (f32[5,8,128]{2,1,0:T(8,128)S(1)}, f32[5,8,128]{2,1,0:T(8,128)S(1)}, u32[]{:S(2)}, u32[]{:S(2)}) collective-permute-start(f32[5,8,128]{2,1,0:T(8,128)S(1)} %get-tuple-element.67), channel_id=1, source_target_pairs={{0,28},{4,8},{8,4},{12,16},{16,12},{20,24},{24,20},{28,0},{1,29},{... | collective-permute-start | bytes 61448 | tf_op jit(solution)/shard_map/ppermute | solution.py:717
  22.1 0.0 collective-permute-start.9
  22.1 0.0 collective-permute-start.10
  22.1 1.6 %collective-permute-start.11 = (f32[5,8,128]{2,1,0:T(8,128)S(1)}, f32[5,8,128]{2,1,0:T(8,128)S(1)}, u32[]{:S(2)}, u32[]{:S(2)}) collective-permute-start(f32[5,8,128]{2,1,0:T(8,128)S(1)} %get-tuple-element.70), channel_id=1, source_target_pairs={{0,1},{1,0},{2,3},{3,2},{4,5},{5,4},{6,7},{7,6},{8,9},{9,8},{10,11... | collective-permute-start | bytes 61448 | tf_op jit(solution)/shard_map/ppermute | solution.py:720
  23.7 0.3 shard_map.71
  24.0 2.1 %collective-permute-done.8.rxo = f32[5,8,128]{2,1,0:T(8,128)S(1)} collective-permute-done((f32[5,8,128]{2,1,0:T(8,128)S(1)}, f32[5,8,128]{2,1,0:T(8,128)S(1)}, u32[]{:S(2)}, u32[]{:S(2)}) %collective-permute-start.8) | collective-permute-done | bytes 20512 | tf_op jit(solution)/shard_map/ppermute | solution.py:717
  26.1 0.0 collective-permute-done.9.rxe
  26.1 0.0 collective-permute-done.10.ryo
  26.1 0.0 collective-permute-done.11.rye
  26.1 0.1 shard_map.72
  26.2 2.5 %collective-permute-start.12 = (f32[5,8,128]{2,1,0:T(8,128)S(1)}, f32[5,8,128]{2,1,0:T(8,128)S(1)}, u32[]{:S(2)}, u32[]{:S(2)}) collective-permute-start(f32[5,8,128]{2,1,0:T(8,128)S(1)} %get-tuple-element.73), channel_id=1, source_target_pairs={{0,28},{4,8},{8,4},{12,16},{16,12},{20,24},{24,20},{28,0},{1,29},{... | collective-permute-start | bytes 61448 | tf_op jit(solution)/shard_map/ppermute | solution.py:717
  28.8 0.0 collective-permute-start.13
  28.8 0.0 collective-permute-start.14
  28.8 1.6 %collective-permute-start.15 = (f32[5,8,128]{2,1,0:T(8,128)S(1)}, f32[5,8,128]{2,1,0:T(8,128)S(1)}, u32[]{:S(2)}, u32[]{:S(2)}) collective-permute-start(f32[5,8,128]{2,1,0:T(8,128)S(1)} %get-tuple-element.76), channel_id=1, source_target_pairs={{0,1},{1,0},{2,3},{3,2},{4,5},{5,4},{6,7},{7,6},{8,9},{9,8},{10,11... | collective-permute-start | bytes 61448 | tf_op jit(solution)/shard_map/ppermute | solution.py:720
  30.4 0.2 shard_map.73.c_ref
  30.6 2.1 %collective-permute-done.12.rxo = f32[5,8,128]{2,1,0:T(8,128)S(1)} collective-permute-done((f32[5,8,128]{2,1,0:T(8,128)S(1)}, f32[5,8,128]{2,1,0:T(8,128)S(1)}, u32[]{:S(2)}, u32[]{:S(2)}) %collective-permute-start.12) | collective-permute-done | bytes 20512 | tf_op jit(solution)/shard_map/ppermute | solution.py:717
  32.8 0.0 collective-permute-done.13.rxe
  32.8 0.0 collective-permute-done.14.ryo
  32.8 0.0 collective-permute-done.15.rye
  32.8 0.9 %shard_map.74 = f32[5,4,4,2,8,128]{5,4,3,2,1,0:T(8,128)} custom-call(f32[5,2,2,8,128]{4,3,2,1,0:T(8,128)S(1)} %shard_map.73.c_ref, s32[3,8,128]{2,1,0:T(8,128)S(1)} %get-tuple-element.44.flag_ref, f32[4,25,8,128]{3,2,1,0:T(8,128)S(1)} %shard_map.69.response_ref, f32[5,8,128]{2,1,0:T(8,128)S(1)} %collective-permute-done.12.rxo, ...), custom_call_target="tpu_custom_call" | custom-call | flops 1048576 | bytes 4194304 | tf_op jit(solution)/shard_map/pallas_call | solution.py:695
Async XLA Ops:
  0.0 9.4 %copy-start.2 = (f32[2,2,128]{2,1,0:T(2,128)S(1)}, f32[2,2,128]{2,1,0:T(2,128)}, u32[]{:S(2)}) copy-start(f32[2,2,128]{2,1,0:T(2,128)} %param.8) | copy-start | bytes 6148
  0.0 9.4 %copy-start.1 = (f32[3,5,5,2,2,128]{5,4,3,2,1,0:T(2,128)S(1)}, f32[3,5,5,2,2,128]{5,4,3,2,1,0:T(2,128)}, u32[]{:S(2)}) copy-start(f32[3,5,5,2,2,128]{5,4,3,2,1,0:T(2,128)} %param.7) | copy-start | bytes 460804
  1.7 10.4 %collective-permute-start.2 = (f32[5,4,8,128]{3,2,1,0:T(8,128)S(1)}, f32[5,4,8,128]{3,2,1,0:T(8,128)S(1)}, u32[]{:S(2)}, u32[]{:S(2)}) collective-permute-start(f32[5,4,8,128]{3,2,1,0:T(8,128)S(1)} %get-tuple-element.51), channel_id=1, source_target_pairs={{0,28},{4,8},{8,4},{12,16},{16,12},{20,24},{24,20},{28,0},{1,29},{... | collective-permute-start | bytes 245768 | tf_op jit(solution)/shard_map/ppermute | solution.py:717
  7.7 4.4 %collective-permute-start.3 = (f32[5,4,8,128]{3,2,1,0:T(8,128)S(1)}, f32[5,4,8,128]{3,2,1,0:T(8,128)S(1)}, u32[]{:S(2)}, u32[]{:S(2)}) collective-permute-start(f32[5,4,8,128]{3,2,1,0:T(8,128)S(1)} %get-tuple-element.52), channel_id=1, source_target_pairs={{0,4},{4,0},{8,12},{12,8},{16,20},{20,16},{24,28},{28,24},{1,5},{5... | collective-permute-start | bytes 245768 | tf_op jit(solution)/shard_map/ppermute | solution.py:718
  7.7 4.7 %collective-permute-start = (f32[5,4,8,128]{3,2,1,0:T(8,128)S(1)}, f32[5,4,8,128]{3,2,1,0:T(8,128)S(1)}, u32[]{:S(2)}, u32[]{:S(2)}) collective-permute-start(f32[5,4,8,128]{3,2,1,0:T(8,128)S(1)} %get-tuple-element.49), channel_id=1, source_target_pairs={{0,3},{1,2},{2,1},{3,0},{4,7},{5,6},{6,5},{7,4},{8,11},{9,10},{10,... | collective-permute-start | bytes 245768 | tf_op jit(solution)/shard_map/ppermute | solution.py:719
  8.4 4.0 %collective-permute-start.1 = (f32[5,4,8,128]{3,2,1,0:T(8,128)S(1)}, f32[5,4,8,128]{3,2,1,0:T(8,128)S(1)}, u32[]{:S(2)}, u32[]{:S(2)}) collective-permute-start(f32[5,4,8,128]{3,2,1,0:T(8,128)S(1)} %get-tuple-element.50), channel_id=1, source_target_pairs={{0,1},{1,0},{2,3},{3,2},{4,5},{5,4},{6,7},{7,6},{8,9},{9,8},{10,11... | collective-permute-start | bytes 245768 | tf_op jit(solution)/shard_map/ppermute | solution.py:720
  12.4 4.7 %copy-start = (bf16[5,5,2,2,2,2,2,128]{7,6,5,4,3,2,1,0:T(2,128)(2,1)S(1)}, bf16[5,5,2,2,2,2,2,128]{7,6,5,4,3,2,1,0:T(2,128)(2,1)}, u32[]{:S(2)}) copy-start(bf16[5,5,2,2,2,2,2,128]{7,6,5,4,3,2,1,0:T(2,128)(2,1)} %param.11) | copy-start | bytes 614404
  12.7 6.7 %collective-permute-start.4 = (f32[5,8,128]{2,1,0:T(8,128)S(1)}, f32[5,8,128]{2,1,0:T(8,128)S(1)}, u32[]{:S(2)}, u32[]{:S(2)}) collective-permute-start(f32[5,8,128]{2,1,0:T(8,128)S(1)} %get-tuple-element.60), channel_id=1, source_target_pairs={{0,28},{4,8},{8,4},{12,16},{16,12},{20,24},{24,20},{28,0},{1,29},{... | collective-permute-start | bytes 61448 | tf_op jit(solution)/shard_map/ppermute | solution.py:717
  15.5 4.0 %collective-permute-start.5 = (f32[5,8,128]{2,1,0:T(8,128)S(1)}, f32[5,8,128]{2,1,0:T(8,128)S(1)}, u32[]{:S(2)}, u32[]{:S(2)}) collective-permute-start(f32[5,8,128]{2,1,0:T(8,128)S(1)} %get-tuple-element.61), channel_id=1, source_target_pairs={{0,4},{4,0},{8,12},{12,8},{16,20},{20,16},{24,28},{28,24},{1,5},{5... | collective-permute-start | bytes 61448 | tf_op jit(solution)/shard_map/ppermute | solution.py:718
  15.5 4.0 %collective-permute-start.6 = (f32[5,8,128]{2,1,0:T(8,128)S(1)}, f32[5,8,128]{2,1,0:T(8,128)S(1)}, u32[]{:S(2)}, u32[]{:S(2)}) collective-permute-start(f32[5,8,128]{2,1,0:T(8,128)S(1)} %get-tuple-element.62), channel_id=1, source_target_pairs={{0,3},{1,2},{2,1},{3,0},{4,7},{5,6},{6,5},{7,4},{8,11},{9,10},{10,... | collective-permute-start | bytes 61448 | tf_op jit(solution)/shard_map/ppermute | solution.py:719
  15.5 4.0 %collective-permute-start.7 = (f32[5,8,128]{2,1,0:T(8,128)S(1)}, f32[5,8,128]{2,1,0:T(8,128)S(1)}, u32[]{:S(2)}, u32[]{:S(2)}) collective-permute-start(f32[5,8,128]{2,1,0:T(8,128)S(1)} %get-tuple-element.63), channel_id=1, source_target_pairs={{0,1},{1,0},{2,3},{3,2},{4,5},{5,4},{6,7},{7,6},{8,9},{9,8},{10,11... | collective-permute-start | bytes 61448 | tf_op jit(solution)/shard_map/ppermute | solution.py:720
  19.6 6.6 %collective-permute-start.8 = (f32[5,8,128]{2,1,0:T(8,128)S(1)}, f32[5,8,128]{2,1,0:T(8,128)S(1)}, u32[]{:S(2)}, u32[]{:S(2)}) collective-permute-start(f32[5,8,128]{2,1,0:T(8,128)S(1)} %get-tuple-element.67), channel_id=1, source_target_pairs={{0,28},{4,8},{8,4},{12,16},{16,12},{20,24},{24,20},{28,0},{1,29},{... | collective-permute-start | bytes 61448 | tf_op jit(solution)/shard_map/ppermute | solution.py:717
  22.1 4.0 %collective-permute-start.9 = (f32[5,8,128]{2,1,0:T(8,128)S(1)}, f32[5,8,128]{2,1,0:T(8,128)S(1)}, u32[]{:S(2)}, u32[]{:S(2)}) collective-permute-start(f32[5,8,128]{2,1,0:T(8,128)S(1)} %get-tuple-element.68), channel_id=1, source_target_pairs={{0,4},{4,0},{8,12},{12,8},{16,20},{20,16},{24,28},{28,24},{1,5},{5... | collective-permute-start | bytes 61448 | tf_op jit(solution)/shard_map/ppermute | solution.py:718
  22.1 4.0 %collective-permute-start.10 = (f32[5,8,128]{2,1,0:T(8,128)S(1)}, f32[5,8,128]{2,1,0:T(8,128)S(1)}, u32[]{:S(2)}, u32[]{:S(2)}) collective-permute-start(f32[5,8,128]{2,1,0:T(8,128)S(1)} %get-tuple-element.69), channel_id=1, source_target_pairs={{0,3},{1,2},{2,1},{3,0},{4,7},{5,6},{6,5},{7,4},{8,11},{9,10},{10,... | collective-permute-start | bytes 61448 | tf_op jit(solution)/shard_map/ppermute | solution.py:719
  22.1 4.0 %collective-permute-start.11 = (f32[5,8,128]{2,1,0:T(8,128)S(1)}, f32[5,8,128]{2,1,0:T(8,128)S(1)}, u32[]{:S(2)}, u32[]{:S(2)}) collective-permute-start(f32[5,8,128]{2,1,0:T(8,128)S(1)} %get-tuple-element.70), channel_id=1, source_target_pairs={{0,1},{1,0},{2,3},{3,2},{4,5},{5,4},{6,7},{7,6},{8,9},{9,8},{10,11... | collective-permute-start | bytes 61448 | tf_op jit(solution)/shard_map/ppermute | solution.py:720
  26.2 6.5 %collective-permute-start.12 = (f32[5,8,128]{2,1,0:T(8,128)S(1)}, f32[5,8,128]{2,1,0:T(8,128)S(1)}, u32[]{:S(2)}, u32[]{:S(2)}) collective-permute-start(f32[5,8,128]{2,1,0:T(8,128)S(1)} %get-tuple-element.73), channel_id=1, source_target_pairs={{0,28},{4,8},{8,4},{12,16},{16,12},{20,24},{24,20},{28,0},{1,29},{... | collective-permute-start | bytes 61448 | tf_op jit(solution)/shard_map/ppermute | solution.py:717
  28.8 4.0 %collective-permute-start.13 = (f32[5,8,128]{2,1,0:T(8,128)S(1)}, f32[5,8,128]{2,1,0:T(8,128)S(1)}, u32[]{:S(2)}, u32[]{:S(2)}) collective-permute-start(f32[5,8,128]{2,1,0:T(8,128)S(1)} %get-tuple-element.74), channel_id=1, source_target_pairs={{0,4},{4,0},{8,12},{12,8},{16,20},{20,16},{24,28},{28,24},{1,5},{5... | collective-permute-start | bytes 61448 | tf_op jit(solution)/shard_map/ppermute | solution.py:718
  28.8 4.0 %collective-permute-start.14 = (f32[5,8,128]{2,1,0:T(8,128)S(1)}, f32[5,8,128]{2,1,0:T(8,128)S(1)}, u32[]{:S(2)}, u32[]{:S(2)}) collective-permute-start(f32[5,8,128]{2,1,0:T(8,128)S(1)} %get-tuple-element.75), channel_id=1, source_target_pairs={{0,3},{1,2},{2,1},{3,0},{4,7},{5,6},{6,5},{7,4},{8,11},{9,10},{10,... | collective-permute-start | bytes 61448 | tf_op jit(solution)/shard_map/ppermute | solution.py:719
  28.8 4.0 %collective-permute-start.15 = (f32[5,8,128]{2,1,0:T(8,128)S(1)}, f32[5,8,128]{2,1,0:T(8,128)S(1)}, u32[]{:S(2)}, u32[]{:S(2)}) collective-permute-start(f32[5,8,128]{2,1,0:T(8,128)S(1)} %get-tuple-element.76), channel_id=1, source_target_pairs={{0,1},{1,0},{2,3},{3,2},{4,5},{5,4},{6,7},{7,6},{8,9},{9,8},{10,11... | collective-permute-start | bytes 61448 | tf_op jit(solution)/shard_map/ppermute | solution.py:720

commit v16 on v15

--- a/solution.py
+++ b/solution.py
@@ -117,14 +117,19 @@
     odd_ref[index] = jnp.where(is_even, low_face, high_face)
 
 
-def fine_faces(u_ref, flag_ref, xo, xe, yo, ye):
-    even_x, even_y = parity("gx"), parity("gy")
-    fx, fy = flag_ref[0] != 0, flag_ref[1] != 0
+def fine_x_faces(u_ref, flag_ref, xo, xe):
+    even_x, fx = parity("gx"), flag_ref[0] != 0
     for v in range(5):
         for n in range(4):
             low = pack_low(u_ref[v, 0, n, 0], u_ref[v, 0, n, 1], 0)
             h = [jnp.where(fx, u_ref[v, 3, 3 - n, q], u_ref[v, 3, n, q]) for q in range(2)]
             put_pair(xe, xo, (v, n), low, pack_high(h[0], h[1], 0), even_x)
+
+
+def fine_y_faces(u_ref, flag_ref, yo, ye):
+    even_y, fy = parity("gy"), flag_ref[1] != 0
+    for v in range(5):
+        for n in range(4):
             low = pack_low(u_ref[v, n, 0, 0], u_ref[v, n, 0, 1], 1)
             h = [jnp.where(fy, u_ref[v, 3 - n, 3, q], u_ref[v, n, 3, q]) for q in range(2)]
             put_pair(ye, yo, (v, n), low, pack_high(h[0], h[1], 1), even_y)
@@ -201,14 +206,16 @@
         one.start()
     lines = [[(0, b) for b in range(4)], [(3, b) for b in range(4)], [(1, 0), (2, 0)], [(1, 3), (2, 3)]]
     src_copy.wait()
-    for one, group in zip(copies, lines):
+    for slot, (one, group) in enumerate(zip(copies, lines)):
         one.wait()
         for a, b in group:
             first_line(src_ref, smooth_ref, u_ref, a, b)
-    orient_copy.wait()
-    for d in range(3):
-        flag_ref[d] = twice(orient_ref[d])
-    fine_faces(u_ref, flag_ref, xo, xe, yo, ye)
+        if slot == 1:
+            orient_copy.wait()
+            for d in range(3):
+                flag_ref[d] = twice(orient_ref[d])
+            fine_x_faces(u_ref, flag_ref, xo, xe)
+    fine_y_faces(u_ref, flag_ref, yo, ye)
 
 
 def prepare_tables(jac_ref, damp_ref, jac8_ref, damp8_ref, face_ref):
@@ -663,9 +670,11 @@
             for b in range(4):
                 for a, value in enumerate(spread(lines[0][b], lines[1][b])):
                     out_ref[v, a, b, q] = second_ref[v, a, b, q] + value
-        copy = pltpu.make_async_copy(out_ref.at[v], out_hbm.at[v], sems.at[v])
-        copy.start()
-        copies.append(copy)
+        if v in (2, 4):
+            part = slice(0, 3) if v == 2 else slice(3, 5)
+            copy = pltpu.make_async_copy(out_ref.at[part], out_hbm.at[part], sems.at[len(copies)])
+            copy.start()
+            copies.append(copy)
     for copy in copies:
         copy.wait()
 
@@ -797,7 +806,7 @@
         (coarse, flag, response, *got, second),
         [jax.ShapeDtypeStruct(FINE, F32)],
         out_hbm=(0,),
-        scratch=[pltpu.VMEM(FINE, F32), pltpu.SemaphoreType.DMA((5,))],
+        scratch=[pltpu.VMEM(FINE, F32), pltpu.SemaphoreType.DMA((2,))],
         flops=2**20,
     )
     return out.reshape(5, 4, 4, 4, 2, 2, 128)

time: 33.9 us -> 33.9 us (level)
  no operation moved by 1% of the time
where the time goes in v16:
time: 33.9 us; the launch traced here: 33.7 us
  starting transfers between devices  20.4 us (60%)
  Pallas kernels  7.36 us (22%)
  waiting for transfers between devices  5.85 us (17%)
    ppermute x4, starting transfers between devices, exchange(): xo = lax.ppermute(xo, 'gx', odd_x)  13.9 us
    pallas_call x11, Pallas kernels, call(): pl.pallas_call(kernel, out_shape=outs, in_specs=in_specs, out_specs=out_s...  7.36 us
    ppermute x4, starting transfers between devices, exchange(): ye = lax.ppermute(ye, 'gy', even_y)  5.85 us
    ppermute x4, waiting for transfers between devices, exchange(): xo = lax.ppermute(xo, 'gx', odd_x)  5.62 us
    ppermute x4, starting transfers between devices, exchange(): yo = lax.ppermute(yo, 'gy', odd_y)  0.69 us
  transfers between devices with their start and end apart: 16, of which 6 were waited for; matrix products, arithmetic and copies ran while one was open for 0% of the time, Pallas kernels for 13%

profile of v16, /device:TPU:0, one launch (start us, length us, event | category | flops | bytes accessed | tf_op | source)
XLA Modules:
  0.0 33.7 jit_solution(6708812140811958570)
XLA Ops:
  0.0 0.0 copy-start.2
  0.0 0.0 copy-start.1
  0.0 1.7 %shard_map.64 = (f32[5,4,4,2,8,128]{5,4,3,2,1,0:T(8,128)S(1)}, bf16[25,4,4,16,128]{4,3,2,1,0:T(8,128)(2,1)S(1)}, f32[5,4,4,2,8,128]{5,4,3,2,1,0:T(8,128)S(1)}, s...) custom-call(f32[5,4,4,2,8,128]{5,4,3,2,1,0:T(8,128)} %bitcast.15, ...), custom_call_target="tpu_custom_call" | custom-call | flops 1638400 | bytes 4194304 | tf_op jit(solution)/shard_map/pallas_call | solution.py:704
  1.7 6.0 %collective-permute-start.2 = (f32[5,4,8,128]{3,2,1,0:T(8,128)S(1)}, f32[5,4,8,128]{3,2,1,0:T(8,128)S(1)}, u32[]{:S(2)}, u32[]{:S(2)}) collective-permute-start(f32[5,4,8,128]{3,2,1,0:T(8,128)S(1)} %get-tuple-element.51), channel_id=1, source_target_pairs={{0,28},{4,8},{8,4},{12,16},{16,12},{20,24},{24,20},{28,0},{1,29},{... | collective-permute-start | bytes 245768 | tf_op jit(solution)/shard_map/ppermute | solution.py:726
  7.7 0.0 collective-permute-start.3
  7.7 0.7 %collective-permute-start = (f32[5,4,8,128]{3,2,1,0:T(8,128)S(1)}, f32[5,4,8,128]{3,2,1,0:T(8,128)S(1)}, u32[]{:S(2)}, u32[]{:S(2)}) collective-permute-start(f32[5,4,8,128]{3,2,1,0:T(8,128)S(1)} %get-tuple-element.49), channel_id=1, source_target_pairs={{0,3},{1,2},{2,1},{3,0},{4,7},{5,6},{6,5},{7,4},{8,11},{9,10},{10,... | collective-permute-start | bytes 245768 | tf_op jit(solution)/shard_map/ppermute | solution.py:728
  8.4 1.0 %collective-permute-start.1 = (f32[5,4,8,128]{3,2,1,0:T(8,128)S(1)}, f32[5,4,8,128]{3,2,1,0:T(8,128)S(1)}, u32[]{:S(2)}, u32[]{:S(2)}) collective-permute-start(f32[5,4,8,128]{3,2,1,0:T(8,128)S(1)} %get-tuple-element.50), channel_id=1, source_target_pairs={{0,1},{1,0},{2,3},{3,2},{4,5},{5,4},{6,7},{7,6},{8,9},{9,8},{10,11... | collective-permute-start | bytes 245768 | tf_op jit(solution)/shard_map/ppermute | solution.py:729
  9.4 0.0 copy-done.2
  9.4 0.0 copy-done.1
  9.4 2.7 %shard_map.65 = (bf16[25,4,4,16,128]{4,3,2,1,0:T(8,128)(2,1)S(1)}, f32[5,4,4,2,8,128]{5,4,3,2,1,0:T(8,128)S(1)}, f32[5,4,4,2,8,128]{5,4,3,2,1,0:T(8,128)S(1)}, f...) custom-call(bf16[25,4,4,16,128]{4,3,2,1,0:T(8,128)(2,1)} %bitcast.14, ...), custom_call_target="tpu_custom_call", output_to_operand_aliasing={{0}: (2, {}), {1}: (3, {})} | custom-call | flops 9437184 | bytes 4194304 | tf_op jit(solution)/shard_map/pallas_call | solution.py:704
  12.1 0.0 collective-permute-done.2.rxo
  12.1 0.1 collective-permute-done.3.rxe
  12.2 0.2 shard_map.66
  12.3 0.1 collective-permute-done.ryo
  12.4 0.0 collective-permute-done.1.rye
  12.4 0.0 copy-start
  12.4 0.3 shard_map.67
  12.7 2.7 %collective-permute-start.4 = (f32[5,8,128]{2,1,0:T(8,128)S(1)}, f32[5,8,128]{2,1,0:T(8,128)S(1)}, u32[]{:S(2)}, u32[]{:S(2)}) collective-permute-start(f32[5,8,128]{2,1,0:T(8,128)S(1)} %get-tuple-element.60), channel_id=1, source_target_pairs={{0,28},{4,8},{8,4},{12,16},{16,12},{20,24},{24,20},{28,0},{1,29},{... | collective-permute-start | bytes 61448 | tf_op jit(solution)/shard_map/ppermute | solution.py:726
  15.5 0.0 collective-permute-start.5
  15.5 0.0 collective-permute-start.6
  15.5 1.6 %collective-permute-start.7 = (f32[5,8,128]{2,1,0:T(8,128)S(1)}, f32[5,8,128]{2,1,0:T(8,128)S(1)}, u32[]{:S(2)}, u32[]{:S(2)}) collective-permute-start(f32[5,8,128]{2,1,0:T(8,128)S(1)} %get-tuple-element.63), channel_id=1, source_target_pairs={{0,1},{1,0},{2,3},{3,2},{4,5},{5,4},{6,7},{7,6},{8,9},{9,8},{10,11... | collective-permute-start | bytes 61448 | tf_op jit(solution)/shard_map/ppermute | solution.py:729
  17.1 0.0 copy-done
  17.1 0.2 shard_map.69.response_ref
  17.3 0.6 %shard_map.68 = (f32[5,2,2,8,128]{4,3,2,1,0:T(8,128)S(1)}, f32[5,2,2,8,128]{4,3,2,1,0:T(8,128)S(1)}) custom-call(f32[5,4,4,2,8,128]{5,4,3,2,1,0:T(8,128)S(1)} %get-tuple-element.41.src_ref, f32[5,4,4,2,8,128]{5,4,3,2,1,0:T(8,128)S(1)} %get-tuple-element.56.u_ref.second_ref, s32[3,8,128]{2,1,0:T(8,128)S(1)} %get-tuple-element.44.flag_ref, ...), custom_call_target="tpu_custom_call" | custom-call | flops 4194304 | bytes 4194304 | tf_op jit(solution)/shard_map/pallas_call | solution.py:704
  17.9 1.4 %collective-permute-done.4.rxo = f32[5,8,128]{2,1,0:T(8,128)S(1)} collective-permute-done((f32[5,8,128]{2,1,0:T(8,128)S(1)}, f32[5,8,128]{2,1,0:T(8,128)S(1)}, u32[]{:S(2)}, u32[]{:S(2)}) %collective-permute-start.4) | collective-permute-done | bytes 20512 | tf_op jit(solution)/shard_map/ppermute | solution.py:726
  19.4 0.1 collective-permute-done.5.rxe
  19.5 0.0 collective-permute-done.6.ryo
  19.5 0.0 collective-permute-done.7.rye
  19.5 0.1 shard_map.70
  19.6 2.6 %collective-permute-start.8 = (f32[5,8,128]{2,1,0:T(8,128)S(1)}, f32[5,8,128]{2,1,0:T(8,128)S(1)}, u32[]{:S(2)}, u32[]{:S(2)}) collective-permute-start(f32[5,8,128]{2,1,0:T(8,128)S(1)} %get-tuple-element.67), channel_id=1, source_target_pairs={{0,28},{4,8},{8,4},{12,16},{16,12},{20,24},{24,20},{28,0},{1,29},{... | collective-permute-start | bytes 61448 | tf_op jit(solution)/shard_map/ppermute | solution.py:726
  22.1 0.0 collective-permute-start.9
  22.1 0.0 collective-permute-start.10
  22.1 1.6 %collective-permute-start.11 = (f32[5,8,128]{2,1,0:T(8,128)S(1)}, f32[5,8,128]{2,1,0:T(8,128)S(1)}, u32[]{:S(2)}, u32[]{:S(2)}) collective-permute-start(f32[5,8,128]{2,1,0:T(8,128)S(1)} %get-tuple-element.70), channel_id=1, source_target_pairs={{0,1},{1,0},{2,3},{3,2},{4,5},{5,4},{6,7},{7,6},{8,9},{9,8},{10,11... | collective-permute-start | bytes 61448 | tf_op jit(solution)/shard_map/ppermute | solution.py:729
  23.7 0.3 shard_map.71
  24.0 2.1 %collective-permute-done.8.rxo = f32[5,8,128]{2,1,0:T(8,128)S(1)} collective-permute-done((f32[5,8,128]{2,1,0:T(8,128)S(1)}, f32[5,8,128]{2,1,0:T(8,128)S(1)}, u32[]{:S(2)}, u32[]{:S(2)}) %collective-permute-start.8) | collective-permute-done | bytes 20512 | tf_op jit(solution)/shard_map/ppermute | solution.py:726
  26.1 0.0 collective-permute-done.9.rxe
  26.1 0.0 collective-permute-done.10.ryo
  26.1 0.0 collective-permute-done.11.rye
  26.1 0.1 shard_map.72
  26.2 2.5 %collective-permute-start.12 = (f32[5,8,128]{2,1,0:T(8,128)S(1)}, f32[5,8,128]{2,1,0:T(8,128)S(1)}, u32[]{:S(2)}, u32[]{:S(2)}) collective-permute-start(f32[5,8,128]{2,1,0:T(8,128)S(1)} %get-tuple-element.73), channel_id=1, source_target_pairs={{0,28},{4,8},{8,4},{12,16},{16,12},{20,24},{24,20},{28,0},{1,29},{... | collective-permute-start | bytes 61448 | tf_op jit(solution)/shard_map/ppermute | solution.py:726
  28.7 0.0 collective-permute-start.13
  28.8 0.0 collective-permute-start.14
  28.8 1.6 %collective-permute-start.15 = (f32[5,8,128]{2,1,0:T(8,128)S(1)}, f32[5,8,128]{2,1,0:T(8,128)S(1)}, u32[]{:S(2)}, u32[]{:S(2)}) collective-permute-start(f32[5,8,128]{2,1,0:T(8,128)S(1)} %get-tuple-element.76), channel_id=1, source_target_pairs={{0,1},{1,0},{2,3},{3,2},{4,5},{5,4},{6,7},{7,6},{8,9},{9,8},{10,11... | collective-permute-start | bytes 61448 | tf_op jit(solution)/shard_map/ppermute | solution.py:729
  30.4 0.2 shard_map.73.c_ref
  30.6 2.1 %collective-permute-done.12.rxo = f32[5,8,128]{2,1,0:T(8,128)S(1)} collective-permute-done((f32[5,8,128]{2,1,0:T(8,128)S(1)}, f32[5,8,128]{2,1,0:T(8,128)S(1)}, u32[]{:S(2)}, u32[]{:S(2)}) %collective-permute-start.12) | collective-permute-done | bytes 20512 | tf_op jit(solution)/shard_map/ppermute | solution.py:726
  32.8 0.0 collective-permute-done.13.rxe
  32.8 0.0 collective-permute-done.14.ryo
  32.8 0.0 collective-permute-done.15.rye
  32.8 1.0 %shard_map.74 = f32[5,4,4,2,8,128]{5,4,3,2,1,0:T(8,128)} custom-call(f32[5,2,2,8,128]{4,3,2,1,0:T(8,128)S(1)} %shard_map.73.c_ref, s32[3,8,128]{2,1,0:T(8,128)S(1)} %get-tuple-element.44.flag_ref, f32[4,25,8,128]{3,2,1,0:T(8,128)S(1)} %shard_map.69.response_ref, f32[5,8,128]{2,1,0:T(8,128)S(1)} %collective-permute-done.12.rxo, ...), custom_call_target="tpu_custom_call" | custom-call | flops 1048576 | bytes 4194304 | tf_op jit(solution)/shard_map/pallas_call | solution.py:704
Async XLA Ops:
  0.0 9.4 %copy-start.2 = (f32[2,2,128]{2,1,0:T(2,128)S(1)}, f32[2,2,128]{2,1,0:T(2,128)}, u32[]{:S(2)}) copy-start(f32[2,2,128]{2,1,0:T(2,128)} %param.8) | copy-start | bytes 6148
  0.0 9.4 %copy-start.1 = (f32[3,5,5,2,2,128]{5,4,3,2,1,0:T(2,128)S(1)}, f32[3,5,5,2,2,128]{5,4,3,2,1,0:T(2,128)}, u32[]{:S(2)}) copy-start(f32[3,5,5,2,2,128]{5,4,3,2,1,0:T(2,128)} %param.7) | copy-start | bytes 460804
  1.7 10.4 %collective-permute-start.2 = (f32[5,4,8,128]{3,2,1,0:T(8,128)S(1)}, f32[5,4,8,128]{3,2,1,0:T(8,128)S(1)}, u32[]{:S(2)}, u32[]{:S(2)}) collective-permute-start(f32[5,4,8,128]{3,2,1,0:T(8,128)S(1)} %get-tuple-element.51), channel_id=1, source_target_pairs={{0,28},{4,8},{8,4},{12,16},{16,12},{20,24},{24,20},{28,0},{1,29},{... | collective-permute-start | bytes 245768 | tf_op jit(solution)/shard_map/ppermute | solution.py:726
  7.7 4.4 %collective-permute-start.3 = (f32[5,4,8,128]{3,2,1,0:T(8,128)S(1)}, f32[5,4,8,128]{3,2,1,0:T(8,128)S(1)}, u32[]{:S(2)}, u32[]{:S(2)}) collective-permute-start(f32[5,4,8,128]{3,2,1,0:T(8,128)S(1)} %get-tuple-element.52), channel_id=1, source_target_pairs={{0,4},{4,0},{8,12},{12,8},{16,20},{20,16},{24,28},{28,24},{1,5},{5... | collective-permute-start | bytes 245768 | tf_op jit(solution)/shard_map/ppermute | solution.py:727
  7.7 4.7 %collective-permute-start = (f32[5,4,8,128]{3,2,1,0:T(8,128)S(1)}, f32[5,4,8,128]{3,2,1,0:T(8,128)S(1)}, u32[]{:S(2)}, u32[]{:S(2)}) collective-permute-start(f32[5,4,8,128]{3,2,1,0:T(8,128)S(1)} %get-tuple-element.49), channel_id=1, source_target_pairs={{0,3},{1,2},{2,1},{3,0},{4,7},{5,6},{6,5},{7,4},{8,11},{9,10},{10,... | collective-permute-start | bytes 245768 | tf_op jit(solution)/shard_map/ppermute | solution.py:728
  8.4 4.0 %collective-permute-start.1 = (f32[5,4,8,128]{3,2,1,0:T(8,128)S(1)}, f32[5,4,8,128]{3,2,1,0:T(8,128)S(1)}, u32[]{:S(2)}, u32[]{:S(2)}) collective-permute-start(f32[5,4,8,128]{3,2,1,0:T(8,128)S(1)} %get-tuple-element.50), channel_id=1, source_target_pairs={{0,1},{1,0},{2,3},{3,2},{4,5},{5,4},{6,7},{7,6},{8,9},{9,8},{10,11... | collective-permute-start | bytes 245768 | tf_op jit(solution)/shard_map/ppermute | solution.py:729
  12.4 4.7 %copy-start = (bf16[5,5,2,2,2,2,2,128]{7,6,5,4,3,2,1,0:T(2,128)(2,1)S(1)}, bf16[5,5,2,2,2,2,2,128]{7,6,5,4,3,2,1,0:T(2,128)(2,1)}, u32[]{:S(2)}) copy-start(bf16[5,5,2,2,2,2,2,128]{7,6,5,4,3,2,1,0:T(2,128)(2,1)} %param.11) | copy-start | bytes 614404
  12.7 6.7 %collective-permute-start.4 = (f32[5,8,128]{2,1,0:T(8,128)S(1)}, f32[5,8,128]{2,1,0:T(8,128)S(1)}, u32[]{:S(2)}, u32[]{:S(2)}) collective-permute-start(f32[5,8,128]{2,1,0:T(8,128)S(1)} %get-tuple-element.60), channel_id=1, source_target_pairs={{0,28},{4,8},{8,4},{12,16},{16,12},{20,24},{24,20},{28,0},{1,29},{... | collective-permute-start | bytes 61448 | tf_op jit(solution)/shard_map/ppermute | solution.py:726
  15.5 4.0 %collective-permute-start.5 = (f32[5,8,128]{2,1,0:T(8,128)S(1)}, f32[5,8,128]{2,1,0:T(8,128)S(1)}, u32[]{:S(2)}, u32[]{:S(2)}) collective-permute-start(f32[5,8,128]{2,1,0:T(8,128)S(1)} %get-tuple-element.61), channel_id=1, source_target_pairs={{0,4},{4,0},{8,12},{12,8},{16,20},{20,16},{24,28},{28,24},{1,5},{5... | collective-permute-start | bytes 61448 | tf_op jit(solution)/shard_map/ppermute | solution.py:727
  15.5 4.0 %collective-permute-start.6 = (f32[5,8,128]{2,1,0:T(8,128)S(1)}, f32[5,8,128]{2,1,0:T(8,128)S(1)}, u32[]{:S(2)}, u32[]{:S(2)}) collective-permute-start(f32[5,8,128]{2,1,0:T(8,128)S(1)} %get-tuple-element.62), channel_id=1, source_target_pairs={{0,3},{1,2},{2,1},{3,0},{4,7},{5,6},{6,5},{7,4},{8,11},{9,10},{10,... | collective-permute-start | bytes 61448 | tf_op jit(solution)/shard_map/ppermute | solution.py:728
  15.5 4.0 %collective-permute-start.7 = (f32[5,8,128]{2,1,0:T(8,128)S(1)}, f32[5,8,128]{2,1,0:T(8,128)S(1)}, u32[]{:S(2)}, u32[]{:S(2)}) collective-permute-start(f32[5,8,128]{2,1,0:T(8,128)S(1)} %get-tuple-element.63), channel_id=1, source_target_pairs={{0,1},{1,0},{2,3},{3,2},{4,5},{5,4},{6,7},{7,6},{8,9},{9,8},{10,11... | collective-permute-start | bytes 61448 | tf_op jit(solution)/shard_map/ppermute | solution.py:729
  19.6 6.6 %collective-permute-start.8 = (f32[5,8,128]{2,1,0:T(8,128)S(1)}, f32[5,8,128]{2,1,0:T(8,128)S(1)}, u32[]{:S(2)}, u32[]{:S(2)}) collective-permute-start(f32[5,8,128]{2,1,0:T(8,128)S(1)} %get-tuple-element.67), channel_id=1, source_target_pairs={{0,28},{4,8},{8,4},{12,16},{16,12},{20,24},{24,20},{28,0},{1,29},{... | collective-permute-start | bytes 61448 | tf_op jit(solution)/shard_map/ppermute | solution.py:726
  22.1 4.0 %collective-permute-start.9 = (f32[5,8,128]{2,1,0:T(8,128)S(1)}, f32[5,8,128]{2,1,0:T(8,128)S(1)}, u32[]{:S(2)}, u32[]{:S(2)}) collective-permute-start(f32[5,8,128]{2,1,0:T(8,128)S(1)} %get-tuple-element.68), channel_id=1, source_target_pairs={{0,4},{4,0},{8,12},{12,8},{16,20},{20,16},{24,28},{28,24},{1,5},{5... | collective-permute-start | bytes 61448 | tf_op jit(solution)/shard_map/ppermute | solution.py:727
  22.1 4.0 %collective-permute-start.10 = (f32[5,8,128]{2,1,0:T(8,128)S(1)}, f32[5,8,128]{2,1,0:T(8,128)S(1)}, u32[]{:S(2)}, u32[]{:S(2)}) collective-permute-start(f32[5,8,128]{2,1,0:T(8,128)S(1)} %get-tuple-element.69), channel_id=1, source_target_pairs={{0,3},{1,2},{2,1},{3,0},{4,7},{5,6},{6,5},{7,4},{8,11},{9,10},{10,... | collective-permute-start | bytes 61448 | tf_op jit(solution)/shard_map/ppermute | solution.py:728
  22.1 4.0 %collective-permute-start.11 = (f32[5,8,128]{2,1,0:T(8,128)S(1)}, f32[5,8,128]{2,1,0:T(8,128)S(1)}, u32[]{:S(2)}, u32[]{:S(2)}) collective-permute-start(f32[5,8,128]{2,1,0:T(8,128)S(1)} %get-tuple-element.70), channel_id=1, source_target_pairs={{0,1},{1,0},{2,3},{3,2},{4,5},{5,4},{6,7},{7,6},{8,9},{9,8},{10,11... | collective-permute-start | bytes 61448 | tf_op jit(solution)/shard_map/ppermute | solution.py:729
  26.2 6.5 %collective-permute-start.12 = (f32[5,8,128]{2,1,0:T(8,128)S(1)}, f32[5,8,128]{2,1,0:T(8,128)S(1)}, u32[]{:S(2)}, u32[]{:S(2)}) collective-permute-start(f32[5,8,128]{2,1,0:T(8,128)S(1)} %get-tuple-element.73), channel_id=1, source_target_pairs={{0,28},{4,8},{8,4},{12,16},{16,12},{20,24},{24,20},{28,0},{1,29},{... | collective-permute-start | bytes 61448 | tf_op jit(solution)/shard_map/ppermute | solution.py:726
  28.7 4.0 %collective-permute-start.13 = (f32[5,8,128]{2,1,0:T(8,128)S(1)}, f32[5,8,128]{2,1,0:T(8,128)S(1)}, u32[]{:S(2)}, u32[]{:S(2)}) collective-permute-start(f32[5,8,128]{2,1,0:T(8,128)S(1)} %get-tuple-element.74), channel_id=1, source_target_pairs={{0,4},{4,0},{8,12},{12,8},{16,20},{20,16},{24,28},{28,24},{1,5},{5... | collective-permute-start | bytes 61448 | tf_op jit(solution)/shard_map/ppermute | solution.py:727
  28.8 4.0 %collective-permute-start.14 = (f32[5,8,128]{2,1,0:T(8,128)S(1)}, f32[5,8,128]{2,1,0:T(8,128)S(1)}, u32[]{:S(2)}, u32[]{:S(2)}) collective-permute-start(f32[5,8,128]{2,1,0:T(8,128)S(1)} %get-tuple-element.75), channel_id=1, source_target_pairs={{0,3},{1,2},{2,1},{3,0},{4,7},{5,6},{6,5},{7,4},{8,11},{9,10},{10,... | collective-permute-start | bytes 61448 | tf_op jit(solution)/shard_map/ppermute | solution.py:728
  28.8 4.0 %collective-permute-start.15 = (f32[5,8,128]{2,1,0:T(8,128)S(1)}, f32[5,8,128]{2,1,0:T(8,128)S(1)}, u32[]{:S(2)}, u32[]{:S(2)}) collective-permute-start(f32[5,8,128]{2,1,0:T(8,128)S(1)} %get-tuple-element.76), channel_id=1, source_target_pairs={{0,1},{1,0},{2,3},{3,2},{4,5},{5,4},{6,7},{7,6},{8,9},{9,8},{10,11... | collective-permute-start | bytes 61448 | tf_op jit(solution)/shard_map/ppermute | solution.py:729

commit v17 on v15

--- a/solution.py
+++ b/solution.py
@@ -324,7 +324,7 @@
 
 def first_volume_kernel(
     smooth_hbm, src_ref, smooth_in, u_in, flag_ref, jac_ref, damp_ref,
-    smooth_ref, u_ref, acc_ref, jac8_ref, damp8_ref, face_ref, second_ref, scaled_ref, sem,
+    smooth_ref, u_ref, acc_ref, jac8_ref, damp8_ref, face_ref, scaled_ref, sem,
 ):
     inner = slice(1, 3)
     copy = line_copy(smooth_hbm, smooth_ref, sem, inner, inner)
@@ -338,11 +338,6 @@
             first_line(src_ref, smooth_ref, u_ref, a, b)
 
     volume(src_ref, u_ref, flag_ref, jac8_ref, damp8_ref, acc_ref, finish_lines)
-    for a, b in lines:
-        change = smoothed(smooth_ref, [[acc_ref[v, a, b, q] for q in range(2)] for v in range(5)], a, b)
-        for v in range(5):
-            for q in range(2):
-                second_ref[v, a, b, q] = u_ref[v, a, b, q] + change[v][q]
     for line, (a, b) in enumerate(FACE_LINES):
         for k in range(25):
             block = OMEGA * smooth_ref[k, a, b].astype(F32)
@@ -388,7 +383,7 @@
 X_LINES = [(a, b) for a in (0, 3) for b in (1, 2)]
 
 
-def second_x_kernel(acc_ref, u_ref, scaled_ref, flag_ref, face_ref, rxo, rxe, inner_ref, out_ref, part_ref):
+def second_x_kernel(acc_ref, u_ref, scaled_ref, flag_ref, face_ref, rxo, rxe, out_ref, part_ref):
     remote_parts(0, rxo, rxe, flag_ref, face_ref, part_ref)
     second_lines(X_LINES, acc_ref, part_ref, None, scaled_ref, u_ref, out_ref)
 
@@ -447,7 +442,17 @@
                 response_ref[f, 5 * o + i] = (OMEGA / 6.0) * total
 
 
-def restricted_volume_kernel(src_ref, u_ref, flag_ref, jac_ref, damp_ref, smooth_ref, acc_ref, c_ref):
+def restricted_volume_kernel(
+    src_ref, flag_ref, jac_ref, damp_ref, smooth_ref, fine_acc_ref, first_ref, fine_smooth_ref, faces_ref,
+    acc_ref, c_ref, u_ref,
+):
+    for a in (1, 2):
+        for b in (1, 2):
+            left = [[fine_acc_ref[v, a, b, q] for q in range(2)] for v in range(5)]
+            change = smoothed(fine_smooth_ref, left, a, b)
+            for v in range(5):
+                for q in range(2):
+                    u_ref[v, a, b, q] = first_ref[v, a, b, q] + change[v][q]
     damp = H4 * damp_ref[...]
     low_c = c_low()
     slope = [
@@ -742,10 +747,10 @@
         flops=2 * 25 * 64 * 512,
     )
     got = exchange(*sent)
-    _, first, acc, jac8, damp8, face, second, scaled = call(
+    smoother, first, acc, jac8, damp8, face, scaled = call(
         first_volume_kernel,
         (smoother_in, source, smoother, first, flag, jacobian, damping),
-        [held, vmem(FINE), vmem(FINE), vmem((75, 8, 128)), vmem((8, 128)), vmem((4, 25, 8, 128)), vmem(FINE), vmem((12, 25, 2, 8, 128))],
+        [held, vmem(FINE), vmem(FINE), vmem((75, 8, 128)), vmem((8, 128)), vmem((4, 25, 8, 128)), vmem((12, 25, 2, 8, 128))],
         in_hbm=(0,),
         aliases={2: 0, 3: 1},
         scratch=[pltpu.SemaphoreType.DMA],
@@ -754,9 +759,8 @@
     part = vmem((2, 5, 4, 2, 8, 128))
     second, x_part = call(
         second_x_kernel,
-        (acc, first, scaled, flag, face, *got[:2], second),
+        (acc, first, scaled, flag, face, *got[:2]),
         [vmem(FINE), part],
-        aliases={7: 0},
         flops=2**20,
     )
     second, *sent = call(
@@ -769,10 +773,11 @@
     )
     got = exchange(*sent)
     (response,) = call(response_kernel, (coarse_smoother, face), [vmem((4, 25, 8, 128))], flops=2**20)
-    acc, coarse = call(
+    acc, coarse, second = call(
         restricted_volume_kernel,
-        (source, second, flag, jac8, damp8, coarse_smoother),
-        [vmem(COARSE), vmem(COARSE)],
+        (source, flag, jac8, damp8, coarse_smoother, acc, first, smoother, second),
+        [vmem(COARSE), vmem(COARSE), vmem(FINE)],
+        aliases={8: 2},
         flops=4 * 2**20,
     )
     coarse, *sent = call(

time: 33.9 us -> 33.9 us (level)
  no operation moved by 1% of the time
where the time goes in v17:
time: 33.9 us; the launch traced here: 33.7 us
  starting transfers between devices  20.4 us (60%)
  Pallas kernels  7.38 us (22%)
  waiting for transfers between devices  5.82 us (17%)
    ppermute x4, starting transfers between devices, exchange(): xo = lax.ppermute(xo, 'gx', odd_x)  13.9 us
    pallas_call x11, Pallas kernels, call(): pl.pallas_call(kernel, out_shape=outs, in_specs=in_specs, out_specs=out_s...  7.38 us
    ppermute x4, starting transfers between devices, exchange(): ye = lax.ppermute(ye, 'gy', even_y)  5.85 us
    ppermute x4, waiting for transfers between devices, exchange(): xo = lax.ppermute(xo, 'gx', odd_x)  5.52 us
    ppermute x4, starting transfers between devices, exchange(): yo = lax.ppermute(yo, 'gy', odd_y)  0.69 us
  transfers between devices with their start and end apart: 16, of which 6 were waited for; matrix products, arithmetic and copies ran while one was open for 0% of the time, Pallas kernels for 13%

profile of v17, /device:TPU:0, one launch (start us, length us, event | category | flops | bytes accessed | tf_op | source)
XLA Modules:
  0.0 33.7 jit_solution(4934845450884457558)
XLA Ops:
  0.0 0.0 copy-start.2
  0.0 0.0 copy-start.1
  0.0 1.7 %shard_map.64 = (f32[5,4,4,2,8,128]{5,4,3,2,1,0:T(8,128)S(1)}, bf16[25,4,4,16,128]{4,3,2,1,0:T(8,128)(2,1)S(1)}, f32[5,4,4,2,8,128]{5,4,3,2,1,0:T(8,128)S(1)}, s...) custom-call(f32[5,4,4,2,8,128]{5,4,3,2,1,0:T(8,128)} %bitcast.15, ...), custom_call_target="tpu_custom_call" | custom-call | flops 1638400 | bytes 4194304 | tf_op jit(solution)/shard_map/pallas_call | solution.py:700
  1.7 6.0 %collective-permute-start.2 = (f32[5,4,8,128]{3,2,1,0:T(8,128)S(1)}, f32[5,4,8,128]{3,2,1,0:T(8,128)S(1)}, u32[]{:S(2)}, u32[]{:S(2)}) collective-permute-start(f32[5,4,8,128]{3,2,1,0:T(8,128)S(1)} %get-tuple-element.55), channel_id=1, source_target_pairs={{0,28},{4,8},{8,4},{12,16},{16,12},{20,24},{24,20},{28,0},{1,29},{... | collective-permute-start | bytes 245768 | tf_op jit(solution)/shard_map/ppermute | solution.py:722
  7.7 0.0 collective-permute-start.3
  7.7 0.7 %collective-permute-start = (f32[5,4,8,128]{3,2,1,0:T(8,128)S(1)}, f32[5,4,8,128]{3,2,1,0:T(8,128)S(1)}, u32[]{:S(2)}, u32[]{:S(2)}) collective-permute-start(f32[5,4,8,128]{3,2,1,0:T(8,128)S(1)} %get-tuple-element.53), channel_id=1, source_target_pairs={{0,3},{1,2},{2,1},{3,0},{4,7},{5,6},{6,5},{7,4},{8,11},{9,10},{10,... | collective-permute-start | bytes 245768 | tf_op jit(solution)/shard_map/ppermute | solution.py:724
  8.4 1.0 %collective-permute-start.1 = (f32[5,4,8,128]{3,2,1,0:T(8,128)S(1)}, f32[5,4,8,128]{3,2,1,0:T(8,128)S(1)}, u32[]{:S(2)}, u32[]{:S(2)}) collective-permute-start(f32[5,4,8,128]{3,2,1,0:T(8,128)S(1)} %get-tuple-element.54), channel_id=1, source_target_pairs={{0,1},{1,0},{2,3},{3,2},{4,5},{5,4},{6,7},{7,6},{8,9},{9,8},{10,11... | collective-permute-start | bytes 245768 | tf_op jit(solution)/shard_map/ppermute | solution.py:725
  9.4 0.0 copy-done.2
  9.4 0.0 copy-done.1
  9.4 2.6 %shard_map.65 = (bf16[25,4,4,16,128]{4,3,2,1,0:T(8,128)(2,1)S(1)}, f32[5,4,4,2,8,128]{5,4,3,2,1,0:T(8,128)S(1)}, f32[5,4,4,2,8,128]{5,4,3,2,1,0:T(8,128)S(1)}, f...) custom-call(bf16[25,4,4,16,128]{4,3,2,1,0:T(8,128)(2,1)} %bitcast.14, ...), custom_call_target="tpu_custom_call", output_to_operand_aliasing={{0}: (2, {}), {1}: (3, {})} | custom-call | flops 9437184 | bytes 4194304 | tf_op jit(solution)/shard_map/pallas_call | solution.py:700
  12.0 0.0 collective-permute-done.2.rxo
  12.0 0.1 collective-permute-done.3.rxe
  12.2 0.2 shard_map.66
  12.3 0.1 collective-permute-done.ryo
  12.4 0.0 collective-permute-done.1.rye
  12.4 0.0 copy-start
  12.4 0.4 %shard_map.67 = (f32[5,4,4,2,8,128]{5,4,3,2,1,0:T(8,128)S(1)}, f32[5,8,128]{2,1,0:T(8,128)S(1)}, f32[5,8,128]{2,1,0:T(8,128)S(1)}, f32[5,8,128]{2,1,0:T(8,128)S(1)}, f32[5,8,128]{2,1,0:T(8,128)S(1)}) custom-call(f32[5,4,4,2,8,128]{5,4,3,2,1,0:T(8,128)S(1)} %get-tuple-element.48.acc_ref.fine_acc_ref, ...), custom_call_target="tpu_custom_call", output_to_operand_aliasing={{0}: (8, {})} | custom-call | flops 2097152 | bytes 4194304 | tf_op jit(solution)/shard_map/pallas_call | solution.py:700
  12.8 2.7 %collective-permute-start.4 = (f32[5,8,128]{2,1,0:T(8,128)S(1)}, f32[5,8,128]{2,1,0:T(8,128)S(1)}, u32[]{:S(2)}, u32[]{:S(2)}) collective-permute-start(f32[5,8,128]{2,1,0:T(8,128)S(1)} %get-tuple-element.61), channel_id=1, source_target_pairs={{0,28},{4,8},{8,4},{12,16},{16,12},{20,24},{24,20},{28,0},{1,29},{... | collective-permute-start | bytes 61448 | tf_op jit(solution)/shard_map/ppermute | solution.py:722
  15.5 0.0 collective-permute-start.5
  15.5 0.0 collective-permute-start.6
  15.5 1.6 %collective-permute-start.7 = (f32[5,8,128]{2,1,0:T(8,128)S(1)}, f32[5,8,128]{2,1,0:T(8,128)S(1)}, u32[]{:S(2)}, u32[]{:S(2)}) collective-permute-start(f32[5,8,128]{2,1,0:T(8,128)S(1)} %get-tuple-element.64), channel_id=1, source_target_pairs={{0,1},{1,0},{2,3},{3,2},{4,5},{5,4},{6,7},{7,6},{8,9},{9,8},{10,11... | collective-permute-start | bytes 61448 | tf_op jit(solution)/shard_map/ppermute | solution.py:725
  17.1 0.0 copy-done
  17.1 0.2 shard_map.69.response_ref
  17.3 0.7 %shard_map.68 = (f32[5,2,2,8,128]{4,3,2,1,0:T(8,128)S(1)}, f32[5,2,2,8,128]{4,3,2,1,0:T(8,128)S(1)}, f32[5,4,4,2,8,128]{5,4,3,2,1,0:T(8,128)S(1)}) custom-call(f32[5,4,4,2,8,128]{5,4,3,2,1,0:T(8,128)S(1)} %get-tuple-element.42.src_ref, s32[3,8,128]{2,1,0:T(8,128)S(1)} %get-tuple-element.43.flag_ref, ...), custom_call_target="tpu_custom_call", output_to_operand_aliasing={{2}: (8, {})} | custom-call | flops 4194304 | bytes 4194304 | tf_op jit(solution)/shard_map/pallas_call | solution.py:700
  18.1 1.3 %collective-permute-done.4.rxo = f32[5,8,128]{2,1,0:T(8,128)S(1)} collective-permute-done((f32[5,8,128]{2,1,0:T(8,128)S(1)}, f32[5,8,128]{2,1,0:T(8,128)S(1)}, u32[]{:S(2)}, u32[]{:S(2)}) %collective-permute-start.4) | collective-permute-done | bytes 20512 | tf_op jit(solution)/shard_map/ppermute | solution.py:722
  19.4 0.1 collective-permute-done.5.rxe
  19.5 0.0 collective-permute-done.6.ryo
  19.5 0.0 collective-permute-done.7.rye
  19.5 0.1 shard_map.70
  19.6 2.6 %collective-permute-start.8 = (f32[5,8,128]{2,1,0:T(8,128)S(1)}, f32[5,8,128]{2,1,0:T(8,128)S(1)}, u32[]{:S(2)}, u32[]{:S(2)}) collective-permute-start(f32[5,8,128]{2,1,0:T(8,128)S(1)} %get-tuple-element.68), channel_id=1, source_target_pairs={{0,28},{4,8},{8,4},{12,16},{16,12},{20,24},{24,20},{28,0},{1,29},{... | collective-permute-start | bytes 61448 | tf_op jit(solution)/shard_map/ppermute | solution.py:722
  22.1 0.0 collective-permute-start.9
  22.1 0.0 collective-permute-start.10
  22.1 1.6 %collective-permute-start.11 = (f32[5,8,128]{2,1,0:T(8,128)S(1)}, f32[5,8,128]{2,1,0:T(8,128)S(1)}, u32[]{:S(2)}, u32[]{:S(2)}) collective-permute-start(f32[5,8,128]{2,1,0:T(8,128)S(1)} %get-tuple-element.71), channel_id=1, source_target_pairs={{0,1},{1,0},{2,3},{3,2},{4,5},{5,4},{6,7},{7,6},{8,9},{9,8},{10,11... | collective-permute-start | bytes 61448 | tf_op jit(solution)/shard_map/ppermute | solution.py:725
  23.8 0.3 shard_map.71
  24.1 2.1 %collective-permute-done.8.rxo = f32[5,8,128]{2,1,0:T(8,128)S(1)} collective-permute-done((f32[5,8,128]{2,1,0:T(8,128)S(1)}, f32[5,8,128]{2,1,0:T(8,128)S(1)}, u32[]{:S(2)}, u32[]{:S(2)}) %collective-permute-start.8) | collective-permute-done | bytes 20512 | tf_op jit(solution)/shard_map/ppermute | solution.py:722
  26.1 0.0 collective-permute-done.9.rxe
  26.1 0.0 collective-permute-done.10.ryo
  26.2 0.0 collective-permute-done.11.rye
  26.2 0.1 shard_map.72
  26.2 2.5 %collective-permute-start.12 = (f32[5,8,128]{2,1,0:T(8,128)S(1)}, f32[5,8,128]{2,1,0:T(8,128)S(1)}, u32[]{:S(2)}, u32[]{:S(2)}) collective-permute-start(f32[5,8,128]{2,1,0:T(8,128)S(1)} %get-tuple-element.74), channel_id=1, source_target_pairs={{0,28},{4,8},{8,4},{12,16},{16,12},{20,24},{24,20},{28,0},{1,29},{... | collective-permute-start | bytes 61448 | tf_op jit(solution)/shard_map/ppermute | solution.py:722
  28.8 0.0 collective-permute-start.13
  28.8 0.0 collective-permute-start.14
  28.8 1.6 %collective-permute-start.15 = (f32[5,8,128]{2,1,0:T(8,128)S(1)}, f32[5,8,128]{2,1,0:T(8,128)S(1)}, u32[]{:S(2)}, u32[]{:S(2)}) collective-permute-start(f32[5,8,128]{2,1,0:T(8,128)S(1)} %get-tuple-element.77), channel_id=1, source_target_pairs={{0,1},{1,0},{2,3},{3,2},{4,5},{5,4},{6,7},{7,6},{8,9},{9,8},{10,11... | collective-permute-start | bytes 61448 | tf_op jit(solution)/shard_map/ppermute | solution.py:725
  30.4 0.2 shard_map.73.c_ref
  30.7 2.1 %collective-permute-done.12.rxo = f32[5,8,128]{2,1,0:T(8,128)S(1)} collective-permute-done((f32[5,8,128]{2,1,0:T(8,128)S(1)}, f32[5,8,128]{2,1,0:T(8,128)S(1)}, u32[]{:S(2)}, u32[]{:S(2)}) %collective-permute-start.12) | collective-permute-done | bytes 20512 | tf_op jit(solution)/shard_map/ppermute | solution.py:722
  32.8 0.0 collective-permute-done.13.rxe
  32.8 0.0 collective-permute-done.14.ryo
  32.8 0.0 collective-permute-done.15.rye
  32.8 0.9 %shard_map.74 = f32[5,4,4,2,8,128]{5,4,3,2,1,0:T(8,128)} custom-call(f32[5,2,2,8,128]{4,3,2,1,0:T(8,128)S(1)} %shard_map.73.c_ref, s32[3,8,128]{2,1,0:T(8,128)S(1)} %get-tuple-element.43.flag_ref, f32[4,25,8,128]{3,2,1,0:T(8,128)S(1)} %shard_map.69.response_ref, f32[5,8,128]{2,1,0:T(8,128)S(1)} %collective-permute-done.12.rxo, ...), custom_call_target="tpu_custom_call" | custom-call | flops 1048576 | bytes 4194304 | tf_op jit(solution)/shard_map/pallas_call | solution.py:700
Async XLA Ops:
  0.0 9.4 %copy-start.2 = (f32[2,2,128]{2,1,0:T(2,128)S(1)}, f32[2,2,128]{2,1,0:T(2,128)}, u32[]{:S(2)}) copy-start(f32[2,2,128]{2,1,0:T(2,128)} %param.8) | copy-start | bytes 6148
  0.0 9.4 %copy-start.1 = (f32[3,5,5,2,2,128]{5,4,3,2,1,0:T(2,128)S(1)}, f32[3,5,5,2,2,128]{5,4,3,2,1,0:T(2,128)}, u32[]{:S(2)}) copy-start(f32[3,5,5,2,2,128]{5,4,3,2,1,0:T(2,128)} %param.7) | copy-start | bytes 460804
  1.7 10.3 %collective-permute-start.2 = (f32[5,4,8,128]{3,2,1,0:T(8,128)S(1)}, f32[5,4,8,128]{3,2,1,0:T(8,128)S(1)}, u32[]{:S(2)}, u32[]{:S(2)}) collective-permute-start(f32[5,4,8,128]{3,2,1,0:T(8,128)S(1)} %get-tuple-element.55), channel_id=1, source_target_pairs={{0,28},{4,8},{8,4},{12,16},{16,12},{20,24},{24,20},{28,0},{1,29},{... | collective-permute-start | bytes 245768 | tf_op jit(solution)/shard_map/ppermute | solution.py:722
  7.7 4.4 %collective-permute-start.3 = (f32[5,4,8,128]{3,2,1,0:T(8,128)S(1)}, f32[5,4,8,128]{3,2,1,0:T(8,128)S(1)}, u32[]{:S(2)}, u32[]{:S(2)}) collective-permute-start(f32[5,4,8,128]{3,2,1,0:T(8,128)S(1)} %get-tuple-element.56), channel_id=1, source_target_pairs={{0,4},{4,0},{8,12},{12,8},{16,20},{20,16},{24,28},{28,24},{1,5},{5... | collective-permute-start | bytes 245768 | tf_op jit(solution)/shard_map/ppermute | solution.py:723
  7.7 4.7 %collective-permute-start = (f32[5,4,8,128]{3,2,1,0:T(8,128)S(1)}, f32[5,4,8,128]{3,2,1,0:T(8,128)S(1)}, u32[]{:S(2)}, u32[]{:S(2)}) collective-permute-start(f32[5,4,8,128]{3,2,1,0:T(8,128)S(1)} %get-tuple-element.53), channel_id=1, source_target_pairs={{0,3},{1,2},{2,1},{3,0},{4,7},{5,6},{6,5},{7,4},{8,11},{9,10},{10,... | collective-permute-start | bytes 245768 | tf_op jit(solution)/shard_map/ppermute | solution.py:724
  8.4 4.0 %collective-permute-start.1 = (f32[5,4,8,128]{3,2,1,0:T(8,128)S(1)}, f32[5,4,8,128]{3,2,1,0:T(8,128)S(1)}, u32[]{:S(2)}, u32[]{:S(2)}) collective-permute-start(f32[5,4,8,128]{3,2,1,0:T(8,128)S(1)} %get-tuple-element.54), channel_id=1, source_target_pairs={{0,1},{1,0},{2,3},{3,2},{4,5},{5,4},{6,7},{7,6},{8,9},{9,8},{10,11... | collective-permute-start | bytes 245768 | tf_op jit(solution)/shard_map/ppermute | solution.py:725
  12.4 4.7 %copy-start = (bf16[5,5,2,2,2,2,2,128]{7,6,5,4,3,2,1,0:T(2,128)(2,1)S(1)}, bf16[5,5,2,2,2,2,2,128]{7,6,5,4,3,2,1,0:T(2,128)(2,1)}, u32[]{:S(2)}) copy-start(bf16[5,5,2,2,2,2,2,128]{7,6,5,4,3,2,1,0:T(2,128)(2,1)} %param.11) | copy-start | bytes 614404
  12.8 6.7 %collective-permute-start.4 = (f32[5,8,128]{2,1,0:T(8,128)S(1)}, f32[5,8,128]{2,1,0:T(8,128)S(1)}, u32[]{:S(2)}, u32[]{:S(2)}) collective-permute-start(f32[5,8,128]{2,1,0:T(8,128)S(1)} %get-tuple-element.61), channel_id=1, source_target_pairs={{0,28},{4,8},{8,4},{12,16},{16,12},{20,24},{24,20},{28,0},{1,29},{... | collective-permute-start | bytes 61448 | tf_op jit(solution)/shard_map/ppermute | solution.py:722
  15.5 4.0 %collective-permute-start.5 = (f32[5,8,128]{2,1,0:T(8,128)S(1)}, f32[5,8,128]{2,1,0:T(8,128)S(1)}, u32[]{:S(2)}, u32[]{:S(2)}) collective-permute-start(f32[5,8,128]{2,1,0:T(8,128)S(1)} %get-tuple-element.62), channel_id=1, source_target_pairs={{0,4},{4,0},{8,12},{12,8},{16,20},{20,16},{24,28},{28,24},{1,5},{5... | collective-permute-start | bytes 61448 | tf_op jit(solution)/shard_map/ppermute | solution.py:723
  15.5 4.0 %collective-permute-start.6 = (f32[5,8,128]{2,1,0:T(8,128)S(1)}, f32[5,8,128]{2,1,0:T(8,128)S(1)}, u32[]{:S(2)}, u32[]{:S(2)}) collective-permute-start(f32[5,8,128]{2,1,0:T(8,128)S(1)} %get-tuple-element.63), channel_id=1, source_target_pairs={{0,3},{1,2},{2,1},{3,0},{4,7},{5,6},{6,5},{7,4},{8,11},{9,10},{10,... | collective-permute-start | bytes 61448 | tf_op jit(solution)/shard_map/ppermute | solution.py:724
  15.5 4.0 %collective-permute-start.7 = (f32[5,8,128]{2,1,0:T(8,128)S(1)}, f32[5,8,128]{2,1,0:T(8,128)S(1)}, u32[]{:S(2)}, u32[]{:S(2)}) collective-permute-start(f32[5,8,128]{2,1,0:T(8,128)S(1)} %get-tuple-element.64), channel_id=1, source_target_pairs={{0,1},{1,0},{2,3},{3,2},{4,5},{5,4},{6,7},{7,6},{8,9},{9,8},{10,11... | collective-permute-start | bytes 61448 | tf_op jit(solution)/shard_map/ppermute | solution.py:725
  19.6 6.6 %collective-permute-start.8 = (f32[5,8,128]{2,1,0:T(8,128)S(1)}, f32[5,8,128]{2,1,0:T(8,128)S(1)}, u32[]{:S(2)}, u32[]{:S(2)}) collective-permute-start(f32[5,8,128]{2,1,0:T(8,128)S(1)} %get-tuple-element.68), channel_id=1, source_target_pairs={{0,28},{4,8},{8,4},{12,16},{16,12},{20,24},{24,20},{28,0},{1,29},{... | collective-permute-start | bytes 61448 | tf_op jit(solution)/shard_map/ppermute | solution.py:722
  22.1 4.0 %collective-permute-start.9 = (f32[5,8,128]{2,1,0:T(8,128)S(1)}, f32[5,8,128]{2,1,0:T(8,128)S(1)}, u32[]{:S(2)}, u32[]{:S(2)}) collective-permute-start(f32[5,8,128]{2,1,0:T(8,128)S(1)} %get-tuple-element.69), channel_id=1, source_target_pairs={{0,4},{4,0},{8,12},{12,8},{16,20},{20,16},{24,28},{28,24},{1,5},{5... | collective-permute-start | bytes 61448 | tf_op jit(solution)/shard_map/ppermute | solution.py:723
  22.1 4.0 %collective-permute-start.10 = (f32[5,8,128]{2,1,0:T(8,128)S(1)}, f32[5,8,128]{2,1,0:T(8,128)S(1)}, u32[]{:S(2)}, u32[]{:S(2)}) collective-permute-start(f32[5,8,128]{2,1,0:T(8,128)S(1)} %get-tuple-element.70), channel_id=1, source_target_pairs={{0,3},{1,2},{2,1},{3,0},{4,7},{5,6},{6,5},{7,4},{8,11},{9,10},{10,... | collective-permute-start | bytes 61448 | tf_op jit(solution)/shard_map/ppermute | solution.py:724
  22.1 4.0 %collective-permute-start.11 = (f32[5,8,128]{2,1,0:T(8,128)S(1)}, f32[5,8,128]{2,1,0:T(8,128)S(1)}, u32[]{:S(2)}, u32[]{:S(2)}) collective-permute-start(f32[5,8,128]{2,1,0:T(8,128)S(1)} %get-tuple-element.71), channel_id=1, source_target_pairs={{0,1},{1,0},{2,3},{3,2},{4,5},{5,4},{6,7},{7,6},{8,9},{9,8},{10,11... | collective-permute-start | bytes 61448 | tf_op jit(solution)/shard_map/ppermute | solution.py:725
  26.2 6.5 %collective-permute-start.12 = (f32[5,8,128]{2,1,0:T(8,128)S(1)}, f32[5,8,128]{2,1,0:T(8,128)S(1)}, u32[]{:S(2)}, u32[]{:S(2)}) collective-permute-start(f32[5,8,128]{2,1,0:T(8,128)S(1)} %get-tuple-element.74), channel_id=1, source_target_pairs={{0,28},{4,8},{8,4},{12,16},{16,12},{20,24},{24,20},{28,0},{1,29},{... | collective-permute-start | bytes 61448 | tf_op jit(solution)/shard_map/ppermute | solution.py:722
  28.8 4.0 %collective-permute-start.13 = (f32[5,8,128]{2,1,0:T(8,128)S(1)}, f32[5,8,128]{2,1,0:T(8,128)S(1)}, u32[]{:S(2)}, u32[]{:S(2)}) collective-permute-start(f32[5,8,128]{2,1,0:T(8,128)S(1)} %get-tuple-element.75), channel_id=1, source_target_pairs={{0,4},{4,0},{8,12},{12,8},{16,20},{20,16},{24,28},{28,24},{1,5},{5... | collective-permute-start | bytes 61448 | tf_op jit(solution)/shard_map/ppermute | solution.py:723
  28.8 4.0 %collective-permute-start.14 = (f32[5,8,128]{2,1,0:T(8,128)S(1)}, f32[5,8,128]{2,1,0:T(8,128)S(1)}, u32[]{:S(2)}, u32[]{:S(2)}) collective-permute-start(f32[5,8,128]{2,1,0:T(8,128)S(1)} %get-tuple-element.76), channel_id=1, source_target_pairs={{0,3},{1,2},{2,1},{3,0},{4,7},{5,6},{6,5},{7,4},{8,11},{9,10},{10,... | collective-permute-start | bytes 61448 | tf_op jit(solution)/shard_map/ppermute | solution.py:724
  28.8 4.0 %collective-permute-start.15 = (f32[5,8,128]{2,1,0:T(8,128)S(1)}, f32[5,8,128]{2,1,0:T(8,128)S(1)}, u32[]{:S(2)}, u32[]{:S(2)}) collective-permute-start(f32[5,8,128]{2,1,0:T(8,128)S(1)} %get-tuple-element.77), channel_id=1, source_target_pairs={{0,1},{1,0},{2,3},{3,2},{4,5},{5,4},{6,7},{7,6},{8,9},{9,8},{10,11... | collective-permute-start | bytes 61448 | tf_op jit(solution)/shard_map/ppermute | solution.py:725

commit v18 on v15

--- a/solution.py
+++ b/solution.py
@@ -658,14 +658,15 @@
                 value = c[v][i][j]
                 inner = FAR * value + NEAR * sroll(value, 4)
                 by_c[i][j] = (jnp.where(low, value, inner), jnp.where(low, inner, value))
-        for q in range(2):
-            lines = [spread(by_c[i][0][q], by_c[i][1][q]) for i in range(2)]
-            for b in range(4):
-                for a, value in enumerate(spread(lines[0][b], lines[1][b])):
-                    out_ref[v, a, b, q] = second_ref[v, a, b, q] + value
-        copy = pltpu.make_async_copy(out_ref.at[v], out_hbm.at[v], sems.at[v])
-        copy.start()
-        copies.append(copy)
+        lines = [[spread(by_c[i][0][q], by_c[i][1][q]) for i in range(2)] for q in range(2)]
+        for part in (slice(0, 2), slice(2, 4)) if v == 4 else (slice(0, 4),):
+            for b in range(part.start, part.stop):
+                for q in range(2):
+                    for a, value in enumerate(spread(lines[q][0][b], lines[q][1][b])):
+                        out_ref[v, a, b, q] = second_ref[v, a, b, q] + value
+            copy = pltpu.make_async_copy(out_ref.at[v, :, part], out_hbm.at[v, :, part], sems.at[len(copies)])
+            copy.start()
+            copies.append(copy)
     for copy in copies:
         copy.wait()
 
@@ -797,7 +798,7 @@
         (coarse, flag, response, *got, second),
         [jax.ShapeDtypeStruct(FINE, F32)],
         out_hbm=(0,),
-        scratch=[pltpu.VMEM(FINE, F32), pltpu.SemaphoreType.DMA((5,))],
+        scratch=[pltpu.VMEM(FINE, F32), pltpu.SemaphoreType.DMA((6,))],
         flops=2**20,
     )
     return out.reshape(5, 4, 4, 4, 2, 2, 128)

time: 33.9 us -> 33.9 us (level)
  no operation moved by 1% of the time
where the time goes in v18:
time: 33.9 us; the launch traced here: 33.7 us
  starting transfers between devices  20.4 us (60%)
  Pallas kernels  7.34 us (22%)
  waiting for transfers between devices  5.85 us (17%)
    ppermute x4, starting transfers between devices, exchange(): xo = lax.ppermute(xo, 'gx', odd_x)  13.9 us
    pallas_call x11, Pallas kernels, call(): pl.pallas_call(kernel, out_shape=outs, in_specs=in_specs, out_specs=out_s...  7.34 us
    ppermute x4, starting transfers between devices, exchange(): ye = lax.ppermute(ye, 'gy', even_y)  5.85 us
    ppermute x4, waiting for transfers between devices, exchange(): xo = lax.ppermute(xo, 'gx', odd_x)  5.62 us
    ppermute x4, starting transfers between devices, exchange(): yo = lax.ppermute(yo, 'gy', odd_y)  0.69 us
  transfers between devices with their start and end apart: 16, of which 6 were waited for; matrix products, arithmetic and copies ran while one was open for 0% of the time, Pallas kernels for 13%

profile of v18, /device:TPU:0, one launch (start us, length us, event | category | flops | bytes accessed | tf_op | source)
XLA Modules:
  0.0 33.7 jit_solution(5297166264540028531)
XLA Ops:
  0.0 0.0 copy-start.2
  0.0 0.0 copy-start.1
  0.0 1.7 %shard_map.64 = (f32[5,4,4,2,8,128]{5,4,3,2,1,0:T(8,128)S(1)}, bf16[25,4,4,16,128]{4,3,2,1,0:T(8,128)(2,1)S(1)}, f32[5,4,4,2,8,128]{5,4,3,2,1,0:T(8,128)S(1)}, s...) custom-call(f32[5,4,4,2,8,128]{5,4,3,2,1,0:T(8,128)} %bitcast.15, ...), custom_call_target="tpu_custom_call" | custom-call | flops 1638400 | bytes 4194304 | tf_op jit(solution)/shard_map/pallas_call | solution.py:696
  1.7 6.0 %collective-permute-start.2 = (f32[5,4,8,128]{3,2,1,0:T(8,128)S(1)}, f32[5,4,8,128]{3,2,1,0:T(8,128)S(1)}, u32[]{:S(2)}, u32[]{:S(2)}) collective-permute-start(f32[5,4,8,128]{3,2,1,0:T(8,128)S(1)} %get-tuple-element.51), channel_id=1, source_target_pairs={{0,28},{4,8},{8,4},{12,16},{16,12},{20,24},{24,20},{28,0},{1,29},{... | collective-permute-start | bytes 245768 | tf_op jit(solution)/shard_map/ppermute | solution.py:718
  7.7 0.0 collective-permute-start.3
  7.7 0.7 %collective-permute-start = (f32[5,4,8,128]{3,2,1,0:T(8,128)S(1)}, f32[5,4,8,128]{3,2,1,0:T(8,128)S(1)}, u32[]{:S(2)}, u32[]{:S(2)}) collective-permute-start(f32[5,4,8,128]{3,2,1,0:T(8,128)S(1)} %get-tuple-element.49), channel_id=1, source_target_pairs={{0,3},{1,2},{2,1},{3,0},{4,7},{5,6},{6,5},{7,4},{8,11},{9,10},{10,... | collective-permute-start | bytes 245768 | tf_op jit(solution)/shard_map/ppermute | solution.py:720
  8.4 1.0 %collective-permute-start.1 = (f32[5,4,8,128]{3,2,1,0:T(8,128)S(1)}, f32[5,4,8,128]{3,2,1,0:T(8,128)S(1)}, u32[]{:S(2)}, u32[]{:S(2)}) collective-permute-start(f32[5,4,8,128]{3,2,1,0:T(8,128)S(1)} %get-tuple-element.50), channel_id=1, source_target_pairs={{0,1},{1,0},{2,3},{3,2},{4,5},{5,4},{6,7},{7,6},{8,9},{9,8},{10,11... | collective-permute-start | bytes 245768 | tf_op jit(solution)/shard_map/ppermute | solution.py:721
  9.4 0.0 copy-done.2
  9.4 0.0 copy-done.1
  9.4 2.7 %shard_map.65 = (bf16[25,4,4,16,128]{4,3,2,1,0:T(8,128)(2,1)S(1)}, f32[5,4,4,2,8,128]{5,4,3,2,1,0:T(8,128)S(1)}, f32[5,4,4,2,8,128]{5,4,3,2,1,0:T(8,128)S(1)}, f...) custom-call(bf16[25,4,4,16,128]{4,3,2,1,0:T(8,128)(2,1)} %bitcast.14, ...), custom_call_target="tpu_custom_call", output_to_operand_aliasing={{0}: (2, {}), {1}: (3, {})} | custom-call | flops 9437184 | bytes 4194304 | tf_op jit(solution)/shard_map/pallas_call | solution.py:696
  12.1 0.0 collective-permute-done.2.rxo
  12.1 0.1 collective-permute-done.3.rxe
  12.2 0.2 shard_map.66
  12.3 0.1 collective-permute-done.ryo
  12.4 0.0 collective-permute-done.1.rye
  12.4 0.0 copy-start
  12.4 0.3 shard_map.67
  12.7 2.7 %collective-permute-start.4 = (f32[5,8,128]{2,1,0:T(8,128)S(1)}, f32[5,8,128]{2,1,0:T(8,128)S(1)}, u32[]{:S(2)}, u32[]{:S(2)}) collective-permute-start(f32[5,8,128]{2,1,0:T(8,128)S(1)} %get-tuple-element.60), channel_id=1, source_target_pairs={{0,28},{4,8},{8,4},{12,16},{16,12},{20,24},{24,20},{28,0},{1,29},{... | collective-permute-start | bytes 61448 | tf_op jit(solution)/shard_map/ppermute | solution.py:718
  15.5 0.0 collective-permute-start.5
  15.5 0.0 collective-permute-start.6
  15.5 1.6 %collective-permute-start.7 = (f32[5,8,128]{2,1,0:T(8,128)S(1)}, f32[5,8,128]{2,1,0:T(8,128)S(1)}, u32[]{:S(2)}, u32[]{:S(2)}) collective-permute-start(f32[5,8,128]{2,1,0:T(8,128)S(1)} %get-tuple-element.63), channel_id=1, source_target_pairs={{0,1},{1,0},{2,3},{3,2},{4,5},{5,4},{6,7},{7,6},{8,9},{9,8},{10,11... | collective-permute-start | bytes 61448 | tf_op jit(solution)/shard_map/ppermute | solution.py:721
  17.1 0.0 copy-done
  17.1 0.2 shard_map.69.response_ref
  17.3 0.6 %shard_map.68 = (f32[5,2,2,8,128]{4,3,2,1,0:T(8,128)S(1)}, f32[5,2,2,8,128]{4,3,2,1,0:T(8,128)S(1)}) custom-call(f32[5,4,4,2,8,128]{5,4,3,2,1,0:T(8,128)S(1)} %get-tuple-element.41.src_ref, f32[5,4,4,2,8,128]{5,4,3,2,1,0:T(8,128)S(1)} %get-tuple-element.56.u_ref.second_ref, s32[3,8,128]{2,1,0:T(8,128)S(1)} %get-tuple-element.44.flag_ref, ...), custom_call_target="tpu_custom_call" | custom-call | flops 4194304 | bytes 4194304 | tf_op jit(solution)/shard_map/pallas_call | solution.py:696
  17.9 1.4 %collective-permute-done.4.rxo = f32[5,8,128]{2,1,0:T(8,128)S(1)} collective-permute-done((f32[5,8,128]{2,1,0:T(8,128)S(1)}, f32[5,8,128]{2,1,0:T(8,128)S(1)}, u32[]{:S(2)}, u32[]{:S(2)}) %collective-permute-start.4) | collective-permute-done | bytes 20512 | tf_op jit(solution)/shard_map/ppermute | solution.py:718
  19.4 0.1 collective-permute-done.5.rxe
  19.5 0.0 collective-permute-done.6.ryo
  19.5 0.0 collective-permute-done.7.rye
  19.5 0.1 shard_map.70
  19.6 2.6 %collective-permute-start.8 = (f32[5,8,128]{2,1,0:T(8,128)S(1)}, f32[5,8,128]{2,1,0:T(8,128)S(1)}, u32[]{:S(2)}, u32[]{:S(2)}) collective-permute-start(f32[5,8,128]{2,1,0:T(8,128)S(1)} %get-tuple-element.67), channel_id=1, source_target_pairs={{0,28},{4,8},{8,4},{12,16},{16,12},{20,24},{24,20},{28,0},{1,29},{... | collective-permute-start | bytes 61448 | tf_op jit(solution)/shard_map/ppermute | solution.py:718
  22.1 0.0 collective-permute-start.9
  22.1 0.0 collective-permute-start.10
  22.1 1.6 %collective-permute-start.11 = (f32[5,8,128]{2,1,0:T(8,128)S(1)}, f32[5,8,128]{2,1,0:T(8,128)S(1)}, u32[]{:S(2)}, u32[]{:S(2)}) collective-permute-start(f32[5,8,128]{2,1,0:T(8,128)S(1)} %get-tuple-element.70), channel_id=1, source_target_pairs={{0,1},{1,0},{2,3},{3,2},{4,5},{5,4},{6,7},{7,6},{8,9},{9,8},{10,11... | collective-permute-start | bytes 61448 | tf_op jit(solution)/shard_map/ppermute | solution.py:721
  23.7 0.3 shard_map.71
  24.0 2.1 %collective-permute-done.8.rxo = f32[5,8,128]{2,1,0:T(8,128)S(1)} collective-permute-done((f32[5,8,128]{2,1,0:T(8,128)S(1)}, f32[5,8,128]{2,1,0:T(8,128)S(1)}, u32[]{:S(2)}, u32[]{:S(2)}) %collective-permute-start.8) | collective-permute-done | bytes 20512 | tf_op jit(solution)/shard_map/ppermute | solution.py:718
  26.1 0.0 collective-permute-done.9.rxe
  26.1 0.0 collective-permute-done.10.ryo
  26.1 0.0 collective-permute-done.11.rye
  26.1 0.1 shard_map.72
  26.2 2.5 %collective-permute-start.12 = (f32[5,8,128]{2,1,0:T(8,128)S(1)}, f32[5,8,128]{2,1,0:T(8,128)S(1)}, u32[]{:S(2)}, u32[]{:S(2)}) collective-permute-start(f32[5,8,128]{2,1,0:T(8,128)S(1)} %get-tuple-element.73), channel_id=1, source_target_pairs={{0,28},{4,8},{8,4},{12,16},{16,12},{20,24},{24,20},{28,0},{1,29},{... | collective-permute-start | bytes 61448 | tf_op jit(solution)/shard_map/ppermute | solution.py:718
  28.8 0.0 collective-permute-start.13
  28.8 0.0 collective-permute-start.14
  28.8 1.6 %collective-permute-start.15 = (f32[5,8,128]{2,1,0:T(8,128)S(1)}, f32[5,8,128]{2,1,0:T(8,128)S(1)}, u32[]{:S(2)}, u32[]{:S(2)}) collective-permute-start(f32[5,8,128]{2,1,0:T(8,128)S(1)} %get-tuple-element.76), channel_id=1, source_target_pairs={{0,1},{1,0},{2,3},{3,2},{4,5},{5,4},{6,7},{7,6},{8,9},{9,8},{10,11... | collective-permute-start | bytes 61448 | tf_op jit(solution)/shard_map/ppermute | solution.py:721
  30.4 0.2 shard_map.73.c_ref
  30.6 2.1 %collective-permute-done.12.rxo = f32[5,8,128]{2,1,0:T(8,128)S(1)} collective-permute-done((f32[5,8,128]{2,1,0:T(8,128)S(1)}, f32[5,8,128]{2,1,0:T(8,128)S(1)}, u32[]{:S(2)}, u32[]{:S(2)}) %collective-permute-start.12) | collective-permute-done | bytes 20512 | tf_op jit(solution)/shard_map/ppermute | solution.py:718
  32.8 0.0 collective-permute-done.13.rxe
  32.8 0.0 collective-permute-done.14.ryo
  32.8 0.0 collective-permute-done.15.rye
  32.8 0.9 %shard_map.74 = f32[5,4,4,2,8,128]{5,4,3,2,1,0:T(8,128)} custom-call(f32[5,2,2,8,128]{4,3,2,1,0:T(8,128)S(1)} %shard_map.73.c_ref, s32[3,8,128]{2,1,0:T(8,128)S(1)} %get-tuple-element.44.flag_ref, f32[4,25,8,128]{3,2,1,0:T(8,128)S(1)} %shard_map.69.response_ref, f32[5,8,128]{2,1,0:T(8,128)S(1)} %collective-permute-done.12.rxo, ...), custom_call_target="tpu_custom_call" | custom-call | flops 1048576 | bytes 4194304 | tf_op jit(solution)/shard_map/pallas_call | solution.py:696
Async XLA Ops:
  0.0 9.4 %copy-start.2 = (f32[2,2,128]{2,1,0:T(2,128)S(1)}, f32[2,2,128]{2,1,0:T(2,128)}, u32[]{:S(2)}) copy-start(f32[2,2,128]{2,1,0:T(2,128)} %param.8) | copy-start | bytes 6148
  0.0 9.4 %copy-start.1 = (f32[3,5,5,2,2,128]{5,4,3,2,1,0:T(2,128)S(1)}, f32[3,5,5,2,2,128]{5,4,3,2,1,0:T(2,128)}, u32[]{:S(2)}) copy-start(f32[3,5,5,2,2,128]{5,4,3,2,1,0:T(2,128)} %param.7) | copy-start | bytes 460804
  1.7 10.4 %collective-permute-start.2 = (f32[5,4,8,128]{3,2,1,0:T(8,128)S(1)}, f32[5,4,8,128]{3,2,1,0:T(8,128)S(1)}, u32[]{:S(2)}, u32[]{:S(2)}) collective-permute-start(f32[5,4,8,128]{3,2,1,0:T(8,128)S(1)} %get-tuple-element.51), channel_id=1, source_target_pairs={{0,28},{4,8},{8,4},{12,16},{16,12},{20,24},{24,20},{28,0},{1,29},{... | collective-permute-start | bytes 245768 | tf_op jit(solution)/shard_map/ppermute | solution.py:718
  7.7 4.4 %collective-permute-start.3 = (f32[5,4,8,128]{3,2,1,0:T(8,128)S(1)}, f32[5,4,8,128]{3,2,1,0:T(8,128)S(1)}, u32[]{:S(2)}, u32[]{:S(2)}) collective-permute-start(f32[5,4,8,128]{3,2,1,0:T(8,128)S(1)} %get-tuple-element.52), channel_id=1, source_target_pairs={{0,4},{4,0},{8,12},{12,8},{16,20},{20,16},{24,28},{28,24},{1,5},{5... | collective-permute-start | bytes 245768 | tf_op jit(solution)/shard_map/ppermute | solution.py:719
  7.7 4.7 %collective-permute-start = (f32[5,4,8,128]{3,2,1,0:T(8,128)S(1)}, f32[5,4,8,128]{3,2,1,0:T(8,128)S(1)}, u32[]{:S(2)}, u32[]{:S(2)}) collective-permute-start(f32[5,4,8,128]{3,2,1,0:T(8,128)S(1)} %get-tuple-element.49), channel_id=1, source_target_pairs={{0,3},{1,2},{2,1},{3,0},{4,7},{5,6},{6,5},{7,4},{8,11},{9,10},{10,... | collective-permute-start | bytes 245768 | tf_op jit(solution)/shard_map/ppermute | solution.py:720
  8.4 4.0 %collective-permute-start.1 = (f32[5,4,8,128]{3,2,1,0:T(8,128)S(1)}, f32[5,4,8,128]{3,2,1,0:T(8,128)S(1)}, u32[]{:S(2)}, u32[]{:S(2)}) collective-permute-start(f32[5,4,8,128]{3,2,1,0:T(8,128)S(1)} %get-tuple-element.50), channel_id=1, source_target_pairs={{0,1},{1,0},{2,3},{3,2},{4,5},{5,4},{6,7},{7,6},{8,9},{9,8},{10,11... | collective-permute-start | bytes 245768 | tf_op jit(solution)/shard_map/ppermute | solution.py:721
  12.4 4.7 %copy-start = (bf16[5,5,2,2,2,2,2,128]{7,6,5,4,3,2,1,0:T(2,128)(2,1)S(1)}, bf16[5,5,2,2,2,2,2,128]{7,6,5,4,3,2,1,0:T(2,128)(2,1)}, u32[]{:S(2)}) copy-start(bf16[5,5,2,2,2,2,2,128]{7,6,5,4,3,2,1,0:T(2,128)(2,1)} %param.11) | copy-start | bytes 614404
  12.7 6.7 %collective-permute-start.4 = (f32[5,8,128]{2,1,0:T(8,128)S(1)}, f32[5,8,128]{2,1,0:T(8,128)S(1)}, u32[]{:S(2)}, u32[]{:S(2)}) collective-permute-start(f32[5,8,128]{2,1,0:T(8,128)S(1)} %get-tuple-element.60), channel_id=1, source_target_pairs={{0,28},{4,8},{8,4},{12,16},{16,12},{20,24},{24,20},{28,0},{1,29},{... | collective-permute-start | bytes 61448 | tf_op jit(solution)/shard_map/ppermute | solution.py:718
  15.5 4.0 %collective-permute-start.5 = (f32[5,8,128]{2,1,0:T(8,128)S(1)}, f32[5,8,128]{2,1,0:T(8,128)S(1)}, u32[]{:S(2)}, u32[]{:S(2)}) collective-permute-start(f32[5,8,128]{2,1,0:T(8,128)S(1)} %get-tuple-element.61), channel_id=1, source_target_pairs={{0,4},{4,0},{8,12},{12,8},{16,20},{20,16},{24,28},{28,24},{1,5},{5... | collective-permute-start | bytes 61448 | tf_op jit(solution)/shard_map/ppermute | solution.py:719
  15.5 4.0 %collective-permute-start.6 = (f32[5,8,128]{2,1,0:T(8,128)S(1)}, f32[5,8,128]{2,1,0:T(8,128)S(1)}, u32[]{:S(2)}, u32[]{:S(2)}) collective-permute-start(f32[5,8,128]{2,1,0:T(8,128)S(1)} %get-tuple-element.62), channel_id=1, source_target_pairs={{0,3},{1,2},{2,1},{3,0},{4,7},{5,6},{6,5},{7,4},{8,11},{9,10},{10,... | collective-permute-start | bytes 61448 | tf_op jit(solution)/shard_map/ppermute | solution.py:720
  15.5 4.0 %collective-permute-start.7 = (f32[5,8,128]{2,1,0:T(8,128)S(1)}, f32[5,8,128]{2,1,0:T(8,128)S(1)}, u32[]{:S(2)}, u32[]{:S(2)}) collective-permute-start(f32[5,8,128]{2,1,0:T(8,128)S(1)} %get-tuple-element.63), channel_id=1, source_target_pairs={{0,1},{1,0},{2,3},{3,2},{4,5},{5,4},{6,7},{7,6},{8,9},{9,8},{10,11... | collective-permute-start | bytes 61448 | tf_op jit(solution)/shard_map/ppermute | solution.py:721
  19.6 6.6 %collective-permute-start.8 = (f32[5,8,128]{2,1,0:T(8,128)S(1)}, f32[5,8,128]{2,1,0:T(8,128)S(1)}, u32[]{:S(2)}, u32[]{:S(2)}) collective-permute-start(f32[5,8,128]{2,1,0:T(8,128)S(1)} %get-tuple-element.67), channel_id=1, source_target_pairs={{0,28},{4,8},{8,4},{12,16},{16,12},{20,24},{24,20},{28,0},{1,29},{... | collective-permute-start | bytes 61448 | tf_op jit(solution)/shard_map/ppermute | solution.py:718
  22.1 4.0 %collective-permute-start.9 = (f32[5,8,128]{2,1,0:T(8,128)S(1)}, f32[5,8,128]{2,1,0:T(8,128)S(1)}, u32[]{:S(2)}, u32[]{:S(2)}) collective-permute-start(f32[5,8,128]{2,1,0:T(8,128)S(1)} %get-tuple-element.68), channel_id=1, source_target_pairs={{0,4},{4,0},{8,12},{12,8},{16,20},{20,16},{24,28},{28,24},{1,5},{5... | collective-permute-start | bytes 61448 | tf_op jit(solution)/shard_map/ppermute | solution.py:719
  22.1 4.0 %collective-permute-start.10 = (f32[5,8,128]{2,1,0:T(8,128)S(1)}, f32[5,8,128]{2,1,0:T(8,128)S(1)}, u32[]{:S(2)}, u32[]{:S(2)}) collective-permute-start(f32[5,8,128]{2,1,0:T(8,128)S(1)} %get-tuple-element.69), channel_id=1, source_target_pairs={{0,3},{1,2},{2,1},{3,0},{4,7},{5,6},{6,5},{7,4},{8,11},{9,10},{10,... | collective-permute-start | bytes 61448 | tf_op jit(solution)/shard_map/ppermute | solution.py:720
  22.1 4.0 %collective-permute-start.11 = (f32[5,8,128]{2,1,0:T(8,128)S(1)}, f32[5,8,128]{2,1,0:T(8,128)S(1)}, u32[]{:S(2)}, u32[]{:S(2)}) collective-permute-start(f32[5,8,128]{2,1,0:T(8,128)S(1)} %get-tuple-element.70), channel_id=1, source_target_pairs={{0,1},{1,0},{2,3},{3,2},{4,5},{5,4},{6,7},{7,6},{8,9},{9,8},{10,11... | collective-permute-start | bytes 61448 | tf_op jit(solution)/shard_map/ppermute | solution.py:721
  26.2 6.5 %collective-permute-start.12 = (f32[5,8,128]{2,1,0:T(8,128)S(1)}, f32[5,8,128]{2,1,0:T(8,128)S(1)}, u32[]{:S(2)}, u32[]{:S(2)}) collective-permute-start(f32[5,8,128]{2,1,0:T(8,128)S(1)} %get-tuple-element.73), channel_id=1, source_target_pairs={{0,28},{4,8},{8,4},{12,16},{16,12},{20,24},{24,20},{28,0},{1,29},{... | collective-permute-start | bytes 61448 | tf_op jit(solution)/shard_map/ppermute | solution.py:718
  28.8 4.0 %collective-permute-start.13 = (f32[5,8,128]{2,1,0:T(8,128)S(1)}, f32[5,8,128]{2,1,0:T(8,128)S(1)}, u32[]{:S(2)}, u32[]{:S(2)}) collective-permute-start(f32[5,8,128]{2,1,0:T(8,128)S(1)} %get-tuple-element.74), channel_id=1, source_target_pairs={{0,4},{4,0},{8,12},{12,8},{16,20},{20,16},{24,28},{28,24},{1,5},{5... | collective-permute-start | bytes 61448 | tf_op jit(solution)/shard_map/ppermute | solution.py:719
  28.8 4.0 %collective-permute-start.14 = (f32[5,8,128]{2,1,0:T(8,128)S(1)}, f32[5,8,128]{2,1,0:T(8,128)S(1)}, u32[]{:S(2)}, u32[]{:S(2)}) collective-permute-start(f32[5,8,128]{2,1,0:T(8,128)S(1)} %get-tuple-element.75), channel_id=1, source_target_pairs={{0,3},{1,2},{2,1},{3,0},{4,7},{5,6},{6,5},{7,4},{8,11},{9,10},{10,... | collective-permute-start | bytes 61448 | tf_op jit(solution)/shard_map/ppermute | solution.py:720
  28.8 4.0 %collective-permute-start.15 = (f32[5,8,128]{2,1,0:T(8,128)S(1)}, f32[5,8,128]{2,1,0:T(8,128)S(1)}, u32[]{:S(2)}, u32[]{:S(2)}) collective-permute-start(f32[5,8,128]{2,1,0:T(8,128)S(1)} %get-tuple-element.76), channel_id=1, source_target_pairs={{0,1},{1,0},{2,3},{3,2},{4,5},{5,4},{6,7},{7,6},{8,9},{9,8},{10,11... | collective-permute-start | bytes 61448 | tf_op jit(solution)/shard_map/ppermute | solution.py:721
